TPU v7x, 32 devices: a whole 2x2x4 slice. The times are simulated.
32 devices in a mesh: seq: 4 (over x, core), tensor: 4 (over z), dp: 2 (over y).
Axes of the slice: x: 2, y: 2, z: 4, core: 2. Of those that a mesh axis runs over, the one named last changes fastest.
Arguments:
- ssm_input: bfloat16 [2, 1024, 4096], P('dp', 'seq', 'tensor'), may hold values from -6 to 6
- b_input: bfloat16 [2, 1024, 512], P('dp', 'seq', 'tensor'), may hold values from -0.125 to 0.125
- c_input: bfloat16 [2, 1024, 512], P('dp', 'seq', 'tensor'), may hold values from -0.125 to 0.125
- step_size: float32 [2, 64, 1024], P('dp', 'tensor', 'seq'), may hold values from 0 to 1024, as said below
- decay_rate: float32 [64], P('tensor'), may hold values from 0 to 1, as said below
- skip_gain: float32 [64], P('tensor'), may hold values from 0.5 to 2
- resets: int32 [2, 4], P('dp', 'seq'), may hold values 0 or 1
- out_grad: bfloat16 [2, 1024, 4096], P('dp', 'seq'), may hold values from -6 to 6
- out_weight: bfloat16 [4096, 4096], P(('seq', 'dp'), 'tensor'), may hold values from -0.09375 to 0.09375
Outputs:
- grad_input: bfloat16 [2, 1024, 4096], P('dp', 'seq', 'tensor')
- grad_b: float32 [2, 1024, 512], P('dp', 'seq', 'tensor')
- grad_c: float32 [2, 1024, 512], P('dp', 'seq', 'tensor')
- grad_weight: float32 [4096, 4096], P(('seq', 'dp'), 'tensor')
Inputs may be any that keep to these rules, and one draw needn't show every extreme that they name: `step_size`: positive per-position steps. `decay_rate`: positive per-head rates.
All inputs are finite; a program needn't handle non-finite values. No bound on the sum of `resets` on one device may be relied on, other than what follows from the above.
Results may differ from a plain program's by a relative error of at most 0.017.
Values may be sent and summed in bfloat16 or wider, within the bound.
No kernel may reach another device: no remote copies, remote signals or barrier semaphores. Data moves between devices by JAX's collectives and lax.ppermute only.
A program may use at most 128 MiB of HBM per device.

v0:
```python
import jax
import jax.numpy as jnp
from jax import lax
from jax.sharding import PartitionSpec as P

P_SIZE = 64
N = 128
Q = 256


def prefix(value, axis, join, neutral, backward):
    count, mine = (lax.axis_size(axis), lax.axis_index(axis))
    pieces = jax.tree.map(lambda part: lax.all_gather(part, axis), value)
    if backward:
        pieces = jax.tree.map(lambda part: part[::-1], pieces)
        mine = count - 1 - mine
    running = jax.tree.map(
        lambda part, zero: jnp.full_like(part, 0) + jnp.asarray(zero, part.dtype), value, neutral
    )

    def step(position, running):
        longer = join(running, jax.tree.map(lambda part: part[position], pieces))
        return jax.tree.map(lambda new, old: jnp.where(position < mine, new, old), longer, running)

    return lax.fori_loop(0, count - 1, step, running)


def contract(pattern, former, latter):
    return jnp.einsum(pattern, former, latter, preferred_element_type=jnp.float32)


def block_tables(step_rows, head_rates):
    log_decay = jnp.cumsum(-step_rows * head_rates[..., None], axis=-1)
    last_log = log_decay[..., -1:]
    damping = jnp.exp(last_log[..., 0])
    to_end = jnp.moveaxis(jnp.exp(last_log - log_decay), -1, 0)[..., None]
    from_start = jnp.moveaxis(jnp.exp(log_decay), -1, 0)[..., None]
    positions = jnp.arange(log_decay.shape[-1])
    causal = positions[:, None] >= positions[None, :]
    spread = log_decay[..., :, None] - log_decay[..., None, :]
    weights = jnp.where(causal, jnp.exp(jnp.minimum(spread, 0.0)), 0.0)
    return (damping, to_end, from_start, weights)


def block_sums(inputs, b_rows, c_rows, grad_rows, to_end, from_start):
    weighted_in = (inputs.astype(jnp.float32) * to_end).astype(jnp.bfloat16)
    weighted_grad = (grad_rows.astype(jnp.float32) * from_start).astype(jnp.bfloat16)
    carried = contract("qgkp,qgn->gkpn", weighted_in, b_rows)
    adjoint = contract("qgkp,qgn->gkpn", weighted_grad, c_rows)
    return (carried, adjoint, weighted_in, weighted_grad)


def block_grads(
    inputs,
    b_rows,
    c_rows,
    grad_rows,
    skip_rows,
    to_end,
    from_start,
    weights,
    weighted_in,
    weighted_grad,
    state_in,
    adjoint_out,
):
    scores = contract("ign,jgn->gij", c_rows, b_rows)
    mixing = (weights * scores[:, None]).astype(jnp.bfloat16)
    skip_term = skip_rows[None, :, :, None]
    output = (
        contract("gkij,jgkp->igkp", mixing, inputs)
        + from_start * contract("gkpn,ign->igkp", state_in, c_rows)
        + skip_term * inputs.astype(jnp.float32)
    )
    grad_in = (
        contract("gkij,igkp->jgkp", mixing, grad_rows)
        + to_end * contract("gkpn,jgn->jgkp", adjoint_out, b_rows)
        + skip_term * grad_rows.astype(jnp.float32)
    )
    products = contract("igkp,jgkp->gkij", grad_rows, inputs)
    paired = (weights * products).astype(jnp.bfloat16)
    grad_b = contract("gkij,ign->jgn", paired, c_rows) + contract(
        "jgkp,gkpn->jgn", weighted_in, adjoint_out
    )
    grad_c = contract("gkij,jgn->ign", paired, b_rows) + contract(
        "igkp,gkpn->ign", weighted_grad, state_in
    )
    return (output.astype(jnp.bfloat16), grad_in.astype(jnp.bfloat16), grad_b, grad_c)


def forward_step(running, sliced):
    kept, carried, damping = sliced
    state_in = kept * running
    return (damping[..., None, None] * state_in + carried, state_in)


def backward_step(running, sliced):
    kept, adjoint, damping = sliced
    return (kept * (damping[..., None, None] * running + adjoint), running)


def compose(earlier, following):
    return (earlier[0] * following[0], following[0][..., None, None] * earlier[1] + following[1])


def body(
    ssm_input, b_input, c_input, step_size, decay_rate, skip_gain, resets, out_grad, out_weight
):
    head_count = decay_rate.shape[0]
    length = ssm_input.shape[1]
    blocks = length // Q
    incoming = out_grad[0]
    columns = incoming
    head_total = jnp.dot(
        columns,
        lax.all_gather(out_weight, ("seq", "dp"), axis=0, tiled=True),
        preferred_element_type=jnp.float32,
    )
    head_grad = head_total.astype(jnp.bfloat16)
    inputs = ssm_input[0].reshape(blocks, Q, 1, head_count, P_SIZE)
    b_rows = b_input[0].reshape(blocks, Q, 1, N)
    c_rows = c_input[0].reshape(blocks, Q, 1, N)
    grad_rows = head_grad.reshape(blocks, Q, 1, head_count, P_SIZE)
    step_rows = step_size[0].reshape(1, head_count, blocks, Q).transpose(2, 0, 1, 3)
    head_rates = decay_rate.reshape(1, head_count)
    skip_rows = skip_gain.reshape(1, head_count)
    keep_rows = (1 - resets[0]).astype(jnp.float32)
    decays, to_end, from_start, weights = jax.vmap(block_tables, in_axes=(0, None))(
        step_rows, head_rates
    )
    carried, adjoint, weighted_in, weighted_grad = jax.vmap(block_sums)(
        inputs, b_rows, c_rows, grad_rows, to_end, from_start
    )
    zero_state = jnp.zeros((1, head_count, P_SIZE, N), jnp.float32)
    local_out, local_states = lax.scan(forward_step, zero_state, (keep_rows, carried, decays))
    local_back, local_adjoints = lax.scan(
        backward_step, zero_state, (keep_rows, adjoint, decays), reverse=True
    )
    factors = keep_rows[:, None, None] * decays
    through = jnp.prod(factors, axis=0)
    unit_gain = jnp.ones_like(through)
    through_before, state_before = prefix(
        (through, local_out), "seq", compose, (unit_gain, zero_state), False
    )
    through_after, adjoint_after = prefix(
        (through, local_back), "seq", compose, (unit_gain, zero_state), True
    )
    final_state, states = lax.scan(forward_step, state_before, (keep_rows, carried, decays))
    final_adjoint, adjoints = lax.scan(
        backward_step, adjoint_after, (keep_rows, adjoint, decays), reverse=True
    )
    output, grad_in, grad_b, grad_c = jax.vmap(
        block_grads, in_axes=(0, 0, 0, 0, None, 0, 0, 0, 0, 0, 0, 0)
    )(
        inputs,
        b_rows,
        c_rows,
        grad_rows,
        skip_rows,
        to_end,
        from_start,
        weights,
        weighted_in,
        weighted_grad,
        states.astype(jnp.bfloat16),
        adjoints.astype(jnp.bfloat16),
    )
    outputs = output.reshape(length, head_count * P_SIZE)
    columns = incoming
    grad_weight = lax.psum_scatter(
        jnp.einsum("ld,lh->dh", columns, outputs, preferred_element_type=jnp.float32).astype(
            jnp.bfloat16
        ),
        ("seq", "dp"),
        scatter_dimension=0,
        tiled=True,
    ).astype(jnp.float32)
    return (
        grad_in.reshape(1, length, head_count * P_SIZE),
        grad_b.reshape(1, length, N),
        grad_c.reshape(1, length, N),
        grad_weight,
    )


def solution(mesh):
    in_specs = (
        P("dp", "seq", "tensor"),
        P("dp", "seq", "tensor"),
        P("dp", "seq", "tensor"),
        P("dp", "tensor", "seq"),
        P("tensor"),
        P("tensor"),
        P("dp", "seq"),
        P("dp", "seq", None),
        P(("seq", "dp"), "tensor"),
    )
    out_specs = (
        P("dp", "seq", "tensor"),
        P("dp", "seq", "tensor"),
        P("dp", "seq", "tensor"),
        P(("seq", "dp"), "tensor"),
    )
    return jax.shard_map(body, mesh=mesh, in_specs=in_specs, out_specs=out_specs, check_vma=False)
```

profile of v0, /device:TPU:0, one launch (start us, length us, event | category | flops | bytes accessed | tf_op | source)
XLA Modules:
  0.0 215.7 jit_solution(6120209170817137466)
XLA Ops:
  11.6 1.3 copy.106
  13.8 1.9 convolution_add_fusion
  17.9 6.1 %all-gather = f32[4,1,16,1]{2,3,1,0:T(1,128)S(1)} all-gather(f32[1,1,16,1]{2,3,1,0:T(1,128)} %get-tuple-element.390), channel_id=2, replica_groups=mesh['seq'=4,'tensor'=4,'dp'=2] {'seq'}, dimensions={0}, use_global_device_ids=true | all-gather | bytes 320 | tf_op jit(solution)/shard_map/all_gather | solution.py:13
  24.9 0.9 fusion.40
  25.8 15.4 %all-gather.11.cloned.1.call-done = f32[64,64,128]{2,1,0:T(8,128)} async-done(((f32[16,64,128]{2,1,0:T(8,128)}), f32[64,64,128]{2,1,0:T(8,128)}) %all-gather.11.cloned.1.call-update) | async-done | bytes 2097168 | tf_op jit(solution)/shard_map/all_gather | solution.py:13
  41.2 3.6 %while.19 = (s32[]{:T(128)}, f32[1,16,64,128]{3,2,1,0:T(8,128)S(1)}, s32[]{:T(128)}, f32[4,1,16]{2,1,0:T(1,128)S(1)}, f32[4,1,16,64,128]{4,3,2,1,0:T(8,128)}, /*index=5*/s32[]{:T(128)}, s32[]{:T(128)}) while((s32[]{:T(128)}, f32[1,16,64,128]{3,2,1,0:T(8,128)S(1)}, s32[]{:T(128)}, f32[4,1,16]{2,1,0:T(1,128)S(1)}, ...), condition=%wide.region_6.7_spmd.clone, body=%wide.region_5.6_spmd.clone.sunk | while | flops 524292 | bytes 1573161 | solution.py:25
  41.2 1.2 fusion.61
  42.5 1.2 fusion.61
  43.7 1.2 fusion.61
  45.2 2.5 %fusion.21 = bf16[1,256,1,16,64]{1,4,3,2,0:T(8,128)(2,1)S(1)} fusion(f32[1,256,1,16,64]{1,4,3,2,0:T(8,128)S(1)} %fusion.12, bf16[256,16,64]{0,2,1:T(8,128)(2,1)S(1)} %bitcast.194, f32[256,256]{1,0:T(8,128)} %fusion.40, f32[16,256]{1,0:T(8,128)S(1)} %bitcast_add_fusion.2, pred[256,256]{1,0:T(8,128)(4,1)S(1)} %iota_compare_fusion, f32[16]{0:T(128)S(1)} %copy-done.11, ...), kind=kOutput, calls=%fused_computation.30 | convolution fusion | flops 140771328 | bytes 2965568 | tf_op jit(solution)/shard_map/vmap(gkij,jgkp->igkp)/dot_general | solution.py:29
  47.7 5.8 %convert_bitcast_fusion = bf16[4096,1024]{0,1:T(8,128)(2,1)} fusion(bf16[256,1024]{0,1:T(8,128)(2,1)S(1)} %bitcast.203, bf16[1,256,4096]{2,1,0:T(8,128)(2,1)S(1)} %copy-done), kind=kOutput, calls=%fused_computation.6 | convolution fusion | flops 2151677952 | bytes 11010048 | tf_op jit(solution)/shard_map/ld,lh->dh/dot_general | solution.py:171
  53.8 1.1 mul.273
  54.8 2.6 %copy.101 = f32[256,1024]{1,0:T(8,128)} copy(f32[256,1024]{0,1:T(8,128)} %bitcast.191) | data formatting | bytes 2097152 | tf_op jit(solution)/shard_map/vmap()/mul | solution.py:47
  57.4 40.2 %all-gather.7.cloned.1.call-done = bf16[4096,1024]{1,0:T(8,128)(2,1)} async-done(((bf16[512,1024]{1,0:T(8,128)(2,1)}), bf16[4096,1024]{1,0:T(8,128)(2,1)}) %all-gather.7.cloned.1.call-update) | async-done | bytes 8388624 | tf_op jit(solution)/shard_map/all_gather | solution.py:116
  97.6 6.9 %multiply_convert_fusion.20 = (bf16[256,1024]{1,0:T(8,128)(2,1)}, bf16[256,1024]{1,0:T(8,128)(2,1)}) fusion(f32[256,1024]{1,0:T(8,128)} %copy.101, bf16[4096,1024]{1,0:T(8,128)(2,1)} %all-gather.7.cloned.1.call-done, bf16[1,256,4096]{2,1,0:T(8,128)(2,1)S(1)} %copy-done), kind=kOutput, calls=%fused_computation.44 | convolution fusion | flops 2148532224 | bytes 12582912 | tf_op jit(solution)/shard_map/dot_general | solution.py:114
  104.5 1.2 copy.102
  105.7 1.1 fusion.22
  106.9 2.1 copy.93
  109.0 2.3 %copy.105 = f32[256,1024]{0,1:T(8,128)} copy(bf16[256,1024]{1,0:T(8,128)(2,1)} %get-tuple-element.393) | data formatting | bytes 1572864 | tf_op jit(solution)/shard_map/vmap()/convert_element_type | solution.py:47
  111.3 1.5 convolution_bitcast_fusion.2
  112.8 2.8 %convert_reduce_fusion = bf16[256,256]{1,0:T(8,128)(2,1)S(1)} fusion(bf16[256,16,64]{0,2,1:T(8,128)(2,1)} %bitcast.200, bf16[256,16,64]{0,2,1:T(8,128)(2,1)} %bitcast.196, f32[16,256]{1,0:T(8,128)S(1)} %bitcast_add_fusion.2, pred[256,256]{1,0:T(8,128)(4,1)S(1)} %iota_compare_fusion), kind=kOutput, calls=%fused_computation.7 | convolution fusion | flops 141492224 | bytes 1261568 | tf_op jit(solution)/shard_map/vmap(igkp,jgkp->gkij)/dot_general | solution.py:29
  116.5 55.9 %reduce-scatter.2.cloned.1.call-done = bf16[512,1024]{0,1:T(8,128)(2,1)} async-done(((bf16[4096,1024]{0,1:T(8,128)(2,1)}), bf16[512,1024]{0,1:T(8,128)(2,1)}) %reduce-scatter.2.cloned.1.call-update) | async-done | bytes 1048592 | tf_op jit(solution)/shard_map/reduce_scatter | solution.py:170
  172.4 2.6 %copy.113 = f32[512,1024]{1,0:T(8,128)} copy(bf16[512,1024]{0,1:T(8,128)(2,1)} %reduce-scatter.2.cloned.1.call-done) | data formatting | bytes 3145728
  174.9 22.1 %all-gather.9.cloned.1.call-done = f32[64,64,128]{2,1,0:T(8,128)} async-done(((f32[16,64,128]{2,1,0:T(8,128)}), f32[64,64,128]{2,1,0:T(8,128)}) %all-gather.9.cloned.1.call-update) | async-done | bytes 2097168 | tf_op jit(solution)/shard_map/all_gather | solution.py:13
  197.0 3.2 %rev.7 = f32[4,1,16,64,128]{4,3,2,1,0:T(8,128)} reverse(f32[4,1,16,64,128]{4,3,2,1,0:T(8,128)} %bitcast.193), dimensions={0} | reverse | bytes 4194304 | tf_op jit(solution)/shard_map/rev | solution.py:15
  200.2 3.7 %while.18 = (s32[]{:T(128)}, f32[1,16,64,128]{3,2,1,0:T(8,128)S(1)}, s32[]{:T(128)}, f32[4,1,16]{2,1,0:T(1,128)S(1)}, f32[4,1,16,64,128]{4,3,2,1,0:T(8,128)}, /*index=5*/s32[]{:T(128)}, s32[]{:T(128)}) while((s32[]{:T(128)}, f32[1,16,64,128]{3,2,1,0:T(8,128)S(1)}, s32[]{:T(128)}, f32[4,1,16]{2,1,0:T(1,128)S(1)}, ...), condition=%wide.region_3.4_spmd.clone, body=%wide.region_2.3_spmd.clone.sunk | while | flops 524292 | bytes 1573161 | solution.py:25
  200.2 1.2 fusion.60
  201.5 1.2 fusion.60
  202.7 1.2 fusion.60
  204.5 2.8 %fusion.20 = bf16[1,256,1,16,64]{1,4,3,2,0:T(8,128)(2,1)S(1)} fusion(f32[1,256,1,16,64]{1,4,3,2,0:T(8,128)S(1)} %fusion.10, bf16[256,16,64]{0,2,1:T(8,128)(2,1)} %bitcast.201, f32[256,256]{1,0:T(8,128)} %fusion.40, f32[16,256]{1,0:T(8,128)} %copy-done.9, pred[256,256]{1,0:T(8,128)(4,1)} %copy-done.8, f32[1,256,1,16,64]{1,4,3,2,0:T(8,128)} %bitcast.199, ...), kind=kOutput, calls=%fused_computation.29 | convolution fusion | flops 140509184 | bytes 3489856 | tf_op jit(solution)/shard_map/vmap(gkij,igkp->jgkp)/dot_general | solution.py:29
  207.3 1.0 copy.112
  208.3 0.9 fusion.24
  (66 shorter events, 9.7 us)
Async XLA Ops:
  7.2 40.5 %copy-start = (bf16[1,256,4096]{2,1,0:T(8,128)(2,1)S(1)}, bf16[1,256,4096]{2,1,0:T(8,128)(2,1)}, u32[]{:S(2)}) copy-start(bf16[1,256,4096]{2,1,0:T(8,128)(2,1)} %param.20) | copy-start | bytes 6291460
  7.2 17.7 %copy-start.5 = (bf16[1,256,128]{2,1,0:T(8,128)(2,1)S(1)}, bf16[1,256,128]{2,1,0:T(8,128)(2,1)}, u32[]{:S(2)}) copy-start(bf16[1,256,128]{2,1,0:T(8,128)(2,1)} %param.14) | copy-start | bytes 196612
  7.2 17.7 %copy-start.6 = (bf16[1,256,128]{2,1,0:T(8,128)(2,1)S(1)}, bf16[1,256,128]{2,1,0:T(8,128)(2,1)}, u32[]{:S(2)}) copy-start(bf16[1,256,128]{2,1,0:T(8,128)(2,1)} %param.15) | copy-start | bytes 196612
  7.2 34.0 %all-gather.11.cloned.1.call-start = ((), (), s32[]{:S(2)}) async-start(), calls=%async_computation.4 | async-start | bytes 2621440 | tf_op jit(solution)/shard_map/all_gather | solution.py:13
  12.9 32.3 %copy-start.4 = (bf16[1,256,1024]{1,2,0:T(8,128)(2,1)}, bf16[1,256,1024]{1,2,0:T(8,128)(2,1)S(1)}, u32[]{:S(2)}) copy-start(bf16[1,256,1024]{1,2,0:T(8,128)(2,1)S(1)} %copy.106) | copy-start | bytes 1572868
  13.0 0.9 copy-start.2
  15.8 81.8 %all-gather.7.cloned.1.call-start = ((), (), s32[]{:S(2)}) async-start(), calls=%async_computation.1 | async-start | bytes 9437184 | tf_op jit(solution)/shard_map/all_gather | solution.py:116
  16.5 155.8 %reduce-scatter.2.cloned.1.call-start = ((), (), s32[]{:S(2)}) async-start(), calls=%async_computation.2 | async-start | bytes 9437184 | tf_op jit(solution)/shard_map/reduce_scatter | solution.py:170
  24.1 88.7 %copy-start.8 = (pred[256,256]{1,0:T(8,128)(4,1)}, pred[256,256]{1,0:T(8,128)(4,1)S(1)}, u32[]{:S(2)}) copy-start(pred[256,256]{1,0:T(8,128)(4,1)S(1)} %iota_compare_fusion) | copy-start | bytes 196612
  24.9 87.9 %copy-start.9 = (f32[16,256]{1,0:T(8,128)}, f32[16,256]{1,0:T(8,128)S(1)}, u32[]{:S(2)}) copy-start(f32[16,256]{1,0:T(8,128)S(1)} %bitcast_add_fusion.2) | copy-start | bytes 49156
  24.9 20.0 %copy-start.7 = (f32[256,16]{0,1:T(8,128)S(1)}, f32[256,16]{0,1:T(8,128)}, u32[]{:S(2)}) copy-start(f32[256,16]{0,1:T(8,128)} %copy.100) | copy-start | bytes 49156
  41.2 3.9 %copy-start.11 = (f32[16]{0:T(128)S(1)}, f32[16]{0:T(128)}, u32[]{:S(2)}) copy-start(f32[16]{0:T(128)} %param.18) | copy-start | bytes 196
  53.5 143.5 %all-gather.9.cloned.1.call-start = ((), (), s32[]{:S(2)}) async-start(), calls=%async_computation.3 | async-start | bytes 2621440 | tf_op jit(solution)/shard_map/all_gather | solution.py:13
  57.4 48.4 %copy-start.10 = (f32[16]{0:T(128)S(1)}, f32[16]{0:T(128)}, u32[]{:S(2)}) copy-start(f32[16]{0:T(128)} %get-tuple-element.389) | copy-start | bytes 196
  105.7 1.1 copy-start.1
  200.2 4.0 %copy-start.3 = (bf16[1,256,1024]{1,2,0:T(8,128)(2,1)S(1)}, bf16[1,256,1024]{1,2,0:T(8,128)(2,1)}, u32[]{:S(2)}) copy-start(bf16[1,256,1024]{1,2,0:T(8,128)(2,1)} %copy-done.2) | copy-start | bytes 1572868
Sparse Core Ops, SparseCore 0:
  15.9 25.2 all-gather.10
  43.1 54.4 all-gather.6
  101.0 71.2 reduce-scatter.1
  174.4 22.5 all-gather.8
where the time goes:
time: 217 us; the launch traced here: 216 us
  waiting for transfers between devices  134 us (62%)
  matrix products  28.9 us (13%)
  local copies, waits for them, and re-layouts  19.9 us (9%)
  between operations  14.7 us (7%)
  other arithmetic  11.3 us (5%)
  blocking collectives  6.14 us (3%)
    reduce_scatter x1, waiting for transfers between devices, body(): lax.psum_scatter(jnp.einsum('ld,lh->dh', columns, outputs, preferred_elem...  55.9 us
    all_gather x1, waiting for transfers between devices, body(): lax.all_gather(out_weight, ('seq', 'dp'), axis=0, tiled=True)  40.2 us
    all_gather x2, waiting for transfers between devices, prefix(): pieces = jax.tree.map(lambda part: lax.all_gather(part, axis), value)  37.5 us
    dot_general x12, matrix products, contract(): jnp.einsum(pattern, former, latter, preferred_element_type=jnp.float32)  16.2 us
    select_n x6, other arithmetic, step(): jnp.where(position < mine, new, old)  7.1 us
    dot_general x1, matrix products, body(): jnp.dot(columns, lax.all_gather(out_weight, ('seq', 'dp'), axis=0, tiled=...  6.91 us
    all_gather x1, blocking collectives, prefix(): pieces = jax.tree.map(lambda part: lax.all_gather(part, axis), value)  6.14 us
    dot_general x1, matrix products, body(): jnp.einsum('ld,lh->dh', columns, outputs, preferred_element_type=jnp.floa...  5.8 us
  transfers between devices with their start and end apart: 4, of which 4 were waited for; matrix products, arithmetic and copies ran while one was open for 19% of the time, Pallas kernels for 0%

commit v1 on v0

v1 whole, which is shorter than its diff:
```python
import functools

import jax
import jax.numpy as jnp
from jax import lax
from jax.experimental import pallas as pl
from jax.experimental.pallas import tpu as pltpu
from jax.sharding import PartitionSpec as P

P_SIZE = 64
N = 128
Q = 256
HALF = 128
PAIR = 2 * P_SIZE
CHUNKS = 2
BF = jnp.bfloat16
F32 = jnp.float32

VMEM = pl.BlockSpec(memory_space=pltpu.VMEM)
SMEM = pl.BlockSpec(memory_space=pltpu.SMEM)


def call(kernel, args, outs, flops=0, scalars=0, mib=24):
    out_shape = [jax.ShapeDtypeStruct(shape, kind) for shape, kind in outs]
    moved = sum(a.size * a.dtype.itemsize for a in list(args) + out_shape)
    return pl.pallas_call(
        kernel,
        out_shape=out_shape,
        in_specs=[SMEM] * scalars + [VMEM] * (len(args) - scalars),
        out_specs=[VMEM] * len(outs),
        cost_estimate=pl.CostEstimate(flops=flops, bytes_accessed=moved, transcendentals=0),
        compiler_params=pltpu.CompilerParams(vmem_limit_bytes=mib * 2**20),
    )(*args)


def dot(a, b, left, right):
    return lax.dot_general(a, b, (((left,), (right,)), ((), ())), preferred_element_type=F32)


def first_head(rows=Q):
    return lax.broadcasted_iota(jnp.int32, (rows, PAIR), 1) < P_SIZE


def spread(table, pair, first):
    return jnp.where(first, table[:, 2 * pair : 2 * pair + 1], table[:, 2 * pair + 1 : 2 * pair + 2])


def gains(skip_ref, head):
    first = lax.broadcasted_iota(jnp.int32, (1, PAIR), 1) < P_SIZE
    return jnp.where(first, skip_ref[head], skip_ref[head + 1])


def tables_kernel(rate_ref, x_ref, b_ref, step_ref, state_ref, weighted_ref, rows_ref, cols_ref, decay_ref):
    heads = step_ref.shape[0]
    head_id = lax.broadcasted_iota(jnp.int32, (heads, Q), 0)
    lane = lax.broadcasted_iota(jnp.int32, (heads, Q), 1)
    rate = jnp.zeros((heads, Q), F32)
    for head in range(heads):
        rate = jnp.where(head_id == head, rate_ref[head], rate)
    log = -step_ref[...] * rate
    shift = 1
    while shift < Q:
        log = log + jnp.where(lane >= shift, pltpu.roll(log, shift, 1), 0.0)
        shift *= 2
    rows_ref[...] = log
    cols = log.T
    cols_ref[...] = cols
    first = first_head()
    for pair in range(heads // 2):
        at = slice(pair * PAIR, (pair + 1) * PAIR)
        log_pair = spread(cols, pair, first)
        last = log_pair[Q - 1 : Q, :]
        weighted_ref[:, at] = (x_ref[:, at].astype(F32) * jnp.exp(last - log_pair)).astype(BF)
        decay_ref[:, at] = jnp.broadcast_to(jnp.exp(last), (8, PAIR))
    state_ref[...] = dot(b_ref[...], weighted_ref[...], 0, 0)


def local_output_kernel(skip_ref, x_ref, b_ref, c_ref, rows_ref, cols_ref, out_ref):
    heads = rows_ref.shape[0]
    scores = dot(c_ref[...], b_ref[...], 1, 1)
    at_row = lax.broadcasted_iota(jnp.int32, (HALF, HALF), 0)
    at_lane = lax.broadcasted_iota(jnp.int32, (HALF, HALF), 1)
    causal = at_row >= at_lane
    first = first_head()
    zero = jnp.zeros((Q, PAIR), BF)
    for pair in range(heads // 2):
        at = slice(pair * PAIR, (pair + 1) * PAIR)
        x_pair = x_ref[:, at]
        skip = gains(skip_ref, 2 * pair) * x_pair.astype(F32)
        top, bottom = skip[:HALF], skip[HALF:]
        for side in range(2):
            head = 2 * pair + side
            x_head = jnp.where(first, x_pair, zero) if side == 0 else jnp.where(first, zero, x_pair)
            col = cols_ref[:, head : head + 1]
            row = rows_ref[head : head + 1, :]

            def mix(i, j):
                span = col[i * HALF : (i + 1) * HALF] - row[:, j * HALF : (j + 1) * HALF]
                weight = jnp.exp(jnp.minimum(span, 0.0))
                if i == j:
                    weight = jnp.where(causal, weight, 0.0)
                return (weight * scores[i * HALF : (i + 1) * HALF, j * HALF : (j + 1) * HALF]).astype(BF)

            top += dot(mix(0, 0), x_head[:HALF], 1, 0)
            bottom += dot(jnp.concatenate([mix(1, 0), mix(1, 1)], axis=1), x_head, 1, 0)
        out_ref[:HALF, at] = top
        out_ref[HALF:, at] = bottom


def output_kernel(local_ref, c_ref, cols_ref, state_ref, out_ref):
    first = first_head()
    cols = cols_ref[...]
    for pair in range(out_ref.shape[1] // PAIR):
        at = slice(pair * PAIR, (pair + 1) * PAIR)
        term = dot(c_ref[...], state_ref[:, at], 1, 0)
        out_ref[:, at] = (local_ref[:, at] + jnp.exp(spread(cols, pair, first)) * term).astype(BF)


def head_partial_kernel(blocks, index_ref, *refs):
    grads, weights, outs = refs[: -blocks - 0], None, None
    count = (len(refs) - blocks) // 2
    grads, weights, outs = refs[:count], refs[count : count + blocks], refs[count + blocks :]
    depth = weights[0].shape[0]
    for number in reversed(range(count)):
        total = None
        for block in range(blocks):
            columns = pl.ds(pl.multiple_of(index_ref[block] * depth, depth), depth)
            term = dot(grads[number][:, columns], weights[block][...], 1, 0)
            total = term if total is None else total + term
        outs[number][...] = total.astype(outs[number].dtype)


def adjoint_kernel(others, own_ref, *refs):
    parts, (c_ref, cols_ref, head_ref, weighted_ref, adjoint_ref) = refs[:others], refs[others:]
    first = first_head()
    cols = cols_ref[...]
    for pair in range(head_ref.shape[1] // PAIR):
        at = slice(pair * PAIR, (pair + 1) * PAIR)
        total = own_ref[:, at]
        for part in parts:
            total = total + part[:, at].astype(F32)
        head = total.astype(BF)
        head_ref[:, at] = head
        weighted_ref[:, at] = (head.astype(F32) * jnp.exp(spread(cols, pair, first))).astype(BF)
    adjoint_ref[...] = dot(c_ref[...], weighted_ref[...], 0, 0)


def local_grads_kernel(
    skip_ref, x_ref, grad_ref, b_ref, c_ref, rows_ref, cols_ref, weighted_ref, state_ref, in_ref, paired_ref, c_out_ref
):
    heads = rows_ref.shape[0]
    scores = dot(b_ref[...], c_ref[...], 1, 1)
    at_row = lax.broadcasted_iota(jnp.int32, (HALF, HALF), 0)
    at_lane = lax.broadcasted_iota(jnp.int32, (HALF, HALF), 1)
    causal = at_lane >= at_row
    first = first_head()
    zero = jnp.zeros((Q, PAIR), BF)
    paired_ref[...] = jnp.zeros_like(paired_ref)
    for pair in range(heads // 2):
        at = slice(pair * PAIR, (pair + 1) * PAIR)
        x_pair = x_ref[:, at]
        g_pair = grad_ref[:, at]
        skip = gains(skip_ref, 2 * pair) * g_pair.astype(F32)
        top, bottom = skip[:HALF], skip[HALF:]
        for side in range(2):
            head = 2 * pair + side
            g_head = jnp.where(first, g_pair, zero) if side == 0 else jnp.where(first, zero, g_pair)
            col = cols_ref[:, head : head + 1]
            row = rows_ref[head : head + 1, :]

            def weigh(j, i):
                span = row[:, i * HALF : (i + 1) * HALF] - col[j * HALF : (j + 1) * HALF]
                weight = jnp.exp(jnp.minimum(span, 0.0))
                return jnp.where(causal, weight, 0.0) if i == j else weight

            early = jnp.concatenate([weigh(0, 0), weigh(0, 1)], axis=1)
            late = weigh(1, 1)
            top += dot((early * scores[:HALF]).astype(BF), g_head, 1, 0)
            bottom += dot((late * scores[HALF:, HALF:]).astype(BF), g_head[HALF:], 1, 0)
            paired_ref[:HALF, :] += early * dot(x_pair[:HALF], g_head, 1, 1)
            paired_ref[HALF:, HALF:] += late * dot(x_pair[HALF:], g_head[HALF:], 1, 1)
        in_ref[:HALF, at] = top
        in_ref[HALF:, at] = bottom
    c_out_ref[...] = dot(weighted_ref[...], state_ref[...], 1, 1)


def final_kernel(parts, *refs):
    b_ref, c_ref, cols_ref, weighted_ref = refs[:4]
    locals_, pairs, c_parts, adjoints = (refs[4 + i * parts : 4 + (i + 1) * parts] for i in range(4))
    in_ref, grad_b_ref, grad_c_ref = refs[4 + 4 * parts :]
    first = first_head()
    cols = cols_ref[...]
    paired = functools.reduce(jnp.add, [ref[...] for ref in pairs]).astype(BF)
    grad_b = dot(paired, c_ref[...], 1, 0)
    grad_c = dot(paired, b_ref[...], 0, 0)
    for part in range(parts):
        grad_c += c_parts[part][...]
        width = locals_[part].shape[1]
        grad_b += dot(weighted_ref[:, part * width : (part + 1) * width], adjoints[part][...], 1, 1)
        for number in range(width // PAIR):
            at = slice(number * PAIR, (number + 1) * PAIR)
            pair = part * (width // PAIR) + number
            whole = slice(pair * PAIR, (pair + 1) * PAIR)
            log_pair = spread(cols, pair, first)
            to_end = jnp.exp(log_pair[Q - 1 : Q, :] - log_pair)
            term = dot(b_ref[...], adjoints[part][:, at], 1, 0)
            in_ref[:, whole] = (locals_[part][:, at] + to_end * term).astype(BF)
    grad_b_ref[...] = grad_b
    grad_c_ref[...] = grad_c


def weight_partial_kernel(count, index_ref, *refs):
    grads, outputs, (sent_ref, kept_ref) = refs[:count], refs[count : 2 * count], refs[2 * count :]
    depth = sent_ref.shape[0]
    for slot, target in ((1, sent_ref), (0, kept_ref)):
        columns = pl.ds(pl.multiple_of(index_ref[slot] * depth, depth), depth)
        total = None
        for grad, output in zip(grads, outputs):
            term = dot(grad[:, columns], output[...], 0, 0)
            total = term if total is None else total + term
        target[...] = total.astype(target.dtype)


def body(
    ssm_input, b_input, c_input, step_size, decay_rate, skip_gain, resets, out_grad, out_weight
):
    seq, dp = lax.axis_size("seq"), lax.axis_size("dp")
    chips = seq // 2
    me, dialogue = lax.axis_index("seq"), lax.axis_index("dp")
    chip, core = me // 2, me % 2
    heads = decay_rate.shape[0]
    wide = heads * P_SIZE
    width = wide // CHUNKS
    chunk_heads = heads // CHUNKS
    depth = out_weight.shape[0]
    span = 2 * dp * depth
    assert ssm_input.shape[1] == Q and dp == 2 and seq % 2 == 0

    across = [(i, i ^ 1) for i in range(seq)]

    def core_swap(value):
        return lax.ppermute(value, "seq", across)

    def chip_shift(value, by):
        return lax.ppermute(value, "seq", [(i, (i + 2 * by) % seq) for i in range(seq)])

    def dialogue_swap(value):
        return lax.ppermute(value, "dp", [(0, 1), (1, 0)])

    x, b_rows, c_rows, steps, incoming = (
        ssm_input[0], b_input[0], c_input[0], step_size[0], out_grad[0]
    )
    keep = (1 - resets[0, 0]).astype(F32)
    chunk = lambda value, part: value[:, part * width : (part + 1) * width]

    weights = []
    for part in range(CHUNKS):
        own = chunk(out_weight, part)
        other = dialogue_swap(own)
        weights.append([own, other, core_swap(own), core_swap(other)])
    rows_of = [core * dp + dialogue, core * dp + 1 - dialogue, (1 - core) * dp + dialogue, (1 - core) * dp + 1 - dialogue]
    weight_index = jnp.stack(rows_of).astype(jnp.int32)

    own_columns = lax.dynamic_slice_in_dim(incoming, chip * span, span, axis=1)
    columns = [own_columns]
    for by in range(1, chips):
        there = (chip + by) % chips
        columns.append(chip_shift(lax.dynamic_slice_in_dim(incoming, there * span, span, axis=1), by))

    state, weighted_in, log_rows, log_cols, decay = call(
        tables_kernel,
        (decay_rate, x, b_rows, steps),
        [((N, wide), F32), ((Q, wide), BF), ((heads, Q), F32), ((Q, heads), F32), ((8, wide), F32)],
        scalars=1,
    )
    through = keep * decay[:1]
    entering = jnp.zeros((N, wide), BF)
    for hop in range(chips):
        leaving = through * entering.astype(F32) + state
        from_even = core_swap(leaving.astype(BF))
        if hop < chips - 1:
            total = (through * from_even.astype(F32) + state).astype(BF)
            entering = lax.ppermute(
                total, "seq", [(2 * i + 1, 2 * i + 2) for i in range(chips - 1)]
            )
    state_in = (keep * jnp.where(core == 1, from_even, entering).astype(F32)).astype(BF)
    local_output, = call(
        local_output_kernel,
        (skip_gain, x, b_rows, c_rows, log_rows, log_cols),
        [((Q, wide), F32)],
        flops=2 * heads * Q * Q * P_SIZE,
        scalars=1,
    )
    outputs = []
    for part in range(CHUNKS):
        cols = log_cols[:, part * chunk_heads : (part + 1) * chunk_heads]
        output, = call(
            output_kernel,
            (chunk(local_output, part), c_rows, cols, chunk(state_in, part)),
            [((Q, width), BF)],
            flops=2 * Q * N * width,
        )
        mine = [output] + [chip_shift(output, by) for by in range(1, chips)]
        outputs.append(mine + [core_swap(piece) for piece in mine])

    half = dp * depth
    own_half = [lax.dynamic_slice_in_dim(piece, core * half, half, axis=1) for piece in columns]
    other_half = [
        core_swap(lax.dynamic_slice_in_dim(piece, (1 - core) * half, half, axis=1)) for piece in columns
    ]
    dialogue_index = jnp.stack([dialogue, 1 - dialogue]).astype(jnp.int32)
    weight_grads = []
    for part in range(CHUNKS):
        sent, kept = call(
            functools.partial(weight_partial_kernel, 2 * chips),
            (dialogue_index, *own_half, *other_half, *outputs[part]),
            [((depth, width), BF), ((depth, width), F32)],
            flops=2 * seq * Q * half * width,
            scalars=1,
        )
        weight_grads.append(kept + dialogue_swap(sent).astype(F32))
    grad_weight = jnp.concatenate(weight_grads, axis=1)

    locals_, pairs, c_parts, adjoints_out = [], [], [], []
    for part in range(CHUNKS):
        partials = call(
            functools.partial(head_partial_kernel, len(weights[part])),
            (weight_index, *columns, *weights[part]),
            [((Q, width), F32)] + [((Q, width), BF)] * (chips - 1),
            flops=2 * chips * Q * span * width,
            scalars=1,
        )
        returned = [chip_shift(partials[by], -by) for by in range(1, chips)]
        cols = log_cols[:, part * chunk_heads : (part + 1) * chunk_heads]
        rows = log_rows[part * chunk_heads : (part + 1) * chunk_heads]
        head_grad, weighted_grad, adjoint = call(
            functools.partial(adjoint_kernel, chips - 1),
            (partials[0], *returned, c_rows, cols),
            [((Q, width), BF), ((Q, width), BF), ((N, width), F32)],
            flops=2 * Q * N * width,
        )
        decayed = chunk(decay[:1], part)
        entering = jnp.zeros((N, width), BF)
        for hop in range(chips):
            leaving = keep * (decayed * entering.astype(F32) + adjoint)
            from_odd = core_swap(leaving.astype(BF))
            if hop < chips - 1:
                total = (keep * (decayed * from_odd.astype(F32) + adjoint)).astype(BF)
                entering = lax.ppermute(
                    total, "seq", [(2 * i + 2, 2 * i + 1) for i in range(chips - 1)]
                )
        adjoints_out.append(jnp.where(core == 0, from_odd, entering))
        local_in, paired, c_part = call(
            local_grads_kernel,
            (
                skip_gain[part * chunk_heads : (part + 1) * chunk_heads],
                chunk(x, part),
                head_grad,
                b_rows,
                c_rows,
                rows,
                cols,
                weighted_grad,
                chunk(state_in, part),
            ),
            [((Q, width), F32), ((Q, Q), F32), ((Q, N), F32)],
            flops=4 * chunk_heads * Q * Q * P_SIZE,
            scalars=1,
        )
        locals_.append(local_in)
        pairs.append(paired)
        c_parts.append(c_part)
    grad_in, grad_b, grad_c = call(
        functools.partial(final_kernel, CHUNKS),
        (b_rows, c_rows, log_cols, weighted_in, *locals_, *pairs, *c_parts, *adjoints_out),
        [((Q, wide), BF), ((Q, N), F32), ((Q, N), F32)],
        flops=4 * Q * N * wide,
    )
    return grad_in[None], grad_b[None], grad_c[None], grad_weight


def solution(mesh):
    in_specs = (
        P("dp", "seq", "tensor"),
        P("dp", "seq", "tensor"),
        P("dp", "seq", "tensor"),
        P("dp", "tensor", "seq"),
        P("tensor"),
        P("tensor"),
        P("dp", "seq"),
        P("dp", "seq", None),
        P(("seq", "dp"), "tensor"),
    )
    out_specs = (
        P("dp", "seq", "tensor"),
        P("dp", "seq", "tensor"),
        P("dp", "seq", "tensor"),
        P(("seq", "dp"), "tensor"),
    )
    return jax.shard_map(body, mesh=mesh, in_specs=in_specs, out_specs=out_specs, check_vma=False)
```

time: 217 us -> 117 us (0.54)
  waiting for transfers between devices: 134 us -> 38.9 us
  starting transfers between devices: 0.34 us -> 36.3 us
  matrix products: 28.9 us -> 0 us
  Pallas kernels: 0 us -> 19.3 us
  between operations: 14.7 us -> 1.87 us
  local copies, waits for them, and re-layouts: 19.9 us -> 11.6 us
  blocking collectives: 6.14 us -> 0 us
  other arithmetic: 11.3 us -> 9.09 us
    all_gather x3 -> x0, waiting for transfers between devices: 77.7 us -> none  [the longest x1 40.2 us: body(): lax.all_gather(out_weight, ('seq', 'dp'), axis=0, tiled=True)]
    reduce_scatter x1 -> x0, waiting for transfers between devices: 55.9 us -> none  [body(): lax.psum_scatter(jnp.einsum('ld,lh->dh', columns, outputs, preferred_elem...]
    ppermute x0 -> x28, waiting for transfers between devices: none -> 38.9 us  [the longest x4 19.4 us: dialogue_swap(): return lax.ppermute(value, 'dp', [(0, 1), (1, 0)])]
    ppermute x0 -> x28, starting transfers between devices: none -> 36.3 us  [the longest x16 21.6 us: core_swap(): return lax.ppermute(value, 'seq', across)]
    dot_general x14 -> x0, matrix products: 28.9 us -> none  [the longest x12 16.2 us: contract(): jnp.einsum(pattern, former, latter, preferred_element_type=jnp.float32)]
    pallas_call x0 -> x13, Pallas kernels: none -> 19.3 us  [call(): pl.pallas_call(kernel, out_shape=out_shape, in_specs=[SMEM] * scalars + [...]
    select_n x6 -> x2, other arithmetic: 7.1 us -> 0.03 us  [body(): adjoints_out.append(jnp.where(core == 0, from_odd, entering))]
    all_gather x1 -> x0, blocking collectives: 6.14 us -> none  [prefix(): pieces = jax.tree.map(lambda part: lax.all_gather(part, axis), value)]
  transfers between devices with their start and end apart: 4 -> 28, of which waited for: 4 -> 6; matrix products, arithmetic and copies ran while one was open for 19% -> 13% of each run, Pallas kernels for 0% -> 16%
where the time goes in v1:
time: 117 us
  waiting for transfers between devices  38.9 us (33%)
  starting transfers between devices  36.3 us (31%)
  Pallas kernels  19.3 us (16%)
  local copies, waits for them, and re-layouts  11.6 us (10%)
  other arithmetic  9.09 us (8%)
  between operations  1.87 us (2%)
    ppermute x16, starting transfers between devices, core_swap(): return lax.ppermute(value, 'seq', across)  21.6 us
    ppermute x4, waiting for transfers between devices, dialogue_swap(): return lax.ppermute(value, 'dp', [(0, 1), (1, 0)])  19.4 us
    pallas_call x13, Pallas kernels, call(): pl.pallas_call(kernel, out_shape=out_shape, in_specs=[SMEM] * scalars + [...  19.3 us
    ppermute x5, waiting for transfers between devices, chip_shift(): lax.ppermute(value, 'seq', [(i, (i + 2 * by) % seq) for i in range(seq)])  17.5 us
    ppermute x5, starting transfers between devices, chip_shift(): lax.ppermute(value, 'seq', [(i, (i + 2 * by) % seq) for i in range(seq)])  6.3 us
    ppermute x4, starting transfers between devices, dialogue_swap(): return lax.ppermute(value, 'dp', [(0, 1), (1, 0)])  5.62 us
    dynamic_slice x2, local copies, waits for them, and re-layouts, body(): lax.dynamic_slice_in_dim(piece, (1 - core) * half, half, axis=1)  2.98 us
    dynamic_slice x1, local copies, waits for them, and re-layouts, body(): lax.dynamic_slice_in_dim(incoming, there * span, span, axis=1)  2.76 us
  transfers between devices with their start and end apart: 28, of which 6 were waited for; matrix products, arithmetic and copies ran while one was open for 13% of the time, Pallas kernels for 16%

profile of v1, /device:TPU:0, one launch (start us, length us, event | category | flops | bytes accessed | tf_op | source)
XLA Modules:
  0.0 117.0 jit_solution(9802482419864903204)
XLA Ops:
  0.6 2.3 %fusion.1 = (bf16[512,512]{1,0:T(8,128)(2,1)}, bf16[512,512]{1,0:T(8,128)(2,1)}) fusion(bf16[512,1024]{1,0:T(8,128)(2,1)} %param.17), kind=kLoop, calls=%fused_computation.28 | loop fusion | bytes 2097152 | tf_op jit(solution)/shard_map/slice | solution.py:254
  2.9 3.0 %collective-permute-start.1 = (bf16[512,512]{1,0:T(8,128)(2,1)}, bf16[512,512]{1,0:T(8,128)(2,1)}, u32[]{:S(2)}, u32[]{:S(2)}) collective-permute-start(bf16[512,512]{1,0:T(8,128)(2,1)} %get-tuple-element.69.refs_2_), channel_id=1, source_target_pairs={{0,1},{1,0},{2,3},{3,2},{4,5},{5,4},{6,7},{7,6},{8,9},{9,8},{10,11... | collective-permute-start | bytes 1572872 | tf_op jit(solution)/shard_map/ppermute | solution.py:248
  5.9 2.8 %dynamic-slice_bitcast_fusion = (bf16[256,2048]{1,0:T(8,128)(2,1)}, bf16[256,2048]{1,0:T(8,128)(2,1)S(1)}) fusion(bf16[1,256,4096]{2,1,0:T(8,128)(2,1)} %param.16, s32[]{:T(128)S(6)} %select_n.59, s32[]{:T(128)S(6)} %select_n.57), kind=kLoop, calls=%fused_computation.3 | loop fusion | bytes 4194312 | tf_op jit(solution)/shard_map/dynamic_slice | solution.py:268
  8.7 1.5 %collective-permute-start = (bf16[256,2048]{1,0:T(8,128)(2,1)}, bf16[256,2048]{1,0:T(8,128)(2,1)S(1)}, u32[]{:S(2)}, u32[]{:S(2)}) collective-permute-start(bf16[256,2048]{1,0:T(8,128)(2,1)} %get-tuple-element.62), channel_id=1, source_target_pairs={{0,16},{8,24},{16,0},{24,8},{1,17},{9,25},{17,1},{25,9},{2,18},{10... | collective-permute-start | bytes 3145736 | tf_op jit(solution)/shard_map/ppermute | solution.py:245
  10.9 2.2 %shard_map.120 = (f32[128,1024]{1,0:T(8,128)S(1)}, bf16[256,1024]{1,0:T(8,128)(2,1)S(1)}, f32[16,256]{1,0:T(8,128)S(1)}, f32[256,16]{1,0:T(8,128)S(1)}, f32[8,1024]{1,0:T(8,128)S(1)}) custom-call(f32[16]{0:T(128)S(1)} %copy-done.15, bf16[256,1024]{1,0:T(8,128)(2,1)S(1)} %bitcast.25, bf16[256,128]{1,0:T(8,128)(2,1)S(1)} %bitcast.36, f32[16,256]{1,0:T(8,128)S(1)} %bitcast.41), custom_call_target="tpu_custom_call" | custom-call | bytes 1720384 | tf_op jit(solution)/shard_map/pallas_call | solution.py:26
  17.8 2.9 %dynamic-slice_bitcast_fusion.2 = (bf16[256,1024]{1,0:T(8,128)(2,1)}, bf16[256,1024]{1,0:T(8,128)(2,1)}) fusion(bf16[1,256,4096]{2,1,0:T(8,128)(2,1)} %param.16, s32[]{:T(128)S(6)} %dynamic_slice.38, s32[]{:T(128)S(6)} %dynamic_slice.34), kind=kLoop, calls=%fused_computation.5 | loop fusion | bytes 2097160 | tf_op jit(solution)/shard_map/dynamic_slice | solution.py:309
  22.0 1.7 %add_convert_fusion.1 = bf16[128,1024]{1,0:T(8,128)(2,1)} fusion(f32[128,1024]{1,0:T(8,128)S(1)} %get-tuple-element.40, bf16[128,1024]{1,0:T(8,128)(2,1)} %collective-permute-done.5, f32[1024]{0:T(1024)} %bitcast.43), kind=kLoop, calls=%fused_computation.9 | loop fusion | flops 524288 | bytes 1052672 | tf_op jit(solution)/shard_map/convert_element_type | solution.py:282
  23.8 1.4 %collective-permute-start.6 = (bf16[128,1024]{1,0:T(8,128)(2,1)}, bf16[128,1024]{1,0:T(8,128)(2,1)}, u32[]{:S(2)}, u32[]{:S(2)}) collective-permute-start(bf16[128,1024]{1,0:T(8,128)(2,1)} %add_convert_fusion.1), channel_id=1, source_target_pairs={{8,16},{9,17},{10,18},{11,19},{12,20},{13,21},{14,22},{15,23}} | collective-permute-start | bytes 786440 | tf_op jit(solution)/shard_map/ppermute | solution.py:283
  26.4 1.7 %shard_map.128 = f32[256,1024]{1,0:T(8,128)S(1)} custom-call(f32[16]{0:T(128)S(1)} %copy-done.12, bf16[256,1024]{1,0:T(8,128)(2,1)S(1)} %bitcast.27, bf16[256,128]{1,0:T(8,128)(2,1)S(1)} %bitcast.37, bf16[256,128]{1,0:T(8,128)(2,1)S(1)} %bitcast.28, f32[16,256]{1,0:T(8,128)S(1)} %get-tuple-element.37.rows_ref, f32[256,16]{1,0:T(8,128)S(1)} %get-tuple-element.32.refs_2_.cols_ref), custom_call_target="tpu_custom_call" | custom-call | flops 134217728 | bytes 1736768 | tf_op jit(solution)/shard_map/pallas_call | solution.py:26
  28.1 1.7 %collective-permute-start.3 = (bf16[512,512]{1,0:T(8,128)(2,1)}, bf16[512,512]{1,0:T(8,128)(2,1)S(1)}, u32[]{:S(2)}, u32[]{:S(2)}) collective-permute-start(bf16[512,512]{1,0:T(8,128)(2,1)} %collective-permute-done.1.refs_3_), channel_id=1, source_target_pairs={{0,8},{8,0},{16,24},{24,16},{1,9},{9,1},{17,25},{25,17},{2,10},{10... | collective-permute-start | bytes 1572872 | tf_op jit(solution)/shard_map/ppermute | solution.py:242
  29.8 1.0 add_convert_fusion
  30.9 6.7 %collective-permute-start.7 = (bf16[128,1024]{1,0:T(8,128)(2,1)S(1)}, bf16[128,1024]{1,0:T(8,128)(2,1)S(1)}, u32[]{:S(2)}, u32[]{:S(2)}) collective-permute-start(bf16[128,1024]{1,0:T(8,128)(2,1)S(1)} %add_convert_fusion), channel_id=1, source_target_pairs={{0,8},{8,0},{16,24},{24,16},{1,9},{9,1},{17,25},{25,17},{2,10},{10... | collective-permute-start | bytes 786440 | tf_op jit(solution)/shard_map/ppermute | solution.py:242
  37.8 1.0 collective-permute-done.7
  39.1 1.0 multiply_convert_fusion
  40.3 2.6 %shard_map.121 = (f32[256,512]{1,0:T(8,128)S(1)}, bf16[256,512]{1,0:T(8,128)(2,1)S(1)}) custom-call(s32[4]{0:T(128)S(1)} %copy-done.10, bf16[256,2048]{1,0:T(8,128)(2,1)S(1)} %get-tuple-element.63.refs_0_, bf16[256,2048]{1,0:T(8,128)(2,1)S(1)} %collective-permute-done.refs_1_, bf16[512,512]{1,0:T(8,128)(2,1)} %get-tuple-element.69.refs_2_, ...), custom_call_target="tpu_custom_call" | custom-call | flops 1073741824 | bytes 4980752 | tf_op jit(solution)/shard_map/pallas_call | solution.py:26
  43.0 2.6 %collective-permute-start.4 = (bf16[256,512]{1,0:T(8,128)(2,1)S(1)}, bf16[256,512]{1,0:T(8,128)(2,1)S(1)}, u32[]{:S(2)}, u32[]{:S(2)}) collective-permute-start(bf16[256,512]{1,0:T(8,128)(2,1)S(1)} %get-tuple-element.35), channel_id=1, source_target_pairs={{0,16},{8,24},{16,0},{24,8},{1,17},{9,25},{17,1},{25,9},{2,18},{10... | collective-permute-start | bytes 786440 | tf_op jit(solution)/shard_map/ppermute | solution.py:245
  46.4 2.1 %collective-permute-start.20 = (bf16[256,512]{1,0:T(8,128)(2,1)S(1)}, bf16[256,512]{1,0:T(8,128)(2,1)S(1)}, u32[]{:S(2)}, u32[]{:S(2)}) collective-permute-start(bf16[256,512]{1,0:T(8,128)(2,1)S(1)} %shard_map.129.refs_4_), channel_id=1, source_target_pairs={{0,16},{8,24},{16,0},{24,8},{1,17},{9,25},{17,1},{25,9},{2,18},{10... | collective-permute-start | bytes 786440 | tf_op jit(solution)/shard_map/ppermute | solution.py:245
  48.5 2.4 %shard_map.124 = (f32[256,512]{1,0:T(8,128)S(1)}, bf16[256,512]{1,0:T(8,128)(2,1)S(1)}) custom-call(s32[4]{0:T(128)S(1)} %copy-done.10, bf16[256,2048]{1,0:T(8,128)(2,1)S(1)} %get-tuple-element.63.refs_0_, bf16[256,2048]{1,0:T(8,128)(2,1)S(1)} %collective-permute-done.refs_1_, bf16[512,512]{1,0:T(8,128)(2,1)} %get-tuple-element.68.refs_2_, ...), custom_call_target="tpu_custom_call" | custom-call | flops 1073741824 | bytes 4980752 | tf_op jit(solution)/shard_map/pallas_call | solution.py:26
  51.2 1.5 %collective-permute-done.4.refs_0_ = bf16[256,512]{1,0:T(8,128)(2,1)S(1)} collective-permute-done((bf16[256,512]{1,0:T(8,128)(2,1)S(1)}, bf16[256,512]{1,0:T(8,128)(2,1)S(1)}, u32[]{:S(2)}, u32[]{:S(2)}) %collective-permute-start.4) | collective-permute-done | bytes 262176 | tf_op jit(solution)/shard_map/ppermute | solution.py:245
  53.4 16.0 %collective-permute-done.11.refs_0_ = bf16[256,512]{1,0:T(8,128)(2,1)S(1)} collective-permute-done((bf16[256,512]{1,0:T(8,128)(2,1)S(1)}, bf16[256,512]{1,0:T(8,128)(2,1)S(1)}, u32[]{:S(2)}, u32[]{:S(2)}) %collective-permute-start.11) | collective-permute-done | bytes 262176 | tf_op jit(solution)/shard_map/ppermute | solution.py:245
  70.0 1.5 %shard_map.123 = (f32[256,512]{1,0:T(8,128)S(1)}, f32[256,256]{1,0:T(8,128)S(1)}, f32[256,128]{1,0:T(8,128)S(1)}) custom-call(f32[8]{0:T(128)S(1)} %copy-done.14, bf16[256,512]{1,0:T(8,128)(2,1)S(1)} %get-tuple-element.71.x_ref, bf16[256,512]{1,0:T(8,128)(2,1)S(1)} %get-tuple-element.36.grad_ref, bf16[256,128]{1,0:T(8,128)(2,1)S(1)} %bitcast.38, ...), custom_call_target="tpu_custom_call" | custom-call | flops 134217728 | bytes 1982496 | tf_op jit(solution)/shard_map/pallas_call | solution.py:26
  71.6 1.5 %shard_map.126 = (f32[256,512]{1,0:T(8,128)S(1)}, f32[256,256]{1,0:T(8,128)S(1)}, f32[256,128]{1,0:T(8,128)S(1)}) custom-call(f32[8]{0:T(128)S(1)} %copy-done.13, bf16[256,512]{1,0:T(8,128)(2,1)S(1)} %get-tuple-element.70.x_ref, bf16[256,512]{1,0:T(8,128)(2,1)S(1)} %get-tuple-element.44.grad_ref, bf16[256,128]{1,0:T(8,128)(2,1)S(1)} %bitcast.39, ...), custom_call_target="tpu_custom_call" | custom-call | flops 134217728 | bytes 1982496 | tf_op jit(solution)/shard_map/pallas_call | solution.py:26
  75.4 1.1 collective-permute-start.25
  77.5 5.4 %collective-permute-start.21 = (bf16[256,512]{1,0:T(8,128)(2,1)S(1)}, bf16[256,512]{1,0:T(8,128)(2,1)S(1)}, u32[]{:S(2)}, u32[]{:S(2)}) collective-permute-start(bf16[256,512]{1,0:T(8,128)(2,1)S(1)} %shard_map.129.refs_4_), channel_id=1, source_target_pairs={{0,8},{8,0},{16,24},{24,16},{1,9},{9,1},{17,25},{25,17},{2,10},{10... | collective-permute-start | bytes 786440 | tf_op jit(solution)/shard_map/ppermute | solution.py:242
  82.9 4.7 %collective-permute-start.22 = (bf16[256,512]{1,0:T(8,128)(2,1)S(1)}, bf16[256,512]{1,0:T(8,128)(2,1)S(1)}, u32[]{:S(2)}, u32[]{:S(2)}) collective-permute-start(bf16[256,512]{1,0:T(8,128)(2,1)S(1)} %collective-permute-done.20.refs_5_), channel_id=1, source_target_pairs={{0,8},{8,0},{16,24},{24,16},{1,9},{9,1},{17,25},{25,17},{2,10},{10... | collective-permute-start | bytes 786440 | tf_op jit(solution)/shard_map/ppermute | solution.py:242
  88.3 1.8 %shard_map.132 = (bf16[512,512]{1,0:T(8,128)(2,1)S(1)}, f32[512,512]{1,0:T(8,128)S(1)}) custom-call(s32[2]{0:T(128)S(1)} %copy-done.16, bf16[256,1024]{1,0:T(8,128)(2,1)S(1)} %copy-done.6, bf16[256,1024]{1,0:T(8,128)(2,1)S(1)} %get-tuple-element.67.refs_1_, bf16[256,1024]{1,0:T(8,128)(2,1)S(1)} %collective-permute-done.18.refs_2_, ...), custom_call_target="tpu_custom_call" | custom-call | flops 1073741824 | bytes 4718600 | tf_op jit(solution)/shard_map/pallas_call | solution.py:26
  90.7 1.8 %shard_map.130 = (bf16[512,512]{1,0:T(8,128)(2,1)S(1)}, f32[512,512]{1,0:T(8,128)S(1)}) custom-call(s32[2]{0:T(128)S(1)} %copy-done.16, bf16[256,1024]{1,0:T(8,128)(2,1)S(1)} %copy-done.6, bf16[256,1024]{1,0:T(8,128)(2,1)S(1)} %get-tuple-element.67.refs_1_, bf16[256,1024]{1,0:T(8,128)(2,1)S(1)} %collective-permute-done.18.refs_2_, ...), custom_call_target="tpu_custom_call" | custom-call | flops 1073741824 | bytes 4718600 | tf_op jit(solution)/shard_map/pallas_call | solution.py:26
  92.5 1.6 %collective-permute-start.23 = (bf16[512,512]{1,0:T(8,128)(2,1)S(1)}, bf16[512,512]{1,0:T(8,128)(2,1)S(1)}, u32[]{:S(2)}, u32[]{:S(2)}) collective-permute-start(bf16[512,512]{1,0:T(8,128)(2,1)S(1)} %get-tuple-element.57), channel_id=1, source_target_pairs={{0,1},{1,0},{2,3},{3,2},{4,5},{5,4},{6,7},{7,6},{8,9},{9,8},{10,11... | collective-permute-start | bytes 1572872 | tf_op jit(solution)/shard_map/ppermute | solution.py:248
  94.2 1.6 %shard_map.127 = (bf16[256,1024]{1,0:T(8,128)(2,1)}, f32[256,128]{1,0:T(8,128)}, f32[256,128]{1,0:T(8,128)}) custom-call(bf16[256,128]{1,0:T(8,128)(2,1)S(1)} %bitcast.40, bf16[256,128]{1,0:T(8,128)(2,1)S(1)} %bitcast.35, f32[256,16]{1,0:T(8,128)S(1)} %get-tuple-element.32.refs_2_.cols_ref, bf16[256,1024]{1,0:T(8,128)(2,1)S(1)} %copy-done.5, ...), custom_call_target="tpu_custom_call" | custom-call | flops 134217728 | bytes 3555328 | tf_op jit(solution)/shard_map/pallas_call | solution.py:26
  95.8 9.2 %collective-permute-done.27 = bf16[512,512]{1,0:T(8,128)(2,1)S(1)} collective-permute-done((bf16[512,512]{1,0:T(8,128)(2,1)S(1)}, bf16[512,512]{1,0:T(8,128)(2,1)S(1)}, u32[]{:S(2)}, u32[]{:S(2)}) %collective-permute-start.27) | collective-permute-done | bytes 524320 | tf_op jit(solution)/shard_map/ppermute | solution.py:248
  105.2 10.2 %collective-permute-done.23 = bf16[512,512]{1,0:T(8,128)(2,1)S(1)} collective-permute-done((bf16[512,512]{1,0:T(8,128)(2,1)S(1)}, bf16[512,512]{1,0:T(8,128)(2,1)S(1)}, u32[]{:S(2)}, u32[]{:S(2)}) %collective-permute-start.23) | collective-permute-done | bytes 524320 | tf_op jit(solution)/shard_map/ppermute | solution.py:248
  115.5 1.5 %pad_maximum_fusion = f32[512,1024]{1,0:T(8,128)} fusion(f32[512,512]{1,0:T(8,128)S(1)} %convert_add_fusion, f32[512,512]{1,0:T(8,128)S(1)} %convert_add_fusion.1), kind=kLoop, calls=%fused_computation | loop fusion | flops 524288 | bytes 4194304 | tf_op jit(solution)/shard_map/concatenate | solution.py:322
  (121 shorter events, 15.1 us)
Async XLA Ops:
  2.9 25.2 %collective-permute-start.1 = (bf16[512,512]{1,0:T(8,128)(2,1)}, bf16[512,512]{1,0:T(8,128)(2,1)}, u32[]{:S(2)}, u32[]{:S(2)}) collective-permute-start(bf16[512,512]{1,0:T(8,128)(2,1)} %get-tuple-element.69.refs_2_), channel_id=1, source_target_pairs={{0,1},{1,0},{2,3},{3,2},{4,5},{5,4},{6,7},{7,6},{8,9},{9,8},{10,11... | collective-permute-start | bytes 1572872 | tf_op jit(solution)/shard_map/ppermute | solution.py:248
  5.9 34.3 %collective-permute-start.2 = (bf16[512,512]{1,0:T(8,128)(2,1)}, bf16[512,512]{1,0:T(8,128)(2,1)}, u32[]{:S(2)}, u32[]{:S(2)}) collective-permute-start(bf16[512,512]{1,0:T(8,128)(2,1)} %get-tuple-element.69.refs_2_), channel_id=1, source_target_pairs={{0,8},{8,0},{16,24},{24,16},{1,9},{9,1},{17,25},{25,17},{2,10},{10... | collective-permute-start | bytes 1572872 | tf_op jit(solution)/shard_map/ppermute | solution.py:242
  8.7 31.6 %collective-permute-start = (bf16[256,2048]{1,0:T(8,128)(2,1)}, bf16[256,2048]{1,0:T(8,128)(2,1)S(1)}, u32[]{:S(2)}, u32[]{:S(2)}) collective-permute-start(bf16[256,2048]{1,0:T(8,128)(2,1)} %get-tuple-element.62), channel_id=1, source_target_pairs={{0,16},{8,24},{16,0},{24,8},{1,17},{9,25},{17,1},{25,9},{2,18},{10... | collective-permute-start | bytes 3145736 | tf_op jit(solution)/shard_map/ppermute | solution.py:245
  14.7 7.4 %collective-permute-start.5 = (bf16[128,1024]{1,0:T(8,128)(2,1)}, bf16[128,1024]{1,0:T(8,128)(2,1)}, u32[]{:S(2)}, u32[]{:S(2)}) collective-permute-start(bf16[128,1024]{1,0:T(8,128)(2,1)} %add_convert_fusion.2), channel_id=1, source_target_pairs={{0,8},{8,0},{16,24},{24,16},{1,9},{9,1},{17,25},{25,17},{2,10},{10... | collective-permute-start | bytes 786440 | tf_op jit(solution)/shard_map/ppermute | solution.py:242
  14.9 22.8 %collective-permute-start.8 = (bf16[512,512]{1,0:T(8,128)(2,1)}, bf16[512,512]{1,0:T(8,128)(2,1)}, u32[]{:S(2)}, u32[]{:S(2)}) collective-permute-start(bf16[512,512]{1,0:T(8,128)(2,1)} %get-tuple-element.68.refs_2_), channel_id=1, source_target_pairs={{0,1},{1,0},{2,3},{3,2},{4,5},{5,4},{6,7},{7,6},{8,9},{9,8},{10,11... | collective-permute-start | bytes 1572872 | tf_op jit(solution)/shard_map/ppermute | solution.py:248
  23.8 6.1 %collective-permute-start.6 = (bf16[128,1024]{1,0:T(8,128)(2,1)}, bf16[128,1024]{1,0:T(8,128)(2,1)}, u32[]{:S(2)}, u32[]{:S(2)}) collective-permute-start(bf16[128,1024]{1,0:T(8,128)(2,1)} %add_convert_fusion.1), channel_id=1, source_target_pairs={{8,16},{9,17},{10,18},{11,19},{12,20},{13,21},{14,22},{15,23}} | collective-permute-start | bytes 786440 | tf_op jit(solution)/shard_map/ppermute | solution.py:283
  28.1 12.2 %collective-permute-start.3 = (bf16[512,512]{1,0:T(8,128)(2,1)}, bf16[512,512]{1,0:T(8,128)(2,1)S(1)}, u32[]{:S(2)}, u32[]{:S(2)}) collective-permute-start(bf16[512,512]{1,0:T(8,128)(2,1)} %collective-permute-done.1.refs_3_), channel_id=1, source_target_pairs={{0,8},{8,0},{16,24},{24,16},{1,9},{9,1},{17,25},{25,17},{2,10},{10... | collective-permute-start | bytes 1572872 | tf_op jit(solution)/shard_map/ppermute | solution.py:242
  30.9 7.9 %collective-permute-start.7 = (bf16[128,1024]{1,0:T(8,128)(2,1)S(1)}, bf16[128,1024]{1,0:T(8,128)(2,1)S(1)}, u32[]{:S(2)}, u32[]{:S(2)}) collective-permute-start(bf16[128,1024]{1,0:T(8,128)(2,1)S(1)} %add_convert_fusion), channel_id=1, source_target_pairs={{0,8},{8,0},{16,24},{24,16},{1,9},{9,1},{17,25},{25,17},{2,10},{10... | collective-permute-start | bytes 786440 | tf_op jit(solution)/shard_map/ppermute | solution.py:242
  37.7 8.7 %collective-permute-start.9 = (bf16[512,512]{1,0:T(8,128)(2,1)}, bf16[512,512]{1,0:T(8,128)(2,1)S(1)}, u32[]{:S(2)}, u32[]{:S(2)}) collective-permute-start(bf16[512,512]{1,0:T(8,128)(2,1)} %get-tuple-element.68.refs_2_), channel_id=1, source_target_pairs={{0,8},{8,0},{16,24},{24,16},{1,9},{9,1},{17,25},{25,17},{2,10},{10... | collective-permute-start | bytes 1572872 | tf_op jit(solution)/shard_map/ppermute | solution.py:242
  38.8 9.7 %collective-permute-start.10 = (bf16[512,512]{1,0:T(8,128)(2,1)}, bf16[512,512]{1,0:T(8,128)(2,1)S(1)}, u32[]{:S(2)}, u32[]{:S(2)}) collective-permute-start(bf16[512,512]{1,0:T(8,128)(2,1)} %collective-permute-done.8.refs_3_), channel_id=1, source_target_pairs={{0,8},{8,0},{16,24},{24,16},{1,9},{9,1},{17,25},{25,17},{2,10},{10... | collective-permute-start | bytes 1572872 | tf_op jit(solution)/shard_map/ppermute | solution.py:242
  40.2 35.2 %collective-permute-start.18 = (bf16[256,1024]{1,0:T(8,128)(2,1)S(1)}, bf16[256,1024]{1,0:T(8,128)(2,1)S(1)}, u32[]{:S(2)}, u32[]{:S(2)}) collective-permute-start(bf16[256,1024]{1,0:T(8,128)(2,1)S(1)} %copy-done.17), channel_id=1, source_target_pairs={{0,8},{8,0},{16,24},{24,16},{1,9},{9,1},{17,25},{25,17},{2,10},{10... | collective-permute-start | bytes 1572872 | tf_op jit(solution)/shard_map/ppermute | solution.py:242
  43.0 9.7 %collective-permute-start.4 = (bf16[256,512]{1,0:T(8,128)(2,1)S(1)}, bf16[256,512]{1,0:T(8,128)(2,1)S(1)}, u32[]{:S(2)}, u32[]{:S(2)}) collective-permute-start(bf16[256,512]{1,0:T(8,128)(2,1)S(1)} %get-tuple-element.35), channel_id=1, source_target_pairs={{0,16},{8,24},{16,0},{24,8},{1,17},{9,25},{17,1},{25,9},{2,18},{10... | collective-permute-start | bytes 786440 | tf_op jit(solution)/shard_map/ppermute | solution.py:245
  45.9 30.6 %collective-permute-start.24 = (bf16[256,512]{1,0:T(8,128)(2,1)S(1)}, bf16[256,512]{1,0:T(8,128)(2,1)S(1)}, u32[]{:S(2)}, u32[]{:S(2)}) collective-permute-start(bf16[256,512]{1,0:T(8,128)(2,1)S(1)} %shard_map.131.refs_4_), channel_id=1, source_target_pairs={{0,16},{8,24},{16,0},{24,8},{1,17},{9,25},{17,1},{25,9},{2,18},{10... | collective-permute-start | bytes 786440 | tf_op jit(solution)/shard_map/ppermute | solution.py:245
  46.4 31.1 %collective-permute-start.20 = (bf16[256,512]{1,0:T(8,128)(2,1)S(1)}, bf16[256,512]{1,0:T(8,128)(2,1)S(1)}, u32[]{:S(2)}, u32[]{:S(2)}) collective-permute-start(bf16[256,512]{1,0:T(8,128)(2,1)S(1)} %shard_map.129.refs_4_), channel_id=1, source_target_pairs={{0,16},{8,24},{16,0},{24,8},{1,17},{9,25},{17,1},{25,9},{2,18},{10... | collective-permute-start | bytes 786440 | tf_op jit(solution)/shard_map/ppermute | solution.py:245
  51.0 19.0 %copy-start.8 = (f32[8,256]{1,0:T(8,128)S(1)}, f32[8,256]{1,0:T(8,128)}, u32[]{:S(2)}) copy-start(f32[8,256]{1,0:T(8,128)} %get-tuple-element.79.rows_ref) | copy-start | bytes 24580
  51.0 18.4 %collective-permute-start.11 = (bf16[256,512]{1,0:T(8,128)(2,1)S(1)}, bf16[256,512]{1,0:T(8,128)(2,1)S(1)}, u32[]{:S(2)}, u32[]{:S(2)}) collective-permute-start(bf16[256,512]{1,0:T(8,128)(2,1)S(1)} %get-tuple-element.43), channel_id=1, source_target_pairs={{0,16},{8,24},{16,0},{24,8},{1,17},{9,25},{17,1},{25,9},{2,18},{10... | collective-permute-start | bytes 786440 | tf_op jit(solution)/shard_map/ppermute | solution.py:245
  51.2 20.4 %copy-start.7 = (f32[8,256]{1,0:T(8,128)S(1)}, f32[8,256]{1,0:T(8,128)}, u32[]{:S(2)}) copy-start(f32[8,256]{1,0:T(8,128)} %get-tuple-element.78.rows_ref) | copy-start | bytes 24580
  51.2 20.4 %copy-start.13 = (f32[8]{0:T(128)S(1)}, f32[8]{0:T(128)}, u32[]{:S(2)}) copy-start(f32[8]{0:T(128)} %get-tuple-element.80.skip_ref) | copy-start | bytes 100
  52.7 35.6 %collective-permute-start.19 = (bf16[256,1024]{1,0:T(8,128)(2,1)S(1)}, bf16[256,1024]{1,0:T(8,128)(2,1)S(1)}, u32[]{:S(2)}, u32[]{:S(2)}) collective-permute-start(bf16[256,1024]{1,0:T(8,128)(2,1)S(1)} %get-tuple-element.66), channel_id=1, source_target_pairs={{0,8},{8,0},{16,24},{24,16},{1,9},{9,1},{17,25},{25,17},{2,10},{10... | collective-permute-start | bytes 1572872 | tf_op jit(solution)/shard_map/ppermute | solution.py:242
  53.3 20.4 %copy-start.23 = (f32[1,512]{1,0:T(1,128)S(1)}, f32[1,512]{1,0:T(1,128)}, u32[]{:S(2)}) copy-start(f32[1,512]{1,0:T(1,128)} %copy-done.22) | copy-start | bytes 6148
  69.3 3.8 %collective-permute-start.12 = (bf16[128,512]{1,0:T(8,128)(2,1)S(1)}, bf16[128,512]{1,0:T(8,128)(2,1)S(1)}, u32[]{:S(2)}, u32[]{:S(2)}) collective-permute-start(bf16[128,512]{1,0:T(8,128)(2,1)S(1)} %multiply_convert_fusion.6), channel_id=1, source_target_pairs={{0,8},{8,0},{16,24},{24,16},{1,9},{9,1},{17,25},{25,17},{2,10},{10... | collective-permute-start | bytes 393224 | tf_op jit(solution)/shard_map/ppermute | solution.py:242
  73.2 1.6 %collective-permute-start.15 = (bf16[128,512]{1,0:T(8,128)(2,1)S(1)}, bf16[128,512]{1,0:T(8,128)(2,1)S(1)}, u32[]{:S(2)}, u32[]{:S(2)}) collective-permute-start(bf16[128,512]{1,0:T(8,128)(2,1)S(1)} %multiply_convert_fusion.3), channel_id=1, source_target_pairs={{0,8},{8,0},{16,24},{24,16},{1,9},{9,1},{17,25},{25,17},{2,10},{10... | collective-permute-start | bytes 393224 | tf_op jit(solution)/shard_map/ppermute | solution.py:242
  74.7 1.9 %collective-permute-start.13 = (bf16[128,512]{1,0:T(8,128)(2,1)S(1)}, bf16[128,512]{1,0:T(8,128)(2,1)S(1)}, u32[]{:S(2)}, u32[]{:S(2)}) collective-permute-start(bf16[128,512]{1,0:T(8,128)(2,1)S(1)} %multiply_convert_fusion.5), channel_id=1, source_target_pairs={{16,8},{17,9},{18,10},{19,11},{20,12},{21,13},{22,14},{23,15}} | collective-permute-start | bytes 393224 | tf_op jit(solution)/shard_map/ppermute | solution.py:349
  75.4 12.2 %collective-permute-start.25 = (bf16[256,512]{1,0:T(8,128)(2,1)S(1)}, bf16[256,512]{1,0:T(8,128)(2,1)S(1)}, u32[]{:S(2)}, u32[]{:S(2)}) collective-permute-start(bf16[256,512]{1,0:T(8,128)(2,1)S(1)} %shard_map.131.refs_4_), channel_id=1, source_target_pairs={{0,8},{8,0},{16,24},{24,16},{1,9},{9,1},{17,25},{25,17},{2,10},{10... | collective-permute-start | bytes 786440 | tf_op jit(solution)/shard_map/ppermute | solution.py:242
  76.5 11.3 %collective-permute-start.26 = (bf16[256,512]{1,0:T(8,128)(2,1)S(1)}, bf16[256,512]{1,0:T(8,128)(2,1)S(1)}, u32[]{:S(2)}, u32[]{:S(2)}) collective-permute-start(bf16[256,512]{1,0:T(8,128)(2,1)S(1)} %collective-permute-done.24.refs_5_), channel_id=1, source_target_pairs={{0,8},{8,0},{16,24},{24,16},{1,9},{9,1},{17,25},{25,17},{2,10},{10... | collective-permute-start | bytes 786440 | tf_op jit(solution)/shard_map/ppermute | solution.py:242
  76.6 6.4 %collective-permute-start.16 = (bf16[128,512]{1,0:T(8,128)(2,1)S(1)}, bf16[128,512]{1,0:T(8,128)(2,1)S(1)}, u32[]{:S(2)}, u32[]{:S(2)}) collective-permute-start(bf16[128,512]{1,0:T(8,128)(2,1)S(1)} %multiply_convert_fusion.2), channel_id=1, source_target_pairs={{16,8},{17,9},{18,10},{19,11},{20,12},{21,13},{22,14},{23,15}} | collective-permute-start | bytes 393224 | tf_op jit(solution)/shard_map/ppermute | solution.py:349
  77.5 13.2 %collective-permute-start.21 = (bf16[256,512]{1,0:T(8,128)(2,1)S(1)}, bf16[256,512]{1,0:T(8,128)(2,1)S(1)}, u32[]{:S(2)}, u32[]{:S(2)}) collective-permute-start(bf16[256,512]{1,0:T(8,128)(2,1)S(1)} %shard_map.129.refs_4_), channel_id=1, source_target_pairs={{0,8},{8,0},{16,24},{24,16},{1,9},{9,1},{17,25},{25,17},{2,10},{10... | collective-permute-start | bytes 786440 | tf_op jit(solution)/shard_map/ppermute | solution.py:242
  82.9 7.8 %collective-permute-start.22 = (bf16[256,512]{1,0:T(8,128)(2,1)S(1)}, bf16[256,512]{1,0:T(8,128)(2,1)S(1)}, u32[]{:S(2)}, u32[]{:S(2)}) collective-permute-start(bf16[256,512]{1,0:T(8,128)(2,1)S(1)} %collective-permute-done.20.refs_5_), channel_id=1, source_target_pairs={{0,8},{8,0},{16,24},{24,16},{1,9},{9,1},{17,25},{25,17},{2,10},{10... | collective-permute-start | bytes 786440 | tf_op jit(solution)/shard_map/ppermute | solution.py:242
  87.7 6.4 %collective-permute-start.14 = (bf16[128,512]{1,0:T(8,128)(2,1)S(1)}, bf16[128,512]{1,0:T(8,128)(2,1)S(1)}, u32[]{:S(2)}, u32[]{:S(2)}) collective-permute-start(bf16[128,512]{1,0:T(8,128)(2,1)S(1)} %multiply_convert_fusion.4), channel_id=1, source_target_pairs={{0,8},{8,0},{16,24},{24,16},{1,9},{9,1},{17,25},{25,17},{2,10},{10... | collective-permute-start | bytes 393224 | tf_op jit(solution)/shard_map/ppermute | solution.py:242
  87.8 6.4 %collective-permute-start.17 = (bf16[128,512]{1,0:T(8,128)(2,1)S(1)}, bf16[128,512]{1,0:T(8,128)(2,1)S(1)}, u32[]{:S(2)}, u32[]{:S(2)}) collective-permute-start(bf16[128,512]{1,0:T(8,128)(2,1)S(1)} %multiply_convert_fusion.1), channel_id=1, source_target_pairs={{0,8},{8,0},{16,24},{24,16},{1,9},{9,1},{17,25},{25,17},{2,10},{10... | collective-permute-start | bytes 393224 | tf_op jit(solution)/shard_map/ppermute | solution.py:242
  90.1 14.8 %collective-permute-start.27 = (bf16[512,512]{1,0:T(8,128)(2,1)S(1)}, bf16[512,512]{1,0:T(8,128)(2,1)S(1)}, u32[]{:S(2)}, u32[]{:S(2)}) collective-permute-start(bf16[512,512]{1,0:T(8,128)(2,1)S(1)} %get-tuple-element.59), channel_id=1, source_target_pairs={{0,1},{1,0},{2,3},{3,2},{4,5},{5,4},{6,7},{7,6},{8,9},{9,8},{10,11... | collective-permute-start | bytes 1572872 | tf_op jit(solution)/shard_map/ppermute | solution.py:248
  92.5 22.8 %collective-permute-start.23 = (bf16[512,512]{1,0:T(8,128)(2,1)S(1)}, bf16[512,512]{1,0:T(8,128)(2,1)S(1)}, u32[]{:S(2)}, u32[]{:S(2)}) collective-permute-start(bf16[512,512]{1,0:T(8,128)(2,1)S(1)} %get-tuple-element.57), channel_id=1, source_target_pairs={{0,1},{1,0},{2,3},{3,2},{4,5},{5,4},{6,7},{7,6},{8,9},{9,8},{10,11... | collective-permute-start | bytes 1572872 | tf_op jit(solution)/shard_map/ppermute | solution.py:248
  (22 other events, 168.5 us)

commit v2 on v1

v2 whole, which is shorter than its diff:
```python
import functools

import jax
import jax.numpy as jnp
import numpy as np
from jax import lax
from jax.experimental import pallas as pl
from jax.experimental.pallas import tpu as pltpu
from jax.sharding import PartitionSpec as P

P_SIZE = 64
N = 128
Q = 256
HALF = 128
PAIR = 2 * P_SIZE
CHUNKS = 2
PARITY, CORE, ODD, CHIP = 4, 6, 7, 8
BF = jnp.bfloat16
F32 = jnp.float32

SMEM = pl.BlockSpec(memory_space=pltpu.SMEM)
ANY = pl.BlockSpec(memory_space=pl.ANY)
FREE = pl.CostEstimate(flops=0, bytes_accessed=0, transcendentals=0)
LIMIT = pltpu.CompilerParams(vmem_limit_bytes=16 * 2**20)


def name_of(kernel):
    return getattr(kernel, "func", kernel).__name__


def whole(shape):
    return pl.BlockSpec(shape, lambda *_: (0,) * len(shape))


def columns_of(array, width, part):
    return array, pl.BlockSpec((array.shape[0], width), lambda *_: (0, part))


def call(kernel, scalars, arrays, outs, after=(), aliases=None):
    pairs = [item if isinstance(item, tuple) else (item, whole(item.shape)) for item in arrays]
    outs = [item if len(item) == 3 else (*item, whole(item[0])) for item in outs]
    count = len(scalars)

    def run(*refs):
        kernel(*refs[: count + len(pairs)], *refs[count + len(pairs) + len(after) :])

    return pl.pallas_call(
        run,
        grid=(1,),
        out_shape=[jax.ShapeDtypeStruct(shape, kind) for shape, kind, _ in outs],
        in_specs=[SMEM] * count + [spec for _, spec in pairs] + [ANY] * len(after),
        out_specs=[spec for _, _, spec in outs],
        input_output_aliases=aliases or {},
        cost_estimate=FREE,
        compiler_params=LIMIT,
        name=name_of(kernel),
    )(*scalars, *[array for array, _ in pairs], *after)


def column_call(kernel, at, ids, grads, others, span, outs, after=()):
    def run(*refs):
        kernel(*refs[: 2 + len(others)], *refs[2 + len(others) + len(after) :])

    return pl.pallas_call(
        run,
        out_shape=[jax.ShapeDtypeStruct(shape, kind) for shape, kind in outs],
        grid_spec=pltpu.PrefetchScalarGridSpec(
            num_scalar_prefetch=1,
            grid=(1,),
            in_specs=[pl.BlockSpec((Q, span), lambda i, ids_ref: (0, ids_ref[at]))]
            + [whole(other.shape) for other in others]
            + [ANY] * len(after),
            out_specs=[whole(shape) for shape, _ in outs],
        ),
        cost_estimate=FREE,
        compiler_params=LIMIT,
        name=name_of(kernel),
    )(ids, grads, *others, *after)


def dot(a, b, left, right):
    return lax.dot_general(a, b, (((left,), (right,)), ((), ())), preferred_element_type=F32)


def first_head(rows=Q):
    return lax.broadcasted_iota(jnp.int32, (rows, PAIR), 1) < P_SIZE


def spread(table, pair, first):
    return jnp.where(first, table[:, 2 * pair : 2 * pair + 1], table[:, 2 * pair + 1 : 2 * pair + 2])


def gains(skip_ref, head):
    first = lax.broadcasted_iota(jnp.int32, (1, PAIR), 1) < P_SIZE
    return jnp.where(first, skip_ref[head], skip_ref[head + 1])


def tables_kernel(
    rate_ref, resets_ref, x_ref, b_ref, step_ref, state_ref, left_ref, right_ref, weighted_ref, rows_ref, cols_ref, through_ref
):
    heads = step_ref.shape[0]
    keep = (1 - resets_ref[0, 0]).astype(F32)
    head_id = lax.broadcasted_iota(jnp.int32, (heads, Q), 0)
    lane = lax.broadcasted_iota(jnp.int32, (heads, Q), 1)
    rate = jnp.zeros((heads, Q), F32)
    for head in range(heads):
        rate = jnp.where(head_id == head, rate_ref[head], rate)
    log = -step_ref[...] * rate
    shift = 1
    while shift < Q:
        log = log + jnp.where(lane >= shift, pltpu.roll(log, shift, 1), 0.0)
        shift *= 2
    rows_ref[...] = log
    cols = log.T
    cols_ref[...] = cols
    first = first_head()
    for pair in range(heads // 2):
        at = slice(pair * PAIR, (pair + 1) * PAIR)
        log_pair = spread(cols, pair, first)
        last = log_pair[Q - 1 : Q, :]
        weighted_ref[:, at] = (x_ref[:, at].astype(F32) * jnp.exp(last - log_pair)).astype(BF)
        through_ref[:, at] = jnp.broadcast_to(keep * jnp.exp(last), (8, PAIR))
    state = dot(b_ref[...], weighted_ref[...], 0, 0)
    state_ref[...] = state
    middle = left_ref.shape[1]
    left_ref[...] = state[:, :middle].astype(BF)
    right_ref[...] = state[:, middle:].astype(BF)


def local_output_kernel(skip_ref, x_ref, b_ref, c_ref, rows_ref, cols_ref, out_ref):
    heads = rows_ref.shape[0]
    scores = dot(c_ref[...], b_ref[...], 1, 1)
    at_row = lax.broadcasted_iota(jnp.int32, (HALF, HALF), 0)
    at_lane = lax.broadcasted_iota(jnp.int32, (HALF, HALF), 1)
    causal = at_row >= at_lane
    first = first_head()
    zero = jnp.zeros((Q, PAIR), BF)
    for pair in range(heads // 2):
        at = slice(pair * PAIR, (pair + 1) * PAIR)
        x_pair = x_ref[:, at]
        skip = gains(skip_ref, 2 * pair) * x_pair.astype(F32)
        top, bottom = skip[:HALF], skip[HALF:]
        for side in range(2):
            head = 2 * pair + side
            x_head = jnp.where(first, x_pair, zero) if side == 0 else jnp.where(first, zero, x_pair)
            col = cols_ref[:, head : head + 1]
            row = rows_ref[head : head + 1, :]

            def mix(i, j):
                span = col[i * HALF : (i + 1) * HALF] - row[:, j * HALF : (j + 1) * HALF]
                weight = jnp.exp(jnp.minimum(span, 0.0))
                if i == j:
                    weight = jnp.where(causal, weight, 0.0)
                return (weight * scores[i * HALF : (i + 1) * HALF, j * HALF : (j + 1) * HALF]).astype(BF)

            top += dot(mix(0, 0), x_head[:HALF], 1, 0)
            bottom += dot(jnp.concatenate([mix(1, 0), mix(1, 1)], axis=1), x_head, 1, 0)
        out_ref[:HALF, at] = top
        out_ref[HALF:, at] = bottom


def output_kernel(offset, ids_ref, resets_ref, local_ref, c_ref, cols_ref, before_ref, even_ref, out_ref, state_ref):
    first = first_head()
    cols = cols_ref[...]
    keep = (1 - resets_ref[0, 0]).astype(F32)
    state = jnp.where(ids_ref[CORE] == 1, even_ref[...].astype(F32), before_ref[...].astype(F32))
    state_ref[...] = (keep * state).astype(BF)
    for pair in range(out_ref.shape[1] // PAIR):
        at = slice(pair * PAIR, (pair + 1) * PAIR)
        term = dot(c_ref[...], state_ref[:, at], 1, 0)
        out_ref[:, at] = (local_ref[:, at] + jnp.exp(spread(cols, offset + pair, first)) * term).astype(BF)


def block_of(ids_ref, grad_ref, slot):
    depth = grad_ref.shape[1] // 4
    return grad_ref[:, pl.ds(pl.multiple_of(ids_ref[slot] * depth, depth), depth)]


def send_kernel(ids_ref, grad_ref, mine_ref, other_ref):
    mine_ref[...] = block_of(ids_ref, grad_ref, PARITY)
    other_ref[...] = block_of(ids_ref, grad_ref, PARITY + 1)


def assemble_kernel(half, ids_ref, grad_ref, *refs):
    pieces, out_ref = refs[:-1], refs[-1]
    depth = out_ref.shape[1] // 2
    even = ids_ref[ODD] == 0
    for slot in range(2):
        columns = slice(slot * depth, (slot + 1) * depth)
        out_ref[:Q, columns] = block_of(ids_ref, grad_ref, 2 * half + slot)
        for number in range(len(pieces) // 2):
            near, far = pieces[2 * number], pieces[2 * number + 1]
            first, second = (near, far) if slot == 0 else (far, near)
            out_ref[(number + 1) * Q : (number + 2) * Q, columns] = jnp.where(even, first[...], second[...])


def combine_kernel(through_ref, state_ref, *refs):
    parts, out_ref = refs[:-1], refs[-1]
    width = out_ref.shape[1] // len(parts)
    for number, part in enumerate(parts):
        at = slice(number * width, (number + 1) * width)
        out_ref[:, at] = (through_ref[:1, at] * part[...].astype(F32) + state_ref[:, at]).astype(BF)


def head_partial_kernel(mine_ref, other_ref, *refs):
    weights, outs = refs[:4], refs[4:]
    depth = weights[0].shape[0]
    for number in reversed(range(len(outs))):
        rows = slice(number * Q, (number + 1) * Q)
        total = None
        for block, weight in enumerate(weights):
            half = mine_ref if block < 2 else other_ref
            term = dot(half[rows, (block % 2) * depth : (block % 2 + 1) * depth], weight[...], 1, 0)
            total = term if total is None else total + term
        outs[number][...] = total.astype(outs[number].dtype)


def adjoint_kernel(others, offset, resets_ref, own_ref, *refs):
    parts, (c_ref, cols_ref, head_ref, weighted_ref, adjoint_ref, sent_ref) = refs[:others], refs[others:]
    first = first_head()
    cols = cols_ref[...]
    keep = (1 - resets_ref[0, 0]).astype(F32)
    for pair in range(head_ref.shape[1] // PAIR):
        at = slice(pair * PAIR, (pair + 1) * PAIR)
        total = own_ref[:, at]
        for part in parts:
            total = total + part[:, at].astype(F32)
        head = total.astype(BF)
        head_ref[:, at] = head
        weighted_ref[:, at] = (head.astype(F32) * jnp.exp(spread(cols, offset + pair, first))).astype(BF)
    adjoint = keep * dot(c_ref[...], weighted_ref[...], 0, 0)
    adjoint_ref[...] = adjoint
    sent_ref[...] = adjoint.astype(BF)


def chip_total_kernel(ids_ref, own_ref, partner_ref, through_ref, partner_through_ref, *refs):
    entering, out_ref = refs[:-1], refs[-1]
    even = ids_ref[CORE] == 0
    own, partner = own_ref[...], partner_ref[...].astype(F32)
    mine, theirs = through_ref[:1], partner_through_ref[:1]
    total = jnp.where(even, mine * partner + own, theirs * own + partner)
    for value in entering:
        total += mine * theirs * value[...].astype(F32)
    out_ref[...] = total.astype(BF)


def local_grads_kernel(
    offset, skip_ref, x_ref, grad_ref, b_ref, c_ref, rows_ref, cols_ref, weighted_ref, state_ref, in_ref, paired_ref, c_out_ref
):
    heads = x_ref.shape[1] // P_SIZE
    scores = dot(b_ref[...], c_ref[...], 1, 1)
    at_row = lax.broadcasted_iota(jnp.int32, (HALF, HALF), 0)
    at_lane = lax.broadcasted_iota(jnp.int32, (HALF, HALF), 1)
    causal = at_lane >= at_row
    first = first_head()
    zero = jnp.zeros((Q, PAIR), BF)
    paired_ref[...] = jnp.zeros_like(paired_ref)
    for pair in range(heads // 2):
        at = slice(pair * PAIR, (pair + 1) * PAIR)
        x_pair = x_ref[:, at]
        g_pair = grad_ref[:, at]
        skip = gains(skip_ref, offset + 2 * pair) * g_pair.astype(F32)
        top, bottom = skip[:HALF], skip[HALF:]
        for side in range(2):
            head = offset + 2 * pair + side
            g_head = jnp.where(first, g_pair, zero) if side == 0 else jnp.where(first, zero, g_pair)
            col = cols_ref[:, head : head + 1]
            row = rows_ref[head : head + 1, :]

            def weigh(j, i):
                span = row[:, i * HALF : (i + 1) * HALF] - col[j * HALF : (j + 1) * HALF]
                weight = jnp.exp(jnp.minimum(span, 0.0))
                return jnp.where(causal, weight, 0.0) if i == j else weight

            early = jnp.concatenate([weigh(0, 0), weigh(0, 1)], axis=1)
            late = weigh(1, 1)
            top += dot((early * scores[:HALF]).astype(BF), g_head, 1, 0)
            bottom += dot((late * scores[HALF:, HALF:]).astype(BF), g_head[HALF:], 1, 0)
            paired_ref[:HALF, :] += early * dot(x_pair[:HALF], g_head, 1, 1)
            paired_ref[HALF:, HALF:] += late * dot(x_pair[HALF:], g_head[HALF:], 1, 1)
        in_ref[:HALF, at] = top
        in_ref[HALF:, at] = bottom
    c_out_ref[...] = dot(weighted_ref[...], state_ref[...], 1, 1)


def group_sums_kernel(parts, b_ref, c_ref, *refs):
    pairs, c_parts, (grad_b_ref, grad_c_ref) = refs[:parts], refs[parts : 2 * parts], refs[2 * parts :]
    paired = functools.reduce(jnp.add, [ref[...] for ref in pairs]).astype(BF)
    grad_b_ref[...] = dot(paired, c_ref[...], 1, 0)
    grad_c_ref[...] = functools.reduce(jnp.add, [ref[...] for ref in c_parts], dot(paired, b_ref[...], 0, 0))


def final_kernel(
    offset, ids_ref, b_ref, cols_ref, sums_ref, local_ref, weighted_ref, through_ref, after_ref, partner_ref, *refs
):
    in_ref, grad_b_ref = refs[-2:]
    first = first_head()
    cols = cols_ref[...]
    entering = after_ref[...].astype(F32)
    inner = through_ref[:1] * entering + partner_ref[...].astype(F32)
    adjoint = jnp.where(ids_ref[CORE] == 1, entering, inner).astype(BF)
    grad_b_ref[...] = sums_ref[...] + dot(weighted_ref[...], adjoint, 1, 1)
    for number in range(local_ref.shape[1] // PAIR):
        at = slice(number * PAIR, (number + 1) * PAIR)
        log_pair = spread(cols, offset + number, first)
        to_end = jnp.exp(log_pair[Q - 1 : Q, :] - log_pair)
        term = dot(b_ref[...], adjoint[:, at], 1, 0)
        in_ref[:, at] = (local_ref[:, at] + to_end * term).astype(BF)


def add_kernel(kept_ref, came_ref, sum_ref, token_ref):
    sum_ref[...] = kept_ref[...] + came_ref[...].astype(F32)
    token_ref[...] = jnp.zeros_like(token_ref)


def weight_partial_kernel(count, mine_ref, other_ref, *refs):
    outputs, (sent_ref, kept_ref) = refs[:count], refs[count:]
    depth = sent_ref.shape[0]
    for slot, target in ((1, sent_ref), (0, kept_ref)):
        columns = slice(slot * depth, (slot + 1) * depth)
        total = None
        for number, output in enumerate(outputs):
            half = mine_ref if number < count // 2 else other_ref
            rows = slice(number % (count // 2) * Q, (number % (count // 2) + 1) * Q)
            term = dot(half[rows, columns], output[...], 0, 0)
            total = term if total is None else total + term
        target[...] = total.astype(target.dtype)


def body(
    ssm_input, b_input, c_input, step_size, decay_rate, skip_gain, resets, out_grad, out_weight
):
    seq, dp, planes = lax.axis_size("seq"), lax.axis_size("dp"), lax.axis_size("tensor")
    chips = seq // 2
    me = lax.axis_index(("seq", "tensor", "dp"))
    heads = decay_rate.shape[0]
    wide = heads * P_SIZE
    width = wide // CHUNKS
    chunk_heads = heads // CHUNKS
    depth = out_weight.shape[0]
    span = 4 * depth
    assert ssm_input.shape[1] == Q and dp == 2 and seq % 2 == 0 and planes % 2 == 0
    def later(value, other):
        return lax.optimization_barrier((value, other))[0]

    across = [(i, i ^ 1) for i in range(seq)]

    def core_swap(value):
        return lax.ppermute(value, "seq", across)

    def chip_shift(value, by):
        return lax.ppermute(value, "seq", [(i, (i + 2 * by) % seq) for i in range(seq)])

    def plane_swap(value):
        return lax.ppermute(value, "tensor", [(i, i ^ 1) for i in range(planes)])

    def dialogue_swap(value):
        return lax.ppermute(value, "dp", [(0, 1), (1, 0)])

    x, b_rows, c_rows, steps, incoming = (
        ssm_input[0], b_input[0], c_input[0], step_size[0], out_grad[0]
    )
    table = []
    for at in range(seq * planes * dp):
        chip, core, odd, dialogue = at // (2 * planes * dp), at // (planes * dp) % 2, at // dp % 2, at % dp
        order = [core * 2 + dialogue, core * 2 + 1 - dialogue, (1 - core) * 2 + dialogue, (1 - core) * 2 + 1 - dialogue]
        table.append(order + [order[odd], order[2 + odd], core, odd] + [(chip + by) % chips for by in range(chips)])
    ids = lax.dynamic_index_in_dim(np.array(table, np.int32), me, keepdims=False)
    part_of = lambda array, part: columns_of(array, width, part)

    weight_other = dialogue_swap(out_weight)
    weights = [out_weight, weight_other, core_swap(out_weight)]

    to_send = [
        column_call(send_kernel, CHIP + by, ids, incoming, [], span, [((Q, depth), BF)] * 2)
        for by in range(1, chips)
    ]

    def exchange(pieces, other=None):
        got = []
        for by in range(1, chips):
            near = chip_shift(pieces[by - 1], by)
            got += [near, plane_swap(near if other is None else later(near, other))]
        return got

    state, left, right, weighted_in, log_rows, log_cols, through = call(
        tables_kernel,
        (decay_rate, resets),
        (x, b_rows, steps),
        [((N, wide), F32), ((N, wide // 2), BF), ((N, wide // 2), BF), ((Q, wide), BF)]
        + [((heads, Q), F32), ((Q, heads), F32), ((8, wide), F32)],
        after=[pieces[1] for pieces in to_send],
    )
    local_output, = call(
        local_output_kernel,
        (skip_gain,),
        (x, b_rows, c_rows, log_rows, log_cols),
        [((Q, wide), F32)],
    )
    other_pieces = exchange([pieces[1] for pieces in to_send], local_output)
    even = [core_swap(left), core_swap(right)]
    through_partner = core_swap(through)
    before = jnp.zeros((N, wide), BF)
    late = [pieces[0] for pieces in to_send]
    for hop in range(1, chips):
        total, = call(
            combine_kernel, (), (through, state, *even), [((N, wide), BF)],
            after=other_pieces[::2] if hop == 1 else (),
        )
        if hop == 1:
            total, late = lax.optimization_barrier((total, late))
        before = lax.ppermute(total, "seq", [(2 * i + 1, 2 * i + 2) for i in range(chips - 1)])
        leaving, = call(combine_kernel, (), (through, state, before), [((N, wide), BF)], after=[through_partner])
        even = [core_swap(leaving)]
    mine_pieces = exchange(late)
    outputs, states = [], []
    for part in range(CHUNKS):
        output, state_in = call(
            functools.partial(output_kernel, part * chunk_heads // 2),
            (ids, resets),
            (part_of(local_output, part), c_rows, log_cols, part_of(before, part), part_of(even[0], part)),
            [((Q, width), BF), ((N, width), BF)],
            after=[weights[2], weight_other, *mine_pieces[::2], *other_pieces] if part == 0 else [outputs[0][0]],
        )
        states.append(state_in)
        outputs.append([output] + [chip_shift(output, by) for by in range(1, chips)])

    half = [((chips * Q, span // 2), BF)]
    other, = column_call(functools.partial(assemble_kernel, 1), CHIP, ids, incoming, other_pieces, span, half)
    partner = core_swap(other)
    mine, = column_call(
        functools.partial(assemble_kernel, 0), CHIP, ids, incoming, mine_pieces, span, half,
        after=[partner, outputs[-1][0], *outputs[0][1:]],
    )
    weights.append(core_swap(later(weight_other, outputs[-1][0])))

    partials, returned = [], []
    for part in range(CHUNKS):
        partials.append(
            call(
                head_partial_kernel,
                (),
                (mine, other, *[part_of(weight, part) for weight in weights]),
                [((Q, width), F32)] + [((Q, width), BF)] * (chips - 1),
                after=[partial[0] for partial in partials],
            )
        )
        returned.append([chip_shift(partials[part][by], -by) for by in range(1, chips)])

    grad_weight, tokens = None, []
    for part in range(CHUNKS):
        pieces = outputs[part] + [core_swap(outputs[part][0])]
        pieces += [core_swap(later(piece, partials[-1][0])) for piece in outputs[part][1:]]
        sent, kept = call(
            functools.partial(weight_partial_kernel, 2 * chips),
            (),
            (mine, partner, *pieces),
            [((depth, width), BF), ((depth, width), F32)],
            after=[partial[0] for partial in partials],
        )
        grad_weight, token = call(
            add_kernel,
            (),
            (kept, dialogue_swap(sent)),
            [
                ((depth, wide), F32, pl.BlockSpec((depth, width), lambda *_, part=part: (0, part))),
                ((8, 128), F32),
            ],
            after=() if part == 0 else (grad_weight,),
            aliases=None if part == 0 else {2: 0},
        )
        tokens.append(token)

    locals_, pairs, c_parts, after, odd, totals = [], [], [], [], [], []
    for part in range(CHUNKS):
        head_grad, weighted_grad, adjoint, adjoint_sent = call(
            functools.partial(adjoint_kernel, chips - 1, part * chunk_heads // 2),
            (resets,),
            (partials[part][0], *returned[part], c_rows, log_cols),
            [((Q, width), BF), ((Q, width), BF), ((N, width), F32), ((N, width), BF)],
            after=[through_partner, *locals_, *totals],
        )
        adjoint_partner = core_swap(adjoint_sent)
        entering = []
        for hop in range(1, chips):
            total, = call(
                chip_total_kernel,
                (ids,),
                (adjoint, adjoint_partner, part_of(through, part), part_of(through_partner, part), *entering),
                [((N, width), BF)],
            )
            totals.append(total)
            entering = [lax.ppermute(total, "seq", [(i, i - 2) for i in range(2, seq)])]
        after += entering
        odd.append(adjoint_partner)
        local_in, paired, c_part = call(
            functools.partial(local_grads_kernel, part * chunk_heads),
            (skip_gain,),
            (part_of(x, part), head_grad, b_rows, c_rows, log_rows, log_cols, weighted_grad, states[part]),
            [((Q, width), F32), ((Q, Q), F32), ((Q, N), F32)],
        )
        locals_.append(local_in)
        pairs.append(paired)
        c_parts.append(c_part)
    grad_b, grad_c = call(
        functools.partial(group_sums_kernel, CHUNKS),
        (),
        (b_rows, c_rows, *pairs, *c_parts),
        [((Q, N), F32), ((Q, N), F32)],
        after=tokens[:-1],
    )
    grad_in = None
    for part in range(CHUNKS):
        grad_in, grad_b = call(
            functools.partial(final_kernel, part * chunk_heads // 2),
            (ids,),
            (
                b_rows, log_cols, grad_b, locals_[part], part_of(weighted_in, part), part_of(through_partner, part),
                after[part], odd[part],
            ),
            [
                ((Q, wide), BF, pl.BlockSpec((Q, width), lambda *_, part=part: (0, part))),
                ((Q, N), F32),
            ],
            after=() if part == 0 else (grad_in,),
            aliases=None if part == 0 else {9: 0},
        )
    return grad_in[None], grad_b[None], grad_c[None], grad_weight


def solution(mesh):
    in_specs = (
        P("dp", "seq", "tensor"),
        P("dp", "seq", "tensor"),
        P("dp", "seq", "tensor"),
        P("dp", "tensor", "seq"),
        P("tensor"),
        P("tensor"),
        P("dp", "seq"),
        P("dp", "seq", None),
        P(("seq", "dp"), "tensor"),
    )
    out_specs = (
        P("dp", "seq", "tensor"),
        P("dp", "seq", "tensor"),
        P("dp", "seq", "tensor"),
        P(("seq", "dp"), "tensor"),
    )
    return jax.shard_map(body, mesh=mesh, in_specs=in_specs, out_specs=out_specs, check_vma=False)
```

time: 117 us -> 79.3 us (0.68)
  starting transfers between devices: 36.3 us -> 21.7 us
  waiting for transfers between devices: 38.9 us -> 28.5 us
  local copies, waits for them, and re-layouts: 11.6 us -> 2.32 us
  other arithmetic: 9.09 us -> 0 us
  Pallas kernels: 19.3 us -> 24.9 us
    ppermute x16 -> x13, starting transfers between devices: 21.6 us -> 4.42 us  [core_swap(): return lax.ppermute(value, 'seq', across)]
    ppermute x4 -> x3, waiting for transfers between devices: 19.4 us -> 5.23 us  [dialogue_swap(): return lax.ppermute(value, 'dp', [(0, 1), (1, 0)])]
    ppermute x2 -> x4, waiting for transfers between devices: 0.01 us -> 11.6 us  [the longest x2 11.6 us: plane_swap(): return lax.ppermute(value, 'tensor', [(i, i ^ 1) for i in range(planes)])]
    ppermute x5 -> x6, waiting for transfers between devices: 17.5 us -> 10.5 us  [chip_shift(): lax.ppermute(value, 'seq', [(i, (i + 2 * by) % seq) for i in range(seq)])]
    dynamic_slice x3 -> x0, local copies, waits for them, and re-layouts: 5.74 us -> none  [the longest x2 2.98 us: body(): lax.dynamic_slice_in_dim(piece, (1 - core) * half, half, axis=1)]
    pallas_call x13 -> x24, Pallas kernels: 19.3 us -> 24.9 us  [the longest x21 22.8 us: call(): pl.pallas_call(run, grid=(1,), out_shape=[jax.ShapeDtypeStruct(shape, kin...]
    convert_element_type x10 -> x0, other arithmetic: 4.79 us -> none  [the longest x2 1.77 us: body(): from_even = core_swap(leaving.astype(BF))]
    slice x8 -> x0, local copies, waits for them, and re-layouts: 4.31 us -> none  [the longest x5 2.42 us: body(): chunk = lambda value, part: value[:, part * width:(part + 1) * width]]
  transfers between devices with their start and end apart: 28 -> 27, of which waited for: 6 -> 12; matrix products, arithmetic and copies ran while one was open for 13% -> 1% of each run, Pallas kernels for 16% -> 29%
where the time goes in v2:
time: 79.3 us; the launch traced here: 79.1 us
  waiting for transfers between devices  28.5 us (36%)
  Pallas kernels  24.9 us (31%)
  starting transfers between devices  21.7 us (27%)
  local copies, waits for them, and re-layouts  2.32 us (3%)
  between operations  1.6 us (2%)
    pallas_call x21, Pallas kernels, call(): pl.pallas_call(run, grid=(1,), out_shape=[jax.ShapeDtypeStruct(shape, kin...  22.8 us
    ppermute x2, waiting for transfers between devices, plane_swap(): return lax.ppermute(value, 'tensor', [(i, i ^ 1) for i in range(planes)])  11.6 us
    ppermute x6, waiting for transfers between devices, chip_shift(): lax.ppermute(value, 'seq', [(i, (i + 2 * by) % seq) for i in range(seq)])  10.5 us
    ppermute x6, starting transfers between devices, chip_shift(): lax.ppermute(value, 'seq', [(i, (i + 2 * by) % seq) for i in range(seq)])  5.55 us
    ppermute x3, waiting for transfers between devices, dialogue_swap(): return lax.ppermute(value, 'dp', [(0, 1), (1, 0)])  5.23 us
    ppermute x3, starting transfers between devices, dialogue_swap(): return lax.ppermute(value, 'dp', [(0, 1), (1, 0)])  5.18 us
    ppermute x13, starting transfers between devices, core_swap(): return lax.ppermute(value, 'seq', across)  4.42 us
    ppermute x2, starting transfers between devices, plane_swap(): return lax.ppermute(value, 'tensor', [(i, i ^ 1) for i in range(planes)])  3.2 us
  transfers between devices with their start and end apart: 27, of which 12 were waited for; matrix products, arithmetic and copies ran while one was open for 1% of the time, Pallas kernels for 29%

profile of v2, /device:TPU:0, one launch (start us, length us, event | category | flops | bytes accessed | tf_op | source)
XLA Modules:
  0.0 79.1 jit_solution(1536175205160142442)
XLA Ops:
  0.7 3.0 %collective-permute-start.11 = (bf16[512,1024]{1,0:T(8,128)(2,1)}, bf16[512,1024]{1,0:T(8,128)(2,1)S(1)}, u32[]{:S(2)}, u32[]{:S(2)}) collective-permute-start(bf16[512,1024]{1,0:T(8,128)(2,1)} %refs_2_.3), channel_id=1, source_target_pairs={{0,1},{1,0},{2,3},{3,2},{4,5},{5,4},{6,7},{7,6},{8,9},{9,8},{10,11... | collective-permute-start | bytes 3145736 | tf_op jit(solution)/shard_map/ppermute | solution.py:358
  4.4 1.6 %copy-done = bf16[1,256,4096]{2,1,0:T(8,128)(2,1)S(1)} copy-done((bf16[1,256,4096]{2,1,0:T(8,128)(2,1)S(1)}, bf16[1,256,4096]{2,1,0:T(8,128)(2,1)}, u32[]{:S(2)}) %copy-start) | copy-done | bytes 2097176
  6.6 1.6 %collective-permute-start.2 = (bf16[256,512]{1,0:T(8,128)(2,1)S(1)}, bf16[256,512]{1,0:T(8,128)(2,1)S(1)}, u32[]{:S(2)}, u32[]{:S(2)}) collective-permute-start(bf16[256,512]{1,0:T(8,128)(2,1)S(1)} %get-tuple-element.54.refs_5_), channel_id=1, source_target_pairs={{0,16},{8,24},{16,0},{24,8},{1,17},{9,25},{17,1},{25,9},{2,18},{10... | collective-permute-start | bytes 786440 | tf_op jit(solution)/shard_map/ppermute | solution.py:352
  8.9 2.2 %tables_kernel.1 = (f32[128,1024]{1,0:T(8,128)S(1)}, bf16[128,512]{1,0:T(8,128)(2,1)S(1)}, bf16[128,512]{1,0:T(8,128)(2,1)S(1)}, bf16[256,1024]{1,0:T(8,128)(2,1...) custom-call(f32[16]{0:T(128)S(1)} %copy-done.8, s32[1,1]{1,0:T(1,128)S(6)} %copy.18.refs_1_.refs_0_, ...), custom_call_target="tpu_custom_call" | custom-call | tf_op jit(solution)/shard_map/tables_kernel/pallas_call | solution.py:47
  12.8 2.7 %collective-permute-done.2.refs_4_.refs_2_.refs_10_ = bf16[256,512]{1,0:T(8,128)(2,1)S(1)} collective-permute-done((bf16[256,512]{1,0:T(8,128)(2,1)S(1)}, bf16[256,512]{1,0:T(8,128)(2,1)S(1)}, u32[]{:S(2)}, u32[]{:S(2)}) %collective-permute-start.2) | collective-permute-done | bytes 262176 | tf_op jit(solution)/shard_map/ppermute | solution.py:352
  16.3 2.9 %collective-permute-start.8 = (f32[8,1024]{1,0:T(8,128)S(1)}, f32[8,1024]{1,0:T(8,128)S(1)}, u32[]{:S(2)}, u32[]{:S(2)}) collective-permute-start(f32[8,1024]{1,0:T(8,128)S(1)} %get-tuple-element.56.refs_0_.refs_3_), channel_id=1, source_target_pairs={{0,8},{8,0},{16,24},{24,16},{1,9},{9,1},{17,25},{25,17},{2,10},{10... | collective-permute-start | bytes 98312 | tf_op jit(solution)/shard_map/ppermute | solution.py:349
  19.2 1.7 %local_output_kernel.1.refs_2_ = f32[256,1024]{1,0:T(8,128)S(1)} custom-call(f32[16]{0:T(128)S(1)} %copy-done.7, bf16[256,1024]{1,0:T(8,128)(2,1)S(1)} %bitcast.14, bf16[256,128]{1,0:T(8,128)(2,1)S(1)} %bitcast.26, bf16[256,128]{1,0:T(8,128)(2,1)S(1)} %bitcast.17, f32[16,256]{1,0:T(8,128)S(1)} %get-tuple-element.62.refs_4_.refs_5_, ...), custom_call_target="tpu_custom_call" | custom-call | tf_op jit(solution)/shard_map/local_output_kernel/pallas_call | solution.py:47
  20.9 1.6 %collective-permute-start.5 = (bf16[256,512]{1,0:T(8,128)(2,1)S(1)}, bf16[256,512]{1,0:T(8,128)(2,1)S(1)}, u32[]{:S(2)}, u32[]{:S(2)}) collective-permute-start(bf16[256,512]{1,0:T(8,128)(2,1)S(1)} %collective-permute-done.2.refs_4_.refs_2_.refs_10_), channel_id=1, source_target_pairs={{0,2},{2,0},{4,6},{6,4},{1,3},{3,1},{5,7},{7,5},{8,10},{10,8},{12,... | collective-permute-start | bytes 786440 | tf_op jit(solution)/shard_map/ppermute | solution.py:355
  22.7 6.5 %collective-permute-done.5.refs_3_.refs_11_ = bf16[256,512]{1,0:T(8,128)(2,1)S(1)} collective-permute-done((bf16[256,512]{1,0:T(8,128)(2,1)S(1)}, bf16[256,512]{1,0:T(8,128)(2,1)S(1)}, u32[]{:S(2)}, u32[]{:S(2)}) %collective-permute-start.5) | collective-permute-done | bytes 262176 | tf_op jit(solution)/shard_map/ppermute | solution.py:355
  30.5 0.9 %output_kernel.2 = (bf16[256,512]{1,0:T(8,128)(2,1)S(1)}, bf16[128,512]{1,0:T(8,128)(2,1)S(1)}) custom-call(s32[10]{0:T(128)S(1)} %dynamic-slice_bitcast_fusion.refs_0_, s32[1,1]{1,0:T(1,128)S(6)} %copy.18.refs_1_.refs_0_, f32[256,1024]{1,0:T(8,128)S(1)} %local_output_kernel.1.refs_2_, bf16[256,128]{1,0:T(8,128)(2,1)S(1)} %bitcast.18, ...), custom_call_target="tpu_custom_call" | custom-call | tf_op jit(solution)/shard_map/output_kernel/pallas_call | solution.py:47
  31.5 0.9 %output_kernel.3 = (bf16[256,512]{1,0:T(8,128)(2,1)S(1)}, bf16[128,512]{1,0:T(8,128)(2,1)S(1)}) custom-call(s32[10]{0:T(128)S(1)} %dynamic-slice_bitcast_fusion.refs_0_, s32[1,1]{1,0:T(1,128)S(6)} %copy.18.refs_1_.refs_0_, f32[256,1024]{1,0:T(8,128)S(1)} %local_output_kernel.1.refs_2_, bf16[256,128]{1,0:T(8,128)(2,1)S(1)} %bitcast.19, ...), custom_call_target="tpu_custom_call" | custom-call | tf_op jit(solution)/shard_map/output_kernel/pallas_call | solution.py:47
  32.5 1.6 %collective-permute-start.4 = (bf16[256,512]{1,0:T(8,128)(2,1)S(1)}, bf16[256,512]{1,0:T(8,128)(2,1)S(1)}, u32[]{:S(2)}, u32[]{:S(2)}) collective-permute-start(bf16[256,512]{1,0:T(8,128)(2,1)S(1)} %collective-permute-done.3.refs_9_.refs_2_), channel_id=1, source_target_pairs={{0,2},{2,0},{4,6},{6,4},{1,3},{3,1},{5,7},{7,5},{8,10},{10,8},{12,... | collective-permute-start | bytes 786440 | tf_op jit(solution)/shard_map/ppermute | solution.py:355
  34.1 2.0 %collective-permute-start.23 = (bf16[256,512]{1,0:T(8,128)(2,1)S(1)}, bf16[256,512]{1,0:T(8,128)(2,1)S(1)}, u32[]{:S(2)}, u32[]{:S(2)}) collective-permute-start(bf16[256,512]{1,0:T(8,128)(2,1)S(1)} %get-tuple-element.66.refs_5_.refs_2_), channel_id=1, source_target_pairs={{0,16},{8,24},{16,0},{24,8},{1,17},{9,25},{17,1},{25,9},{2,18},{10... | collective-permute-start | bytes 786440 | tf_op jit(solution)/shard_map/ppermute | solution.py:352
  36.1 5.1 %collective-permute-done.4.refs_3_ = bf16[256,512]{1,0:T(8,128)(2,1)S(1)} collective-permute-done((bf16[256,512]{1,0:T(8,128)(2,1)S(1)}, bf16[256,512]{1,0:T(8,128)(2,1)S(1)}, u32[]{:S(2)}, u32[]{:S(2)}) %collective-permute-start.4) | collective-permute-done | bytes 262176 | tf_op jit(solution)/shard_map/ppermute | solution.py:355
  41.2 2.0 %collective-permute-done.12.refs_6_.refs_3_ = bf16[256,512]{1,0:T(8,128)(2,1)S(1)} collective-permute-done((bf16[256,512]{1,0:T(8,128)(2,1)S(1)}, bf16[256,512]{1,0:T(8,128)(2,1)S(1)}, u32[]{:S(2)}, u32[]{:S(2)}) %collective-permute-start.12) | collective-permute-done | bytes 262176 | tf_op jit(solution)/shard_map/ppermute | solution.py:352
  44.0 1.3 %head_partial_kernel.2 = (f32[256,512]{1,0:T(8,128)S(1)}, bf16[256,512]{1,0:T(8,128)(2,1)S(1)}) custom-call(bf16[512,1024]{1,0:T(8,128)(2,1)S(1)} %assemble_kernel.3.refs_0_, bf16[512,1024]{1,0:T(8,128)(2,1)S(1)} %assemble_kernel.2.refs_1_, bf16[512,1024]{1,0:T(8,128)(2,1)S(1)} %copy-done.4, bf16[512,1024]{1,0:T(8,128)(2,1)S(1)} %collective-permute-done.11.refs_8_.refs_3_, ...), custom_call_target="tpu_custom_call" | custom-call | tf_op jit(solution)/shard_map/head_partial_kernel/pallas_call | solution.py:47
  45.3 1.3 %head_partial_kernel.3 = (f32[256,512]{1,0:T(8,128)S(1)}, bf16[256,512]{1,0:T(8,128)(2,1)S(1)}) custom-call(bf16[512,1024]{1,0:T(8,128)(2,1)S(1)} %assemble_kernel.3.refs_0_, bf16[512,1024]{1,0:T(8,128)(2,1)S(1)} %assemble_kernel.2.refs_1_, bf16[512,1024]{1,0:T(8,128)(2,1)S(1)} %copy-done.4, bf16[512,1024]{1,0:T(8,128)(2,1)S(1)} %collective-permute-done.11.refs_8_.refs_3_, ...), custom_call_target="tpu_custom_call" | custom-call | tf_op jit(solution)/shard_map/head_partial_kernel/pallas_call | solution.py:47
  48.1 1.3 %weight_partial_kernel.2 = (bf16[512,512]{1,0:T(8,128)(2,1)S(1)}, f32[512,512]{1,0:T(8,128)S(1)}) custom-call(bf16[512,1024]{1,0:T(8,128)(2,1)S(1)} %assemble_kernel.3.refs_0_, bf16[512,1024]{1,0:T(8,128)(2,1)S(1)} %collective-permute-done.6.refs_4_.refs_1_, bf16[256,512]{1,0:T(8,128)(2,1)S(1)} %get-tuple-element.65.refs_7_.refs_2_, ...), custom_call_target="tpu_custom_call" | custom-call | tf_op jit(solution)/shard_map/weight_partial_kernel/pallas_call | solution.py:47
  50.0 1.3 %weight_partial_kernel.3 = (bf16[512,512]{1,0:T(8,128)(2,1)S(1)}, f32[512,512]{1,0:T(8,128)S(1)}) custom-call(bf16[512,1024]{1,0:T(8,128)(2,1)S(1)} %assemble_kernel.3.refs_0_, bf16[512,1024]{1,0:T(8,128)(2,1)S(1)} %collective-permute-done.6.refs_4_.refs_1_, bf16[256,512]{1,0:T(8,128)(2,1)S(1)} %get-tuple-element.66.refs_5_.refs_2_, ...), custom_call_target="tpu_custom_call" | custom-call | tf_op jit(solution)/shard_map/weight_partial_kernel/pallas_call | solution.py:47
  51.3 1.6 %collective-permute-start.26 = (bf16[512,512]{1,0:T(8,128)(2,1)S(1)}, bf16[512,512]{1,0:T(8,128)(2,1)S(1)}, u32[]{:S(2)}, u32[]{:S(2)}) collective-permute-start(bf16[512,512]{1,0:T(8,128)(2,1)S(1)} %get-tuple-element.101), channel_id=1, source_target_pairs={{0,1},{1,0},{2,3},{3,2},{4,5},{5,4},{6,7},{7,6},{8,9},{9,8},{10,11... | collective-permute-start | bytes 1572872 | tf_op jit(solution)/shard_map/ppermute | solution.py:358
  52.9 1.6 %collective-permute-start.15 = (bf16[256,512]{1,0:T(8,128)(2,1)S(1)}, bf16[256,512]{1,0:T(8,128)(2,1)S(1)}, u32[]{:S(2)}, u32[]{:S(2)}) collective-permute-start(bf16[256,512]{1,0:T(8,128)(2,1)S(1)} %get-tuple-element.75), channel_id=1, source_target_pairs={{0,16},{8,24},{16,0},{24,8},{1,17},{9,25},{17,1},{25,9},{2,18},{10... | collective-permute-start | bytes 786440 | tf_op jit(solution)/shard_map/ppermute | solution.py:352
  54.5 2.3 %collective-permute-done.14.refs_2_ = bf16[256,512]{1,0:T(8,128)(2,1)S(1)} collective-permute-done((bf16[256,512]{1,0:T(8,128)(2,1)S(1)}, bf16[256,512]{1,0:T(8,128)(2,1)S(1)}, u32[]{:S(2)}, u32[]{:S(2)}) %collective-permute-start.14) | collective-permute-done | bytes 262176 | tf_op jit(solution)/shard_map/ppermute | solution.py:352
  57.5 1.5 %local_grads_kernel.2 = (f32[256,512]{1,0:T(8,128)S(1)}, f32[256,256]{1,0:T(8,128)S(1)}, f32[256,128]{1,0:T(8,128)S(1)}) custom-call(f32[16]{0:T(128)S(1)} %copy-done.7, bf16[256,1024]{1,0:T(8,128)(2,1)S(1)} %bitcast.15, bf16[256,512]{1,0:T(8,128)(2,1)S(1)} %get-tuple-element.70.refs_2_, bf16[256,128]{1,0:T(8,128)(2,1)S(1)} %bitcast.27, ...), custom_call_target="tpu_custom_call" | custom-call | tf_op jit(solution)/shard_map/local_grads_kernel/pallas_call | solution.py:47
  59.7 2.4 %collective-permute-done.15.refs_2_ = bf16[256,512]{1,0:T(8,128)(2,1)S(1)} collective-permute-done((bf16[256,512]{1,0:T(8,128)(2,1)S(1)}, bf16[256,512]{1,0:T(8,128)(2,1)S(1)}, u32[]{:S(2)}, u32[]{:S(2)}) %collective-permute-start.15) | collective-permute-done | bytes 262176 | tf_op jit(solution)/shard_map/ppermute | solution.py:352
  62.7 1.3 %collective-permute-start.20 = (bf16[128,512]{1,0:T(8,128)(2,1)S(1)}, bf16[128,512]{1,0:T(8,128)(2,1)S(1)}, u32[]{:S(2)}, u32[]{:S(2)}) collective-permute-start(bf16[128,512]{1,0:T(8,128)(2,1)S(1)} %chip_total_kernel.2.refs_7_), channel_id=1, source_target_pairs={{16,0},{24,8},{17,1},{25,9},{18,2},{26,10},{19,3},{27,11},{20,4},{... | collective-permute-start | bytes 393224 | tf_op jit(solution)/shard_map/ppermute | solution.py:493
  64.7 1.3 %collective-permute-start.22 = (bf16[128,512]{1,0:T(8,128)(2,1)S(1)}, bf16[128,512]{1,0:T(8,128)(2,1)S(1)}, u32[]{:S(2)}, u32[]{:S(2)}) collective-permute-start(bf16[128,512]{1,0:T(8,128)(2,1)S(1)} %chip_total_kernel.3), channel_id=1, source_target_pairs={{16,0},{24,8},{17,1},{25,9},{18,2},{26,10},{19,3},{27,11},{20,4},{... | collective-permute-start | bytes 393224 | tf_op jit(solution)/shard_map/ppermute | solution.py:493
  66.0 1.5 %local_grads_kernel.3 = (f32[256,512]{1,0:T(8,128)S(1)}, f32[256,256]{1,0:T(8,128)S(1)}, f32[256,128]{1,0:T(8,128)S(1)}) custom-call(f32[16]{0:T(128)S(1)} %copy-done.7, bf16[256,1024]{1,0:T(8,128)(2,1)S(1)} %bitcast.16, bf16[256,512]{1,0:T(8,128)(2,1)S(1)} %get-tuple-element.79.refs_2_, bf16[256,128]{1,0:T(8,128)(2,1)S(1)} %bitcast.28, ...), custom_call_target="tpu_custom_call" | custom-call | tf_op jit(solution)/shard_map/local_grads_kernel/pallas_call | solution.py:47
  67.5 1.1 %add_kernel.2 = (f32[512,1024]{1,0:T(8,128)}, f32[8,128]{1,0:T(8,128)S(1)}) custom-call(f32[512,512]{1,0:T(8,128)S(1)} %get-tuple-element.86.refs_0_, bf16[512,512]{1,0:T(8,128)(2,1)S(1)} %collective-permute-done.19.refs_1_), custom_call_target="tpu_custom_call" | custom-call | tf_op jit(solution)/shard_map/add_kernel/pallas_call | solution.py:47
  69.5 5.2 %collective-permute-done.26.refs_1_ = bf16[512,512]{1,0:T(8,128)(2,1)S(1)} collective-permute-done((bf16[512,512]{1,0:T(8,128)(2,1)S(1)}, bf16[512,512]{1,0:T(8,128)(2,1)S(1)}, u32[]{:S(2)}, u32[]{:S(2)}) %collective-permute-start.26) | collective-permute-done | bytes 524320 | tf_op jit(solution)/shard_map/ppermute | solution.py:358
  74.7 1.1 %add_kernel.3 = (f32[512,1024]{1,0:T(8,128)}, f32[8,128]{1,0:T(8,128)}) custom-call(f32[512,512]{1,0:T(8,128)S(1)} %get-tuple-element.100.refs_0_, bf16[512,512]{1,0:T(8,128)(2,1)S(1)} %collective-permute-done.26.refs_1_, f32[512,1024]{1,0:T(8,128)} %get-tuple-element.102.refs_2_), custom_call_target="tpu_custom_call", output_to_operand_aliasing={{0}: (2, {})} | custom-call | tf_op jit(solution)/shard_map/add_kernel/pallas_call | solution.py:47
  75.8 1.6 %final_kernel.2 = (bf16[256,1024]{1,0:T(8,128)(2,1)}, f32[256,128]{1,0:T(8,128)S(1)}) custom-call(s32[10]{0:T(128)S(1)} %dynamic-slice_bitcast_fusion.refs_0_, bf16[256,128]{1,0:T(8,128)(2,1)S(1)} %bitcast.30, f32[256,16]{1,0:T(8,128)S(1)} %get-tuple-element.55.refs_5_.refs_4_.refs_6_.refs_2_, f32[256,128]{1,0:T(8,128)S(1)} %get-tuple-element.89.refs_3_, ...), custom_call_target="tpu_custom_call" | custom-call | tf_op jit(solution)/shard_map/final_kernel/pallas_call | solution.py:47
  77.4 1.7 %final_kernel.3 = (bf16[256,1024]{1,0:T(8,128)(2,1)}, f32[256,128]{1,0:T(8,128)}) custom-call(s32[10]{0:T(128)S(1)} %dynamic-slice_bitcast_fusion.refs_0_, bf16[256,128]{1,0:T(8,128)(2,1)S(1)} %bitcast.31, f32[256,16]{1,0:T(8,128)S(1)} %get-tuple-element.55.refs_5_.refs_4_.refs_6_.refs_2_, ...), custom_call_target="tpu_custom_call", output_to_operand_aliasing={{0}: (9, {})} | custom-call | tf_op jit(solution)/shard_map/final_kernel/pallas_call | solution.py:47
  (65 shorter events, 11.8 us)
Async XLA Ops:
  0.6 8.2 %copy-start.6 = (f32[1,16,256]{2,1,0:T(8,128)S(1)}, f32[1,16,256]{2,1,0:T(8,128)}, u32[]{:S(2)}) copy-start(f32[1,16,256]{2,1,0:T(8,128)} %param.13) | copy-start | bytes 49156
  0.7 29.9 %collective-permute-start.11 = (bf16[512,1024]{1,0:T(8,128)(2,1)}, bf16[512,1024]{1,0:T(8,128)(2,1)S(1)}, u32[]{:S(2)}, u32[]{:S(2)}) collective-permute-start(bf16[512,1024]{1,0:T(8,128)(2,1)} %refs_2_.3), channel_id=1, source_target_pairs={{0,1},{1,0},{2,3},{3,2},{4,5},{5,4},{6,7},{7,6},{8,9},{9,8},{10,11... | collective-permute-start | bytes 3145736 | tf_op jit(solution)/shard_map/ppermute | solution.py:358
  3.7 26.8 %collective-permute-start.10 = (bf16[512,1024]{1,0:T(8,128)(2,1)}, bf16[512,1024]{1,0:T(8,128)(2,1)S(1)}, u32[]{:S(2)}, u32[]{:S(2)}) collective-permute-start(bf16[512,1024]{1,0:T(8,128)(2,1)} %refs_2_.3), channel_id=1, source_target_pairs={{0,8},{8,0},{16,24},{24,16},{1,9},{9,1},{17,25},{25,17},{2,10},{10... | collective-permute-start | bytes 3145736 | tf_op jit(solution)/shard_map/ppermute | solution.py:349
  6.0 13.3 %copy-start.3 = (bf16[1,256,128]{2,1,0:T(8,128)(2,1)S(1)}, bf16[1,256,128]{2,1,0:T(8,128)(2,1)}, u32[]{:S(2)}) copy-start(bf16[1,256,128]{2,1,0:T(8,128)(2,1)} %param.12) | copy-start | bytes 196612
  6.0 13.3 %copy-start.7 = (f32[16]{0:T(128)S(1)}, f32[16]{0:T(128)}, u32[]{:S(2)}) copy-start(f32[16]{0:T(128)} %refs_0_.9) | copy-start | bytes 196
  6.6 8.8 %collective-permute-start.2 = (bf16[256,512]{1,0:T(8,128)(2,1)S(1)}, bf16[256,512]{1,0:T(8,128)(2,1)S(1)}, u32[]{:S(2)}, u32[]{:S(2)}) collective-permute-start(bf16[256,512]{1,0:T(8,128)(2,1)S(1)} %get-tuple-element.54.refs_5_), channel_id=1, source_target_pairs={{0,16},{8,24},{16,0},{24,8},{1,17},{9,25},{17,1},{25,9},{2,18},{10... | collective-permute-start | bytes 786440 | tf_op jit(solution)/shard_map/ppermute | solution.py:352
  11.1 1.4 %collective-permute-start = (bf16[128,512]{1,0:T(8,128)(2,1)S(1)}, bf16[128,512]{1,0:T(8,128)(2,1)S(1)}, u32[]{:S(2)}, u32[]{:S(2)}) collective-permute-start(bf16[128,512]{1,0:T(8,128)(2,1)S(1)} %get-tuple-element.58), channel_id=1, source_target_pairs={{0,8},{8,0},{16,24},{24,16},{1,9},{9,1},{17,25},{25,17},{2,10},{10... | collective-permute-start | bytes 393224 | tf_op jit(solution)/shard_map/ppermute | solution.py:349
  11.4 1.3 %collective-permute-start.1 = (bf16[128,512]{1,0:T(8,128)(2,1)S(1)}, bf16[128,512]{1,0:T(8,128)(2,1)S(1)}, u32[]{:S(2)}, u32[]{:S(2)}) collective-permute-start(bf16[128,512]{1,0:T(8,128)(2,1)S(1)} %get-tuple-element.59), channel_id=1, source_target_pairs={{0,8},{8,0},{16,24},{24,16},{1,9},{9,1},{17,25},{25,17},{2,10},{10... | collective-permute-start | bytes 393224 | tf_op jit(solution)/shard_map/ppermute | solution.py:349
  15.4 13.8 %copy-start.1 = (bf16[1,256,4096]{2,1,0:T(8,128)(2,1)S(1)}, bf16[1,256,4096]{2,1,0:T(8,128)(2,1)}, u32[]{:S(2)}) copy-start(bf16[1,256,4096]{2,1,0:T(8,128)(2,1)} %param.17) | copy-start | bytes 6291460
  15.5 7.1 %collective-permute-start.7 = (bf16[128,1024]{1,0:T(8,128)(2,1)S(1)}, bf16[128,1024]{1,0:T(8,128)(2,1)S(1)}, u32[]{:S(2)}, u32[]{:S(2)}) collective-permute-start(bf16[128,1024]{1,0:T(8,128)(2,1)S(1)} %combine_kernel.2), channel_id=1, source_target_pairs={{8,16},{9,17},{10,18},{11,19},{12,20},{13,21},{14,22},{15,23}} | collective-permute-start | bytes 786440 | tf_op jit(solution)/shard_map/ppermute | solution.py:412
  16.3 6.2 %collective-permute-start.8 = (f32[8,1024]{1,0:T(8,128)S(1)}, f32[8,1024]{1,0:T(8,128)S(1)}, u32[]{:S(2)}, u32[]{:S(2)}) collective-permute-start(f32[8,1024]{1,0:T(8,128)S(1)} %get-tuple-element.56.refs_0_.refs_3_), channel_id=1, source_target_pairs={{0,8},{8,0},{16,24},{24,16},{1,9},{9,1},{17,25},{25,17},{2,10},{10... | collective-permute-start | bytes 98312 | tf_op jit(solution)/shard_map/ppermute | solution.py:349
  20.9 8.3 %collective-permute-start.5 = (bf16[256,512]{1,0:T(8,128)(2,1)S(1)}, bf16[256,512]{1,0:T(8,128)(2,1)S(1)}, u32[]{:S(2)}, u32[]{:S(2)}) collective-permute-start(bf16[256,512]{1,0:T(8,128)(2,1)S(1)} %collective-permute-done.2.refs_4_.refs_2_.refs_10_), channel_id=1, source_target_pairs={{0,2},{2,0},{4,6},{6,4},{1,3},{3,1},{5,7},{7,5},{8,10},{10,8},{12,... | collective-permute-start | bytes 786440 | tf_op jit(solution)/shard_map/ppermute | solution.py:355
  22.6 8.0 %collective-permute-start.3 = (bf16[256,512]{1,0:T(8,128)(2,1)S(1)}, bf16[256,512]{1,0:T(8,128)(2,1)S(1)}, u32[]{:S(2)}, u32[]{:S(2)}) collective-permute-start(bf16[256,512]{1,0:T(8,128)(2,1)S(1)} %get-tuple-element.61), channel_id=1, source_target_pairs={{0,16},{8,24},{16,0},{24,8},{1,17},{9,25},{17,1},{25,9},{2,18},{10... | collective-permute-start | bytes 786440 | tf_op jit(solution)/shard_map/ppermute | solution.py:352
  22.6 7.9 %collective-permute-start.9 = (bf16[128,1024]{1,0:T(8,128)(2,1)S(1)}, bf16[128,1024]{1,0:T(8,128)(2,1)S(1)}, u32[]{:S(2)}, u32[]{:S(2)}) collective-permute-start(bf16[128,1024]{1,0:T(8,128)(2,1)S(1)} %combine_kernel.3), channel_id=1, source_target_pairs={{0,8},{8,0},{16,24},{24,16},{1,9},{9,1},{17,25},{25,17},{2,10},{10... | collective-permute-start | bytes 786440 | tf_op jit(solution)/shard_map/ppermute | solution.py:349
  29.9 13.3 %collective-permute-start.6 = (bf16[512,1024]{1,0:T(8,128)(2,1)S(1)}, bf16[512,1024]{1,0:T(8,128)(2,1)S(1)}, u32[]{:S(2)}, u32[]{:S(2)}) collective-permute-start(bf16[512,1024]{1,0:T(8,128)(2,1)S(1)} %assemble_kernel.2.refs_1_), channel_id=1, source_target_pairs={{0,8},{8,0},{16,24},{24,16},{1,9},{9,1},{17,25},{25,17},{2,10},{10... | collective-permute-start | bytes 3145736 | tf_op jit(solution)/shard_map/ppermute | solution.py:349
  32.4 11.6 %copy-start.4 = (bf16[512,1024]{1,0:T(8,128)(2,1)S(1)}, bf16[512,1024]{1,0:T(8,128)(2,1)}, u32[]{:S(2)}) copy-start(bf16[512,1024]{1,0:T(8,128)(2,1)} %refs_2_.3) | copy-start | bytes 3145732
  32.4 11.6 %collective-permute-start.13 = (bf16[512,1024]{1,0:T(8,128)(2,1)S(1)}, bf16[512,1024]{1,0:T(8,128)(2,1)S(1)}, u32[]{:S(2)}, u32[]{:S(2)}) collective-permute-start(bf16[512,1024]{1,0:T(8,128)(2,1)S(1)} %collective-permute-done.11.refs_8_.refs_3_), channel_id=1, source_target_pairs={{0,8},{8,0},{16,24},{24,16},{1,9},{9,1},{17,25},{25,17},{2,10},{10... | collective-permute-start | bytes 3145736 | tf_op jit(solution)/shard_map/ppermute | solution.py:349
  32.5 8.7 %collective-permute-start.4 = (bf16[256,512]{1,0:T(8,128)(2,1)S(1)}, bf16[256,512]{1,0:T(8,128)(2,1)S(1)}, u32[]{:S(2)}, u32[]{:S(2)}) collective-permute-start(bf16[256,512]{1,0:T(8,128)(2,1)S(1)} %collective-permute-done.3.refs_9_.refs_2_), channel_id=1, source_target_pairs={{0,2},{2,0},{4,6},{6,4},{1,3},{3,1},{5,7},{7,5},{8,10},{10,8},{12,... | collective-permute-start | bytes 786440 | tf_op jit(solution)/shard_map/ppermute | solution.py:355
  34.1 9.2 %collective-permute-start.12 = (bf16[256,512]{1,0:T(8,128)(2,1)S(1)}, bf16[256,512]{1,0:T(8,128)(2,1)S(1)}, u32[]{:S(2)}, u32[]{:S(2)}) collective-permute-start(bf16[256,512]{1,0:T(8,128)(2,1)S(1)} %get-tuple-element.65.refs_7_.refs_2_), channel_id=1, source_target_pairs={{0,16},{8,24},{16,0},{24,8},{1,17},{9,25},{17,1},{25,9},{2,18},{10... | collective-permute-start | bytes 786440 | tf_op jit(solution)/shard_map/ppermute | solution.py:352
  34.1 13.6 %collective-permute-start.23 = (bf16[256,512]{1,0:T(8,128)(2,1)S(1)}, bf16[256,512]{1,0:T(8,128)(2,1)S(1)}, u32[]{:S(2)}, u32[]{:S(2)}) collective-permute-start(bf16[256,512]{1,0:T(8,128)(2,1)S(1)} %get-tuple-element.66.refs_5_.refs_2_), channel_id=1, source_target_pairs={{0,16},{8,24},{16,0},{24,8},{1,17},{9,25},{17,1},{25,9},{2,18},{10... | collective-permute-start | bytes 786440 | tf_op jit(solution)/shard_map/ppermute | solution.py:352
  41.2 6.8 %collective-permute-start.17 = (bf16[256,512]{1,0:T(8,128)(2,1)S(1)}, bf16[256,512]{1,0:T(8,128)(2,1)S(1)}, u32[]{:S(2)}, u32[]{:S(2)}) collective-permute-start(bf16[256,512]{1,0:T(8,128)(2,1)S(1)} %get-tuple-element.65.refs_7_.refs_2_), channel_id=1, source_target_pairs={{0,8},{8,0},{16,24},{24,16},{1,9},{9,1},{17,25},{25,17},{2,10},{10... | collective-permute-start | bytes 786440 | tf_op jit(solution)/shard_map/ppermute | solution.py:349
  46.5 1.6 %collective-permute-start.18 = (bf16[256,512]{1,0:T(8,128)(2,1)S(1)}, bf16[256,512]{1,0:T(8,128)(2,1)S(1)}, u32[]{:S(2)}, u32[]{:S(2)}) collective-permute-start(bf16[256,512]{1,0:T(8,128)(2,1)S(1)} %collective-permute-done.12.refs_6_.refs_3_), channel_id=1, source_target_pairs={{0,8},{8,0},{16,24},{24,16},{1,9},{9,1},{17,25},{25,17},{2,10},{10... | collective-permute-start | bytes 786440 | tf_op jit(solution)/shard_map/ppermute | solution.py:349
  46.6 3.4 %collective-permute-start.24 = (bf16[256,512]{1,0:T(8,128)(2,1)S(1)}, bf16[256,512]{1,0:T(8,128)(2,1)S(1)}, u32[]{:S(2)}, u32[]{:S(2)}) collective-permute-start(bf16[256,512]{1,0:T(8,128)(2,1)S(1)} %get-tuple-element.66.refs_5_.refs_2_), channel_id=1, source_target_pairs={{0,8},{8,0},{16,24},{24,16},{1,9},{9,1},{17,25},{25,17},{2,10},{10... | collective-permute-start | bytes 786440 | tf_op jit(solution)/shard_map/ppermute | solution.py:349
  47.7 2.3 %collective-permute-start.25 = (bf16[256,512]{1,0:T(8,128)(2,1)S(1)}, bf16[256,512]{1,0:T(8,128)(2,1)S(1)}, u32[]{:S(2)}, u32[]{:S(2)}) collective-permute-start(bf16[256,512]{1,0:T(8,128)(2,1)S(1)} %collective-permute-done.23.refs_3_), channel_id=1, source_target_pairs={{0,8},{8,0},{16,24},{24,16},{1,9},{9,1},{17,25},{25,17},{2,10},{10... | collective-permute-start | bytes 786440 | tf_op jit(solution)/shard_map/ppermute | solution.py:349
  47.7 9.1 %collective-permute-start.14 = (bf16[256,512]{1,0:T(8,128)(2,1)S(1)}, bf16[256,512]{1,0:T(8,128)(2,1)S(1)}, u32[]{:S(2)}, u32[]{:S(2)}) collective-permute-start(bf16[256,512]{1,0:T(8,128)(2,1)S(1)} %get-tuple-element.69), channel_id=1, source_target_pairs={{0,16},{8,24},{16,0},{24,8},{1,17},{9,25},{17,1},{25,9},{2,18},{10... | collective-permute-start | bytes 786440 | tf_op jit(solution)/shard_map/ppermute | solution.py:352
  49.4 18.1 %collective-permute-start.19 = (bf16[512,512]{1,0:T(8,128)(2,1)S(1)}, bf16[512,512]{1,0:T(8,128)(2,1)S(1)}, u32[]{:S(2)}, u32[]{:S(2)}) collective-permute-start(bf16[512,512]{1,0:T(8,128)(2,1)S(1)} %get-tuple-element.87), channel_id=1, source_target_pairs={{0,1},{1,0},{2,3},{3,2},{4,5},{5,4},{6,7},{7,6},{8,9},{9,8},{10,11... | collective-permute-start | bytes 1572872 | tf_op jit(solution)/shard_map/ppermute | solution.py:358
  51.3 23.4 %collective-permute-start.26 = (bf16[512,512]{1,0:T(8,128)(2,1)S(1)}, bf16[512,512]{1,0:T(8,128)(2,1)S(1)}, u32[]{:S(2)}, u32[]{:S(2)}) collective-permute-start(bf16[512,512]{1,0:T(8,128)(2,1)S(1)} %get-tuple-element.101), channel_id=1, source_target_pairs={{0,1},{1,0},{2,3},{3,2},{4,5},{5,4},{6,7},{7,6},{8,9},{9,8},{10,11... | collective-permute-start | bytes 1572872 | tf_op jit(solution)/shard_map/ppermute | solution.py:358
  52.9 9.1 %collective-permute-start.15 = (bf16[256,512]{1,0:T(8,128)(2,1)S(1)}, bf16[256,512]{1,0:T(8,128)(2,1)S(1)}, u32[]{:S(2)}, u32[]{:S(2)}) collective-permute-start(bf16[256,512]{1,0:T(8,128)(2,1)S(1)} %get-tuple-element.75), channel_id=1, source_target_pairs={{0,16},{8,24},{16,0},{24,8},{1,17},{9,25},{17,1},{25,9},{2,18},{10... | collective-permute-start | bytes 786440 | tf_op jit(solution)/shard_map/ppermute | solution.py:352
  57.4 1.6 %collective-permute-start.16 = (bf16[128,512]{1,0:T(8,128)(2,1)S(1)}, bf16[128,512]{1,0:T(8,128)(2,1)S(1)}, u32[]{:S(2)}, u32[]{:S(2)}) collective-permute-start(bf16[128,512]{1,0:T(8,128)(2,1)S(1)} %get-tuple-element.78), channel_id=1, source_target_pairs={{0,8},{8,0},{16,24},{24,16},{1,9},{9,1},{17,25},{25,17},{2,10},{10... | collective-permute-start | bytes 393224 | tf_op jit(solution)/shard_map/ppermute | solution.py:349
  62.6 1.4 %collective-permute-start.21 = (bf16[128,512]{1,0:T(8,128)(2,1)S(1)}, bf16[128,512]{1,0:T(8,128)(2,1)S(1)}, u32[]{:S(2)}, u32[]{:S(2)}) collective-permute-start(bf16[128,512]{1,0:T(8,128)(2,1)S(1)} %get-tuple-element.94), channel_id=1, source_target_pairs={{0,8},{8,0},{16,24},{24,16},{1,9},{9,1},{17,25},{25,17},{2,10},{10... | collective-permute-start | bytes 393224 | tf_op jit(solution)/shard_map/ppermute | solution.py:349
  62.7 13.1 %collective-permute-start.20 = (bf16[128,512]{1,0:T(8,128)(2,1)S(1)}, bf16[128,512]{1,0:T(8,128)(2,1)S(1)}, u32[]{:S(2)}, u32[]{:S(2)}) collective-permute-start(bf16[128,512]{1,0:T(8,128)(2,1)S(1)} %chip_total_kernel.2.refs_7_), channel_id=1, source_target_pairs={{16,0},{24,8},{17,1},{25,9},{18,2},{26,10},{19,3},{27,11},{20,4},{... | collective-permute-start | bytes 393224 | tf_op jit(solution)/shard_map/ppermute | solution.py:493
  64.7 12.8 %collective-permute-start.22 = (bf16[128,512]{1,0:T(8,128)(2,1)S(1)}, bf16[128,512]{1,0:T(8,128)(2,1)S(1)}, u32[]{:S(2)}, u32[]{:S(2)}) collective-permute-start(bf16[128,512]{1,0:T(8,128)(2,1)S(1)} %chip_total_kernel.3), channel_id=1, source_target_pairs={{16,0},{24,8},{17,1},{25,9},{18,2},{26,10},{19,3},{27,11},{20,4},{... | collective-permute-start | bytes 393224 | tf_op jit(solution)/shard_map/ppermute | solution.py:493
  (4 other events, 15.6 us)

commit v3 on v2

v3 whole, which is shorter than its diff:
```python
import functools

import jax
import jax.numpy as jnp
import numpy as np
from jax import lax
from jax.experimental import pallas as pl
from jax.experimental.pallas import tpu as pltpu
from jax.sharding import PartitionSpec as P

P_SIZE = 64
N = 128
Q = 256
HALF = 128
PAIR = 2 * P_SIZE
SHARES = (6, 10)
CUTS = 1
BACK = 1
PARITY, CORE, ODD, CHIP = 4, 6, 7, 8
BF = jnp.bfloat16
F32 = jnp.float32

SMEM = pl.BlockSpec(memory_space=pltpu.SMEM)
ANY = pl.BlockSpec(memory_space=pl.ANY)
FREE = pl.CostEstimate(flops=0, bytes_accessed=0, transcendentals=0)
LIMIT = pltpu.CompilerParams(vmem_limit_bytes=16 * 2**20)


def name_of(kernel):
    return getattr(kernel, "func", kernel).__name__


def whole(shape):
    return pl.BlockSpec(shape, lambda *_: (0,) * len(shape))


def columns_of(array, width, part):
    return array, pl.BlockSpec((array.shape[0], width), lambda *_: (0, part))


def call(kernel, scalars, arrays, outs, after=(), aliases=None):
    pairs = [item if isinstance(item, tuple) else (item, whole(item.shape)) for item in arrays]
    outs = [item if len(item) == 3 else (*item, whole(item[0])) for item in outs]
    count = len(scalars)

    def run(*refs):
        kernel(*refs[: count + len(pairs)], *refs[count + len(pairs) + len(after) :])

    return pl.pallas_call(
        run,
        grid=(1,),
        out_shape=[jax.ShapeDtypeStruct(shape, kind) for shape, kind, _ in outs],
        in_specs=[SMEM] * count + [spec for _, spec in pairs] + [ANY] * len(after),
        out_specs=[spec for _, _, spec in outs],
        input_output_aliases=aliases or {},
        cost_estimate=FREE,
        compiler_params=LIMIT,
        name=name_of(kernel),
    )(*scalars, *[array for array, _ in pairs], *after)


def column_call(kernel, at, ids, grads, others, span, outs, after=()):
    def run(*refs):
        kernel(*refs[: 2 + len(others)], *refs[2 + len(others) + len(after) :])

    return pl.pallas_call(
        run,
        out_shape=[jax.ShapeDtypeStruct(shape, kind) for shape, kind in outs],
        grid_spec=pltpu.PrefetchScalarGridSpec(
            num_scalar_prefetch=1,
            grid=(1,),
            in_specs=[pl.BlockSpec((Q, span), lambda i, ids_ref: (0, ids_ref[at]))]
            + [whole(other.shape) for other in others]
            + [ANY] * len(after),
            out_specs=[whole(shape) for shape, _ in outs],
        ),
        cost_estimate=FREE,
        compiler_params=LIMIT,
        name=name_of(kernel),
    )(ids, grads, *others, *after)


def dot(a, b, left, right):
    return lax.dot_general(a, b, (((left,), (right,)), ((), ())), preferred_element_type=F32)


def first_head(rows=Q):
    return lax.broadcasted_iota(jnp.int32, (rows, PAIR), 1) < P_SIZE


def spread(table, pair, first):
    return jnp.where(first, table[:, 2 * pair : 2 * pair + 1], table[:, 2 * pair + 1 : 2 * pair + 2])


def gains(skip_ref, head):
    first = lax.broadcasted_iota(jnp.int32, (1, PAIR), 1) < P_SIZE
    return jnp.where(first, skip_ref[head], skip_ref[head + 1])


def tables_kernel(
    rate_ref, resets_ref, x_ref, b_ref, step_ref, *refs
):
    states, sent, (weighted_ref, rows_ref, cols_ref, through_ref) = refs[:2], refs[2:4], refs[4:]
    heads = step_ref.shape[0]
    keep = (1 - resets_ref[0, 0]).astype(F32)
    head_id = lax.broadcasted_iota(jnp.int32, (heads, Q), 0)
    lane = lax.broadcasted_iota(jnp.int32, (heads, Q), 1)
    rate = jnp.zeros((heads, Q), F32)
    for head in range(heads):
        rate = jnp.where(head_id == head, rate_ref[head], rate)
    log = -step_ref[...] * rate
    shift = 1
    while shift < Q:
        log = log + jnp.where(lane >= shift, pltpu.roll(log, shift, 1), 0.0)
        shift *= 2
    rows_ref[...] = log
    cols = log.T
    cols_ref[...] = cols
    first = first_head()
    for pair in range(heads // 2):
        at = slice(pair * PAIR, (pair + 1) * PAIR)
        log_pair = spread(cols, pair, first)
        last = log_pair[Q - 1 : Q, :]
        weighted_ref[:, at] = (x_ref[:, at].astype(F32) * jnp.exp(last - log_pair)).astype(BF)
        through_ref[:, at] = jnp.broadcast_to(keep * jnp.exp(last), (8, PAIR))
    state = dot(b_ref[...], weighted_ref[...], 0, 0)
    middle = state.shape[1] // 2
    for number in range(2):
        half = state[:, number * middle : (number + 1) * middle]
        states[number][...] = half
        sent[number][...] = half.astype(BF)


def local_output_kernel(skip_ref, x_ref, b_ref, c_ref, rows_ref, cols_ref, out_ref):
    heads = rows_ref.shape[0]
    scores = dot(c_ref[...], b_ref[...], 1, 1)
    at_row = lax.broadcasted_iota(jnp.int32, (HALF, HALF), 0)
    at_lane = lax.broadcasted_iota(jnp.int32, (HALF, HALF), 1)
    causal = at_row >= at_lane
    first = first_head()
    zero = jnp.zeros((Q, PAIR), BF)
    for pair in range(heads // 2):
        at = slice(pair * PAIR, (pair + 1) * PAIR)
        x_pair = x_ref[:, at]
        skip = gains(skip_ref, 2 * pair) * x_pair.astype(F32)
        top, bottom = skip[:HALF], skip[HALF:]
        for side in range(2):
            head = 2 * pair + side
            x_head = jnp.where(first, x_pair, zero) if side == 0 else jnp.where(first, zero, x_pair)
            col = cols_ref[:, head : head + 1]
            row = rows_ref[head : head + 1, :]

            def mix(i, j):
                span = col[i * HALF : (i + 1) * HALF] - row[:, j * HALF : (j + 1) * HALF]
                weight = jnp.exp(jnp.minimum(span, 0.0))
                if i == j:
                    weight = jnp.where(causal, weight, 0.0)
                return (weight * scores[i * HALF : (i + 1) * HALF, j * HALF : (j + 1) * HALF]).astype(BF)

            top += dot(mix(0, 0), x_head[:HALF], 1, 0)
            bottom += dot(jnp.concatenate([mix(1, 0), mix(1, 1)], axis=1), x_head, 1, 0)
        out_ref[:HALF, at] = top
        out_ref[HALF:, at] = bottom


def output_kernel(
    start, ids_ref, resets_ref, local_ref, c_ref, cols_ref, through_ref, before_ref, left_ref, right_ref, out_ref, state_ref
):
    first = first_head()
    cols = cols_ref[...]
    keep = (1 - resets_ref[0, 0]).astype(F32)
    part = slice(start, start + out_ref.shape[1])
    partner = jnp.concatenate([left_ref[...], right_ref[...]], axis=1)[:, part].astype(F32)
    before = before_ref[:, part].astype(F32)
    state = jnp.where(ids_ref[CORE] == 1, through_ref[:1, part] * before + partner, before)
    state_ref[...] = (keep * state).astype(BF)
    for pair in range(out_ref.shape[1] // PAIR):
        at = slice(pair * PAIR, (pair + 1) * PAIR)
        whole = slice(start + pair * PAIR, start + (pair + 1) * PAIR)
        term = dot(c_ref[...], state_ref[:, at], 1, 0)
        decay = jnp.exp(spread(cols, start // PAIR + pair, first))
        out_ref[:, at] = (local_ref[:, whole] + decay * term).astype(BF)


def block_of(ids_ref, grad_ref, slot):
    depth = grad_ref.shape[1] // 4
    return grad_ref[:, pl.ds(pl.multiple_of(ids_ref[slot] * depth, depth), depth)]


def send_kernel(ids_ref, grad_ref, out_ref):
    depth = out_ref.shape[1] // 2
    for half in range(2):
        out_ref[:, half * depth : (half + 1) * depth] = block_of(ids_ref, grad_ref, PARITY + half)


def own_kernel(ids_ref, grad_ref, *halves):
    depth = halves[0].shape[1] // 2
    for slot in range(4):
        halves[slot // 2][:, slot % 2 * depth : (slot % 2 + 1) * depth] = block_of(ids_ref, grad_ref, slot)


def assemble_kernel(ids_ref, *refs):
    pieces, blocks = refs[:-4], refs[-4:]
    depth = blocks[0].shape[1]
    even = ids_ref[ODD] == 0
    for number, out_ref in enumerate(blocks):
        taken = slice(number // 2 * depth, (number // 2 + 1) * depth)
        for other in range(len(pieces) // 2):
            near, far = pieces[2 * other], pieces[2 * other + 1]
            first, second = (near, far) if number % 2 == 0 else (far, near)
            rows = slice(other * Q, (other + 1) * Q)
            out_ref[rows, :] = jnp.where(even, first[:, taken], second[:, taken])


def head_partial_kernel(cuts, mine_ref, other_ref, *refs):
    came, weights, outs = refs[:4], refs[4:9], refs[9:]
    depth = weights[0].shape[0]
    middle = weights[3].shape[0]
    for number in reversed(range(1 + (len(outs) - 1) // cuts)):
        total = None
        for block in range(4):
            rows = slice((number - 1) * Q, number * Q)
            if number == 0:
                grad = (mine_ref, other_ref)[block // 2][:, block % 2 * depth : (block % 2 + 1) * depth]
            else:
                grad = came[block][rows, :]
            if block < 3:
                term = dot(grad, weights[block][...], 1, 0)
            else:
                term = dot(grad[:, :middle], weights[3][...], 1, 0) + dot(grad[:, middle:], weights[4][...], 1, 0)
            total = term if total is None else total + term
        if number == 0:
            outs[0][...] = total
            continue
        width = total.shape[1] // cuts
        for cut in range(cuts):
            part = total[:, cut * width : (cut + 1) * width]
            outs[1 + (number - 1) * cuts + cut][...] = part.astype(BF)


def adjoint_kernel(others, cuts, offset, resets_ref, own_ref, *refs):
    parts, (c_ref, cols_ref, head_ref, weighted_ref, adjoint_ref, sent_ref) = refs[: others * cuts], refs[others * cuts :]
    first = first_head()
    cols = cols_ref[...]
    width = own_ref.shape[1] // cuts
    keep = (1 - resets_ref[0, 0]).astype(F32)
    for pair in range(head_ref.shape[1] // PAIR):
        at = slice(pair * PAIR, (pair + 1) * PAIR)
        total = own_ref[:, at]
        cut, place = pair * PAIR // width, pair * PAIR % width
        for other in range(others):
            total = total + parts[other * cuts + cut][:, place : place + PAIR].astype(F32)
        head = total.astype(BF)
        head_ref[:, at] = head
        weighted_ref[:, at] = (head.astype(F32) * jnp.exp(spread(cols, offset + pair, first))).astype(BF)
    adjoint = keep * dot(c_ref[...], weighted_ref[...], 0, 0)
    adjoint_ref[...] = adjoint
    sent_ref[...] = adjoint.astype(BF)


def chip_total_kernel(last, parts, ids_ref, through_ref, partner_through_ref, *refs):
    owns, partners, entering, out_ref = refs[:parts], refs[parts : 2 * parts], refs[2 * parts : -1], refs[-1]
    leaves = ids_ref[CORE] == last
    width = owns[0].shape[1]
    for part in range(parts):
        at = slice(part * width, (part + 1) * width)
        own, partner = owns[part][...], partners[part][...].astype(F32)
        mine, theirs = through_ref[:1, at], partner_through_ref[:1, at]
        total = jnp.where(leaves, mine * partner + own, theirs * own + partner)
        for value in entering:
            total += mine * theirs * value[:, at].astype(F32)
        out_ref[:, at] = total.astype(BF)


def local_grads_kernel(
    offset, skip_ref, x_ref, grad_ref, b_ref, c_ref, rows_ref, cols_ref, weighted_ref, *refs
):
    states, (in_ref, paired_ref, c_out_ref) = refs[:-3], refs[-3:]
    heads = x_ref.shape[1] // P_SIZE
    scores = dot(b_ref[...], c_ref[...], 1, 1)
    at_row = lax.broadcasted_iota(jnp.int32, (HALF, HALF), 0)
    at_lane = lax.broadcasted_iota(jnp.int32, (HALF, HALF), 1)
    causal = at_lane >= at_row
    first = first_head()
    zero = jnp.zeros((Q, PAIR), BF)
    paired_ref[...] = jnp.zeros_like(paired_ref)
    for pair in range(heads // 2):
        at = slice(pair * PAIR, (pair + 1) * PAIR)
        x_pair = x_ref[:, at]
        g_pair = grad_ref[:, at]
        skip = gains(skip_ref, offset + 2 * pair) * g_pair.astype(F32)
        top, bottom = skip[:HALF], skip[HALF:]
        for side in range(2):
            head = offset + 2 * pair + side
            g_head = jnp.where(first, g_pair, zero) if side == 0 else jnp.where(first, zero, g_pair)
            col = cols_ref[:, head : head + 1]
            row = rows_ref[head : head + 1, :]

            def weigh(j, i):
                span = row[:, i * HALF : (i + 1) * HALF] - col[j * HALF : (j + 1) * HALF]
                weight = jnp.exp(jnp.minimum(span, 0.0))
                return jnp.where(causal, weight, 0.0) if i == j else weight

            early = jnp.concatenate([weigh(0, 0), weigh(0, 1)], axis=1)
            late = weigh(1, 1)
            top += dot((early * scores[:HALF]).astype(BF), g_head, 1, 0)
            bottom += dot((late * scores[HALF:, HALF:]).astype(BF), g_head[HALF:], 1, 0)
            paired_ref[:HALF, :] += early * dot(x_pair[:HALF], g_head, 1, 1)
            paired_ref[HALF:, HALF:] += late * dot(x_pair[HALF:], g_head[HALF:], 1, 1)
        in_ref[:HALF, at] = top
        in_ref[HALF:, at] = bottom
    start, total = 0, None
    for state in states:
        width = state.shape[1]
        term = dot(weighted_ref[:, start : start + width], state[...], 1, 1)
        total = term if total is None else total + term
        start += width
    c_out_ref[...] = total


def group_sums_kernel(parts, b_ref, c_ref, *refs):
    pairs, c_parts, (grad_b_ref, grad_c_ref) = refs[:parts], refs[parts : 2 * parts], refs[2 * parts :]
    paired = functools.reduce(jnp.add, [ref[...] for ref in pairs]).astype(BF)
    grad_b_ref[...] = dot(paired, c_ref[...], 1, 0)
    grad_c_ref[...] = functools.reduce(jnp.add, [ref[...] for ref in c_parts], dot(paired, b_ref[...], 0, 0))


def final_kernel(parts, ids_ref, b_ref, cols_ref, sums_ref, weighted_ref, through_ref, after_ref, *refs):
    locals_, partners, (in_ref, grad_b_ref) = refs[:parts], refs[parts : 2 * parts], refs[2 * parts :]
    first = first_head()
    cols = cols_ref[...]
    grad_b = sums_ref[...]
    width = locals_[0].shape[1]
    for part in range(parts):
        here = slice(part * width, (part + 1) * width)
        entering = after_ref[:, here].astype(F32)
        inner = through_ref[:1, here] * entering + partners[part][...].astype(F32)
        adjoint = jnp.where(ids_ref[CORE] == 1, entering, inner).astype(BF)
        grad_b += dot(weighted_ref[:, here], adjoint, 1, 1)
        for number in range(width // PAIR):
            at = slice(number * PAIR, (number + 1) * PAIR)
            pair = part * (width // PAIR) + number
            log_pair = spread(cols, pair, first)
            to_end = jnp.exp(log_pair[Q - 1 : Q, :] - log_pair)
            term = dot(b_ref[...], adjoint[:, at], 1, 0)
            in_ref[:, pair * PAIR : (pair + 1) * PAIR] = (locals_[part][:, at] + to_end * term).astype(BF)
    grad_b_ref[...] = grad_b


def add_kernel(parts, *refs):
    start = 0
    for kept, came in zip(refs[:parts], refs[parts:-1]):
        width = kept.shape[1]
        refs[-1][:, start : start + width] = kept[...] + came[...].astype(F32)
        start += width


def weight_partial_kernel(chips, *refs):
    owns, came, refs = refs[:2], (refs[2:4], refs[4:6]), refs[6:]
    outputs, (sent_ref, kept_ref) = refs[: 2 * chips], refs[2 * chips :]
    depth = sent_ref.shape[0]
    for slot, target in ((1, sent_ref), (0, kept_ref)):
        total = None
        for number, output in enumerate(outputs):
            core, by = number // chips, number % chips
            if by == 0:
                grad = owns[core][:, slot * depth : (slot + 1) * depth]
            else:
                grad = came[core][slot][(by - 1) * Q : by * Q, :]
            term = dot(grad, output[...], 0, 0)
            total = term if total is None else total + term
        target[...] = total.astype(target.dtype)


def body(
    ssm_input, b_input, c_input, step_size, decay_rate, skip_gain, resets, out_grad, out_weight
):
    seq, dp, planes = lax.axis_size("seq"), lax.axis_size("dp"), lax.axis_size("tensor")
    chips = seq // 2
    me = lax.axis_index(("seq", "tensor", "dp"))
    heads = decay_rate.shape[0]
    wide = heads * P_SIZE
    widths = [wide * share // sum(SHARES) // PAIR * PAIR for share in SHARES]
    starts = [sum(widths[:part]) for part in range(len(widths))]
    depth = out_weight.shape[0]
    span = 4 * depth
    assert ssm_input.shape[1] == Q and dp == 2 and seq % 2 == 0 and seq > 2 and planes % 2 == 0
    def later(value, other):
        return lax.optimization_barrier((value, other))[0]

    across = [(i, i ^ 1) for i in range(seq)]

    def core_swap(value):
        return lax.ppermute(value, "seq", across)

    def chip_shift(value, by):
        return lax.ppermute(value, "seq", [(i, (i + 2 * by) % seq) for i in range(seq)])

    def plane_swap(value):
        return lax.ppermute(value, "tensor", [(i, i ^ 1) for i in range(planes)])

    def dialogue_swap(value):
        return lax.ppermute(value, "dp", [(0, 1), (1, 0)])

    x, b_rows, c_rows, steps, incoming = (
        ssm_input[0], b_input[0], c_input[0], step_size[0], out_grad[0]
    )
    table = []
    for at in range(seq * planes * dp):
        chip, core, odd, dialogue = at // (2 * planes * dp), at // (planes * dp) % 2, at // dp % 2, at % dp
        order = [core * 2 + dialogue, core * 2 + 1 - dialogue, (1 - core) * 2 + dialogue, (1 - core) * 2 + 1 - dialogue]
        table.append(order + [order[odd], order[2 + odd], core, odd] + [(chip + by) % chips for by in range(chips)])
    ids = lax.dynamic_index_in_dim(np.array(table, np.int32), me, keepdims=False)
    back_width, back_heads = wide // BACK, heads // BACK
    back_of = lambda array, part: columns_of(array, back_width, part)

    to_send = [
        column_call(send_kernel, CHIP + by, ids, incoming, [], span, [((Q, 2 * depth), BF)])
        for by in range(1, chips)
    ]

    weight_other = dialogue_swap(out_weight)
    weight_core = core_swap(out_weight)

    near = [chip_shift(to_send[by - 1][0], by) for by in range(1, chips)]
    pieces = []
    for piece in near:
        pieces += [piece, plane_swap(piece)]

    *both, weighted_in, log_rows, log_cols, through = call(
        tables_kernel,
        (decay_rate, resets),
        (x, b_rows, steps),
        [((N, wide // 2), F32)] * 2 + [((N, wide // 2), BF)] * 2 + [((Q, wide), BF)]
        + [((heads, Q), F32), ((Q, heads), F32), ((8, wide), F32)],
        after=[weight_core, *[sent[0] for sent in to_send]],
    )
    local_output, = call(
        local_output_kernel,
        (skip_gain,),
        (x, b_rows, c_rows, log_rows, log_cols),
        [((Q, wide), F32)],
    )
    state_partner = [core_swap(half) for half in both[2:]]
    through_partner = core_swap(through)
    mine, other = column_call(
        own_kernel, CHIP, ids, incoming, [], span, [((Q, span // 2), BF)] * 2, after=[through]
    )
    partner = core_swap(other)
    before = []
    for hop in range(1, chips):
        total, = call(
            functools.partial(chip_total_kernel, 1, 2),
            (ids,),
            (through, through_partner, *both[:2], *state_partner, *before),
            [((N, wide), BF)],
            after=[local_output] if hop == 1 else (),
        )
        before = [lax.ppermute(total, "seq", [(i, i + 2) for i in range(seq - 2)])]
    outputs, swapped, states = [], [], []
    for start, width in zip(starts, widths):
        output, state_in = call(
            functools.partial(output_kernel, start),
            (ids, resets),
            (local_output, c_rows, log_cols, through_partner, *before, *state_partner),
            [((Q, width), BF), ((N, width), BF)],
            after=outputs[-1][:1] if outputs else [partner],
        )
        states.append(state_in)
        outputs.append([output] + [chip_shift(output, by) for by in range(1, chips)])
        swapped.append(core_swap(output))

    came = call(
        assemble_kernel, (ids,), pieces, [(((chips - 1) * Q, depth), BF)] * 4, after=[outputs[-1][0]],
    )
    partner_came = [core_swap(block) for block in came[2:]]
    weight_late = later(weight_other, outputs[-1][0])
    weights = [out_weight, weight_other, weight_core]
    weights += [core_swap(weight_late[: depth // 2]), core_swap(weight_late[depth // 2 :])]

    partials, returned = [], []
    for part in range(BACK):
        partials.append(
            call(
                functools.partial(head_partial_kernel, CUTS),
                (),
                (mine, other, *came, *[back_of(weight, part) for weight in weights]),
                [((Q, back_width), F32)] + [((Q, back_width // CUTS), BF)] * (CUTS * (chips - 1)),
                after=[] if part == 0 else [partials[-1][0]],
            )
        )
        returned.append(
            [chip_shift(partials[part][1 + i], -(1 + i // CUTS)) for i in range(CUTS * (chips - 1))]
        )

    sent, kept = [], []
    for part, width in enumerate(widths):
        pieces = [later(piece, sent[-1]) if sent else piece for piece in outputs[part][1:]]
        own, partial = call(
            functools.partial(weight_partial_kernel, chips),
            (),
            (mine, partner, *came[:2], *partner_came, *outputs[part], swapped[part], *map(core_swap, pieces)),
            [((depth, width), BF), ((depth, width), F32)],
            after=[partial[0] for partial in partials] + sent[-1:],
        )
        sent.append(own)
        kept.append(partial)
    sums = [dialogue_swap(value) for value in sent]
    grad_weight, = call(
        functools.partial(add_kernel, len(widths)),
        (),
        (*kept, *sums),
        [((depth, wide), F32)],
    )

    locals_, pairs, c_parts, adjoints, partners = [], [], [], [], []
    for part in range(BACK):
        head_grad, weighted_grad, adjoint, adjoint_sent = call(
            functools.partial(adjoint_kernel, chips - 1, CUTS, part * back_heads // 2),
            (resets,),
            (partials[part][0], *returned[part], c_rows, log_cols),
            [((Q, back_width), BF), ((Q, back_width), BF), ((N, back_width), F32), ((N, back_width), BF)],
            after=[sums[0], *sent, *locals_],
        )
        adjoints.append(adjoint)
        partners.append(core_swap(adjoint_sent))
        local_in, paired, c_part = call(
            functools.partial(local_grads_kernel, part * back_heads),
            (skip_gain,),
            (back_of(x, part), head_grad, b_rows, c_rows, log_rows, log_cols, weighted_grad)
            + tuple(states),
            [((Q, back_width), F32), ((Q, Q), F32), ((Q, N), F32)],
        )
        locals_.append(local_in)
        pairs.append(paired)
        c_parts.append(c_part)
    entering = []
    for hop in range(1, chips):
        total, = call(
            functools.partial(chip_total_kernel, 0, BACK),
            (ids,),
            (through, through_partner, *adjoints, *partners, *entering),
            [((N, wide), BF)],
        )
        entering = [lax.ppermute(total, "seq", [(i, i - 2) for i in range(2, seq)])]
    grad_b, grad_c = call(
        functools.partial(group_sums_kernel, BACK),
        (),
        (b_rows, c_rows, *pairs, *c_parts),
        [((Q, N), F32), ((Q, N), F32)],
    )
    grad_in, grad_b = call(
        functools.partial(final_kernel, BACK),
        (ids,),
        (b_rows, log_cols, grad_b, weighted_in, through_partner, *entering, *locals_, *partners),
        [((Q, wide), BF), ((Q, N), F32)],
    )
    return grad_in[None], grad_b[None], grad_c[None], grad_weight


def solution(mesh):
    in_specs = (
        P("dp", "seq", "tensor"),
        P("dp", "seq", "tensor"),
        P("dp", "seq", "tensor"),
        P("dp", "tensor", "seq"),
        P("tensor"),
        P("tensor"),
        P("dp", "seq"),
        P("dp", "seq", None),
        P(("seq", "dp"), "tensor"),
    )
    out_specs = (
        P("dp", "seq", "tensor"),
        P("dp", "seq", "tensor"),
        P("dp", "seq", "tensor"),
        P(("seq", "dp"), "tensor"),
    )
    return jax.shard_map(body, mesh=mesh, in_specs=in_specs, out_specs=out_specs, check_vma=False)
```

time: 79.3 us -> 72.6 us (0.916)
  Pallas kernels: 24.9 us -> 22.4 us
  starting transfers between devices: 21.7 us -> 19.2 us
  waiting for transfers between devices: 28.5 us -> 26 us
  local copies, waits for them, and re-layouts: 2.32 us -> 3.22 us
    ppermute x2 -> x1, waiting for transfers between devices: 11.6 us -> 3 us  [plane_swap(): return lax.ppermute(value, 'tensor', [(i, i ^ 1) for i in range(planes)])]
    ppermute x3, waiting for transfers between devices: 5.23 us -> 13.1 us  [dialogue_swap(): return lax.ppermute(value, 'dp', [(0, 1), (1, 0)])]
    ppermute x6 -> x4, waiting for transfers between devices: 10.5 us -> 2.97 us  [chip_shift(): lax.ppermute(value, 'seq', [(i, (i + 2 * by) % seq) for i in range(seq)])]
    ppermute x1, waiting for transfers between devices: 0.01 us -> 3.47 us  [body(): before = [lax.ppermute(total, 'seq', [(i, i + 2) for i in range(seq - 2)])]]
    ppermute x13 -> x14, waiting for transfers between devices: 1.19 us -> 3.46 us  [core_swap(): return lax.ppermute(value, 'seq', across)]
    pallas_call x21 -> x15, Pallas kernels: 22.8 us -> 21 us  [call(): pl.pallas_call(run, grid=(1,), out_shape=[jax.ShapeDtypeStruct(shape, kin...]
    ppermute x1, starting transfers between devices: 0.81 us -> 2.47 us  [body(): before = [lax.ppermute(total, 'seq', [(i, i + 2) for i in range(seq - 2)])]]
    ppermute x2 -> x1, starting transfers between devices: 3.2 us -> 1.58 us  [plane_swap(): return lax.ppermute(value, 'tensor', [(i, i ^ 1) for i in range(planes)])]
  transfers between devices with their start and end apart: 27 -> 24, of which waited for: 12 -> 9; matrix products, arithmetic and copies ran while one was open for 1% -> 1% of each run, Pallas kernels for 29% -> 28%
where the time goes in v3:
time: 72.6 us; the launch traced here: 72.3 us
  waiting for transfers between devices  26 us (36%)
  Pallas kernels  22.4 us (31%)
  starting transfers between devices  19.2 us (26%)
  local copies, waits for them, and re-layouts  3.22 us (4%)
  between operations  1.56 us (2%)
    pallas_call x15, Pallas kernels, call(): pl.pallas_call(run, grid=(1,), out_shape=[jax.ShapeDtypeStruct(shape, kin...  21 us
    ppermute x3, waiting for transfers between devices, dialogue_swap(): return lax.ppermute(value, 'dp', [(0, 1), (1, 0)])  13.1 us
    ppermute x4, starting transfers between devices, chip_shift(): lax.ppermute(value, 'seq', [(i, (i + 2 * by) % seq) for i in range(seq)])  6.2 us
    ppermute x3, starting transfers between devices, dialogue_swap(): return lax.ppermute(value, 'dp', [(0, 1), (1, 0)])  4.29 us
    ppermute x1, waiting for transfers between devices, body(): before = [lax.ppermute(total, 'seq', [(i, i + 2) for i in range(seq - 2)])]  3.47 us
    ppermute x14, waiting for transfers between devices, core_swap(): return lax.ppermute(value, 'seq', across)  3.46 us
    ppermute x14, starting transfers between devices, core_swap(): return lax.ppermute(value, 'seq', across)  3.17 us
    ppermute x1, waiting for transfers between devices, plane_swap(): return lax.ppermute(value, 'tensor', [(i, i ^ 1) for i in range(planes)])  3 us
  transfers between devices with their start and end apart: 24, of which 9 were waited for; matrix products, arithmetic and copies ran while one was open for 1% of the time, Pallas kernels for 28%

profile of v3, /device:TPU:0, one launch (start us, length us, event | category | flops | bytes accessed | tf_op | source)
XLA Modules:
  0.0 72.3 jit_solution(5755724407729059897)
XLA Ops:
  1.2 2.6 %collective-permute-start.8 = (bf16[512,1024]{1,0:T(8,128)(2,1)}, bf16[512,1024]{1,0:T(8,128)(2,1)S(1)}, u32[]{:S(2)}, u32[]{:S(2)}) collective-permute-start(bf16[512,1024]{1,0:T(8,128)(2,1)} %refs_6_.1), channel_id=1, source_target_pairs={{0,1},{1,0},{2,3},{3,2},{4,5},{5,4},{6,7},{7,6},{8,9},{9,8},{10,11... | collective-permute-start | bytes 3145736 | tf_op jit(solution)/shard_map/ppermute | solution.py:403
  4.5 1.6 %copy-done = bf16[1,256,4096]{2,1,0:T(8,128)(2,1)S(1)} copy-done((bf16[1,256,4096]{2,1,0:T(8,128)(2,1)S(1)}, bf16[1,256,4096]{2,1,0:T(8,128)(2,1)}, u32[]{:S(2)}) %copy-start) | copy-done | bytes 2097176
  6.7 1.6 %collective-permute-start.1 = (bf16[256,1024]{1,0:T(8,128)(2,1)S(1)}, bf16[256,1024]{1,0:T(8,128)(2,1)S(1)}, u32[]{:S(2)}, u32[]{:S(2)}) collective-permute-start(bf16[256,1024]{1,0:T(8,128)(2,1)S(1)} %send_kernel.1.refs_6_), channel_id=1, source_target_pairs={{0,16},{8,24},{16,0},{24,8},{1,17},{9,25},{17,1},{25,9},{2,18},{10... | collective-permute-start | bytes 1572872 | tf_op jit(solution)/shard_map/ppermute | solution.py:397
  9.0 0.8 %copy-done.4 = bf16[1,256,128]{2,1,0:T(8,128)(2,1)S(1)} copy-done((bf16[1,256,128]{2,1,0:T(8,128)(2,1)S(1)}, bf16[1,256,128]{2,1,0:T(8,128)(2,1)}, u32[]{:S(2)}) %copy-start.4) | copy-done | bytes 65560
  9.8 2.2 %tables_kernel.1 = (f32[128,512]{1,0:T(8,128)S(1)}, f32[128,512]{1,0:T(8,128)S(1)}, bf16[128,512]{1,0:T(8,128)(2,1)S(1)}, bf16[128,512]{1,0:T(8,128)(2,1)S(1)}, ...) custom-call(f32[16]{0:T(128)S(1)} %copy-done.9, ...), custom_call_target="tpu_custom_call" | custom-call | tf_op jit(solution)/shard_map/tables_kernel/pallas_call | solution.py:49
  12.0 0.7 own_kernel.1
  13.4 1.4 %collective-permute-done.3.refs_2_.refs_5_ = f32[8,1024]{1,0:T(8,128)S(1)} collective-permute-done((f32[8,1024]{1,0:T(8,128)S(1)}, f32[8,1024]{1,0:T(8,128)S(1)}, u32[]{:S(2)}, u32[]{:S(2)}) %collective-permute-start.3) | collective-permute-done | bytes 32800 | tf_op jit(solution)/shard_map/ppermute | solution.py:394
  14.9 1.7 %local_output_kernel.1.refs_7_.refs_2_ = f32[256,1024]{1,0:T(8,128)S(1)} custom-call(f32[16]{0:T(128)S(1)} %copy-done.8, bf16[256,1024]{1,0:T(8,128)(2,1)S(1)} %bitcast.13, bf16[256,128]{1,0:T(8,128)(2,1)S(1)} %bitcast.22, bf16[256,128]{1,0:T(8,128)(2,1)S(1)} %bitcast.15, f32[16,256]{1,0:T(8,128)S(1)} %get-tuple-element.45.refs_4_.refs_5_, ...), custom_call_target="tpu_custom_call" | custom-call | tf_op jit(solution)/shard_map/local_output_kernel/pallas_call | solution.py:49
  17.3 2.5 %collective-permute-start.6 = (bf16[128,1024]{1,0:T(8,128)(2,1)S(1)}, bf16[128,1024]{1,0:T(8,128)(2,1)S(1)}, u32[]{:S(2)}, u32[]{:S(2)}) collective-permute-start(bf16[128,1024]{1,0:T(8,128)(2,1)S(1)} %chip_total_kernel.2), channel_id=1, source_target_pairs={{0,16},{8,24},{1,17},{9,25},{2,18},{10,26},{3,19},{11,27},{4,20},{... | collective-permute-start | bytes 786440 | tf_op jit(solution)/shard_map/ppermute | solution.py:459
  19.8 1.0 %collective-permute-done.1.refs_1_ = bf16[256,1024]{1,0:T(8,128)(2,1)S(1)} collective-permute-done((bf16[256,1024]{1,0:T(8,128)(2,1)S(1)}, bf16[256,1024]{1,0:T(8,128)(2,1)S(1)}, u32[]{:S(2)}, u32[]{:S(2)}) %collective-permute-start.1) | collective-permute-done | bytes 524320 | tf_op jit(solution)/shard_map/ppermute | solution.py:397
  20.8 1.6 %collective-permute-start.2 = (bf16[256,1024]{1,0:T(8,128)(2,1)S(1)}, bf16[256,1024]{1,0:T(8,128)(2,1)S(1)}, u32[]{:S(2)}, u32[]{:S(2)}) collective-permute-start(bf16[256,1024]{1,0:T(8,128)(2,1)S(1)} %collective-permute-done.1.refs_1_), channel_id=1, source_target_pairs={{0,2},{2,0},{4,6},{6,4},{1,3},{3,1},{5,7},{7,5},{8,10},{10,8},{12,... | collective-permute-start | bytes 1572872 | tf_op jit(solution)/shard_map/ppermute | solution.py:400
  22.3 3.5 %collective-permute-done.6.refs_6_ = bf16[128,1024]{1,0:T(8,128)(2,1)S(1)} collective-permute-done((bf16[128,1024]{1,0:T(8,128)(2,1)S(1)}, bf16[128,1024]{1,0:T(8,128)(2,1)S(1)}, u32[]{:S(2)}, u32[]{:S(2)}) %collective-permute-start.6) | collective-permute-done | bytes 262176 | tf_op jit(solution)/shard_map/ppermute | solution.py:459
  25.8 0.9 %output_kernel.2 = (bf16[256,384]{1,0:T(8,128)(2,1)S(1)}, bf16[128,384]{1,0:T(8,128)(2,1)S(1)}) custom-call(s32[10]{0:T(128)S(1)} %dynamic-slice_bitcast_fusion.refs_0_, s32[1,1]{1,0:T(1,128)S(6)} %copy.14.refs_1_.refs_0_, f32[256,1024]{1,0:T(8,128)S(1)} %local_output_kernel.1.refs_7_.refs_2_, bf16[256,128]{1,0:T(8,128)(2,1)S(1)} %bitcast.16, ...), custom_call_target="tpu_custom_call" | custom-call | tf_op jit(solution)/shard_map/output_kernel/pallas_call | solution.py:49
  26.7 1.0 %output_kernel.3 = (bf16[256,640]{1,0:T(8,128)(2,1)S(1)}, bf16[128,640]{1,0:T(8,128)(2,1)S(1)}) custom-call(s32[10]{0:T(128)S(1)} %dynamic-slice_bitcast_fusion.refs_0_, s32[1,1]{1,0:T(1,128)S(6)} %copy.14.refs_1_.refs_0_, f32[256,1024]{1,0:T(8,128)S(1)} %local_output_kernel.1.refs_7_.refs_2_, bf16[256,128]{1,0:T(8,128)(2,1)S(1)} %bitcast.17, ...), custom_call_target="tpu_custom_call" | custom-call | tf_op jit(solution)/shard_map/output_kernel/pallas_call | solution.py:49
  28.4 2.5 %collective-permute-start.14 = (bf16[256,384]{1,0:T(8,128)(2,1)S(1)}, bf16[256,384]{1,0:T(8,128)(2,1)S(1)}, u32[]{:S(2)}, u32[]{:S(2)}) collective-permute-start(bf16[256,384]{1,0:T(8,128)(2,1)S(1)} %get-tuple-element.50.refs_9_.refs_6_), channel_id=1, source_target_pairs={{0,16},{8,24},{16,0},{24,8},{1,17},{9,25},{17,1},{25,9},{2,18},{10... | collective-permute-start | bytes 589832 | tf_op jit(solution)/shard_map/ppermute | solution.py:397
  30.9 3.0 %collective-permute-done.2.refs_2_ = bf16[256,1024]{1,0:T(8,128)(2,1)S(1)} collective-permute-done((bf16[256,1024]{1,0:T(8,128)(2,1)S(1)}, bf16[256,1024]{1,0:T(8,128)(2,1)S(1)}, u32[]{:S(2)}, u32[]{:S(2)}) %collective-permute-start.2) | collective-permute-done | bytes 524320 | tf_op jit(solution)/shard_map/ppermute | solution.py:400
  34.6 2.0 %collective-permute-done.14.refs_7_ = bf16[256,384]{1,0:T(8,128)(2,1)S(1)} collective-permute-done((bf16[256,384]{1,0:T(8,128)(2,1)S(1)}, bf16[256,384]{1,0:T(8,128)(2,1)S(1)}, u32[]{:S(2)}, u32[]{:S(2)}) %collective-permute-start.14) | collective-permute-done | bytes 196640 | tf_op jit(solution)/shard_map/ppermute | solution.py:397
  37.2 2.3 %head_partial_kernel.1 = (f32[256,1024]{1,0:T(8,128)S(1)}, bf16[256,1024]{1,0:T(8,128)(2,1)S(1)}) custom-call(bf16[256,1024]{1,0:T(8,128)(2,1)S(1)} %get-tuple-element.43.refs_0_, bf16[256,1024]{1,0:T(8,128)(2,1)S(1)} %get-tuple-element.44.refs_1_, bf16[256,512]{1,0:T(8,128)(2,1)S(1)} %get-tuple-element.52.refs_2_, ...), custom_call_target="tpu_custom_call" | custom-call | tf_op jit(solution)/shard_map/head_partial_kernel/pallas_call | solution.py:49
  39.5 2.1 %collective-permute-start.11 = (bf16[256,1024]{1,0:T(8,128)(2,1)S(1)}, bf16[256,1024]{1,0:T(8,128)(2,1)S(1)}, u32[]{:S(2)}, u32[]{:S(2)}) collective-permute-start(bf16[256,1024]{1,0:T(8,128)(2,1)S(1)} %get-tuple-element.58), channel_id=1, source_target_pairs={{0,16},{8,24},{16,0},{24,8},{1,17},{9,25},{17,1},{25,9},{2,18},{10... | collective-permute-start | bytes 1572872 | tf_op jit(solution)/shard_map/ppermute | solution.py:397
  41.8 1.3 %weight_partial_kernel.2 = (bf16[512,384]{1,0:T(8,128)(2,1)S(1)}, f32[512,384]{1,0:T(8,128)S(1)}) custom-call(bf16[256,1024]{1,0:T(8,128)(2,1)S(1)} %get-tuple-element.43.refs_0_, bf16[256,1024]{1,0:T(8,128)(2,1)S(1)} %collective-permute-done.7.refs_9_.refs_1_, bf16[256,512]{1,0:T(8,128)(2,1)S(1)} %get-tuple-element.52.refs_2_, ...), custom_call_target="tpu_custom_call" | custom-call | tf_op jit(solution)/shard_map/weight_partial_kernel/pallas_call | solution.py:49
  43.5 0.7 %collective-permute-start.17 = (bf16[512,384]{1,0:T(8,128)(2,1)S(1)}, bf16[512,384]{1,0:T(8,128)(2,1)S(1)}, u32[]{:S(2)}, u32[]{:S(2)}) collective-permute-start(bf16[512,384]{1,0:T(8,128)(2,1)S(1)} %get-tuple-element.59.refs_11_.refs_6_), channel_id=1, source_target_pairs={{0,1},{1,0},{2,3},{3,2},{4,5},{5,4},{6,7},{7,6},{8,9},{9,8},{10,11... | collective-permute-start | bytes 1179656 | tf_op jit(solution)/shard_map/ppermute | solution.py:403
  44.8 1.8 %weight_partial_kernel.3 = (bf16[512,640]{1,0:T(8,128)(2,1)S(1)}, f32[512,640]{1,0:T(8,128)S(1)}) custom-call(bf16[256,1024]{1,0:T(8,128)(2,1)S(1)} %get-tuple-element.43.refs_0_, bf16[256,1024]{1,0:T(8,128)(2,1)S(1)} %collective-permute-done.7.refs_9_.refs_1_, bf16[256,512]{1,0:T(8,128)(2,1)S(1)} %get-tuple-element.52.refs_2_, ...), custom_call_target="tpu_custom_call" | custom-call | tf_op jit(solution)/shard_map/weight_partial_kernel/pallas_call | solution.py:49
  46.7 1.0 %collective-permute-start.23 = (bf16[512,640]{1,0:T(8,128)(2,1)S(1)}, bf16[512,640]{1,0:T(8,128)(2,1)S(1)}, u32[]{:S(2)}, u32[]{:S(2)}) collective-permute-start(bf16[512,640]{1,0:T(8,128)(2,1)S(1)} %get-tuple-element.61.refs_7_), channel_id=1, source_target_pairs={{0,1},{1,0},{2,3},{3,2},{4,5},{5,4},{6,7},{7,6},{8,9},{9,8},{10,11... | collective-permute-start | bytes 1966088 | tf_op jit(solution)/shard_map/ppermute | solution.py:403
  47.6 7.9 %collective-permute-done.17.refs_5_.refs_2_ = bf16[512,384]{1,0:T(8,128)(2,1)S(1)} collective-permute-done((bf16[512,384]{1,0:T(8,128)(2,1)S(1)}, bf16[512,384]{1,0:T(8,128)(2,1)S(1)}, u32[]{:S(2)}, u32[]{:S(2)}) %collective-permute-start.17) | collective-permute-done | bytes 393248 | tf_op jit(solution)/shard_map/ppermute | solution.py:403
  55.5 1.0 %adjoint_kernel.1 = (bf16[256,1024]{1,0:T(8,128)(2,1)S(1)}, bf16[256,1024]{1,0:T(8,128)(2,1)S(1)}, f32[128,1024]{1,0:T(8,128)S(1)}, bf16[128,1024]{1,0:T(8,128)(2,1)S(1)}) custom-call(s32[1,1]{1,0:T(1,128)S(6)} %copy.14.refs_1_.refs_0_, f32[256,1024]{1,0:T(8,128)S(1)} %get-tuple-element.57.refs_10_.refs_1_, ...), custom_call_target="tpu_custom_call" | custom-call | tf_op jit(solution)/shard_map/adjoint_kernel/pallas_call | solution.py:49
  56.5 1.5 %collective-permute-done.21.refs_4_.refs_8_ = bf16[128,1024]{1,0:T(8,128)(2,1)S(1)} collective-permute-done((bf16[128,1024]{1,0:T(8,128)(2,1)S(1)}, bf16[128,1024]{1,0:T(8,128)(2,1)S(1)}, u32[]{:S(2)}, u32[]{:S(2)}) %collective-permute-start.21) | collective-permute-done | bytes 262176 | tf_op jit(solution)/shard_map/ppermute | solution.py:394
  58.7 1.5 %collective-permute-start.22 = (bf16[128,1024]{1,0:T(8,128)(2,1)S(1)}, bf16[128,1024]{1,0:T(8,128)(2,1)S(1)}, u32[]{:S(2)}, u32[]{:S(2)}) collective-permute-start(bf16[128,1024]{1,0:T(8,128)(2,1)S(1)} %chip_total_kernel.3), channel_id=1, source_target_pairs={{16,0},{24,8},{17,1},{25,9},{18,2},{26,10},{19,3},{27,11},{20,4},{... | collective-permute-start | bytes 786440 | tf_op jit(solution)/shard_map/ppermute | solution.py:545
  60.2 2.4 %local_grads_kernel.1 = (f32[256,1024]{1,0:T(8,128)S(1)}, f32[256,256]{1,0:T(8,128)S(1)}, f32[256,128]{1,0:T(8,128)S(1)}) custom-call(f32[16]{0:T(128)S(1)} %copy-done.8, bf16[256,1024]{1,0:T(8,128)(2,1)S(1)} %bitcast.14, bf16[256,1024]{1,0:T(8,128)(2,1)S(1)} %get-tuple-element.62.refs_2_, bf16[256,128]{1,0:T(8,128)(2,1)S(1)} %bitcast.23, ...), custom_call_target="tpu_custom_call" | custom-call | tf_op jit(solution)/shard_map/local_grads_kernel/pallas_call | solution.py:49
  62.7 0.9 %group_sums_kernel.1 = (f32[256,128]{1,0:T(8,128)S(1)}, f32[256,128]{1,0:T(8,128)}) custom-call(bf16[256,128]{1,0:T(8,128)(2,1)S(1)} %bitcast.24, bf16[256,128]{1,0:T(8,128)(2,1)S(1)} %bitcast.20, f32[256,256]{1,0:T(8,128)S(1)} %get-tuple-element.66.refs_2_, f32[256,128]{1,0:T(8,128)S(1)} %get-tuple-element.67.refs_3_), custom_call_target="tpu_custom_call" | custom-call | tf_op jit(solution)/shard_map/group_sums_kernel/pallas_call | solution.py:49
  63.6 5.2 %collective-permute-done.23.refs_3_ = bf16[512,640]{1,0:T(8,128)(2,1)S(1)} collective-permute-done((bf16[512,640]{1,0:T(8,128)(2,1)S(1)}, bf16[512,640]{1,0:T(8,128)(2,1)S(1)}, u32[]{:S(2)}, u32[]{:S(2)}) %collective-permute-start.23) | collective-permute-done | bytes 655392 | tf_op jit(solution)/shard_map/ppermute | solution.py:403
  68.8 1.5 %add_kernel.1 = f32[512,1024]{1,0:T(8,128)} custom-call(f32[512,384]{1,0:T(8,128)S(1)} %get-tuple-element.76.refs_0_, f32[512,640]{1,0:T(8,128)S(1)} %get-tuple-element.77.refs_1_, bf16[512,384]{1,0:T(8,128)(2,1)S(1)} %collective-permute-done.17.refs_5_.refs_2_, bf16[512,640]{1,0:T(8,128)(2,1)S(1)} %collective-permute-done.23.refs_3_), custom_call_target="tpu_custom_call" | custom-call | tf_op jit(solution)/shard_map/add_kernel/pallas_call | solution.py:49
  70.3 2.1 %final_kernel.1 = (bf16[256,1024]{1,0:T(8,128)(2,1)}, f32[256,128]{1,0:T(8,128)}) custom-call(s32[10]{0:T(128)S(1)} %dynamic-slice_bitcast_fusion.refs_0_, bf16[256,128]{1,0:T(8,128)(2,1)S(1)} %bitcast.25, f32[256,16]{1,0:T(8,128)S(1)} %get-tuple-element.41.refs_5_.refs_4_.refs_6_.refs_2_, f32[256,128]{1,0:T(8,128)S(1)} %get-tuple-element.68.refs_3_, ...), custom_call_target="tpu_custom_call" | custom-call | tf_op jit(solution)/shard_map/final_kernel/pallas_call | solution.py:49
  (55 shorter events, 7.2 us)
Async XLA Ops:
  0.6 8.3 %copy-start.7 = (f32[1,16,256]{2,1,0:T(8,128)S(1)}, f32[1,16,256]{2,1,0:T(8,128)}, u32[]{:S(2)}) copy-start(f32[1,16,256]{2,1,0:T(8,128)} %param.13) | copy-start | bytes 49156
  0.6 8.3 %copy-start.9 = (f32[16]{0:T(128)S(1)}, f32[16]{0:T(128)}, u32[]{:S(2)}) copy-start(f32[16]{0:T(128)} %refs_0_.4) | copy-start | bytes 196
  0.7 8.3 %collective-permute-start = (bf16[512,1024]{1,0:T(8,128)(2,1)}, bf16[512,1024]{1,0:T(8,128)(2,1)S(1)}, u32[]{:S(2)}, u32[]{:S(2)}) collective-permute-start(bf16[512,1024]{1,0:T(8,128)(2,1)} %refs_6_.1), channel_id=1, source_target_pairs={{0,8},{8,0},{16,24},{24,16},{1,9},{9,1},{17,25},{25,17},{2,10},{10... | collective-permute-start | bytes 3145736 | tf_op jit(solution)/shard_map/ppermute | solution.py:394
  1.2 26.6 %collective-permute-start.8 = (bf16[512,1024]{1,0:T(8,128)(2,1)}, bf16[512,1024]{1,0:T(8,128)(2,1)S(1)}, u32[]{:S(2)}, u32[]{:S(2)}) collective-permute-start(bf16[512,1024]{1,0:T(8,128)(2,1)} %refs_6_.1), channel_id=1, source_target_pairs={{0,1},{1,0},{2,3},{3,2},{4,5},{5,4},{6,7},{7,6},{8,9},{9,8},{10,11... | collective-permute-start | bytes 3145736 | tf_op jit(solution)/shard_map/ppermute | solution.py:403
  6.0 2.9 %copy-start.2 = (bf16[1,256,1024]{2,1,0:T(8,128)(2,1)S(1)}, bf16[1,256,1024]{2,1,0:T(8,128)(2,1)}, u32[]{:S(2)}) copy-start(bf16[1,256,1024]{2,1,0:T(8,128)(2,1)} %param.10) | copy-start | bytes 1572868
  6.0 6.0 %copy-start.1 = (bf16[1,256,4096]{2,1,0:T(8,128)(2,1)S(1)}, bf16[1,256,4096]{2,1,0:T(8,128)(2,1)}, u32[]{:S(2)}) copy-start(bf16[1,256,4096]{2,1,0:T(8,128)(2,1)} %param.17) | copy-start | bytes 6291460
  6.7 14.1 %collective-permute-start.1 = (bf16[256,1024]{1,0:T(8,128)(2,1)S(1)}, bf16[256,1024]{1,0:T(8,128)(2,1)S(1)}, u32[]{:S(2)}, u32[]{:S(2)}) collective-permute-start(bf16[256,1024]{1,0:T(8,128)(2,1)S(1)} %send_kernel.1.refs_6_), channel_id=1, source_target_pairs={{0,16},{8,24},{16,0},{24,8},{1,17},{9,25},{17,1},{25,9},{2,18},{10... | collective-permute-start | bytes 1572872 | tf_op jit(solution)/shard_map/ppermute | solution.py:397
  9.8 5.1 %copy-start.3 = (bf16[1,256,128]{2,1,0:T(8,128)(2,1)S(1)}, bf16[1,256,128]{2,1,0:T(8,128)(2,1)}, u32[]{:S(2)}) copy-start(bf16[1,256,128]{2,1,0:T(8,128)(2,1)} %param.12) | copy-start | bytes 196612
  9.8 5.1 %copy-start.5 = (bf16[1,256,128]{2,1,0:T(8,128)(2,1)S(1)}, bf16[1,256,128]{2,1,0:T(8,128)(2,1)}, u32[]{:S(2)}) copy-start(bf16[1,256,128]{2,1,0:T(8,128)(2,1)} %param.11) | copy-start | bytes 196612
  9.8 5.1 %copy-start.8 = (f32[16]{0:T(128)S(1)}, f32[16]{0:T(128)}, u32[]{:S(2)}) copy-start(f32[16]{0:T(128)} %refs_0_.6) | copy-start | bytes 196
  12.7 13.1 %collective-permute-start.7 = (bf16[256,1024]{1,0:T(8,128)(2,1)S(1)}, bf16[256,1024]{1,0:T(8,128)(2,1)S(1)}, u32[]{:S(2)}, u32[]{:S(2)}) collective-permute-start(bf16[256,1024]{1,0:T(8,128)(2,1)S(1)} %get-tuple-element.44.refs_1_), channel_id=1, source_target_pairs={{0,8},{8,0},{16,24},{24,16},{1,9},{9,1},{17,25},{25,17},{2,10},{10... | collective-permute-start | bytes 1572872 | tf_op jit(solution)/shard_map/ppermute | solution.py:394
  12.8 1.9 %collective-permute-start.3 = (f32[8,1024]{1,0:T(8,128)S(1)}, f32[8,1024]{1,0:T(8,128)S(1)}, u32[]{:S(2)}, u32[]{:S(2)}) collective-permute-start(f32[8,1024]{1,0:T(8,128)S(1)} %get-tuple-element.42.refs_2_.refs_1_), channel_id=1, source_target_pairs={{0,8},{8,0},{16,24},{24,16},{1,9},{9,1},{17,25},{25,17},{2,10},{10... | collective-permute-start | bytes 98312 | tf_op jit(solution)/shard_map/ppermute | solution.py:394
  13.3 3.3 %collective-permute-start.4 = (bf16[128,512]{1,0:T(8,128)(2,1)S(1)}, bf16[128,512]{1,0:T(8,128)(2,1)S(1)}, u32[]{:S(2)}, u32[]{:S(2)}) collective-permute-start(bf16[128,512]{1,0:T(8,128)(2,1)S(1)} %get-tuple-element.48), channel_id=1, source_target_pairs={{0,8},{8,0},{16,24},{24,16},{1,9},{9,1},{17,25},{25,17},{2,10},{10... | collective-permute-start | bytes 393224 | tf_op jit(solution)/shard_map/ppermute | solution.py:394
  14.8 1.8 %collective-permute-start.5 = (bf16[128,512]{1,0:T(8,128)(2,1)S(1)}, bf16[128,512]{1,0:T(8,128)(2,1)S(1)}, u32[]{:S(2)}, u32[]{:S(2)}) collective-permute-start(bf16[128,512]{1,0:T(8,128)(2,1)S(1)} %get-tuple-element.49), channel_id=1, source_target_pairs={{0,8},{8,0},{16,24},{24,16},{1,9},{9,1},{17,25},{25,17},{2,10},{10... | collective-permute-start | bytes 393224 | tf_op jit(solution)/shard_map/ppermute | solution.py:394
  17.3 8.5 %collective-permute-start.6 = (bf16[128,1024]{1,0:T(8,128)(2,1)S(1)}, bf16[128,1024]{1,0:T(8,128)(2,1)S(1)}, u32[]{:S(2)}, u32[]{:S(2)}) collective-permute-start(bf16[128,1024]{1,0:T(8,128)(2,1)S(1)} %chip_total_kernel.2), channel_id=1, source_target_pairs={{0,16},{8,24},{1,17},{9,25},{2,18},{10,26},{3,19},{11,27},{4,20},{... | collective-permute-start | bytes 786440 | tf_op jit(solution)/shard_map/ppermute | solution.py:459
  20.8 13.2 %collective-permute-start.2 = (bf16[256,1024]{1,0:T(8,128)(2,1)S(1)}, bf16[256,1024]{1,0:T(8,128)(2,1)S(1)}, u32[]{:S(2)}, u32[]{:S(2)}) collective-permute-start(bf16[256,1024]{1,0:T(8,128)(2,1)S(1)} %collective-permute-done.1.refs_1_), channel_id=1, source_target_pairs={{0,2},{2,0},{4,6},{6,4},{1,3},{3,1},{5,7},{7,5},{8,10},{10,8},{12,... | collective-permute-start | bytes 1572872 | tf_op jit(solution)/shard_map/ppermute | solution.py:400
  27.7 9.4 %copy-start.6 = (bf16[512,1024]{1,0:T(8,128)(2,1)S(1)}, bf16[512,1024]{1,0:T(8,128)(2,1)}, u32[]{:S(2)}) copy-start(bf16[512,1024]{1,0:T(8,128)(2,1)} %refs_6_.1) | copy-start | bytes 3145732
  27.8 8.8 %collective-permute-start.10 = (bf16[256,1024]{1,0:T(8,128)(2,1)S(1)}, bf16[256,1024]{1,0:T(8,128)(2,1)S(1)}, u32[]{:S(2)}, u32[]{:S(2)}) collective-permute-start(bf16[256,1024]{1,0:T(8,128)(2,1)S(1)} %get-tuple-element.78), channel_id=1, source_target_pairs={{0,8},{8,0},{16,24},{24,16},{1,9},{9,1},{17,25},{25,17},{2,10},{10... | collective-permute-start | bytes 1572872 | tf_op jit(solution)/shard_map/ppermute | solution.py:394
  27.9 9.2 %collective-permute-start.9 = (bf16[256,1024]{1,0:T(8,128)(2,1)S(1)}, bf16[256,1024]{1,0:T(8,128)(2,1)S(1)}, u32[]{:S(2)}, u32[]{:S(2)}) collective-permute-start(bf16[256,1024]{1,0:T(8,128)(2,1)S(1)} %get-tuple-element.79), channel_id=1, source_target_pairs={{0,8},{8,0},{16,24},{24,16},{1,9},{9,1},{17,25},{25,17},{2,10},{10... | collective-permute-start | bytes 1572872 | tf_op jit(solution)/shard_map/ppermute | solution.py:394
  28.4 8.2 %collective-permute-start.14 = (bf16[256,384]{1,0:T(8,128)(2,1)S(1)}, bf16[256,384]{1,0:T(8,128)(2,1)S(1)}, u32[]{:S(2)}, u32[]{:S(2)}) collective-permute-start(bf16[256,384]{1,0:T(8,128)(2,1)S(1)} %get-tuple-element.50.refs_9_.refs_6_), channel_id=1, source_target_pairs={{0,16},{8,24},{16,0},{24,8},{1,17},{9,25},{17,1},{25,9},{2,18},{10... | collective-permute-start | bytes 589832 | tf_op jit(solution)/shard_map/ppermute | solution.py:397
  30.9 12.2 %collective-permute-start.18 = (bf16[256,640]{1,0:T(8,128)(2,1)S(1)}, bf16[256,640]{1,0:T(8,128)(2,1)S(1)}, u32[]{:S(2)}, u32[]{:S(2)}) collective-permute-start(bf16[256,640]{1,0:T(8,128)(2,1)S(1)} %get-tuple-element.51.refs_3_.refs_6_), channel_id=1, source_target_pairs={{0,16},{8,24},{16,0},{24,8},{1,17},{9,25},{17,1},{25,9},{2,18},{10... | collective-permute-start | bytes 983048 | tf_op jit(solution)/shard_map/ppermute | solution.py:397
  34.6 7.1 %collective-permute-start.12 = (bf16[256,512]{1,0:T(8,128)(2,1)S(1)}, bf16[256,512]{1,0:T(8,128)(2,1)S(1)}, u32[]{:S(2)}, u32[]{:S(2)}) collective-permute-start(bf16[256,512]{1,0:T(8,128)(2,1)S(1)} %get-tuple-element.54.refs_4_), channel_id=1, source_target_pairs={{0,8},{8,0},{16,24},{24,16},{1,9},{9,1},{17,25},{25,17},{2,10},{10... | collective-permute-start | bytes 786440 | tf_op jit(solution)/shard_map/ppermute | solution.py:394
  36.6 5.2 %collective-permute-start.13 = (bf16[256,512]{1,0:T(8,128)(2,1)S(1)}, bf16[256,512]{1,0:T(8,128)(2,1)S(1)}, u32[]{:S(2)}, u32[]{:S(2)}) collective-permute-start(bf16[256,512]{1,0:T(8,128)(2,1)S(1)} %get-tuple-element.55.refs_5_), channel_id=1, source_target_pairs={{0,8},{8,0},{16,24},{24,16},{1,9},{9,1},{17,25},{25,17},{2,10},{10... | collective-permute-start | bytes 786440 | tf_op jit(solution)/shard_map/ppermute | solution.py:394
  36.6 2.9 %collective-permute-start.15 = (bf16[256,384]{1,0:T(8,128)(2,1)S(1)}, bf16[256,384]{1,0:T(8,128)(2,1)S(1)}, u32[]{:S(2)}, u32[]{:S(2)}) collective-permute-start(bf16[256,384]{1,0:T(8,128)(2,1)S(1)} %get-tuple-element.50.refs_9_.refs_6_), channel_id=1, source_target_pairs={{0,8},{8,0},{16,24},{24,16},{1,9},{9,1},{17,25},{25,17},{2,10},{10... | collective-permute-start | bytes 589832 | tf_op jit(solution)/shard_map/ppermute | solution.py:394
  37.1 4.7 %collective-permute-start.16 = (bf16[256,384]{1,0:T(8,128)(2,1)S(1)}, bf16[256,384]{1,0:T(8,128)(2,1)S(1)}, u32[]{:S(2)}, u32[]{:S(2)}) collective-permute-start(bf16[256,384]{1,0:T(8,128)(2,1)S(1)} %collective-permute-done.14.refs_7_), channel_id=1, source_target_pairs={{0,8},{8,0},{16,24},{24,16},{1,9},{9,1},{17,25},{25,17},{2,10},{10... | collective-permute-start | bytes 589832 | tf_op jit(solution)/shard_map/ppermute | solution.py:394
  39.5 16.0 %collective-permute-start.11 = (bf16[256,1024]{1,0:T(8,128)(2,1)S(1)}, bf16[256,1024]{1,0:T(8,128)(2,1)S(1)}, u32[]{:S(2)}, u32[]{:S(2)}) collective-permute-start(bf16[256,1024]{1,0:T(8,128)(2,1)S(1)} %get-tuple-element.58), channel_id=1, source_target_pairs={{0,16},{8,24},{16,0},{24,8},{1,17},{9,25},{17,1},{25,9},{2,18},{10... | collective-permute-start | bytes 1572872 | tf_op jit(solution)/shard_map/ppermute | solution.py:397
  41.7 2.6 %collective-permute-start.19 = (bf16[256,640]{1,0:T(8,128)(2,1)S(1)}, bf16[256,640]{1,0:T(8,128)(2,1)S(1)}, u32[]{:S(2)}, u32[]{:S(2)}) collective-permute-start(bf16[256,640]{1,0:T(8,128)(2,1)S(1)} %get-tuple-element.51.refs_3_.refs_6_), channel_id=1, source_target_pairs={{0,8},{8,0},{16,24},{24,16},{1,9},{9,1},{17,25},{25,17},{2,10},{10... | collective-permute-start | bytes 983048 | tf_op jit(solution)/shard_map/ppermute | solution.py:394
  43.1 1.7 %collective-permute-start.20 = (bf16[256,640]{1,0:T(8,128)(2,1)S(1)}, bf16[256,640]{1,0:T(8,128)(2,1)S(1)}, u32[]{:S(2)}, u32[]{:S(2)}) collective-permute-start(bf16[256,640]{1,0:T(8,128)(2,1)S(1)} %collective-permute-done.18.refs_7_), channel_id=1, source_target_pairs={{0,8},{8,0},{16,24},{24,16},{1,9},{9,1},{17,25},{25,17},{2,10},{10... | collective-permute-start | bytes 983048 | tf_op jit(solution)/shard_map/ppermute | solution.py:394
  43.5 12.0 %collective-permute-start.17 = (bf16[512,384]{1,0:T(8,128)(2,1)S(1)}, bf16[512,384]{1,0:T(8,128)(2,1)S(1)}, u32[]{:S(2)}, u32[]{:S(2)}) collective-permute-start(bf16[512,384]{1,0:T(8,128)(2,1)S(1)} %get-tuple-element.59.refs_11_.refs_6_), channel_id=1, source_target_pairs={{0,1},{1,0},{2,3},{3,2},{4,5},{5,4},{6,7},{7,6},{8,9},{9,8},{10,11... | collective-permute-start | bytes 1179656 | tf_op jit(solution)/shard_map/ppermute | solution.py:403
  46.7 22.1 %collective-permute-start.23 = (bf16[512,640]{1,0:T(8,128)(2,1)S(1)}, bf16[512,640]{1,0:T(8,128)(2,1)S(1)}, u32[]{:S(2)}, u32[]{:S(2)}) collective-permute-start(bf16[512,640]{1,0:T(8,128)(2,1)S(1)} %get-tuple-element.61.refs_7_), channel_id=1, source_target_pairs={{0,1},{1,0},{2,3},{3,2},{4,5},{5,4},{6,7},{7,6},{8,9},{9,8},{10,11... | collective-permute-start | bytes 1966088 | tf_op jit(solution)/shard_map/ppermute | solution.py:403
  56.5 1.6 %collective-permute-start.21 = (bf16[128,1024]{1,0:T(8,128)(2,1)S(1)}, bf16[128,1024]{1,0:T(8,128)(2,1)S(1)}, u32[]{:S(2)}, u32[]{:S(2)}) collective-permute-start(bf16[128,1024]{1,0:T(8,128)(2,1)S(1)} %get-tuple-element.71), channel_id=1, source_target_pairs={{0,8},{8,0},{16,24},{24,16},{1,9},{9,1},{17,25},{25,17},{2,10},{10... | collective-permute-start | bytes 786440 | tf_op jit(solution)/shard_map/ppermute | solution.py:394
  58.7 11.5 %collective-permute-start.22 = (bf16[128,1024]{1,0:T(8,128)(2,1)S(1)}, bf16[128,1024]{1,0:T(8,128)(2,1)S(1)}, u32[]{:S(2)}, u32[]{:S(2)}) collective-permute-start(bf16[128,1024]{1,0:T(8,128)(2,1)S(1)} %chip_total_kernel.3), channel_id=1, source_target_pairs={{16,0},{24,8},{17,1},{25,9},{18,2},{26,10},{19,3},{27,11},{20,4},{... | collective-permute-start | bytes 786440 | tf_op jit(solution)/shard_map/ppermute | solution.py:545
  (2 other events, 2.4 us)

commit v4 on v3

--- a/solution.py
+++ b/solution.py
@@ -14,8 +14,6 @@
 HALF = 128
 PAIR = 2 * P_SIZE
 SHARES = (6, 10)
-CUTS = 1
-BACK = 1
 PARITY, CORE, ODD, CHIP = 4, 6, 7, 8
 BF = jnp.bfloat16
 F32 = jnp.float32
@@ -32,10 +30,6 @@
 
 def whole(shape):
     return pl.BlockSpec(shape, lambda *_: (0,) * len(shape))
-
-
-def columns_of(array, width, part):
-    return array, pl.BlockSpec((array.shape[0], width), lambda *_: (0, part))
 
 
 def call(kernel, scalars, arrays, outs, after=(), aliases=None):
@@ -212,11 +206,11 @@
             out_ref[rows, :] = jnp.where(even, first[:, taken], second[:, taken])
 
 
-def head_partial_kernel(cuts, mine_ref, other_ref, *refs):
+def head_partial_kernel(mine_ref, other_ref, *refs):
     came, weights, outs = refs[:4], refs[4:9], refs[9:]
     depth = weights[0].shape[0]
     middle = weights[3].shape[0]
-    for number in reversed(range(1 + (len(outs) - 1) // cuts)):
+    for number in reversed(range(len(outs))):
         total = None
         for block in range(4):
             rows = slice((number - 1) * Q, number * Q)
@@ -229,51 +223,55 @@
             else:
                 term = dot(grad[:, :middle], weights[3][...], 1, 0) + dot(grad[:, middle:], weights[4][...], 1, 0)
             total = term if total is None else total + term
-        if number == 0:
-            outs[0][...] = total
-            continue
-        width = total.shape[1] // cuts
-        for cut in range(cuts):
-            part = total[:, cut * width : (cut + 1) * width]
-            outs[1 + (number - 1) * cuts + cut][...] = part.astype(BF)
-
-
-def adjoint_kernel(others, cuts, offset, resets_ref, own_ref, *refs):
-    parts, (c_ref, cols_ref, head_ref, weighted_ref, adjoint_ref, sent_ref) = refs[: others * cuts], refs[others * cuts :]
+        outs[number][...] = total.astype(outs[number].dtype)
+
+
+def adjoint_kernel(others, resets_ref, own_ref, *refs):
+    parts, (c_ref, cols_ref, head_ref, weighted_ref, *halves) = refs[:others], refs[others:]
     first = first_head()
     cols = cols_ref[...]
-    width = own_ref.shape[1] // cuts
     keep = (1 - resets_ref[0, 0]).astype(F32)
     for pair in range(head_ref.shape[1] // PAIR):
         at = slice(pair * PAIR, (pair + 1) * PAIR)
         total = own_ref[:, at]
-        cut, place = pair * PAIR // width, pair * PAIR % width
-        for other in range(others):
-            total = total + parts[other * cuts + cut][:, place : place + PAIR].astype(F32)
+        for part in parts:
+            total = total + part[:, at].astype(F32)
         head = total.astype(BF)
         head_ref[:, at] = head
-        weighted_ref[:, at] = (head.astype(F32) * jnp.exp(spread(cols, offset + pair, first))).astype(BF)
+        weighted_ref[:, at] = (head.astype(F32) * jnp.exp(spread(cols, pair, first))).astype(BF)
     adjoint = keep * dot(c_ref[...], weighted_ref[...], 0, 0)
-    adjoint_ref[...] = adjoint
-    sent_ref[...] = adjoint.astype(BF)
+    middle = adjoint.shape[1] // 2
+    for number in range(2):
+        half = adjoint[:, number * middle : (number + 1) * middle]
+        halves[number][...] = half
+        halves[2][:, number * middle : (number + 1) * middle] = half.astype(BF)
 
 
 def chip_total_kernel(last, parts, ids_ref, through_ref, partner_through_ref, *refs):
-    owns, partners, entering, out_ref = refs[:parts], refs[parts : 2 * parts], refs[2 * parts : -1], refs[-1]
+    owns, partners, entering, out_ref = refs[:2], refs[2 : 2 + parts], refs[2 + parts : -1], refs[-1]
     leaves = ids_ref[CORE] == last
     width = owns[0].shape[1]
-    for part in range(parts):
+    halved = out_ref.shape[1] < 2 * width
+    partner_state = jnp.concatenate([ref[...] for ref in partners], axis=1)
+    totals = []
+    for part in range(2):
         at = slice(part * width, (part + 1) * width)
-        own, partner = owns[part][...], partners[part][...].astype(F32)
+        own, partner = owns[part][...], partner_state[:, at].astype(F32)
         mine, theirs = through_ref[:1, at], partner_through_ref[:1, at]
         total = jnp.where(leaves, mine * partner + own, theirs * own + partner)
         for value in entering:
-            total += mine * theirs * value[:, at].astype(F32)
-        out_ref[:, at] = total.astype(BF)
+            came = value[...] if halved else value[:, at]
+            total += mine * theirs * came.astype(F32)
+        if halved:
+            totals.append(total)
+        else:
+            out_ref[:, at] = total.astype(BF)
+    if halved:
+        out_ref[...] = jnp.where(ids_ref[CORE] == 0, totals[0], totals[1]).astype(BF)
 
 
 def local_grads_kernel(
-    offset, skip_ref, x_ref, grad_ref, b_ref, c_ref, rows_ref, cols_ref, weighted_ref, *refs
+    skip_ref, x_ref, grad_ref, b_ref, c_ref, rows_ref, cols_ref, weighted_ref, *refs
 ):
     states, (in_ref, paired_ref, c_out_ref) = refs[:-3], refs[-3:]
     heads = x_ref.shape[1] // P_SIZE
@@ -288,10 +286,10 @@
         at = slice(pair * PAIR, (pair + 1) * PAIR)
         x_pair = x_ref[:, at]
         g_pair = grad_ref[:, at]
-        skip = gains(skip_ref, offset + 2 * pair) * g_pair.astype(F32)
+        skip = gains(skip_ref, 2 * pair) * g_pair.astype(F32)
         top, bottom = skip[:HALF], skip[HALF:]
         for side in range(2):
-            head = offset + 2 * pair + side
+            head = 2 * pair + side
             g_head = jnp.where(first, g_pair, zero) if side == 0 else jnp.where(first, zero, g_pair)
             col = cols_ref[:, head : head + 1]
             row = rows_ref[head : head + 1, :]
@@ -318,48 +316,55 @@
     c_out_ref[...] = total
 
 
-def group_sums_kernel(parts, b_ref, c_ref, *refs):
-    pairs, c_parts, (grad_b_ref, grad_c_ref) = refs[:parts], refs[parts : 2 * parts], refs[2 * parts :]
-    paired = functools.reduce(jnp.add, [ref[...] for ref in pairs]).astype(BF)
+def group_sums_kernel(b_ref, c_ref, paired_ref, c_part_ref, grad_b_ref, grad_c_ref):
+    paired = paired_ref[...].astype(BF)
     grad_b_ref[...] = dot(paired, c_ref[...], 1, 0)
-    grad_c_ref[...] = functools.reduce(jnp.add, [ref[...] for ref in c_parts], dot(paired, b_ref[...], 0, 0))
-
-
-def final_kernel(parts, ids_ref, b_ref, cols_ref, sums_ref, weighted_ref, through_ref, after_ref, *refs):
-    locals_, partners, (in_ref, grad_b_ref) = refs[:parts], refs[parts : 2 * parts], refs[2 * parts :]
+    grad_c_ref[...] = c_part_ref[...] + dot(paired, b_ref[...], 0, 0)
+
+
+def final_kernel(ids_ref, b_ref, cols_ref, sums_ref, weighted_ref, through_ref, local_ref, *refs):
+    entered, partner_ref, (in_ref, grad_b_ref, token_ref) = refs[:2], refs[2], refs[3:]
+    token_ref[...] = jnp.zeros_like(token_ref)
     first = first_head()
     cols = cols_ref[...]
     grad_b = sums_ref[...]
-    width = locals_[0].shape[1]
-    for part in range(parts):
-        here = slice(part * width, (part + 1) * width)
-        entering = after_ref[:, here].astype(F32)
-        inner = through_ref[:1, here] * entering + partners[part][...].astype(F32)
-        adjoint = jnp.where(ids_ref[CORE] == 1, entering, inner).astype(BF)
+    core = ids_ref[CORE]
+    width = partner_ref.shape[1] // 2
+    for half in range(2):
+        here = slice(half * width, (half + 1) * width)
+        entering = jnp.where(core == half, entered[0][...].astype(F32), entered[1][...].astype(F32))
+        inner = through_ref[:1, here] * entering + partner_ref[:, here].astype(F32)
+        adjoint = jnp.where(core == 1, entering, inner).astype(BF)
         grad_b += dot(weighted_ref[:, here], adjoint, 1, 1)
         for number in range(width // PAIR):
-            at = slice(number * PAIR, (number + 1) * PAIR)
-            pair = part * (width // PAIR) + number
+            pair = half * (width // PAIR) + number
+            at = slice(pair * PAIR, (pair + 1) * PAIR)
             log_pair = spread(cols, pair, first)
             to_end = jnp.exp(log_pair[Q - 1 : Q, :] - log_pair)
-            term = dot(b_ref[...], adjoint[:, at], 1, 0)
-            in_ref[:, pair * PAIR : (pair + 1) * PAIR] = (locals_[part][:, at] + to_end * term).astype(BF)
+            term = dot(b_ref[...], adjoint[:, number * PAIR : (number + 1) * PAIR], 1, 0)
+            in_ref[:, at] = (local_ref[:, at] + to_end * term).astype(BF)
     grad_b_ref[...] = grad_b
 
 
 def add_kernel(parts, *refs):
-    start = 0
-    for kept, came in zip(refs[:parts], refs[parts:-1]):
-        width = kept.shape[1]
-        refs[-1][:, start : start + width] = kept[...] + came[...].astype(F32)
-        start += width
-
-
-def weight_partial_kernel(chips, *refs):
+    kept, came, out_ref = refs[:parts], refs[parts:-1], refs[-1]
+    for group, change in ((kept, False), (came, True)):
+        start = 0
+        for ref in group:
+            at = slice(start, start + ref.shape[1])
+            out_ref[:, at] = out_ref[:, at] + ref[...].astype(F32) if change else ref[...]
+            start += ref.shape[1]
+
+
+def weight_partial_kernel(chips, pieces, *refs):
     owns, came, refs = refs[:2], (refs[2:4], refs[4:6]), refs[6:]
-    outputs, (sent_ref, kept_ref) = refs[: 2 * chips], refs[2 * chips :]
-    depth = sent_ref.shape[0]
-    for slot, target in ((1, sent_ref), (0, kept_ref)):
+    outputs, kept_ref, sent = refs[: -1 - pieces], refs[-1 - pieces], refs[-pieces:]
+    depth = kept_ref.shape[0]
+    outputs = [ref[...] for ref in outputs]
+    if len(outputs) > 2 * chips:
+        cut = outputs[chips + 1 :]
+        outputs = outputs[: chips + 1] + [jnp.concatenate(cut[i : i + 2], axis=1) for i in range(0, len(cut), 2)]
+    for slot in (1, 0):
         total = None
         for number, output in enumerate(outputs):
             core, by = number // chips, number % chips
@@ -367,9 +372,15 @@
                 grad = owns[core][:, slot * depth : (slot + 1) * depth]
             else:
                 grad = came[core][slot][(by - 1) * Q : by * Q, :]
-            term = dot(grad, output[...], 0, 0)
+            term = dot(grad, output, 0, 0)
             total = term if total is None else total + term
-        target[...] = total.astype(target.dtype)
+        if slot == 0:
+            kept_ref[...] = total
+            continue
+        start = 0
+        for ref in sent:
+            ref[...] = total[:, start : start + ref.shape[1]].astype(BF)
+            start += ref.shape[1]
 
 
 def body(
@@ -411,8 +422,6 @@
         order = [core * 2 + dialogue, core * 2 + 1 - dialogue, (1 - core) * 2 + dialogue, (1 - core) * 2 + 1 - dialogue]
         table.append(order + [order[odd], order[2 + odd], core, odd] + [(chip + by) % chips for by in range(chips)])
     ids = lax.dynamic_index_in_dim(np.array(table, np.int32), me, keepdims=False)
-    back_width, back_heads = wide // BACK, heads // BACK
-    back_of = lambda array, part: columns_of(array, back_width, part)
 
     to_send = [
         column_call(send_kernel, CHIP + by, ids, incoming, [], span, [((Q, 2 * depth), BF)])
@@ -478,82 +487,73 @@
     weights = [out_weight, weight_other, weight_core]
     weights += [core_swap(weight_late[: depth // 2]), core_swap(weight_late[depth // 2 :])]
 
-    partials, returned = [], []
-    for part in range(BACK):
-        partials.append(
-            call(
-                functools.partial(head_partial_kernel, CUTS),
-                (),
-                (mine, other, *came, *[back_of(weight, part) for weight in weights]),
-                [((Q, back_width), F32)] + [((Q, back_width // CUTS), BF)] * (CUTS * (chips - 1)),
-                after=[] if part == 0 else [partials[-1][0]],
-            )
+    partials = call(
+        head_partial_kernel,
+        (),
+        (mine, other, *came, *weights),
+        [((Q, wide), F32)] + [((Q, wide), BF)] * (chips - 1),
+    )
+    returned = [chip_shift(partials[by], -by) for by in range(1, chips)]
+
+    sent, kept, sums = [], [], []
+    for part, width in enumerate(widths):
+        pieces = [later(piece, sent[-1] if sent else partials[0]) for piece in outputs[part][1:]]
+        cut = width // 2 if width > wide // 2 else width
+        swaps = [core_swap(piece[:, at : at + cut]) for piece in pieces for at in range(0, width, cut)]
+        sizes = [width]
+        partial, *own = call(
+            functools.partial(weight_partial_kernel, chips, len(sizes)),
+            (),
+            (mine, partner, *came[:2], *partner_came, *outputs[part], swapped[part], *swaps),
+            [((depth, width), F32)] + [((depth, size), BF) for size in sizes],
+            after=[partials[0], *sent[-1:]],
         )
-        returned.append(
-            [chip_shift(partials[part][1 + i], -(1 + i // CUTS)) for i in range(CUTS * (chips - 1))]
+        sent.append(own[0])
+        kept.append(partial)
+        sums += [dialogue_swap(value) for value in own]
+
+    head_grad, weighted_grad, *both = call(
+        functools.partial(adjoint_kernel, chips - 1),
+        (resets,),
+        (partials[0], *returned, c_rows, log_cols),
+        [((Q, wide), BF), ((Q, wide), BF)] + [((N, wide // 2), F32)] * 2 + [((N, wide), BF)],
+        after=[sums[0], *sent],
+    )
+    adjoint_partner = core_swap(both[2])
+    local_in, paired, c_part = call(
+        local_grads_kernel,
+        (skip_gain,),
+        (x, head_grad, b_rows, c_rows, log_rows, log_cols, weighted_grad, *states),
+        [((Q, wide), F32), ((Q, Q), F32), ((Q, N), F32)],
+    )
+    entering = []
+    for hop in range(1, chips):
+        total, = call(
+            functools.partial(chip_total_kernel, 0, 1),
+            (ids,),
+            (through, through_partner, *both[:2], adjoint_partner, *entering),
+            [((N, wide // 2), BF)],
         )
-
-    sent, kept = [], []
-    for part, width in enumerate(widths):
-        pieces = [later(piece, sent[-1]) if sent else piece for piece in outputs[part][1:]]
-        own, partial = call(
-            functools.partial(weight_partial_kernel, chips),
-            (),
-            (mine, partner, *came[:2], *partner_came, *outputs[part], swapped[part], *map(core_swap, pieces)),
-            [((depth, width), BF), ((depth, width), F32)],
-            after=[partial[0] for partial in partials] + sent[-1:],
-        )
-        sent.append(own)
-        kept.append(partial)
-    sums = [dialogue_swap(value) for value in sent]
+        entering = [lax.ppermute(total, "seq", [(i, i - 2) for i in range(2, seq)])]
+    grad_b, grad_c = call(
+        group_sums_kernel,
+        (),
+        (b_rows, c_rows, paired, c_part),
+        [((Q, N), F32), ((Q, N), F32)],
+    )
+    grad_in, grad_b, token = call(
+        final_kernel,
+        (ids,),
+        (b_rows, log_cols, grad_b, weighted_in, through_partner, local_in)
+        + (*entering, core_swap(later(entering[0], grad_c)), adjoint_partner),
+        [((Q, wide), BF), ((Q, N), F32), ((8, 128), F32)],
+    )
     grad_weight, = call(
         functools.partial(add_kernel, len(widths)),
         (),
         (*kept, *sums),
         [((depth, wide), F32)],
-    )
-
-    locals_, pairs, c_parts, adjoints, partners = [], [], [], [], []
-    for part in range(BACK):
-        head_grad, weighted_grad, adjoint, adjoint_sent = call(
-            functools.partial(adjoint_kernel, chips - 1, CUTS, part * back_heads // 2),
-            (resets,),
-            (partials[part][0], *returned[part], c_rows, log_cols),
-            [((Q, back_width), BF), ((Q, back_width), BF), ((N, back_width), F32), ((N, back_width), BF)],
-            after=[sums[0], *sent, *locals_],
-        )
-        adjoints.append(adjoint)
-        partners.append(core_swap(adjoint_sent))
-        local_in, paired, c_part = call(
-            functools.partial(local_grads_kernel, part * back_heads),
-            (skip_gain,),
-            (back_of(x, part), head_grad, b_rows, c_rows, log_rows, log_cols, weighted_grad)
-            + tuple(states),
-            [((Q, back_width), F32), ((Q, Q), F32), ((Q, N), F32)],
-        )
-        locals_.append(local_in)
-        pairs.append(paired)
-        c_parts.append(c_part)
-    entering = []
-    for hop in range(1, chips):
-        total, = call(
-            functools.partial(chip_total_kernel, 0, BACK),
-            (ids,),
-            (through, through_partner, *adjoints, *partners, *entering),
-            [((N, wide), BF)],
-        )
-        entering = [lax.ppermute(total, "seq", [(i, i - 2) for i in range(2, seq)])]
-    grad_b, grad_c = call(
-        functools.partial(group_sums_kernel, BACK),
-        (),
-        (b_rows, c_rows, *pairs, *c_parts),
-        [((Q, N), F32), ((Q, N), F32)],
-    )
-    grad_in, grad_b = call(
-        functools.partial(final_kernel, BACK),
-        (ids,),
-        (b_rows, log_cols, grad_b, weighted_in, through_partner, *entering, *locals_, *partners),
-        [((Q, wide), BF), ((Q, N), F32)],
+        after=[token],
     )
     return grad_in[None], grad_b[None], grad_c[None], grad_weight
 

time: 72.6 us -> 70.4 us (0.970)
  waiting for transfers between devices: 26 us -> 23.1 us
    ppermute x3, waiting for transfers between devices: 13.1 us -> 0.01 us  [dialogue_swap(): return lax.ppermute(value, 'dp', [(0, 1), (1, 0)])]
    ppermute x4, waiting for transfers between devices: 2.97 us -> 8.67 us  [chip_shift(): lax.ppermute(value, 'seq', [(i, (i + 2 * by) % seq) for i in range(seq)])]
    ppermute x1, waiting for transfers between devices: 0.01 us -> 2.52 us  [body(): entering = [lax.ppermute(total, 'seq', [(i, i - 2) for i in range(2, seq)])]]
    ppermute x14 -> x16, waiting for transfers between devices: 3.46 us -> 5.47 us  [core_swap(): return lax.ppermute(value, 'seq', across)]
    ppermute x14 -> x16, starting transfers between devices: 3.17 us -> 3.73 us  [core_swap(): return lax.ppermute(value, 'seq', across)]
  transfers between devices with their start and end apart: 24 -> 26, of which waited for: 9 -> 11; matrix products, arithmetic and copies ran while one was open for 1% -> 1% of each run, Pallas kernels for 28% -> 30%
where the time goes in v4:
time: 70.4 us; the launch traced here: 70.1 us
  waiting for transfers between devices  23.1 us (33%)
  Pallas kernels  22.7 us (32%)
  starting transfers between devices  19.3 us (27%)
  local copies, waits for them, and re-layouts  3.34 us (5%)
  between operations  1.57 us (2%)
    pallas_call x15, Pallas kernels, call(): pl.pallas_call(run, grid=(1,), out_shape=[jax.ShapeDtypeStruct(shape, kin...  21.3 us
    ppermute x4, waiting for transfers between devices, chip_shift(): lax.ppermute(value, 'seq', [(i, (i + 2 * by) % seq) for i in range(seq)])  8.67 us
    ppermute x4, starting transfers between devices, chip_shift(): lax.ppermute(value, 'seq', [(i, (i + 2 * by) % seq) for i in range(seq)])  5.56 us
    ppermute x16, waiting for transfers between devices, core_swap(): return lax.ppermute(value, 'seq', across)  5.47 us
    ppermute x3, starting transfers between devices, dialogue_swap(): return lax.ppermute(value, 'dp', [(0, 1), (1, 0)])  4.53 us
    ppermute x16, starting transfers between devices, core_swap(): return lax.ppermute(value, 'seq', across)  3.73 us
    ppermute x1, waiting for transfers between devices, body(): before = [lax.ppermute(total, 'seq', [(i, i + 2) for i in range(seq - 2)])]  3.47 us
    ppermute x1, waiting for transfers between devices, plane_swap(): return lax.ppermute(value, 'tensor', [(i, i ^ 1) for i in range(planes)])  3 us
  transfers between devices with their start and end apart: 26, of which 11 were waited for; matrix products, arithmetic and copies ran while one was open for 1% of the time, Pallas kernels for 30%

profile of v4, /device:TPU:0, one launch (start us, length us, event | category | flops | bytes accessed | tf_op | source)
XLA Modules:
  0.0 70.1 jit_solution(5126763464621178465)
XLA Ops:
  1.2 2.6 %collective-permute-start.8 = (bf16[512,1024]{1,0:T(8,128)(2,1)}, bf16[512,1024]{1,0:T(8,128)(2,1)S(1)}, u32[]{:S(2)}, u32[]{:S(2)}) collective-permute-start(bf16[512,1024]{1,0:T(8,128)(2,1)} %refs_6_.1), channel_id=1, source_target_pairs={{0,1},{1,0},{2,3},{3,2},{4,5},{5,4},{6,7},{7,6},{8,9},{9,8},{10,11... | collective-permute-start | bytes 3145736 | tf_op jit(solution)/shard_map/ppermute | solution.py:414
  4.5 1.6 %copy-done = bf16[1,256,4096]{2,1,0:T(8,128)(2,1)S(1)} copy-done((bf16[1,256,4096]{2,1,0:T(8,128)(2,1)S(1)}, bf16[1,256,4096]{2,1,0:T(8,128)(2,1)}, u32[]{:S(2)}) %copy-start) | copy-done | bytes 2097176
  6.7 1.6 %collective-permute-start.1 = (bf16[256,1024]{1,0:T(8,128)(2,1)S(1)}, bf16[256,1024]{1,0:T(8,128)(2,1)S(1)}, u32[]{:S(2)}, u32[]{:S(2)}) collective-permute-start(bf16[256,1024]{1,0:T(8,128)(2,1)S(1)} %send_kernel.1.refs_6_), channel_id=1, source_target_pairs={{0,16},{8,24},{16,0},{24,8},{1,17},{9,25},{17,1},{25,9},{2,18},{10... | collective-permute-start | bytes 1572872 | tf_op jit(solution)/shard_map/ppermute | solution.py:408
  9.0 0.8 %copy-done.4 = bf16[1,256,128]{2,1,0:T(8,128)(2,1)S(1)} copy-done((bf16[1,256,128]{2,1,0:T(8,128)(2,1)S(1)}, bf16[1,256,128]{2,1,0:T(8,128)(2,1)}, u32[]{:S(2)}) %copy-start.4) | copy-done | bytes 65560
  9.8 2.2 %tables_kernel.1 = (f32[128,512]{1,0:T(8,128)S(1)}, f32[128,512]{1,0:T(8,128)S(1)}, bf16[128,512]{1,0:T(8,128)(2,1)S(1)}, bf16[128,512]{1,0:T(8,128)(2,1)S(1)}, ...) custom-call(f32[16]{0:T(128)S(1)} %copy-done.9, ...), custom_call_target="tpu_custom_call" | custom-call | tf_op jit(solution)/shard_map/tables_kernel/pallas_call | solution.py:43
  13.4 1.4 %collective-permute-done.3.refs_2_.refs_5_ = f32[8,1024]{1,0:T(8,128)S(1)} collective-permute-done((f32[8,1024]{1,0:T(8,128)S(1)}, f32[8,1024]{1,0:T(8,128)S(1)}, u32[]{:S(2)}, u32[]{:S(2)}) %collective-permute-start.3) | collective-permute-done | bytes 32800 | tf_op jit(solution)/shard_map/ppermute | solution.py:405
  14.9 1.7 %local_output_kernel.1.refs_7_.refs_2_ = f32[256,1024]{1,0:T(8,128)S(1)} custom-call(f32[16]{0:T(128)S(1)} %copy-done.8, bf16[256,1024]{1,0:T(8,128)(2,1)S(1)} %bitcast.13, bf16[256,128]{1,0:T(8,128)(2,1)S(1)} %bitcast.22, bf16[256,128]{1,0:T(8,128)(2,1)S(1)} %bitcast.15, f32[16,256]{1,0:T(8,128)S(1)} %get-tuple-element.49.refs_4_.refs_5_, ...), custom_call_target="tpu_custom_call" | custom-call | tf_op jit(solution)/shard_map/local_output_kernel/pallas_call | solution.py:43
  17.3 2.5 %collective-permute-start.6 = (bf16[128,1024]{1,0:T(8,128)(2,1)S(1)}, bf16[128,1024]{1,0:T(8,128)(2,1)S(1)}, u32[]{:S(2)}, u32[]{:S(2)}) collective-permute-start(bf16[128,1024]{1,0:T(8,128)(2,1)S(1)} %chip_total_kernel.2), channel_id=1, source_target_pairs={{0,16},{8,24},{1,17},{9,25},{2,18},{10,26},{3,19},{11,27},{4,20},{... | collective-permute-start | bytes 786440 | tf_op jit(solution)/shard_map/ppermute | solution.py:468
  19.8 1.0 %collective-permute-done.1.refs_1_ = bf16[256,1024]{1,0:T(8,128)(2,1)S(1)} collective-permute-done((bf16[256,1024]{1,0:T(8,128)(2,1)S(1)}, bf16[256,1024]{1,0:T(8,128)(2,1)S(1)}, u32[]{:S(2)}, u32[]{:S(2)}) %collective-permute-start.1) | collective-permute-done | bytes 524320 | tf_op jit(solution)/shard_map/ppermute | solution.py:408
  20.8 1.6 %collective-permute-start.2 = (bf16[256,1024]{1,0:T(8,128)(2,1)S(1)}, bf16[256,1024]{1,0:T(8,128)(2,1)S(1)}, u32[]{:S(2)}, u32[]{:S(2)}) collective-permute-start(bf16[256,1024]{1,0:T(8,128)(2,1)S(1)} %collective-permute-done.1.refs_1_), channel_id=1, source_target_pairs={{0,2},{2,0},{4,6},{6,4},{1,3},{3,1},{5,7},{7,5},{8,10},{10,8},{12,... | collective-permute-start | bytes 1572872 | tf_op jit(solution)/shard_map/ppermute | solution.py:411
  22.3 3.5 %collective-permute-done.6.refs_6_ = bf16[128,1024]{1,0:T(8,128)(2,1)S(1)} collective-permute-done((bf16[128,1024]{1,0:T(8,128)(2,1)S(1)}, bf16[128,1024]{1,0:T(8,128)(2,1)S(1)}, u32[]{:S(2)}, u32[]{:S(2)}) %collective-permute-start.6) | collective-permute-done | bytes 262176 | tf_op jit(solution)/shard_map/ppermute | solution.py:468
  25.8 0.9 %output_kernel.2 = (bf16[256,384]{1,0:T(8,128)(2,1)S(1)}, bf16[128,384]{1,0:T(8,128)(2,1)S(1)}) custom-call(s32[10]{0:T(128)S(1)} %dynamic-slice_bitcast_fusion.refs_0_, s32[1,1]{1,0:T(1,128)S(6)} %copy.14.refs_1_.refs_0_, f32[256,1024]{1,0:T(8,128)S(1)} %local_output_kernel.1.refs_7_.refs_2_, bf16[256,128]{1,0:T(8,128)(2,1)S(1)} %bitcast.16, ...), custom_call_target="tpu_custom_call" | custom-call | tf_op jit(solution)/shard_map/output_kernel/pallas_call | solution.py:43
  26.7 1.0 %output_kernel.3 = (bf16[256,640]{1,0:T(8,128)(2,1)S(1)}, bf16[128,640]{1,0:T(8,128)(2,1)S(1)}) custom-call(s32[10]{0:T(128)S(1)} %dynamic-slice_bitcast_fusion.refs_0_, s32[1,1]{1,0:T(1,128)S(6)} %copy.14.refs_1_.refs_0_, f32[256,1024]{1,0:T(8,128)S(1)} %local_output_kernel.1.refs_7_.refs_2_, bf16[256,128]{1,0:T(8,128)(2,1)S(1)} %bitcast.17, ...), custom_call_target="tpu_custom_call" | custom-call | tf_op jit(solution)/shard_map/output_kernel/pallas_call | solution.py:43
  28.4 2.5 %collective-permute-start.14 = (bf16[256,384]{1,0:T(8,128)(2,1)S(1)}, bf16[256,384]{1,0:T(8,128)(2,1)S(1)}, u32[]{:S(2)}, u32[]{:S(2)}) collective-permute-start(bf16[256,384]{1,0:T(8,128)(2,1)S(1)} %get-tuple-element.54.refs_9_.refs_6_), channel_id=1, source_target_pairs={{0,16},{8,24},{16,0},{24,8},{1,17},{9,25},{17,1},{25,9},{2,18},{10... | collective-permute-start | bytes 589832 | tf_op jit(solution)/shard_map/ppermute | solution.py:408
  30.9 3.0 %collective-permute-done.2.refs_2_ = bf16[256,1024]{1,0:T(8,128)(2,1)S(1)} collective-permute-done((bf16[256,1024]{1,0:T(8,128)(2,1)S(1)}, bf16[256,1024]{1,0:T(8,128)(2,1)S(1)}, u32[]{:S(2)}, u32[]{:S(2)}) %collective-permute-start.2) | collective-permute-done | bytes 524320 | tf_op jit(solution)/shard_map/ppermute | solution.py:411
  35.2 2.3 %head_partial_kernel.1 = (f32[256,1024]{1,0:T(8,128)S(1)}, bf16[256,1024]{1,0:T(8,128)(2,1)S(1)}) custom-call(bf16[256,1024]{1,0:T(8,128)(2,1)S(1)} %get-tuple-element.47.refs_0_, bf16[256,1024]{1,0:T(8,128)(2,1)S(1)} %get-tuple-element.48.refs_1_, bf16[256,512]{1,0:T(8,128)(2,1)S(1)} %get-tuple-element.56.refs_2_, ...), custom_call_target="tpu_custom_call" | custom-call | tf_op jit(solution)/shard_map/head_partial_kernel/pallas_call | solution.py:43
  38.2 1.5 %collective-permute-start.11 = (bf16[256,1024]{1,0:T(8,128)(2,1)S(1)}, bf16[256,1024]{1,0:T(8,128)(2,1)S(1)}, u32[]{:S(2)}, u32[]{:S(2)}) collective-permute-start(bf16[256,1024]{1,0:T(8,128)(2,1)S(1)} %get-tuple-element.62), channel_id=1, source_target_pairs={{0,16},{8,24},{16,0},{24,8},{1,17},{9,25},{17,1},{25,9},{2,18},{10... | collective-permute-start | bytes 1572872 | tf_op jit(solution)/shard_map/ppermute | solution.py:408
  39.6 1.3 %weight_partial_kernel.2 = (f32[512,384]{1,0:T(8,128)S(1)}, bf16[512,384]{1,0:T(8,128)(2,1)S(1)}) custom-call(bf16[256,1024]{1,0:T(8,128)(2,1)S(1)} %get-tuple-element.47.refs_0_, bf16[256,1024]{1,0:T(8,128)(2,1)S(1)} %collective-permute-done.7.refs_9_.refs_1_, bf16[256,512]{1,0:T(8,128)(2,1)S(1)} %get-tuple-element.56.refs_2_, ...), custom_call_target="tpu_custom_call" | custom-call | tf_op jit(solution)/shard_map/weight_partial_kernel/pallas_call | solution.py:43
  41.5 2.1 %collective-permute-done.18.refs_7_ = bf16[256,640]{1,0:T(8,128)(2,1)S(1)} collective-permute-done((bf16[256,640]{1,0:T(8,128)(2,1)S(1)}, bf16[256,640]{1,0:T(8,128)(2,1)S(1)}, u32[]{:S(2)}, u32[]{:S(2)}) %collective-permute-start.18) | collective-permute-done | bytes 327712 | tf_op jit(solution)/shard_map/ppermute | solution.py:408
  44.3 0.9 %collective-permute-done.20.refs_9_ = bf16[256,320]{1,0:T(8,128)(2,1)S(1)} collective-permute-done((bf16[256,320]{1,0:T(8,128)(2,1)S(1)}, bf16[256,320]{1,0:T(8,128)(2,1)S(1)}, u32[]{:S(2)}, u32[]{:S(2)}) %collective-permute-start.20) | collective-permute-done | bytes 163872 | tf_op jit(solution)/shard_map/ppermute | solution.py:405
  45.5 1.8 %weight_partial_kernel.3 = (f32[512,640]{1,0:T(8,128)S(1)}, bf16[512,640]{1,0:T(8,128)(2,1)S(1)}) custom-call(bf16[256,1024]{1,0:T(8,128)(2,1)S(1)} %get-tuple-element.47.refs_0_, bf16[256,1024]{1,0:T(8,128)(2,1)S(1)} %collective-permute-done.7.refs_9_.refs_1_, bf16[256,512]{1,0:T(8,128)(2,1)S(1)} %get-tuple-element.56.refs_2_, ...), custom_call_target="tpu_custom_call" | custom-call | tf_op jit(solution)/shard_map/weight_partial_kernel/pallas_call | solution.py:43
  47.4 1.4 %collective-permute-start.25 = (bf16[512,640]{1,0:T(8,128)(2,1)S(1)}, bf16[512,640]{1,0:T(8,128)(2,1)S(1)}, u32[]{:S(2)}, u32[]{:S(2)}) collective-permute-start(bf16[512,640]{1,0:T(8,128)(2,1)S(1)} %get-tuple-element.66.refs_7_), channel_id=1, source_target_pairs={{0,1},{1,0},{2,3},{3,2},{4,5},{5,4},{6,7},{7,6},{8,9},{9,8},{10,11... | collective-permute-start | bytes 1966088 | tf_op jit(solution)/shard_map/ppermute | solution.py:414
  48.7 5.6 %collective-permute-done.11.refs_2_ = bf16[256,1024]{1,0:T(8,128)(2,1)S(1)} collective-permute-done((bf16[256,1024]{1,0:T(8,128)(2,1)S(1)}, bf16[256,1024]{1,0:T(8,128)(2,1)S(1)}, u32[]{:S(2)}, u32[]{:S(2)}) %collective-permute-start.11) | collective-permute-done | bytes 524320 | tf_op jit(solution)/shard_map/ppermute | solution.py:408
  54.3 1.0 %adjoint_kernel.1 = (bf16[256,1024]{1,0:T(8,128)(2,1)S(1)}, bf16[256,1024]{1,0:T(8,128)(2,1)S(1)}, f32[128,512]{1,0:T(8,128)S(1)}, f32[128,512]{1,0:T(8,128)S(1)}, bf16[128,1024]{1,0:T(8,128)(2,1)S(1)}) custom-call(s32[1,1]{1,0:T(1,128)S(6)} %copy.14.refs_1_.refs_0_, f32[256,1024]{1,0:T(8,128)S(1)} %get-tuple-element.61.refs_10_.refs_11_.refs_1_, ...), custom_call_target="tpu_custom_call" | custom-call | tf_op jit(solution)/shard_map/adjoint_kernel/pallas_call | solution.py:43
  55.3 1.5 %collective-permute-done.22.refs_5_.refs_9_ = bf16[128,1024]{1,0:T(8,128)(2,1)S(1)} collective-permute-done((bf16[128,1024]{1,0:T(8,128)(2,1)S(1)}, bf16[128,1024]{1,0:T(8,128)(2,1)S(1)}, u32[]{:S(2)}, u32[]{:S(2)}) %collective-permute-start.22) | collective-permute-done | bytes 262176 | tf_op jit(solution)/shard_map/ppermute | solution.py:405
  57.5 1.5 %collective-permute-start.23 = (bf16[128,512]{1,0:T(8,128)(2,1)S(1)}, bf16[128,512]{1,0:T(8,128)(2,1)S(1)}, u32[]{:S(2)}, u32[]{:S(2)}) collective-permute-start(bf16[128,512]{1,0:T(8,128)(2,1)S(1)} %chip_total_kernel.3), channel_id=1, source_target_pairs={{16,0},{24,8},{17,1},{25,9},{18,2},{26,10},{19,3},{27,11},{20,4},{... | collective-permute-start | bytes 393224 | tf_op jit(solution)/shard_map/ppermute | solution.py:537
  59.0 2.5 %local_grads_kernel.1 = (f32[256,1024]{1,0:T(8,128)S(1)}, f32[256,256]{1,0:T(8,128)S(1)}, f32[256,128]{1,0:T(8,128)S(1)}) custom-call(f32[16]{0:T(128)S(1)} %copy-done.8, bf16[256,1024]{1,0:T(8,128)(2,1)S(1)} %bitcast.14, bf16[256,1024]{1,0:T(8,128)(2,1)S(1)} %get-tuple-element.67.refs_2_, bf16[256,128]{1,0:T(8,128)(2,1)S(1)} %bitcast.23, ...), custom_call_target="tpu_custom_call" | custom-call | tf_op jit(solution)/shard_map/local_grads_kernel/pallas_call | solution.py:43
  61.5 0.9 %group_sums_kernel.1 = (f32[256,128]{1,0:T(8,128)S(1)}, f32[256,128]{1,0:T(8,128)}) custom-call(bf16[256,128]{1,0:T(8,128)(2,1)S(1)} %bitcast.24, bf16[256,128]{1,0:T(8,128)(2,1)S(1)} %bitcast.20, f32[256,256]{1,0:T(8,128)S(1)} %get-tuple-element.71.refs_2_, f32[256,128]{1,0:T(8,128)S(1)} %get-tuple-element.72.refs_3_), custom_call_target="tpu_custom_call" | custom-call | tf_op jit(solution)/shard_map/group_sums_kernel/pallas_call | solution.py:43
  62.4 2.5 %collective-permute-done.23.refs_7_ = bf16[128,512]{1,0:T(8,128)(2,1)S(1)} collective-permute-done((bf16[128,512]{1,0:T(8,128)(2,1)S(1)}, bf16[128,512]{1,0:T(8,128)(2,1)S(1)}, u32[]{:S(2)}, u32[]{:S(2)}) %collective-permute-start.23) | collective-permute-done | bytes 131104 | tf_op jit(solution)/shard_map/ppermute | solution.py:537
  65.0 1.3 %collective-permute-done.24.refs_8_ = bf16[128,512]{1,0:T(8,128)(2,1)S(1)} collective-permute-done((bf16[128,512]{1,0:T(8,128)(2,1)S(1)}, bf16[128,512]{1,0:T(8,128)(2,1)S(1)}, u32[]{:S(2)}, u32[]{:S(2)}) %collective-permute-start.24) | collective-permute-done | bytes 131104 | tf_op jit(solution)/shard_map/ppermute | solution.py:405
  66.3 2.1 %final_kernel.1 = (bf16[256,1024]{1,0:T(8,128)(2,1)}, f32[256,128]{1,0:T(8,128)}, f32[8,128]{1,0:T(8,128)S(1)}) custom-call(s32[10]{0:T(128)S(1)} %dynamic-slice_bitcast_fusion.refs_0_, bf16[256,128]{1,0:T(8,128)(2,1)S(1)} %bitcast.25, f32[256,16]{1,0:T(8,128)S(1)} %get-tuple-element.45.refs_5_.refs_4_.refs_6_.refs_2_, ...), custom_call_target="tpu_custom_call" | custom-call | tf_op jit(solution)/shard_map/final_kernel/pallas_call | solution.py:43
  68.4 1.7 %add_kernel.1 = f32[512,1024]{1,0:T(8,128)} custom-call(f32[512,384]{1,0:T(8,128)S(1)} %get-tuple-element.83.refs_0_, f32[512,640]{1,0:T(8,128)S(1)} %get-tuple-element.84.refs_1_, bf16[512,384]{1,0:T(8,128)(2,1)S(1)} %collective-permute-done.17.refs_5_.refs_2_, bf16[512,640]{1,0:T(8,128)(2,1)S(1)} %collective-permute-done.25.refs_3_, ...), custom_call_target="tpu_custom_call" | custom-call | tf_op jit(solution)/shard_map/add_kernel/pallas_call | solution.py:43
  (60 shorter events, 8.9 us)
Async XLA Ops:
  0.6 8.3 %copy-start.7 = (f32[1,16,256]{2,1,0:T(8,128)S(1)}, f32[1,16,256]{2,1,0:T(8,128)}, u32[]{:S(2)}) copy-start(f32[1,16,256]{2,1,0:T(8,128)} %param.13) | copy-start | bytes 49156
  0.6 8.3 %copy-start.9 = (f32[16]{0:T(128)S(1)}, f32[16]{0:T(128)}, u32[]{:S(2)}) copy-start(f32[16]{0:T(128)} %refs_0_.4) | copy-start | bytes 196
  0.7 8.3 %collective-permute-start = (bf16[512,1024]{1,0:T(8,128)(2,1)}, bf16[512,1024]{1,0:T(8,128)(2,1)S(1)}, u32[]{:S(2)}, u32[]{:S(2)}) collective-permute-start(bf16[512,1024]{1,0:T(8,128)(2,1)} %refs_6_.1), channel_id=1, source_target_pairs={{0,8},{8,0},{16,24},{24,16},{1,9},{9,1},{17,25},{25,17},{2,10},{10... | collective-permute-start | bytes 3145736 | tf_op jit(solution)/shard_map/ppermute | solution.py:405
  1.2 26.6 %collective-permute-start.8 = (bf16[512,1024]{1,0:T(8,128)(2,1)}, bf16[512,1024]{1,0:T(8,128)(2,1)S(1)}, u32[]{:S(2)}, u32[]{:S(2)}) collective-permute-start(bf16[512,1024]{1,0:T(8,128)(2,1)} %refs_6_.1), channel_id=1, source_target_pairs={{0,1},{1,0},{2,3},{3,2},{4,5},{5,4},{6,7},{7,6},{8,9},{9,8},{10,11... | collective-permute-start | bytes 3145736 | tf_op jit(solution)/shard_map/ppermute | solution.py:414
  6.0 6.0 %copy-start.1 = (bf16[1,256,4096]{2,1,0:T(8,128)(2,1)S(1)}, bf16[1,256,4096]{2,1,0:T(8,128)(2,1)}, u32[]{:S(2)}) copy-start(bf16[1,256,4096]{2,1,0:T(8,128)(2,1)} %param.17) | copy-start | bytes 6291460
  6.7 14.1 %collective-permute-start.1 = (bf16[256,1024]{1,0:T(8,128)(2,1)S(1)}, bf16[256,1024]{1,0:T(8,128)(2,1)S(1)}, u32[]{:S(2)}, u32[]{:S(2)}) collective-permute-start(bf16[256,1024]{1,0:T(8,128)(2,1)S(1)} %send_kernel.1.refs_6_), channel_id=1, source_target_pairs={{0,16},{8,24},{16,0},{24,8},{1,17},{9,25},{17,1},{25,9},{2,18},{10... | collective-permute-start | bytes 1572872 | tf_op jit(solution)/shard_map/ppermute | solution.py:408
  9.8 5.1 %copy-start.5 = (bf16[1,256,128]{2,1,0:T(8,128)(2,1)S(1)}, bf16[1,256,128]{2,1,0:T(8,128)(2,1)}, u32[]{:S(2)}) copy-start(bf16[1,256,128]{2,1,0:T(8,128)(2,1)} %param.11) | copy-start | bytes 196612
  9.8 5.1 %copy-start.8 = (f32[16]{0:T(128)S(1)}, f32[16]{0:T(128)}, u32[]{:S(2)}) copy-start(f32[16]{0:T(128)} %refs_0_.6) | copy-start | bytes 196
  12.7 13.1 %collective-permute-start.7 = (bf16[256,1024]{1,0:T(8,128)(2,1)S(1)}, bf16[256,1024]{1,0:T(8,128)(2,1)S(1)}, u32[]{:S(2)}, u32[]{:S(2)}) collective-permute-start(bf16[256,1024]{1,0:T(8,128)(2,1)S(1)} %get-tuple-element.48.refs_1_), channel_id=1, source_target_pairs={{0,8},{8,0},{16,24},{24,16},{1,9},{9,1},{17,25},{25,17},{2,10},{10... | collective-permute-start | bytes 1572872 | tf_op jit(solution)/shard_map/ppermute | solution.py:405
  12.8 1.9 %collective-permute-start.3 = (f32[8,1024]{1,0:T(8,128)S(1)}, f32[8,1024]{1,0:T(8,128)S(1)}, u32[]{:S(2)}, u32[]{:S(2)}) collective-permute-start(f32[8,1024]{1,0:T(8,128)S(1)} %get-tuple-element.46.refs_2_.refs_1_), channel_id=1, source_target_pairs={{0,8},{8,0},{16,24},{24,16},{1,9},{9,1},{17,25},{25,17},{2,10},{10... | collective-permute-start | bytes 98312 | tf_op jit(solution)/shard_map/ppermute | solution.py:405
  13.3 3.3 %collective-permute-start.4 = (bf16[128,512]{1,0:T(8,128)(2,1)S(1)}, bf16[128,512]{1,0:T(8,128)(2,1)S(1)}, u32[]{:S(2)}, u32[]{:S(2)}) collective-permute-start(bf16[128,512]{1,0:T(8,128)(2,1)S(1)} %get-tuple-element.52), channel_id=1, source_target_pairs={{0,8},{8,0},{16,24},{24,16},{1,9},{9,1},{17,25},{25,17},{2,10},{10... | collective-permute-start | bytes 393224 | tf_op jit(solution)/shard_map/ppermute | solution.py:405
  14.8 1.8 %collective-permute-start.5 = (bf16[128,512]{1,0:T(8,128)(2,1)S(1)}, bf16[128,512]{1,0:T(8,128)(2,1)S(1)}, u32[]{:S(2)}, u32[]{:S(2)}) collective-permute-start(bf16[128,512]{1,0:T(8,128)(2,1)S(1)} %get-tuple-element.53), channel_id=1, source_target_pairs={{0,8},{8,0},{16,24},{24,16},{1,9},{9,1},{17,25},{25,17},{2,10},{10... | collective-permute-start | bytes 393224 | tf_op jit(solution)/shard_map/ppermute | solution.py:405
  17.3 8.5 %collective-permute-start.6 = (bf16[128,1024]{1,0:T(8,128)(2,1)S(1)}, bf16[128,1024]{1,0:T(8,128)(2,1)S(1)}, u32[]{:S(2)}, u32[]{:S(2)}) collective-permute-start(bf16[128,1024]{1,0:T(8,128)(2,1)S(1)} %chip_total_kernel.2), channel_id=1, source_target_pairs={{0,16},{8,24},{1,17},{9,25},{2,18},{10,26},{3,19},{11,27},{4,20},{... | collective-permute-start | bytes 786440 | tf_op jit(solution)/shard_map/ppermute | solution.py:468
  20.8 13.2 %collective-permute-start.2 = (bf16[256,1024]{1,0:T(8,128)(2,1)S(1)}, bf16[256,1024]{1,0:T(8,128)(2,1)S(1)}, u32[]{:S(2)}, u32[]{:S(2)}) collective-permute-start(bf16[256,1024]{1,0:T(8,128)(2,1)S(1)} %collective-permute-done.1.refs_1_), channel_id=1, source_target_pairs={{0,2},{2,0},{4,6},{6,4},{1,3},{3,1},{5,7},{7,5},{8,10},{10,8},{12,... | collective-permute-start | bytes 1572872 | tf_op jit(solution)/shard_map/ppermute | solution.py:411
  27.7 7.5 %copy-start.6 = (bf16[512,1024]{1,0:T(8,128)(2,1)S(1)}, bf16[512,1024]{1,0:T(8,128)(2,1)}, u32[]{:S(2)}) copy-start(bf16[512,1024]{1,0:T(8,128)(2,1)} %refs_6_.1) | copy-start | bytes 3145732
  27.8 6.8 %collective-permute-start.10 = (bf16[256,1024]{1,0:T(8,128)(2,1)S(1)}, bf16[256,1024]{1,0:T(8,128)(2,1)S(1)}, u32[]{:S(2)}, u32[]{:S(2)}) collective-permute-start(bf16[256,1024]{1,0:T(8,128)(2,1)S(1)} %get-tuple-element.86), channel_id=1, source_target_pairs={{0,8},{8,0},{16,24},{24,16},{1,9},{9,1},{17,25},{25,17},{2,10},{10... | collective-permute-start | bytes 1572872 | tf_op jit(solution)/shard_map/ppermute | solution.py:405
  27.9 7.2 %collective-permute-start.9 = (bf16[256,1024]{1,0:T(8,128)(2,1)S(1)}, bf16[256,1024]{1,0:T(8,128)(2,1)S(1)}, u32[]{:S(2)}, u32[]{:S(2)}) collective-permute-start(bf16[256,1024]{1,0:T(8,128)(2,1)S(1)} %get-tuple-element.87), channel_id=1, source_target_pairs={{0,8},{8,0},{16,24},{24,16},{1,9},{9,1},{17,25},{25,17},{2,10},{10... | collective-permute-start | bytes 1572872 | tf_op jit(solution)/shard_map/ppermute | solution.py:405
  28.4 9.1 %collective-permute-start.14 = (bf16[256,384]{1,0:T(8,128)(2,1)S(1)}, bf16[256,384]{1,0:T(8,128)(2,1)S(1)}, u32[]{:S(2)}, u32[]{:S(2)}) collective-permute-start(bf16[256,384]{1,0:T(8,128)(2,1)S(1)} %get-tuple-element.54.refs_9_.refs_6_), channel_id=1, source_target_pairs={{0,16},{8,24},{16,0},{24,8},{1,17},{9,25},{17,1},{25,9},{2,18},{10... | collective-permute-start | bytes 589832 | tf_op jit(solution)/shard_map/ppermute | solution.py:408
  30.9 12.7 %collective-permute-start.18 = (bf16[256,640]{1,0:T(8,128)(2,1)S(1)}, bf16[256,640]{1,0:T(8,128)(2,1)S(1)}, u32[]{:S(2)}, u32[]{:S(2)}) collective-permute-start(bf16[256,640]{1,0:T(8,128)(2,1)S(1)} %get-tuple-element.55.refs_3_.refs_6_), channel_id=1, source_target_pairs={{0,16},{8,24},{16,0},{24,8},{1,17},{9,25},{17,1},{25,9},{2,18},{10... | collective-permute-start | bytes 983048 | tf_op jit(solution)/shard_map/ppermute | solution.py:408
  34.6 3.6 %collective-permute-start.12 = (bf16[256,512]{1,0:T(8,128)(2,1)S(1)}, bf16[256,512]{1,0:T(8,128)(2,1)S(1)}, u32[]{:S(2)}, u32[]{:S(2)}) collective-permute-start(bf16[256,512]{1,0:T(8,128)(2,1)S(1)} %get-tuple-element.58.refs_4_), channel_id=1, source_target_pairs={{0,8},{8,0},{16,24},{24,16},{1,9},{9,1},{17,25},{25,17},{2,10},{10... | collective-permute-start | bytes 786440 | tf_op jit(solution)/shard_map/ppermute | solution.py:405
  34.6 5.0 %collective-permute-start.13 = (bf16[256,512]{1,0:T(8,128)(2,1)S(1)}, bf16[256,512]{1,0:T(8,128)(2,1)S(1)}, u32[]{:S(2)}, u32[]{:S(2)}) collective-permute-start(bf16[256,512]{1,0:T(8,128)(2,1)S(1)} %get-tuple-element.59.refs_5_), channel_id=1, source_target_pairs={{0,8},{8,0},{16,24},{24,16},{1,9},{9,1},{17,25},{25,17},{2,10},{10... | collective-permute-start | bytes 786440 | tf_op jit(solution)/shard_map/ppermute | solution.py:405
  35.1 2.9 %collective-permute-start.15 = (bf16[256,384]{1,0:T(8,128)(2,1)S(1)}, bf16[256,384]{1,0:T(8,128)(2,1)S(1)}, u32[]{:S(2)}, u32[]{:S(2)}) collective-permute-start(bf16[256,384]{1,0:T(8,128)(2,1)S(1)} %get-tuple-element.54.refs_9_.refs_6_), channel_id=1, source_target_pairs={{0,8},{8,0},{16,24},{24,16},{1,9},{9,1},{17,25},{25,17},{2,10},{10... | collective-permute-start | bytes 589832 | tf_op jit(solution)/shard_map/ppermute | solution.py:405
  37.6 2.1 %collective-permute-start.16 = (bf16[256,384]{1,0:T(8,128)(2,1)S(1)}, bf16[256,384]{1,0:T(8,128)(2,1)S(1)}, u32[]{:S(2)}, u32[]{:S(2)}) collective-permute-start(bf16[256,384]{1,0:T(8,128)(2,1)S(1)} %collective-permute-done.14.refs_7_), channel_id=1, source_target_pairs={{0,8},{8,0},{16,24},{24,16},{1,9},{9,1},{17,25},{25,17},{2,10},{10... | collective-permute-start | bytes 589832 | tf_op jit(solution)/shard_map/ppermute | solution.py:405
  38.1 6.3 %collective-permute-start.19 = (bf16[256,640]{1,0:T(8,128)(2,1)S(1)}, bf16[256,640]{1,0:T(8,128)(2,1)S(1)}, u32[]{:S(2)}, u32[]{:S(2)}) collective-permute-start(bf16[256,640]{1,0:T(8,128)(2,1)S(1)} %get-tuple-element.55.refs_3_.refs_6_), channel_id=1, source_target_pairs={{0,8},{8,0},{16,24},{24,16},{1,9},{9,1},{17,25},{25,17},{2,10},{10... | collective-permute-start | bytes 983048 | tf_op jit(solution)/shard_map/ppermute | solution.py:405
  38.2 16.1 %collective-permute-start.11 = (bf16[256,1024]{1,0:T(8,128)(2,1)S(1)}, bf16[256,1024]{1,0:T(8,128)(2,1)S(1)}, u32[]{:S(2)}, u32[]{:S(2)}) collective-permute-start(bf16[256,1024]{1,0:T(8,128)(2,1)S(1)} %get-tuple-element.62), channel_id=1, source_target_pairs={{0,16},{8,24},{16,0},{24,8},{1,17},{9,25},{17,1},{25,9},{2,18},{10... | collective-permute-start | bytes 1572872 | tf_op jit(solution)/shard_map/ppermute | solution.py:408
  40.9 13.4 %collective-permute-start.17 = (bf16[512,384]{1,0:T(8,128)(2,1)S(1)}, bf16[512,384]{1,0:T(8,128)(2,1)S(1)}, u32[]{:S(2)}, u32[]{:S(2)}) collective-permute-start(bf16[512,384]{1,0:T(8,128)(2,1)S(1)} %get-tuple-element.64.refs_12_.refs_6_), channel_id=1, source_target_pairs={{0,1},{1,0},{2,3},{3,2},{4,5},{5,4},{6,7},{7,6},{8,9},{9,8},{10,11... | collective-permute-start | bytes 1179656 | tf_op jit(solution)/shard_map/ppermute | solution.py:414
  43.7 1.5 %collective-permute-start.20 = (bf16[256,320]{1,0:T(8,128)(2,1)S(1)}, bf16[256,320]{1,0:T(8,128)(2,1)S(1)}, u32[]{:S(2)}, u32[]{:S(2)}) collective-permute-start(bf16[256,320]{1,0:T(8,128)(2,1)S(1)} %get-tuple-element.89), channel_id=1, source_target_pairs={{0,8},{8,0},{16,24},{24,16},{1,9},{9,1},{17,25},{25,17},{2,10},{10... | collective-permute-start | bytes 491528 | tf_op jit(solution)/shard_map/ppermute | solution.py:405
  43.8 1.7 %collective-permute-start.21 = (bf16[256,320]{1,0:T(8,128)(2,1)S(1)}, bf16[256,320]{1,0:T(8,128)(2,1)S(1)}, u32[]{:S(2)}, u32[]{:S(2)}) collective-permute-start(bf16[256,320]{1,0:T(8,128)(2,1)S(1)} %get-tuple-element.88), channel_id=1, source_target_pairs={{0,8},{8,0},{16,24},{24,16},{1,9},{9,1},{17,25},{25,17},{2,10},{10... | collective-permute-start | bytes 491528 | tf_op jit(solution)/shard_map/ppermute | solution.py:405
  47.4 21.0 %collective-permute-start.25 = (bf16[512,640]{1,0:T(8,128)(2,1)S(1)}, bf16[512,640]{1,0:T(8,128)(2,1)S(1)}, u32[]{:S(2)}, u32[]{:S(2)}) collective-permute-start(bf16[512,640]{1,0:T(8,128)(2,1)S(1)} %get-tuple-element.66.refs_7_), channel_id=1, source_target_pairs={{0,1},{1,0},{2,3},{3,2},{4,5},{5,4},{6,7},{7,6},{8,9},{9,8},{10,11... | collective-permute-start | bytes 1966088 | tf_op jit(solution)/shard_map/ppermute | solution.py:414
  55.3 1.6 %collective-permute-start.22 = (bf16[128,1024]{1,0:T(8,128)(2,1)S(1)}, bf16[128,1024]{1,0:T(8,128)(2,1)S(1)}, u32[]{:S(2)}, u32[]{:S(2)}) collective-permute-start(bf16[128,1024]{1,0:T(8,128)(2,1)S(1)} %get-tuple-element.78), channel_id=1, source_target_pairs={{0,8},{8,0},{16,24},{24,16},{1,9},{9,1},{17,25},{25,17},{2,10},{10... | collective-permute-start | bytes 786440 | tf_op jit(solution)/shard_map/ppermute | solution.py:405
  57.5 7.4 %collective-permute-start.23 = (bf16[128,512]{1,0:T(8,128)(2,1)S(1)}, bf16[128,512]{1,0:T(8,128)(2,1)S(1)}, u32[]{:S(2)}, u32[]{:S(2)}) collective-permute-start(bf16[128,512]{1,0:T(8,128)(2,1)S(1)} %chip_total_kernel.3), channel_id=1, source_target_pairs={{16,0},{24,8},{17,1},{25,9},{18,2},{26,10},{19,3},{27,11},{20,4},{... | collective-permute-start | bytes 393224 | tf_op jit(solution)/shard_map/ppermute | solution.py:537
  65.0 1.3 %collective-permute-start.24 = (bf16[128,512]{1,0:T(8,128)(2,1)S(1)}, bf16[128,512]{1,0:T(8,128)(2,1)S(1)}, u32[]{:S(2)}, u32[]{:S(2)}) collective-permute-start(bf16[128,512]{1,0:T(8,128)(2,1)S(1)} %collective-permute-done.23.refs_7_), channel_id=1, source_target_pairs={{0,8},{8,0},{16,24},{24,16},{1,9},{9,1},{17,25},{25,17},{2,10},{10... | collective-permute-start | bytes 393224 | tf_op jit(solution)/shard_map/ppermute | solution.py:405
  (4 other events, 10.4 us)

commit v5 on v4

--- a/solution.py
+++ b/solution.py
@@ -2,7 +2,6 @@
 
 import jax
 import jax.numpy as jnp
-import numpy as np
 from jax import lax
 from jax.experimental import pallas as pl
 from jax.experimental.pallas import tpu as pltpu
@@ -15,6 +14,7 @@
 PAIR = 2 * P_SIZE
 SHARES = (6, 10)
 PARITY, CORE, ODD, CHIP = 4, 6, 7, 8
+THROUGH, KEEP, CORE_ROW, SKIP, ODD_ROW = (slice(row, row + 1) for row in range(5))
 BF = jnp.bfloat16
 F32 = jnp.float32
 
@@ -36,9 +36,12 @@
     pairs = [item if isinstance(item, tuple) else (item, whole(item.shape)) for item in arrays]
     outs = [item if len(item) == 3 else (*item, whole(item[0])) for item in outs]
     count = len(scalars)
+    views = [item.view if isinstance(item, Ids) else (lambda ref: ref) for item in scalars]
+    scalars = [item.number if isinstance(item, Ids) else item for item in scalars]
 
     def run(*refs):
-        kernel(*refs[: count + len(pairs)], *refs[count + len(pairs) + len(after) :])
+        seen = [view(ref) for view, ref in zip(views, refs)]
+        kernel(*seen, *refs[count : count + len(pairs)], *refs[count + len(pairs) + len(after) :])
 
     return pl.pallas_call(
         run,
@@ -53,9 +56,34 @@
     )(*scalars, *[array for array, _ in pairs], *after)
 
 
+class Ids:
+    def __init__(self, number, chips, planes, dp):
+        self.number, self.sizes = number, (chips, planes, dp)
+
+    def view(self, ref):
+        seen = Ids(None, *self.sizes)
+        seen.ref = ref
+        return seen
+
+    def __getitem__(self, place):
+        chips, planes, dp = self.sizes
+        at = self.ref[0]
+        chip, core, odd, dialogue = at // (2 * planes * dp), at // (planes * dp) % 2, at // dp % 2, at % dp
+        if place >= CHIP:
+            return (chip + place - CHIP) % chips
+        if place in (CORE, ODD):
+            return core if place == CORE else odd
+        if place >= PARITY:
+            half, second = place - PARITY, odd
+        else:
+            half, second = place // 2, place % 2
+        own = core if half == 0 else 1 - core
+        return own * 2 + (dialogue + second) % 2
+
+
 def column_call(kernel, at, ids, grads, others, span, outs, after=()):
-    def run(*refs):
-        kernel(*refs[: 2 + len(others)], *refs[2 + len(others) + len(after) :])
+    def run(ids_ref, *refs):
+        kernel(ids.view(ids_ref), *refs[: 1 + len(others)], *refs[1 + len(others) + len(after) :])
 
     return pl.pallas_call(
         run,
@@ -63,7 +91,7 @@
         grid_spec=pltpu.PrefetchScalarGridSpec(
             num_scalar_prefetch=1,
             grid=(1,),
-            in_specs=[pl.BlockSpec((Q, span), lambda i, ids_ref: (0, ids_ref[at]))]
+            in_specs=[pl.BlockSpec((Q, span), lambda i, ids_ref: (0, ids.view(ids_ref)[at]))]
             + [whole(other.shape) for other in others]
             + [ANY] * len(after),
             out_specs=[whole(shape) for shape, _ in outs],
@@ -71,7 +99,7 @@
         cost_estimate=FREE,
         compiler_params=LIMIT,
         name=name_of(kernel),
-    )(ids, grads, *others, *after)
+    )(ids.number, grads, *others, *after)
 
 
 def dot(a, b, left, right):
@@ -92,9 +120,9 @@
 
 
 def tables_kernel(
-    rate_ref, resets_ref, x_ref, b_ref, step_ref, *refs
+    ids_ref, rate_ref, resets_ref, skip_ref, x_ref, b_ref, step_ref, *refs
 ):
-    states, sent, (weighted_ref, rows_ref, cols_ref, through_ref) = refs[:2], refs[2:4], refs[4:]
+    states, sent, (weighted_ref, rows_ref, cols_ref, table_ref) = refs[:2], refs[2:4], refs[4:]
     heads = step_ref.shape[0]
     keep = (1 - resets_ref[0, 0]).astype(F32)
     head_id = lax.broadcasted_iota(jnp.int32, (heads, Q), 0)
@@ -116,7 +144,13 @@
         log_pair = spread(cols, pair, first)
         last = log_pair[Q - 1 : Q, :]
         weighted_ref[:, at] = (x_ref[:, at].astype(F32) * jnp.exp(last - log_pair)).astype(BF)
-        through_ref[:, at] = jnp.broadcast_to(keep * jnp.exp(last), (8, PAIR))
+        table_ref[THROUGH, at] = keep * jnp.exp(last)
+        table_ref[SKIP, at] = gains(skip_ref, 2 * pair)
+    ones = jnp.ones((1, table_ref.shape[1]), F32)
+    table_ref[KEEP, :] = keep * ones
+    table_ref[CORE_ROW, :] = ids_ref[CORE].astype(F32) * ones
+    table_ref[ODD_ROW, :] = ids_ref[ODD].astype(F32) * ones
+    table_ref[5:, :] = jnp.zeros((3, table_ref.shape[1]), F32)
     state = dot(b_ref[...], weighted_ref[...], 0, 0)
     middle = state.shape[1] // 2
     for number in range(2):
@@ -125,7 +159,7 @@
         sent[number][...] = half.astype(BF)
 
 
-def local_output_kernel(skip_ref, x_ref, b_ref, c_ref, rows_ref, cols_ref, out_ref):
+def local_output_kernel(table_ref, x_ref, b_ref, c_ref, rows_ref, cols_ref, out_ref):
     heads = rows_ref.shape[0]
     scores = dot(c_ref[...], b_ref[...], 1, 1)
     at_row = lax.broadcasted_iota(jnp.int32, (HALF, HALF), 0)
@@ -136,7 +170,7 @@
     for pair in range(heads // 2):
         at = slice(pair * PAIR, (pair + 1) * PAIR)
         x_pair = x_ref[:, at]
-        skip = gains(skip_ref, 2 * pair) * x_pair.astype(F32)
+        skip = table_ref[SKIP, at] * x_pair.astype(F32)
         top, bottom = skip[:HALF], skip[HALF:]
         for side in range(2):
             head = 2 * pair + side
@@ -157,23 +191,23 @@
         out_ref[HALF:, at] = bottom
 
 
-def output_kernel(
-    start, ids_ref, resets_ref, local_ref, c_ref, cols_ref, through_ref, before_ref, left_ref, right_ref, out_ref, state_ref
-):
+def output_kernel(starts, table_ref, local_ref, c_ref, cols_ref, through_ref, before_ref, *refs):
+    partners, outs, states = refs[:2], refs[2 : 2 + len(starts)], refs[2 + len(starts) :]
     first = first_head()
     cols = cols_ref[...]
-    keep = (1 - resets_ref[0, 0]).astype(F32)
-    part = slice(start, start + out_ref.shape[1])
-    partner = jnp.concatenate([left_ref[...], right_ref[...]], axis=1)[:, part].astype(F32)
-    before = before_ref[:, part].astype(F32)
-    state = jnp.where(ids_ref[CORE] == 1, through_ref[:1, part] * before + partner, before)
-    state_ref[...] = (keep * state).astype(BF)
-    for pair in range(out_ref.shape[1] // PAIR):
-        at = slice(pair * PAIR, (pair + 1) * PAIR)
-        whole = slice(start + pair * PAIR, start + (pair + 1) * PAIR)
-        term = dot(c_ref[...], state_ref[:, at], 1, 0)
-        decay = jnp.exp(spread(cols, start // PAIR + pair, first))
-        out_ref[:, at] = (local_ref[:, whole] + decay * term).astype(BF)
+    partner = jnp.concatenate([ref[...] for ref in partners], axis=1)
+    for start, out_ref, state_ref in zip(starts, outs, states):
+        part = slice(start, start + out_ref.shape[1])
+        before = before_ref[:, part].astype(F32)
+        after = through_ref[THROUGH, part] * before + partner[:, part].astype(F32)
+        state = jnp.where(table_ref[CORE_ROW, part] == 1.0, after, before)
+        state_ref[...] = (table_ref[KEEP, part] * state).astype(BF)
+        for pair in range(out_ref.shape[1] // PAIR):
+            at = slice(pair * PAIR, (pair + 1) * PAIR)
+            whole = slice(start + pair * PAIR, start + (pair + 1) * PAIR)
+            term = dot(c_ref[...], state_ref[:, at], 1, 0)
+            decay = jnp.exp(spread(cols, start // PAIR + pair, first))
+            out_ref[:, at] = (local_ref[:, whole] + decay * term).astype(BF)
 
 
 def block_of(ids_ref, grad_ref, slot):
@@ -193,10 +227,10 @@
         halves[slot // 2][:, slot % 2 * depth : (slot % 2 + 1) * depth] = block_of(ids_ref, grad_ref, slot)
 
 
-def assemble_kernel(ids_ref, *refs):
+def assemble_kernel(table_ref, *refs):
     pieces, blocks = refs[:-4], refs[-4:]
     depth = blocks[0].shape[1]
-    even = ids_ref[ODD] == 0
+    even = table_ref[ODD_ROW, :depth] == 0.0
     for number, out_ref in enumerate(blocks):
         taken = slice(number // 2 * depth, (number // 2 + 1) * depth)
         for other in range(len(pieces) // 2):
@@ -226,11 +260,10 @@
         outs[number][...] = total.astype(outs[number].dtype)
 
 
-def adjoint_kernel(others, resets_ref, own_ref, *refs):
+def adjoint_kernel(others, table_ref, own_ref, *refs):
     parts, (c_ref, cols_ref, head_ref, weighted_ref, *halves) = refs[:others], refs[others:]
     first = first_head()
     cols = cols_ref[...]
-    keep = (1 - resets_ref[0, 0]).astype(F32)
     for pair in range(head_ref.shape[1] // PAIR):
         at = slice(pair * PAIR, (pair + 1) * PAIR)
         total = own_ref[:, at]
@@ -239,7 +272,7 @@
         head = total.astype(BF)
         head_ref[:, at] = head
         weighted_ref[:, at] = (head.astype(F32) * jnp.exp(spread(cols, pair, first))).astype(BF)
-    adjoint = keep * dot(c_ref[...], weighted_ref[...], 0, 0)
+    adjoint = table_ref[KEEP, :] * dot(c_ref[...], weighted_ref[...], 0, 0)
     middle = adjoint.shape[1] // 2
     for number in range(2):
         half = adjoint[:, number * middle : (number + 1) * middle]
@@ -247,9 +280,8 @@
         halves[2][:, number * middle : (number + 1) * middle] = half.astype(BF)
 
 
-def chip_total_kernel(last, parts, ids_ref, through_ref, partner_through_ref, *refs):
+def chip_total_kernel(last, parts, through_ref, partner_through_ref, *refs):
     owns, partners, entering, out_ref = refs[:2], refs[2 : 2 + parts], refs[2 + parts : -1], refs[-1]
-    leaves = ids_ref[CORE] == last
     width = owns[0].shape[1]
     halved = out_ref.shape[1] < 2 * width
     partner_state = jnp.concatenate([ref[...] for ref in partners], axis=1)
@@ -257,7 +289,8 @@
     for part in range(2):
         at = slice(part * width, (part + 1) * width)
         own, partner = owns[part][...], partner_state[:, at].astype(F32)
-        mine, theirs = through_ref[:1, at], partner_through_ref[:1, at]
+        mine, theirs = through_ref[THROUGH, at], partner_through_ref[THROUGH, at]
+        leaves = through_ref[CORE_ROW, at] == float(last)
         total = jnp.where(leaves, mine * partner + own, theirs * own + partner)
         for value in entering:
             came = value[...] if halved else value[:, at]
@@ -267,11 +300,12 @@
         else:
             out_ref[:, at] = total.astype(BF)
     if halved:
-        out_ref[...] = jnp.where(ids_ref[CORE] == 0, totals[0], totals[1]).astype(BF)
+        first_core = through_ref[CORE_ROW, :width] == 0.0
+        out_ref[...] = jnp.where(first_core, totals[0], totals[1]).astype(BF)
 
 
 def local_grads_kernel(
-    skip_ref, x_ref, grad_ref, b_ref, c_ref, rows_ref, cols_ref, weighted_ref, *refs
+    table_ref, x_ref, grad_ref, b_ref, c_ref, rows_ref, cols_ref, weighted_ref, *refs
 ):
     states, (in_ref, paired_ref, c_out_ref) = refs[:-3], refs[-3:]
     heads = x_ref.shape[1] // P_SIZE
@@ -286,7 +320,7 @@
         at = slice(pair * PAIR, (pair + 1) * PAIR)
         x_pair = x_ref[:, at]
         g_pair = grad_ref[:, at]
-        skip = gains(skip_ref, 2 * pair) * g_pair.astype(F32)
+        skip = table_ref[SKIP, at] * g_pair.astype(F32)
         top, bottom = skip[:HALF], skip[HALF:]
         for side in range(2):
             head = 2 * pair + side
@@ -322,19 +356,19 @@
     grad_c_ref[...] = c_part_ref[...] + dot(paired, b_ref[...], 0, 0)
 
 
-def final_kernel(ids_ref, b_ref, cols_ref, sums_ref, weighted_ref, through_ref, local_ref, *refs):
+def final_kernel(table_ref, b_ref, cols_ref, sums_ref, weighted_ref, through_ref, local_ref, *refs):
     entered, partner_ref, (in_ref, grad_b_ref, token_ref) = refs[:2], refs[2], refs[3:]
     token_ref[...] = jnp.zeros_like(token_ref)
     first = first_head()
     cols = cols_ref[...]
     grad_b = sums_ref[...]
-    core = ids_ref[CORE]
     width = partner_ref.shape[1] // 2
     for half in range(2):
         here = slice(half * width, (half + 1) * width)
-        entering = jnp.where(core == half, entered[0][...].astype(F32), entered[1][...].astype(F32))
-        inner = through_ref[:1, here] * entering + partner_ref[:, here].astype(F32)
-        adjoint = jnp.where(core == 1, entering, inner).astype(BF)
+        core = table_ref[CORE_ROW, here]
+        entering = jnp.where(core == float(half), entered[0][...].astype(F32), entered[1][...].astype(F32))
+        inner = through_ref[THROUGH, here] * entering + partner_ref[:, here].astype(F32)
+        adjoint = jnp.where(core == 1.0, entering, inner).astype(BF)
         grad_b += dot(weighted_ref[:, here], adjoint, 1, 1)
         for number in range(width // PAIR):
             pair = half * (width // PAIR) + number
@@ -416,12 +450,7 @@
     x, b_rows, c_rows, steps, incoming = (
         ssm_input[0], b_input[0], c_input[0], step_size[0], out_grad[0]
     )
-    table = []
-    for at in range(seq * planes * dp):
-        chip, core, odd, dialogue = at // (2 * planes * dp), at // (planes * dp) % 2, at // dp % 2, at % dp
-        order = [core * 2 + dialogue, core * 2 + 1 - dialogue, (1 - core) * 2 + dialogue, (1 - core) * 2 + 1 - dialogue]
-        table.append(order + [order[odd], order[2 + odd], core, odd] + [(chip + by) % chips for by in range(chips)])
-    ids = lax.dynamic_index_in_dim(np.array(table, np.int32), me, keepdims=False)
+    ids = Ids(me.astype(jnp.int32).reshape(1), chips, planes, dp)
 
     to_send = [
         column_call(send_kernel, CHIP + by, ids, incoming, [], span, [((Q, 2 * depth), BF)])
@@ -438,7 +467,7 @@
 
     *both, weighted_in, log_rows, log_cols, through = call(
         tables_kernel,
-        (decay_rate, resets),
+        (ids, decay_rate, resets, skip_gain),
         (x, b_rows, steps),
         [((N, wide // 2), F32)] * 2 + [((N, wide // 2), BF)] * 2 + [((Q, wide), BF)]
         + [((heads, Q), F32), ((Q, heads), F32), ((8, wide), F32)],
@@ -446,8 +475,8 @@
     )
     local_output, = call(
         local_output_kernel,
-        (skip_gain,),
-        (x, b_rows, c_rows, log_rows, log_cols),
+        (),
+        (through, x, b_rows, c_rows, log_rows, log_cols),
         [((Q, wide), F32)],
     )
     state_partner = [core_swap(half) for half in both[2:]]
@@ -460,27 +489,25 @@
     for hop in range(1, chips):
         total, = call(
             functools.partial(chip_total_kernel, 1, 2),
-            (ids,),
+            (),
             (through, through_partner, *both[:2], *state_partner, *before),
             [((N, wide), BF)],
             after=[local_output] if hop == 1 else (),
         )
         before = [lax.ppermute(total, "seq", [(i, i + 2) for i in range(seq - 2)])]
-    outputs, swapped, states = [], [], []
-    for start, width in zip(starts, widths):
-        output, state_in = call(
-            functools.partial(output_kernel, start),
-            (ids, resets),
-            (local_output, c_rows, log_cols, through_partner, *before, *state_partner),
-            [((Q, width), BF), ((N, width), BF)],
-            after=outputs[-1][:1] if outputs else [partner],
-        )
-        states.append(state_in)
-        outputs.append([output] + [chip_shift(output, by) for by in range(1, chips)])
-        swapped.append(core_swap(output))
+    results = call(
+        functools.partial(output_kernel, starts),
+        (),
+        (through, local_output, c_rows, log_cols, through_partner, *before, *state_partner),
+        [((Q, width), BF) for width in widths] + [((N, width), BF) for width in widths],
+        after=[partner],
+    )
+    outputs, states = results[: len(widths)], results[len(widths) :]
+    swapped = [core_swap(output) for output in outputs]
+    outputs = [[output] + [chip_shift(output, by) for by in range(1, chips)] for output in outputs]
 
     came = call(
-        assemble_kernel, (ids,), pieces, [(((chips - 1) * Q, depth), BF)] * 4, after=[outputs[-1][0]],
+        assemble_kernel, (), (through, *pieces), [(((chips - 1) * Q, depth), BF)] * 4, after=[outputs[-1][0]],
     )
     partner_came = [core_swap(block) for block in came[2:]]
     weight_late = later(weight_other, outputs[-1][0])
@@ -514,23 +541,23 @@
 
     head_grad, weighted_grad, *both = call(
         functools.partial(adjoint_kernel, chips - 1),
-        (resets,),
-        (partials[0], *returned, c_rows, log_cols),
+        (),
+        (through, partials[0], *returned, c_rows, log_cols),
         [((Q, wide), BF), ((Q, wide), BF)] + [((N, wide // 2), F32)] * 2 + [((N, wide), BF)],
         after=[sums[0], *sent],
     )
     adjoint_partner = core_swap(both[2])
     local_in, paired, c_part = call(
         local_grads_kernel,
-        (skip_gain,),
-        (x, head_grad, b_rows, c_rows, log_rows, log_cols, weighted_grad, *states),
+        (),
+        (through, x, head_grad, b_rows, c_rows, log_rows, log_cols, weighted_grad, *states),
         [((Q, wide), F32), ((Q, Q), F32), ((Q, N), F32)],
     )
     entering = []
     for hop in range(1, chips):
         total, = call(
             functools.partial(chip_total_kernel, 0, 1),
-            (ids,),
+            (),
             (through, through_partner, *both[:2], adjoint_partner, *entering),
             [((N, wide // 2), BF)],
         )
@@ -543,8 +570,8 @@
     )
     grad_in, grad_b, token = call(
         final_kernel,
-        (ids,),
-        (b_rows, log_cols, grad_b, weighted_in, through_partner, local_in)
+        (),
+        (through, b_rows, log_cols, grad_b, weighted_in, through_partner, local_in)
         + (*entering, core_swap(later(entering[0], grad_c)), adjoint_partner),
         [((Q, wide), BF), ((Q, N), F32), ((8, 128), F32)],
     )

time: 70.4 us -> 68.4 us (0.972)
  Pallas kernels: 22.7 us -> 17 us
  waiting for transfers between devices: 23.1 us -> 26.4 us
  starting transfers between devices: 19.3 us -> 20.6 us
    pallas_call x15 -> x14, Pallas kernels: 21.3 us -> 16.7 us  [call(): pl.pallas_call(run, grid=(1,), out_shape=[jax.ShapeDtypeStruct(shape, kin...]
    ppermute x3, waiting for transfers between devices: 0.01 us -> 2.84 us  [dialogue_swap(): return lax.ppermute(value, 'dp', [(0, 1), (1, 0)])]
    ppermute x3, starting transfers between devices: 4.53 us -> 6 us  [dialogue_swap(): return lax.ppermute(value, 'dp', [(0, 1), (1, 0)])]
    pallas_call x2, Pallas kernels: 1.35 us -> 0.27 us  [column_call(): pl.pallas_call(run, out_shape=[jax.ShapeDtypeStruct(shape, kind) for shap...]
    ppermute x4, waiting for transfers between devices: 8.67 us -> 9.55 us  [chip_shift(): lax.ppermute(value, 'seq', [(i, (i + 2 * by) % seq) for i in range(seq)])]
  transfers between devices with their start and end apart: 26 -> 26, of which waited for: 11 -> 14; matrix products, arithmetic and copies ran while one was open for 1% -> 0% of each run, Pallas kernels for 30% -> 22%
where the time goes in v5:
time: 68.4 us; the launch traced here: 68.2 us
  waiting for transfers between devices  26.4 us (39%)
  starting transfers between devices  20.6 us (30%)
  Pallas kernels  17 us (25%)
  local copies, waits for them, and re-layouts  2.65 us (4%)
  between operations  1.55 us (2%)
    pallas_call x14, Pallas kernels, call(): pl.pallas_call(run, grid=(1,), out_shape=[jax.ShapeDtypeStruct(shape, kin...  16.7 us
    ppermute x4, waiting for transfers between devices, chip_shift(): lax.ppermute(value, 'seq', [(i, (i + 2 * by) % seq) for i in range(seq)])  9.55 us
    ppermute x3, starting transfers between devices, dialogue_swap(): return lax.ppermute(value, 'dp', [(0, 1), (1, 0)])  6 us
    ppermute x16, waiting for transfers between devices, core_swap(): return lax.ppermute(value, 'seq', across)  5.54 us
    ppermute x4, starting transfers between devices, chip_shift(): lax.ppermute(value, 'seq', [(i, (i + 2 * by) % seq) for i in range(seq)])  5.31 us
    ppermute x16, starting transfers between devices, core_swap(): return lax.ppermute(value, 'seq', across)  3.67 us
    ppermute x1, waiting for transfers between devices, body(): entering = [lax.ppermute(total, 'seq', [(i, i - 2) for i in range(2, seq)])]  3.16 us
    ppermute x1, waiting for transfers between devices, body(): before = [lax.ppermute(total, 'seq', [(i, i + 2) for i in range(seq - 2)])]  3.05 us
  transfers between devices with their start and end apart: 26, of which 14 were waited for; matrix products, arithmetic and copies ran while one was open for 0% of the time, Pallas kernels for 22%

profile of v5, /device:TPU:0, one launch (start us, length us, event | category | flops | bytes accessed | tf_op | source)
XLA Modules:
  0.0 68.2 jit_solution(16236980053313036102)
XLA Ops:
  1.2 2.6 %collective-permute-start.8 = (bf16[512,1024]{1,0:T(8,128)(2,1)}, bf16[512,1024]{1,0:T(8,128)(2,1)S(1)}, u32[]{:S(2)}, u32[]{:S(2)}) collective-permute-start(bf16[512,1024]{1,0:T(8,128)(2,1)} %refs_6_.1), channel_id=1, source_target_pairs={{0,1},{1,0},{2,3},{3,2},{4,5},{5,4},{6,7},{7,6},{8,9},{9,8},{10,11... | collective-permute-start | bytes 3145736 | tf_op jit(solution)/shard_map/ppermute | solution.py:448
  3.8 1.6 %copy-done = bf16[1,256,4096]{2,1,0:T(8,128)(2,1)S(1)} copy-done((bf16[1,256,4096]{2,1,0:T(8,128)(2,1)S(1)}, bf16[1,256,4096]{2,1,0:T(8,128)(2,1)}, u32[]{:S(2)}) %copy-start) | copy-done | bytes 2097176
  5.5 1.6 %collective-permute-start.1 = (bf16[256,1024]{1,0:T(8,128)(2,1)S(1)}, bf16[256,1024]{1,0:T(8,128)(2,1)S(1)}, u32[]{:S(2)}, u32[]{:S(2)}) collective-permute-start(bf16[256,1024]{1,0:T(8,128)(2,1)S(1)} %send_kernel.1.refs_8_), channel_id=1, source_target_pairs={{0,16},{8,24},{16,0},{24,8},{1,17},{9,25},{17,1},{25,9},{2,18},{10... | collective-permute-start | bytes 1572872 | tf_op jit(solution)/shard_map/ppermute | solution.py:442
  7.8 0.8 %copy-done.4 = bf16[1,256,128]{2,1,0:T(8,128)(2,1)S(1)} copy-done((bf16[1,256,128]{2,1,0:T(8,128)(2,1)S(1)}, bf16[1,256,128]{2,1,0:T(8,128)(2,1)}, u32[]{:S(2)}) %copy-start.4) | copy-done | bytes 65560
  8.6 2.2 %tables_kernel.1 = (f32[128,512]{1,0:T(8,128)S(1)}, f32[128,512]{1,0:T(8,128)S(1)}, bf16[128,512]{1,0:T(8,128)(2,1)S(1)}, bf16[128,512]{1,0:T(8,128)(2,1)S(1)}, ...) custom-call(s32[1]{0:T(128)} %bitcast.ids_ref.refs_0_, ...), custom_call_target="tpu_custom_call" | custom-call | tf_op jit(solution)/shard_map/tables_kernel/pallas_call | solution.py:46
  11.7 1.4 %collective-permute-done.3.refs_1_.refs_4_.refs_5_ = f32[8,1024]{1,0:T(8,128)S(1)} collective-permute-done((f32[8,1024]{1,0:T(8,128)S(1)}, f32[8,1024]{1,0:T(8,128)S(1)}, u32[]{:S(2)}, u32[]{:S(2)}) %collective-permute-start.3) | collective-permute-done | bytes 32800 | tf_op jit(solution)/shard_map/ppermute | solution.py:439
  13.2 1.1 %local_output_kernel.1.refs_6_.refs_1_ = f32[256,1024]{1,0:T(8,128)S(1)} custom-call(f32[8,1024]{1,0:T(8,128)S(1)} %get-tuple-element.45.refs_1_.refs_0_, bf16[256,1024]{1,0:T(8,128)(2,1)S(1)} %bitcast.12, bf16[256,128]{1,0:T(8,128)(2,1)S(1)} %bitcast.20, bf16[256,128]{1,0:T(8,128)(2,1)S(1)} %bitcast.14, f32[16,256]{1,0:T(8,128)S(1)} %get-tuple-element.49.refs_4_.refs_5_, ...), custom_call_target="tpu_custom_call" | custom-call | tf_op jit(solution)/shard_map/local_output_kernel/pallas_call | solution.py:46
  14.5 2.5 %collective-permute-start.6 = (bf16[128,1024]{1,0:T(8,128)(2,1)S(1)}, bf16[128,1024]{1,0:T(8,128)(2,1)S(1)}, u32[]{:S(2)}, u32[]{:S(2)}) collective-permute-start(bf16[128,1024]{1,0:T(8,128)(2,1)S(1)} %chip_total_kernel.2), channel_id=1, source_target_pairs={{0,16},{8,24},{1,17},{9,25},{2,18},{10,26},{3,19},{11,27},{4,20},{... | collective-permute-start | bytes 786440 | tf_op jit(solution)/shard_map/ppermute | solution.py:497
  17.0 2.5 %collective-permute-done.1.refs_1_ = bf16[256,1024]{1,0:T(8,128)(2,1)S(1)} collective-permute-done((bf16[256,1024]{1,0:T(8,128)(2,1)S(1)}, bf16[256,1024]{1,0:T(8,128)(2,1)S(1)}, u32[]{:S(2)}, u32[]{:S(2)}) %collective-permute-start.1) | collective-permute-done | bytes 524320 | tf_op jit(solution)/shard_map/ppermute | solution.py:442
  19.5 1.6 %collective-permute-start.2 = (bf16[256,1024]{1,0:T(8,128)(2,1)S(1)}, bf16[256,1024]{1,0:T(8,128)(2,1)S(1)}, u32[]{:S(2)}, u32[]{:S(2)}) collective-permute-start(bf16[256,1024]{1,0:T(8,128)(2,1)S(1)} %collective-permute-done.1.refs_1_), channel_id=1, source_target_pairs={{0,2},{2,0},{4,6},{6,4},{1,3},{3,1},{5,7},{7,5},{8,10},{10,8},{12,... | collective-permute-start | bytes 1572872 | tf_op jit(solution)/shard_map/ppermute | solution.py:445
  21.1 3.1 %collective-permute-done.6.refs_5_ = bf16[128,1024]{1,0:T(8,128)(2,1)S(1)} collective-permute-done((bf16[128,1024]{1,0:T(8,128)(2,1)S(1)}, bf16[128,1024]{1,0:T(8,128)(2,1)S(1)}, u32[]{:S(2)}, u32[]{:S(2)}) %collective-permute-start.6) | collective-permute-done | bytes 262176 | tf_op jit(solution)/shard_map/ppermute | solution.py:497
  24.9 2.8 %collective-permute-done.8.refs_7_ = bf16[512,1024]{1,0:T(8,128)(2,1)S(1)} collective-permute-done((bf16[512,1024]{1,0:T(8,128)(2,1)}, bf16[512,1024]{1,0:T(8,128)(2,1)S(1)}, u32[]{:S(2)}, u32[]{:S(2)}) %collective-permute-start.8) | collective-permute-done | bytes 1048608 | tf_op jit(solution)/shard_map/ppermute | solution.py:448
  28.4 1.7 %collective-permute-start.14 = (bf16[256,384]{1,0:T(8,128)(2,1)S(1)}, bf16[256,384]{1,0:T(8,128)(2,1)S(1)}, u32[]{:S(2)}, u32[]{:S(2)}) collective-permute-start(bf16[256,384]{1,0:T(8,128)(2,1)S(1)} %get-tuple-element.62.refs_6_), channel_id=1, source_target_pairs={{0,16},{8,24},{16,0},{24,8},{1,17},{9,25},{17,1},{25,9},{2,18},{10... | collective-permute-start | bytes 589832 | tf_op jit(solution)/shard_map/ppermute | solution.py:442
  30.4 2.3 %collective-permute-done.2.refs_2_ = bf16[256,1024]{1,0:T(8,128)(2,1)S(1)} collective-permute-done((bf16[256,1024]{1,0:T(8,128)(2,1)S(1)}, bf16[256,1024]{1,0:T(8,128)(2,1)S(1)}, u32[]{:S(2)}, u32[]{:S(2)}) %collective-permute-start.2) | collective-permute-done | bytes 524320 | tf_op jit(solution)/shard_map/ppermute | solution.py:445
  33.5 2.3 %head_partial_kernel.1 = (f32[256,1024]{1,0:T(8,128)S(1)}, bf16[256,1024]{1,0:T(8,128)(2,1)S(1)}) custom-call(bf16[256,1024]{1,0:T(8,128)(2,1)S(1)} %get-tuple-element.47.refs_0_, bf16[256,1024]{1,0:T(8,128)(2,1)S(1)} %get-tuple-element.48.refs_1_, bf16[256,512]{1,0:T(8,128)(2,1)S(1)} %get-tuple-element.55.refs_2_, ...), custom_call_target="tpu_custom_call" | custom-call | tf_op jit(solution)/shard_map/head_partial_kernel/pallas_call | solution.py:46
  36.7 1.7 %collective-permute-start.11 = (bf16[256,1024]{1,0:T(8,128)(2,1)S(1)}, bf16[256,1024]{1,0:T(8,128)(2,1)S(1)}, u32[]{:S(2)}, u32[]{:S(2)}) collective-permute-start(bf16[256,1024]{1,0:T(8,128)(2,1)S(1)} %get-tuple-element.61), channel_id=1, source_target_pairs={{0,16},{8,24},{16,0},{24,8},{1,17},{9,25},{17,1},{25,9},{2,18},{10... | collective-permute-start | bytes 1572872 | tf_op jit(solution)/shard_map/ppermute | solution.py:442
  38.4 1.3 %weight_partial_kernel.2 = (f32[512,384]{1,0:T(8,128)S(1)}, bf16[512,384]{1,0:T(8,128)(2,1)S(1)}) custom-call(bf16[256,1024]{1,0:T(8,128)(2,1)S(1)} %get-tuple-element.47.refs_0_, bf16[256,1024]{1,0:T(8,128)(2,1)S(1)} %collective-permute-done.7.refs_8_.refs_1_, bf16[256,512]{1,0:T(8,128)(2,1)S(1)} %get-tuple-element.55.refs_2_, ...), custom_call_target="tpu_custom_call" | custom-call | tf_op jit(solution)/shard_map/weight_partial_kernel/pallas_call | solution.py:46
  39.7 1.6 %collective-permute-start.17 = (bf16[512,384]{1,0:T(8,128)(2,1)S(1)}, bf16[512,384]{1,0:T(8,128)(2,1)S(1)}, u32[]{:S(2)}, u32[]{:S(2)}) collective-permute-start(bf16[512,384]{1,0:T(8,128)(2,1)S(1)} %get-tuple-element.64.refs_12_.refs_6_), channel_id=1, source_target_pairs={{0,1},{1,0},{2,3},{3,2},{4,5},{5,4},{6,7},{7,6},{8,9},{9,8},{10,11... | collective-permute-start | bytes 1179656 | tf_op jit(solution)/shard_map/ppermute | solution.py:448
  41.3 1.9 %collective-permute-done.18.refs_7_ = bf16[256,640]{1,0:T(8,128)(2,1)S(1)} collective-permute-done((bf16[256,640]{1,0:T(8,128)(2,1)S(1)}, bf16[256,640]{1,0:T(8,128)(2,1)S(1)}, u32[]{:S(2)}, u32[]{:S(2)}) %collective-permute-start.18) | collective-permute-done | bytes 327712 | tf_op jit(solution)/shard_map/ppermute | solution.py:442
  43.9 0.9 %collective-permute-done.20.refs_9_ = bf16[256,320]{1,0:T(8,128)(2,1)S(1)} collective-permute-done((bf16[256,320]{1,0:T(8,128)(2,1)S(1)}, bf16[256,320]{1,0:T(8,128)(2,1)S(1)}, u32[]{:S(2)}, u32[]{:S(2)}) %collective-permute-start.20) | collective-permute-done | bytes 163872 | tf_op jit(solution)/shard_map/ppermute | solution.py:439
  45.1 1.8 %weight_partial_kernel.3 = (f32[512,640]{1,0:T(8,128)S(1)}, bf16[512,640]{1,0:T(8,128)(2,1)S(1)}) custom-call(bf16[256,1024]{1,0:T(8,128)(2,1)S(1)} %get-tuple-element.47.refs_0_, bf16[256,1024]{1,0:T(8,128)(2,1)S(1)} %collective-permute-done.7.refs_8_.refs_1_, bf16[256,512]{1,0:T(8,128)(2,1)S(1)} %get-tuple-element.55.refs_2_, ...), custom_call_target="tpu_custom_call" | custom-call | tf_op jit(solution)/shard_map/weight_partial_kernel/pallas_call | solution.py:46
  46.9 1.8 %collective-permute-start.25 = (bf16[512,640]{1,0:T(8,128)(2,1)S(1)}, bf16[512,640]{1,0:T(8,128)(2,1)S(1)}, u32[]{:S(2)}, u32[]{:S(2)}) collective-permute-start(bf16[512,640]{1,0:T(8,128)(2,1)S(1)} %get-tuple-element.66.refs_7_), channel_id=1, source_target_pairs={{0,1},{1,0},{2,3},{3,2},{4,5},{5,4},{6,7},{7,6},{8,9},{9,8},{10,11... | collective-permute-start | bytes 1966088 | tf_op jit(solution)/shard_map/ppermute | solution.py:448
  48.7 4.8 %collective-permute-done.11.refs_2_ = bf16[256,1024]{1,0:T(8,128)(2,1)S(1)} collective-permute-done((bf16[256,1024]{1,0:T(8,128)(2,1)S(1)}, bf16[256,1024]{1,0:T(8,128)(2,1)S(1)}, u32[]{:S(2)}, u32[]{:S(2)}) %collective-permute-start.11) | collective-permute-done | bytes 524320 | tf_op jit(solution)/shard_map/ppermute | solution.py:442
  53.5 1.0 %adjoint_kernel.1 = (bf16[256,1024]{1,0:T(8,128)(2,1)S(1)}, bf16[256,1024]{1,0:T(8,128)(2,1)S(1)}, f32[128,512]{1,0:T(8,128)S(1)}, f32[128,512]{1,0:T(8,128)S(1)}, bf16[128,1024]{1,0:T(8,128)(2,1)S(1)}) custom-call(f32[8,1024]{1,0:T(8,128)S(1)} %get-tuple-element.45.refs_1_.refs_0_, f32[256,1024]{1,0:T(8,128)S(1)} %get-tuple-element.60.refs_10_.refs_11_.refs_1_, ...), custom_call_target="tpu_custom_call" | custom-call | tf_op jit(solution)/shard_map/adjoint_kernel/pallas_call | solution.py:46
  54.6 1.5 %collective-permute-done.22.refs_4_.refs_9_ = bf16[128,1024]{1,0:T(8,128)(2,1)S(1)} collective-permute-done((bf16[128,1024]{1,0:T(8,128)(2,1)S(1)}, bf16[128,1024]{1,0:T(8,128)(2,1)S(1)}, u32[]{:S(2)}, u32[]{:S(2)}) %collective-permute-start.22) | collective-permute-done | bytes 262176 | tf_op jit(solution)/shard_map/ppermute | solution.py:439
  56.2 1.5 %collective-permute-start.23 = (bf16[128,512]{1,0:T(8,128)(2,1)S(1)}, bf16[128,512]{1,0:T(8,128)(2,1)S(1)}, u32[]{:S(2)}, u32[]{:S(2)}) collective-permute-start(bf16[128,512]{1,0:T(8,128)(2,1)S(1)} %chip_total_kernel.3), channel_id=1, source_target_pairs={{16,0},{24,8},{17,1},{25,9},{18,2},{26,10},{19,3},{27,11},{20,4},{... | collective-permute-start | bytes 393224 | tf_op jit(solution)/shard_map/ppermute | solution.py:564
  57.7 1.9 %local_grads_kernel.1 = (f32[256,1024]{1,0:T(8,128)S(1)}, f32[256,256]{1,0:T(8,128)S(1)}, f32[256,128]{1,0:T(8,128)S(1)}) custom-call(f32[8,1024]{1,0:T(8,128)S(1)} %get-tuple-element.45.refs_1_.refs_0_, bf16[256,1024]{1,0:T(8,128)(2,1)S(1)} %bitcast.13, bf16[256,1024]{1,0:T(8,128)(2,1)S(1)} %get-tuple-element.67.refs_2_, bf16[256,128]{1,0:T(8,128)(2,1)S(1)} %bitcast.21, ...), custom_call_target="tpu_custom_call" | custom-call | tf_op jit(solution)/shard_map/local_grads_kernel/pallas_call | solution.py:46
  59.6 0.9 %group_sums_kernel.1 = (f32[256,128]{1,0:T(8,128)S(1)}, f32[256,128]{1,0:T(8,128)}) custom-call(bf16[256,128]{1,0:T(8,128)(2,1)S(1)} %bitcast.22, bf16[256,128]{1,0:T(8,128)(2,1)S(1)} %bitcast.18, f32[256,256]{1,0:T(8,128)S(1)} %get-tuple-element.71.refs_2_, f32[256,128]{1,0:T(8,128)S(1)} %get-tuple-element.72.refs_3_), custom_call_target="tpu_custom_call" | custom-call | tf_op jit(solution)/shard_map/group_sums_kernel/pallas_call | solution.py:46
  60.5 3.2 %collective-permute-done.23.refs_7_ = bf16[128,512]{1,0:T(8,128)(2,1)S(1)} collective-permute-done((bf16[128,512]{1,0:T(8,128)(2,1)S(1)}, bf16[128,512]{1,0:T(8,128)(2,1)S(1)}, u32[]{:S(2)}, u32[]{:S(2)}) %collective-permute-start.23) | collective-permute-done | bytes 131104 | tf_op jit(solution)/shard_map/ppermute | solution.py:564
  63.6 1.3 %collective-permute-done.24.refs_8_ = bf16[128,512]{1,0:T(8,128)(2,1)S(1)} collective-permute-done((bf16[128,512]{1,0:T(8,128)(2,1)S(1)}, bf16[128,512]{1,0:T(8,128)(2,1)S(1)}, u32[]{:S(2)}, u32[]{:S(2)}) %collective-permute-start.24) | collective-permute-done | bytes 131104 | tf_op jit(solution)/shard_map/ppermute | solution.py:439
  65.0 1.5 %final_kernel.1 = (bf16[256,1024]{1,0:T(8,128)(2,1)}, f32[256,128]{1,0:T(8,128)}, f32[8,128]{1,0:T(8,128)S(1)}) custom-call(f32[8,1024]{1,0:T(8,128)S(1)} %get-tuple-element.45.refs_1_.refs_0_, bf16[256,128]{1,0:T(8,128)(2,1)S(1)} %bitcast.23, f32[256,16]{1,0:T(8,128)S(1)} %get-tuple-element.46.refs_5_.refs_3_.refs_4_.refs_6_.refs_2_, ...), custom_call_target="tpu_custom_call" | custom-call | tf_op jit(solution)/shard_map/final_kernel/pallas_call | solution.py:46
  66.5 1.7 %add_kernel.1 = f32[512,1024]{1,0:T(8,128)} custom-call(f32[512,384]{1,0:T(8,128)S(1)} %get-tuple-element.83.refs_0_, f32[512,640]{1,0:T(8,128)S(1)} %get-tuple-element.84.refs_1_, bf16[512,384]{1,0:T(8,128)(2,1)S(1)} %collective-permute-done.17.refs_5_.refs_2_, bf16[512,640]{1,0:T(8,128)(2,1)S(1)} %collective-permute-done.25.refs_3_, ...), custom_call_target="tpu_custom_call" | custom-call | tf_op jit(solution)/shard_map/add_kernel/pallas_call | solution.py:46
  (58 shorter events, 6.2 us)
Async XLA Ops:
  0.6 7.1 %copy-start.7 = (f32[1,16,256]{2,1,0:T(8,128)S(1)}, f32[1,16,256]{2,1,0:T(8,128)}, u32[]{:S(2)}) copy-start(f32[1,16,256]{2,1,0:T(8,128)} %param.12) | copy-start | bytes 49156
  0.6 7.1 %copy-start.8 = (f32[16]{0:T(128)S(1)}, f32[16]{0:T(128)}, u32[]{:S(2)}) copy-start(f32[16]{0:T(128)} %refs_1_.1) | copy-start | bytes 196
  0.7 7.1 %copy-start.9 = (f32[16]{0:T(128)S(1)}, f32[16]{0:T(128)}, u32[]{:S(2)}) copy-start(f32[16]{0:T(128)} %refs_3_.1) | copy-start | bytes 196
  0.7 7.0 %collective-permute-start = (bf16[512,1024]{1,0:T(8,128)(2,1)}, bf16[512,1024]{1,0:T(8,128)(2,1)S(1)}, u32[]{:S(2)}, u32[]{:S(2)}) collective-permute-start(bf16[512,1024]{1,0:T(8,128)(2,1)} %refs_6_.1), channel_id=1, source_target_pairs={{0,8},{8,0},{16,24},{24,16},{1,9},{9,1},{17,25},{25,17},{2,10},{10... | collective-permute-start | bytes 3145736 | tf_op jit(solution)/shard_map/ppermute | solution.py:439
  1.2 26.6 %collective-permute-start.8 = (bf16[512,1024]{1,0:T(8,128)(2,1)}, bf16[512,1024]{1,0:T(8,128)(2,1)S(1)}, u32[]{:S(2)}, u32[]{:S(2)}) collective-permute-start(bf16[512,1024]{1,0:T(8,128)(2,1)} %refs_6_.1), channel_id=1, source_target_pairs={{0,1},{1,0},{2,3},{3,2},{4,5},{5,4},{6,7},{7,6},{8,9},{9,8},{10,11... | collective-permute-start | bytes 3145736 | tf_op jit(solution)/shard_map/ppermute | solution.py:448
  5.4 5.5 %copy-start.1 = (bf16[1,256,4096]{2,1,0:T(8,128)(2,1)S(1)}, bf16[1,256,4096]{2,1,0:T(8,128)(2,1)}, u32[]{:S(2)}) copy-start(bf16[1,256,4096]{2,1,0:T(8,128)(2,1)} %param.16) | copy-start | bytes 6291460
  5.5 14.1 %collective-permute-start.1 = (bf16[256,1024]{1,0:T(8,128)(2,1)S(1)}, bf16[256,1024]{1,0:T(8,128)(2,1)S(1)}, u32[]{:S(2)}, u32[]{:S(2)}) collective-permute-start(bf16[256,1024]{1,0:T(8,128)(2,1)S(1)} %send_kernel.1.refs_8_), channel_id=1, source_target_pairs={{0,16},{8,24},{16,0},{24,8},{1,17},{9,25},{17,1},{25,9},{2,18},{10... | collective-permute-start | bytes 1572872 | tf_op jit(solution)/shard_map/ppermute | solution.py:442
  8.6 4.6 %copy-start.5 = (bf16[1,256,128]{2,1,0:T(8,128)(2,1)S(1)}, bf16[1,256,128]{2,1,0:T(8,128)(2,1)}, u32[]{:S(2)}) copy-start(bf16[1,256,128]{2,1,0:T(8,128)(2,1)} %param.10) | copy-start | bytes 196612
  11.0 13.2 %collective-permute-start.7 = (bf16[256,1024]{1,0:T(8,128)(2,1)S(1)}, bf16[256,1024]{1,0:T(8,128)(2,1)S(1)}, u32[]{:S(2)}, u32[]{:S(2)}) collective-permute-start(bf16[256,1024]{1,0:T(8,128)(2,1)S(1)} %get-tuple-element.48.refs_1_), channel_id=1, source_target_pairs={{0,8},{8,0},{16,24},{24,16},{1,9},{9,1},{17,25},{25,17},{2,10},{10... | collective-permute-start | bytes 1572872 | tf_op jit(solution)/shard_map/ppermute | solution.py:439
  11.1 1.9 %collective-permute-start.3 = (f32[8,1024]{1,0:T(8,128)S(1)}, f32[8,1024]{1,0:T(8,128)S(1)}, u32[]{:S(2)}, u32[]{:S(2)}) collective-permute-start(f32[8,1024]{1,0:T(8,128)S(1)} %get-tuple-element.45.refs_1_.refs_0_), channel_id=1, source_target_pairs={{0,8},{8,0},{16,24},{24,16},{1,9},{9,1},{17,25},{25,17},{2,10},{10... | collective-permute-start | bytes 98312 | tf_op jit(solution)/shard_map/ppermute | solution.py:439
  11.6 2.7 %collective-permute-start.4 = (bf16[128,512]{1,0:T(8,128)(2,1)S(1)}, bf16[128,512]{1,0:T(8,128)(2,1)S(1)}, u32[]{:S(2)}, u32[]{:S(2)}) collective-permute-start(bf16[128,512]{1,0:T(8,128)(2,1)S(1)} %get-tuple-element.52), channel_id=1, source_target_pairs={{0,8},{8,0},{16,24},{24,16},{1,9},{9,1},{17,25},{25,17},{2,10},{10... | collective-permute-start | bytes 393224 | tf_op jit(solution)/shard_map/ppermute | solution.py:439
  13.0 1.3 %collective-permute-start.5 = (bf16[128,512]{1,0:T(8,128)(2,1)S(1)}, bf16[128,512]{1,0:T(8,128)(2,1)S(1)}, u32[]{:S(2)}, u32[]{:S(2)}) collective-permute-start(bf16[128,512]{1,0:T(8,128)(2,1)S(1)} %get-tuple-element.53), channel_id=1, source_target_pairs={{0,8},{8,0},{16,24},{24,16},{1,9},{9,1},{17,25},{25,17},{2,10},{10... | collective-permute-start | bytes 393224 | tf_op jit(solution)/shard_map/ppermute | solution.py:439
  14.5 9.7 %collective-permute-start.6 = (bf16[128,1024]{1,0:T(8,128)(2,1)S(1)}, bf16[128,1024]{1,0:T(8,128)(2,1)S(1)}, u32[]{:S(2)}, u32[]{:S(2)}) collective-permute-start(bf16[128,1024]{1,0:T(8,128)(2,1)S(1)} %chip_total_kernel.2), channel_id=1, source_target_pairs={{0,16},{8,24},{1,17},{9,25},{2,18},{10,26},{3,19},{11,27},{4,20},{... | collective-permute-start | bytes 786440 | tf_op jit(solution)/shard_map/ppermute | solution.py:497
  19.5 13.2 %collective-permute-start.2 = (bf16[256,1024]{1,0:T(8,128)(2,1)S(1)}, bf16[256,1024]{1,0:T(8,128)(2,1)S(1)}, u32[]{:S(2)}, u32[]{:S(2)}) collective-permute-start(bf16[256,1024]{1,0:T(8,128)(2,1)S(1)} %collective-permute-done.1.refs_1_), channel_id=1, source_target_pairs={{0,2},{2,0},{4,6},{6,4},{1,3},{3,1},{5,7},{7,5},{8,10},{10,8},{12,... | collective-permute-start | bytes 1572872 | tf_op jit(solution)/shard_map/ppermute | solution.py:445
  24.9 8.6 %copy-start.6 = (bf16[512,1024]{1,0:T(8,128)(2,1)S(1)}, bf16[512,1024]{1,0:T(8,128)(2,1)}, u32[]{:S(2)}) copy-start(bf16[512,1024]{1,0:T(8,128)(2,1)} %refs_6_.1) | copy-start | bytes 3145732
  27.8 5.1 %collective-permute-start.10 = (bf16[256,1024]{1,0:T(8,128)(2,1)S(1)}, bf16[256,1024]{1,0:T(8,128)(2,1)S(1)}, u32[]{:S(2)}, u32[]{:S(2)}) collective-permute-start(bf16[256,1024]{1,0:T(8,128)(2,1)S(1)} %get-tuple-element.86), channel_id=1, source_target_pairs={{0,8},{8,0},{16,24},{24,16},{1,9},{9,1},{17,25},{25,17},{2,10},{10... | collective-permute-start | bytes 1572872 | tf_op jit(solution)/shard_map/ppermute | solution.py:439
  27.9 5.5 %collective-permute-start.9 = (bf16[256,1024]{1,0:T(8,128)(2,1)S(1)}, bf16[256,1024]{1,0:T(8,128)(2,1)S(1)}, u32[]{:S(2)}, u32[]{:S(2)}) collective-permute-start(bf16[256,1024]{1,0:T(8,128)(2,1)S(1)} %get-tuple-element.87), channel_id=1, source_target_pairs={{0,8},{8,0},{16,24},{24,16},{1,9},{9,1},{17,25},{25,17},{2,10},{10... | collective-permute-start | bytes 1572872 | tf_op jit(solution)/shard_map/ppermute | solution.py:439
  28.4 7.8 %collective-permute-start.14 = (bf16[256,384]{1,0:T(8,128)(2,1)S(1)}, bf16[256,384]{1,0:T(8,128)(2,1)S(1)}, u32[]{:S(2)}, u32[]{:S(2)}) collective-permute-start(bf16[256,384]{1,0:T(8,128)(2,1)S(1)} %get-tuple-element.62.refs_6_), channel_id=1, source_target_pairs={{0,16},{8,24},{16,0},{24,8},{1,17},{9,25},{17,1},{25,9},{2,18},{10... | collective-permute-start | bytes 589832 | tf_op jit(solution)/shard_map/ppermute | solution.py:442
  30.1 13.1 %collective-permute-start.18 = (bf16[256,640]{1,0:T(8,128)(2,1)S(1)}, bf16[256,640]{1,0:T(8,128)(2,1)S(1)}, u32[]{:S(2)}, u32[]{:S(2)}) collective-permute-start(bf16[256,640]{1,0:T(8,128)(2,1)S(1)} %get-tuple-element.54.refs_3_.refs_6_), channel_id=1, source_target_pairs={{0,16},{8,24},{16,0},{24,8},{1,17},{9,25},{17,1},{25,9},{2,18},{10... | collective-permute-start | bytes 983048 | tf_op jit(solution)/shard_map/ppermute | solution.py:442
  32.8 3.9 %collective-permute-start.12 = (bf16[256,512]{1,0:T(8,128)(2,1)S(1)}, bf16[256,512]{1,0:T(8,128)(2,1)S(1)}, u32[]{:S(2)}, u32[]{:S(2)}) collective-permute-start(bf16[256,512]{1,0:T(8,128)(2,1)S(1)} %get-tuple-element.57.refs_4_), channel_id=1, source_target_pairs={{0,8},{8,0},{16,24},{24,16},{1,9},{9,1},{17,25},{25,17},{2,10},{10... | collective-permute-start | bytes 786440 | tf_op jit(solution)/shard_map/ppermute | solution.py:439
  32.9 5.5 %collective-permute-start.13 = (bf16[256,512]{1,0:T(8,128)(2,1)S(1)}, bf16[256,512]{1,0:T(8,128)(2,1)S(1)}, u32[]{:S(2)}, u32[]{:S(2)}) collective-permute-start(bf16[256,512]{1,0:T(8,128)(2,1)S(1)} %get-tuple-element.58.refs_5_), channel_id=1, source_target_pairs={{0,8},{8,0},{16,24},{24,16},{1,9},{9,1},{17,25},{25,17},{2,10},{10... | collective-permute-start | bytes 786440 | tf_op jit(solution)/shard_map/ppermute | solution.py:439
  33.4 2.9 %collective-permute-start.15 = (bf16[256,384]{1,0:T(8,128)(2,1)S(1)}, bf16[256,384]{1,0:T(8,128)(2,1)S(1)}, u32[]{:S(2)}, u32[]{:S(2)}) collective-permute-start(bf16[256,384]{1,0:T(8,128)(2,1)S(1)} %get-tuple-element.62.refs_6_), channel_id=1, source_target_pairs={{0,8},{8,0},{16,24},{24,16},{1,9},{9,1},{17,25},{25,17},{2,10},{10... | collective-permute-start | bytes 589832 | tf_op jit(solution)/shard_map/ppermute | solution.py:439
  36.1 2.3 %collective-permute-start.16 = (bf16[256,384]{1,0:T(8,128)(2,1)S(1)}, bf16[256,384]{1,0:T(8,128)(2,1)S(1)}, u32[]{:S(2)}, u32[]{:S(2)}) collective-permute-start(bf16[256,384]{1,0:T(8,128)(2,1)S(1)} %collective-permute-done.14.refs_7_), channel_id=1, source_target_pairs={{0,8},{8,0},{16,24},{24,16},{1,9},{9,1},{17,25},{25,17},{2,10},{10... | collective-permute-start | bytes 589832 | tf_op jit(solution)/shard_map/ppermute | solution.py:439
  36.3 7.6 %collective-permute-start.19 = (bf16[256,640]{1,0:T(8,128)(2,1)S(1)}, bf16[256,640]{1,0:T(8,128)(2,1)S(1)}, u32[]{:S(2)}, u32[]{:S(2)}) collective-permute-start(bf16[256,640]{1,0:T(8,128)(2,1)S(1)} %get-tuple-element.54.refs_3_.refs_6_), channel_id=1, source_target_pairs={{0,8},{8,0},{16,24},{24,16},{1,9},{9,1},{17,25},{25,17},{2,10},{10... | collective-permute-start | bytes 983048 | tf_op jit(solution)/shard_map/ppermute | solution.py:439
  36.7 16.9 %collective-permute-start.11 = (bf16[256,1024]{1,0:T(8,128)(2,1)S(1)}, bf16[256,1024]{1,0:T(8,128)(2,1)S(1)}, u32[]{:S(2)}, u32[]{:S(2)}) collective-permute-start(bf16[256,1024]{1,0:T(8,128)(2,1)S(1)} %get-tuple-element.61), channel_id=1, source_target_pairs={{0,16},{8,24},{16,0},{24,8},{1,17},{9,25},{17,1},{25,9},{2,18},{10... | collective-permute-start | bytes 1572872 | tf_op jit(solution)/shard_map/ppermute | solution.py:442
  39.7 13.9 %collective-permute-start.17 = (bf16[512,384]{1,0:T(8,128)(2,1)S(1)}, bf16[512,384]{1,0:T(8,128)(2,1)S(1)}, u32[]{:S(2)}, u32[]{:S(2)}) collective-permute-start(bf16[512,384]{1,0:T(8,128)(2,1)S(1)} %get-tuple-element.64.refs_12_.refs_6_), channel_id=1, source_target_pairs={{0,1},{1,0},{2,3},{3,2},{4,5},{5,4},{6,7},{7,6},{8,9},{9,8},{10,11... | collective-permute-start | bytes 1179656 | tf_op jit(solution)/shard_map/ppermute | solution.py:448
  43.3 1.5 %collective-permute-start.20 = (bf16[256,320]{1,0:T(8,128)(2,1)S(1)}, bf16[256,320]{1,0:T(8,128)(2,1)S(1)}, u32[]{:S(2)}, u32[]{:S(2)}) collective-permute-start(bf16[256,320]{1,0:T(8,128)(2,1)S(1)} %get-tuple-element.89), channel_id=1, source_target_pairs={{0,8},{8,0},{16,24},{24,16},{1,9},{9,1},{17,25},{25,17},{2,10},{10... | collective-permute-start | bytes 491528 | tf_op jit(solution)/shard_map/ppermute | solution.py:439
  43.4 1.7 %collective-permute-start.21 = (bf16[256,320]{1,0:T(8,128)(2,1)S(1)}, bf16[256,320]{1,0:T(8,128)(2,1)S(1)}, u32[]{:S(2)}, u32[]{:S(2)}) collective-permute-start(bf16[256,320]{1,0:T(8,128)(2,1)S(1)} %get-tuple-element.88), channel_id=1, source_target_pairs={{0,8},{8,0},{16,24},{24,16},{1,9},{9,1},{17,25},{25,17},{2,10},{10... | collective-permute-start | bytes 491528 | tf_op jit(solution)/shard_map/ppermute | solution.py:439
  46.9 19.6 %collective-permute-start.25 = (bf16[512,640]{1,0:T(8,128)(2,1)S(1)}, bf16[512,640]{1,0:T(8,128)(2,1)S(1)}, u32[]{:S(2)}, u32[]{:S(2)}) collective-permute-start(bf16[512,640]{1,0:T(8,128)(2,1)S(1)} %get-tuple-element.66.refs_7_), channel_id=1, source_target_pairs={{0,1},{1,0},{2,3},{3,2},{4,5},{5,4},{6,7},{7,6},{8,9},{9,8},{10,11... | collective-permute-start | bytes 1966088 | tf_op jit(solution)/shard_map/ppermute | solution.py:448
  54.5 1.6 %collective-permute-start.22 = (bf16[128,1024]{1,0:T(8,128)(2,1)S(1)}, bf16[128,1024]{1,0:T(8,128)(2,1)S(1)}, u32[]{:S(2)}, u32[]{:S(2)}) collective-permute-start(bf16[128,1024]{1,0:T(8,128)(2,1)S(1)} %get-tuple-element.78), channel_id=1, source_target_pairs={{0,8},{8,0},{16,24},{24,16},{1,9},{9,1},{17,25},{25,17},{2,10},{10... | collective-permute-start | bytes 786440 | tf_op jit(solution)/shard_map/ppermute | solution.py:439
  56.2 7.4 %collective-permute-start.23 = (bf16[128,512]{1,0:T(8,128)(2,1)S(1)}, bf16[128,512]{1,0:T(8,128)(2,1)S(1)}, u32[]{:S(2)}, u32[]{:S(2)}) collective-permute-start(bf16[128,512]{1,0:T(8,128)(2,1)S(1)} %chip_total_kernel.3), channel_id=1, source_target_pairs={{16,0},{24,8},{17,1},{25,9},{18,2},{26,10},{19,3},{27,11},{20,4},{... | collective-permute-start | bytes 393224 | tf_op jit(solution)/shard_map/ppermute | solution.py:564
  63.6 1.3 %collective-permute-start.24 = (bf16[128,512]{1,0:T(8,128)(2,1)S(1)}, bf16[128,512]{1,0:T(8,128)(2,1)S(1)}, u32[]{:S(2)}, u32[]{:S(2)}) collective-permute-start(bf16[128,512]{1,0:T(8,128)(2,1)S(1)} %collective-permute-done.23.refs_7_), channel_id=1, source_target_pairs={{0,8},{8,0},{16,24},{24,16},{1,9},{9,1},{17,25},{25,17},{2,10},{10... | collective-permute-start | bytes 393224 | tf_op jit(solution)/shard_map/ppermute | solution.py:439
  (4 other events, 9.4 us)

commit v6 on v5

--- a/solution.py
+++ b/solution.py
@@ -122,7 +122,7 @@
 def tables_kernel(
     ids_ref, rate_ref, resets_ref, skip_ref, x_ref, b_ref, step_ref, *refs
 ):
-    states, sent, (weighted_ref, rows_ref, cols_ref, table_ref) = refs[:2], refs[2:4], refs[4:]
+    states, sent, (weighted_ref, rows_ref, cols_ref, table_ref, from_ref, end_ref) = refs[:2], refs[2:4], refs[4:]
     heads = step_ref.shape[0]
     keep = (1 - resets_ref[0, 0]).astype(F32)
     head_id = lax.broadcasted_iota(jnp.int32, (heads, Q), 0)
@@ -143,7 +143,10 @@
         at = slice(pair * PAIR, (pair + 1) * PAIR)
         log_pair = spread(cols, pair, first)
         last = log_pair[Q - 1 : Q, :]
-        weighted_ref[:, at] = (x_ref[:, at].astype(F32) * jnp.exp(last - log_pair)).astype(BF)
+        to_end = jnp.exp(last - log_pair)
+        end_ref[:, at] = to_end
+        from_ref[:, at] = jnp.exp(log_pair)
+        weighted_ref[:, at] = (x_ref[:, at].astype(F32) * to_end).astype(BF)
         table_ref[THROUGH, at] = keep * jnp.exp(last)
         table_ref[SKIP, at] = gains(skip_ref, 2 * pair)
     ones = jnp.ones((1, table_ref.shape[1]), F32)
@@ -191,10 +194,8 @@
         out_ref[HALF:, at] = bottom
 
 
-def output_kernel(starts, table_ref, local_ref, c_ref, cols_ref, through_ref, before_ref, *refs):
+def output_kernel(starts, table_ref, local_ref, c_ref, from_ref, through_ref, before_ref, *refs):
     partners, outs, states = refs[:2], refs[2 : 2 + len(starts)], refs[2 + len(starts) :]
-    first = first_head()
-    cols = cols_ref[...]
     partner = jnp.concatenate([ref[...] for ref in partners], axis=1)
     for start, out_ref, state_ref in zip(starts, outs, states):
         part = slice(start, start + out_ref.shape[1])
@@ -206,8 +207,7 @@
             at = slice(pair * PAIR, (pair + 1) * PAIR)
             whole = slice(start + pair * PAIR, start + (pair + 1) * PAIR)
             term = dot(c_ref[...], state_ref[:, at], 1, 0)
-            decay = jnp.exp(spread(cols, start // PAIR + pair, first))
-            out_ref[:, at] = (local_ref[:, whole] + decay * term).astype(BF)
+            out_ref[:, at] = (local_ref[:, whole] + from_ref[:, whole] * term).astype(BF)
 
 
 def block_of(ids_ref, grad_ref, slot):
@@ -261,9 +261,7 @@
 
 
 def adjoint_kernel(others, table_ref, own_ref, *refs):
-    parts, (c_ref, cols_ref, head_ref, weighted_ref, *halves) = refs[:others], refs[others:]
-    first = first_head()
-    cols = cols_ref[...]
+    parts, (c_ref, from_ref, head_ref, weighted_ref, *halves) = refs[:others], refs[others:]
     for pair in range(head_ref.shape[1] // PAIR):
         at = slice(pair * PAIR, (pair + 1) * PAIR)
         total = own_ref[:, at]
@@ -271,7 +269,7 @@
             total = total + part[:, at].astype(F32)
         head = total.astype(BF)
         head_ref[:, at] = head
-        weighted_ref[:, at] = (head.astype(F32) * jnp.exp(spread(cols, pair, first))).astype(BF)
+        weighted_ref[:, at] = (head.astype(F32) * from_ref[:, at]).astype(BF)
     adjoint = table_ref[KEEP, :] * dot(c_ref[...], weighted_ref[...], 0, 0)
     middle = adjoint.shape[1] // 2
     for number in range(2):
@@ -356,11 +354,9 @@
     grad_c_ref[...] = c_part_ref[...] + dot(paired, b_ref[...], 0, 0)
 
 
-def final_kernel(table_ref, b_ref, cols_ref, sums_ref, weighted_ref, through_ref, local_ref, *refs):
+def final_kernel(table_ref, b_ref, end_ref, sums_ref, weighted_ref, through_ref, local_ref, *refs):
     entered, partner_ref, (in_ref, grad_b_ref, token_ref) = refs[:2], refs[2], refs[3:]
     token_ref[...] = jnp.zeros_like(token_ref)
-    first = first_head()
-    cols = cols_ref[...]
     grad_b = sums_ref[...]
     width = partner_ref.shape[1] // 2
     for half in range(2):
@@ -373,10 +369,8 @@
         for number in range(width // PAIR):
             pair = half * (width // PAIR) + number
             at = slice(pair * PAIR, (pair + 1) * PAIR)
-            log_pair = spread(cols, pair, first)
-            to_end = jnp.exp(log_pair[Q - 1 : Q, :] - log_pair)
             term = dot(b_ref[...], adjoint[:, number * PAIR : (number + 1) * PAIR], 1, 0)
-            in_ref[:, at] = (local_ref[:, at] + to_end * term).astype(BF)
+            in_ref[:, at] = (local_ref[:, at] + end_ref[:, at] * term).astype(BF)
     grad_b_ref[...] = grad_b
 
 
@@ -465,12 +459,13 @@
     for piece in near:
         pieces += [piece, plane_swap(piece)]
 
-    *both, weighted_in, log_rows, log_cols, through = call(
+    *both, weighted_in, log_rows, log_cols, through, from_start, to_end = call(
         tables_kernel,
         (ids, decay_rate, resets, skip_gain),
         (x, b_rows, steps),
         [((N, wide // 2), F32)] * 2 + [((N, wide // 2), BF)] * 2 + [((Q, wide), BF)]
-        + [((heads, Q), F32), ((Q, heads), F32), ((8, wide), F32)],
+        + [((heads, Q), F32), ((Q, heads), F32), ((8, wide), F32)]
+        + [((Q, wide), F32)] * 2,
         after=[weight_core, *[sent[0] for sent in to_send]],
     )
     local_output, = call(
@@ -498,7 +493,7 @@
     results = call(
         functools.partial(output_kernel, starts),
         (),
-        (through, local_output, c_rows, log_cols, through_partner, *before, *state_partner),
+        (through, local_output, c_rows, from_start, through_partner, *before, *state_partner),
         [((Q, width), BF) for width in widths] + [((N, width), BF) for width in widths],
         after=[partner],
     )
@@ -542,7 +537,7 @@
     head_grad, weighted_grad, *both = call(
         functools.partial(adjoint_kernel, chips - 1),
         (),
-        (through, partials[0], *returned, c_rows, log_cols),
+        (through, partials[0], *returned, c_rows, from_start),
         [((Q, wide), BF), ((Q, wide), BF)] + [((N, wide // 2), F32)] * 2 + [((N, wide), BF)],
         after=[sums[0], *sent],
     )
@@ -571,7 +566,7 @@
     grad_in, grad_b, token = call(
         final_kernel,
         (),
-        (through, b_rows, log_cols, grad_b, weighted_in, through_partner, local_in)
+        (through, b_rows, to_end, grad_b, weighted_in, through_partner, local_in)
         + (*entering, core_swap(later(entering[0], grad_c)), adjoint_partner),
         [((Q, wide), BF), ((Q, N), F32), ((8, 128), F32)],
     )

time: 68.4 us -> 67.8 us (level)
  Pallas kernels: 17 us -> 16 us
    pallas_call x14, Pallas kernels: 16.7 us -> 15.7 us  [call(): pl.pallas_call(run, grid=(1,), out_shape=[jax.ShapeDtypeStruct(shape, kin...]
  transfers between devices with their start and end apart: 26 -> 26, of which waited for: 14 -> 14; matrix products, arithmetic and copies ran while one was open for 0% -> 0% of each run, Pallas kernels for 22% -> 21%
where the time goes in v6:
time: 67.8 us; the launch traced here: 67.5 us
  waiting for transfers between devices  26.8 us (40%)
  starting transfers between devices  20.6 us (30%)
  Pallas kernels  16 us (24%)
  local copies, waits for them, and re-layouts  2.65 us (4%)
  between operations  1.56 us (2%)
    pallas_call x14, Pallas kernels, call(): pl.pallas_call(run, grid=(1,), out_shape=[jax.ShapeDtypeStruct(shape, kin...  15.7 us
    ppermute x4, waiting for transfers between devices, chip_shift(): lax.ppermute(value, 'seq', [(i, (i + 2 * by) % seq) for i in range(seq)])  9.55 us
    ppermute x3, starting transfers between devices, dialogue_swap(): return lax.ppermute(value, 'dp', [(0, 1), (1, 0)])  6 us
    ppermute x16, waiting for transfers between devices, core_swap(): return lax.ppermute(value, 'seq', across)  5.53 us
    ppermute x4, starting transfers between devices, chip_shift(): lax.ppermute(value, 'seq', [(i, (i + 2 * by) % seq) for i in range(seq)])  5.31 us
    ppermute x16, starting transfers between devices, core_swap(): return lax.ppermute(value, 'seq', across)  3.67 us
    ppermute x3, waiting for transfers between devices, dialogue_swap(): return lax.ppermute(value, 'dp', [(0, 1), (1, 0)])  3.2 us
    ppermute x1, waiting for transfers between devices, body(): entering = [lax.ppermute(total, 'seq', [(i, i - 2) for i in range(2, seq)])]  3.14 us
  transfers between devices with their start and end apart: 26, of which 14 were waited for; matrix products, arithmetic and copies ran while one was open for 0% of the time, Pallas kernels for 21%

profile of v6, /device:TPU:0, one launch (start us, length us, event | category | flops | bytes accessed | tf_op | source)
XLA Modules:
  0.0 67.5 jit_solution(5212411660609669890)
XLA Ops:
  0.7 0.5 collective-permute-start
  1.2 2.6 %collective-permute-start.8 = (bf16[512,1024]{1,0:T(8,128)(2,1)}, bf16[512,1024]{1,0:T(8,128)(2,1)S(1)}, u32[]{:S(2)}, u32[]{:S(2)}) collective-permute-start(bf16[512,1024]{1,0:T(8,128)(2,1)} %refs_6_.1), channel_id=1, source_target_pairs={{0,1},{1,0},{2,3},{3,2},{4,5},{5,4},{6,7},{7,6},{8,9},{9,8},{10,11... | collective-permute-start | bytes 3145736 | tf_op jit(solution)/shard_map/ppermute | solution.py:442
  3.8 1.6 %copy-done = bf16[1,256,4096]{2,1,0:T(8,128)(2,1)S(1)} copy-done((bf16[1,256,4096]{2,1,0:T(8,128)(2,1)S(1)}, bf16[1,256,4096]{2,1,0:T(8,128)(2,1)}, u32[]{:S(2)}) %copy-start) | copy-done | bytes 2097176
  5.5 1.6 %collective-permute-start.1 = (bf16[256,1024]{1,0:T(8,128)(2,1)S(1)}, bf16[256,1024]{1,0:T(8,128)(2,1)S(1)}, u32[]{:S(2)}, u32[]{:S(2)}) collective-permute-start(bf16[256,1024]{1,0:T(8,128)(2,1)S(1)} %send_kernel.1.refs_8_), channel_id=1, source_target_pairs={{0,16},{8,24},{16,0},{24,8},{1,17},{9,25},{17,1},{25,9},{2,18},{10... | collective-permute-start | bytes 1572872 | tf_op jit(solution)/shard_map/ppermute | solution.py:436
  7.8 0.8 %copy-done.4 = bf16[1,256,128]{2,1,0:T(8,128)(2,1)S(1)} copy-done((bf16[1,256,128]{2,1,0:T(8,128)(2,1)S(1)}, bf16[1,256,128]{2,1,0:T(8,128)(2,1)}, u32[]{:S(2)}) %copy-start.4) | copy-done | bytes 65560
  8.6 2.2 %tables_kernel.1 = (f32[128,512]{1,0:T(8,128)S(1)}, f32[128,512]{1,0:T(8,128)S(1)}, bf16[128,512]{1,0:T(8,128)(2,1)S(1)}, bf16[128,512]{1,0:T(8,128)(2,1)S(1)}, ...) custom-call(s32[1]{0:T(128)} %bitcast.ids_ref.refs_0_, ...), custom_call_target="tpu_custom_call" | custom-call | tf_op jit(solution)/shard_map/tables_kernel/pallas_call | solution.py:46
  11.7 1.4 %collective-permute-done.3.refs_1_.refs_4_.refs_5_ = f32[8,1024]{1,0:T(8,128)S(1)} collective-permute-done((f32[8,1024]{1,0:T(8,128)S(1)}, f32[8,1024]{1,0:T(8,128)S(1)}, u32[]{:S(2)}, u32[]{:S(2)}) %collective-permute-start.3) | collective-permute-done | bytes 32800 | tf_op jit(solution)/shard_map/ppermute | solution.py:433
  13.2 1.1 %local_output_kernel.1.refs_6_.refs_1_ = f32[256,1024]{1,0:T(8,128)S(1)} custom-call(f32[8,1024]{1,0:T(8,128)S(1)} %get-tuple-element.47.refs_1_.refs_0_, bf16[256,1024]{1,0:T(8,128)(2,1)S(1)} %bitcast.12, bf16[256,128]{1,0:T(8,128)(2,1)S(1)} %bitcast.20, bf16[256,128]{1,0:T(8,128)(2,1)S(1)} %bitcast.14, f32[16,256]{1,0:T(8,128)S(1)} %get-tuple-element.51.refs_4_.refs_5_, ...), custom_call_target="tpu_custom_call" | custom-call | tf_op jit(solution)/shard_map/local_output_kernel/pallas_call | solution.py:46
  14.5 2.5 %collective-permute-start.6 = (bf16[128,1024]{1,0:T(8,128)(2,1)S(1)}, bf16[128,1024]{1,0:T(8,128)(2,1)S(1)}, u32[]{:S(2)}, u32[]{:S(2)}) collective-permute-start(bf16[128,1024]{1,0:T(8,128)(2,1)S(1)} %chip_total_kernel.2), channel_id=1, source_target_pairs={{0,16},{8,24},{1,17},{9,25},{2,18},{10,26},{3,19},{11,27},{4,20},{... | collective-permute-start | bytes 786440 | tf_op jit(solution)/shard_map/ppermute | solution.py:492
  17.0 2.5 %collective-permute-done.1.refs_1_ = bf16[256,1024]{1,0:T(8,128)(2,1)S(1)} collective-permute-done((bf16[256,1024]{1,0:T(8,128)(2,1)S(1)}, bf16[256,1024]{1,0:T(8,128)(2,1)S(1)}, u32[]{:S(2)}, u32[]{:S(2)}) %collective-permute-start.1) | collective-permute-done | bytes 524320 | tf_op jit(solution)/shard_map/ppermute | solution.py:436
  19.5 1.6 %collective-permute-start.2 = (bf16[256,1024]{1,0:T(8,128)(2,1)S(1)}, bf16[256,1024]{1,0:T(8,128)(2,1)S(1)}, u32[]{:S(2)}, u32[]{:S(2)}) collective-permute-start(bf16[256,1024]{1,0:T(8,128)(2,1)S(1)} %collective-permute-done.1.refs_1_), channel_id=1, source_target_pairs={{0,2},{2,0},{4,6},{6,4},{1,3},{3,1},{5,7},{7,5},{8,10},{10,8},{12,... | collective-permute-start | bytes 1572872 | tf_op jit(solution)/shard_map/ppermute | solution.py:439
  21.1 3.1 %collective-permute-done.6.refs_5_ = bf16[128,1024]{1,0:T(8,128)(2,1)S(1)} collective-permute-done((bf16[128,1024]{1,0:T(8,128)(2,1)S(1)}, bf16[128,1024]{1,0:T(8,128)(2,1)S(1)}, u32[]{:S(2)}, u32[]{:S(2)}) %collective-permute-start.6) | collective-permute-done | bytes 262176 | tf_op jit(solution)/shard_map/ppermute | solution.py:492
  24.5 3.2 %collective-permute-done.8.refs_7_ = bf16[512,1024]{1,0:T(8,128)(2,1)S(1)} collective-permute-done((bf16[512,1024]{1,0:T(8,128)(2,1)}, bf16[512,1024]{1,0:T(8,128)(2,1)S(1)}, u32[]{:S(2)}, u32[]{:S(2)}) %collective-permute-start.8) | collective-permute-done | bytes 1048608 | tf_op jit(solution)/shard_map/ppermute | solution.py:442
  28.4 1.7 %collective-permute-start.14 = (bf16[256,384]{1,0:T(8,128)(2,1)S(1)}, bf16[256,384]{1,0:T(8,128)(2,1)S(1)}, u32[]{:S(2)}, u32[]{:S(2)}) collective-permute-start(bf16[256,384]{1,0:T(8,128)(2,1)S(1)} %get-tuple-element.66.refs_6_), channel_id=1, source_target_pairs={{0,16},{8,24},{16,0},{24,8},{1,17},{9,25},{17,1},{25,9},{2,18},{10... | collective-permute-start | bytes 589832 | tf_op jit(solution)/shard_map/ppermute | solution.py:436
  30.4 2.3 %collective-permute-done.2.refs_2_ = bf16[256,1024]{1,0:T(8,128)(2,1)S(1)} collective-permute-done((bf16[256,1024]{1,0:T(8,128)(2,1)S(1)}, bf16[256,1024]{1,0:T(8,128)(2,1)S(1)}, u32[]{:S(2)}, u32[]{:S(2)}) %collective-permute-start.2) | collective-permute-done | bytes 524320 | tf_op jit(solution)/shard_map/ppermute | solution.py:439
  33.5 2.3 %head_partial_kernel.1 = (f32[256,1024]{1,0:T(8,128)S(1)}, bf16[256,1024]{1,0:T(8,128)(2,1)S(1)}) custom-call(bf16[256,1024]{1,0:T(8,128)(2,1)S(1)} %get-tuple-element.49.refs_0_, bf16[256,1024]{1,0:T(8,128)(2,1)S(1)} %get-tuple-element.50.refs_1_, bf16[256,512]{1,0:T(8,128)(2,1)S(1)} %get-tuple-element.59.refs_2_, ...), custom_call_target="tpu_custom_call" | custom-call | tf_op jit(solution)/shard_map/head_partial_kernel/pallas_call | solution.py:46
  36.7 1.7 %collective-permute-start.11 = (bf16[256,1024]{1,0:T(8,128)(2,1)S(1)}, bf16[256,1024]{1,0:T(8,128)(2,1)S(1)}, u32[]{:S(2)}, u32[]{:S(2)}) collective-permute-start(bf16[256,1024]{1,0:T(8,128)(2,1)S(1)} %get-tuple-element.65), channel_id=1, source_target_pairs={{0,16},{8,24},{16,0},{24,8},{1,17},{9,25},{17,1},{25,9},{2,18},{10... | collective-permute-start | bytes 1572872 | tf_op jit(solution)/shard_map/ppermute | solution.py:436
  38.4 1.3 %weight_partial_kernel.2 = (f32[512,384]{1,0:T(8,128)S(1)}, bf16[512,384]{1,0:T(8,128)(2,1)S(1)}) custom-call(bf16[256,1024]{1,0:T(8,128)(2,1)S(1)} %get-tuple-element.49.refs_0_, bf16[256,1024]{1,0:T(8,128)(2,1)S(1)} %collective-permute-done.7.refs_8_.refs_1_, bf16[256,512]{1,0:T(8,128)(2,1)S(1)} %get-tuple-element.59.refs_2_, ...), custom_call_target="tpu_custom_call" | custom-call | tf_op jit(solution)/shard_map/weight_partial_kernel/pallas_call | solution.py:46
  39.7 1.6 %collective-permute-start.17 = (bf16[512,384]{1,0:T(8,128)(2,1)S(1)}, bf16[512,384]{1,0:T(8,128)(2,1)S(1)}, u32[]{:S(2)}, u32[]{:S(2)}) collective-permute-start(bf16[512,384]{1,0:T(8,128)(2,1)S(1)} %get-tuple-element.68.refs_12_.refs_6_), channel_id=1, source_target_pairs={{0,1},{1,0},{2,3},{3,2},{4,5},{5,4},{6,7},{7,6},{8,9},{9,8},{10,11... | collective-permute-start | bytes 1179656 | tf_op jit(solution)/shard_map/ppermute | solution.py:442
  41.3 1.9 %collective-permute-done.18.refs_7_ = bf16[256,640]{1,0:T(8,128)(2,1)S(1)} collective-permute-done((bf16[256,640]{1,0:T(8,128)(2,1)S(1)}, bf16[256,640]{1,0:T(8,128)(2,1)S(1)}, u32[]{:S(2)}, u32[]{:S(2)}) %collective-permute-start.18) | collective-permute-done | bytes 327712 | tf_op jit(solution)/shard_map/ppermute | solution.py:436
  43.9 0.9 %collective-permute-done.20.refs_9_ = bf16[256,320]{1,0:T(8,128)(2,1)S(1)} collective-permute-done((bf16[256,320]{1,0:T(8,128)(2,1)S(1)}, bf16[256,320]{1,0:T(8,128)(2,1)S(1)}, u32[]{:S(2)}, u32[]{:S(2)}) %collective-permute-start.20) | collective-permute-done | bytes 163872 | tf_op jit(solution)/shard_map/ppermute | solution.py:433
  45.1 1.8 %weight_partial_kernel.3 = (f32[512,640]{1,0:T(8,128)S(1)}, bf16[512,640]{1,0:T(8,128)(2,1)S(1)}) custom-call(bf16[256,1024]{1,0:T(8,128)(2,1)S(1)} %get-tuple-element.49.refs_0_, bf16[256,1024]{1,0:T(8,128)(2,1)S(1)} %collective-permute-done.7.refs_8_.refs_1_, bf16[256,512]{1,0:T(8,128)(2,1)S(1)} %get-tuple-element.59.refs_2_, ...), custom_call_target="tpu_custom_call" | custom-call | tf_op jit(solution)/shard_map/weight_partial_kernel/pallas_call | solution.py:46
  46.9 1.8 %collective-permute-start.25 = (bf16[512,640]{1,0:T(8,128)(2,1)S(1)}, bf16[512,640]{1,0:T(8,128)(2,1)S(1)}, u32[]{:S(2)}, u32[]{:S(2)}) collective-permute-start(bf16[512,640]{1,0:T(8,128)(2,1)S(1)} %get-tuple-element.70.refs_7_), channel_id=1, source_target_pairs={{0,1},{1,0},{2,3},{3,2},{4,5},{5,4},{6,7},{7,6},{8,9},{9,8},{10,11... | collective-permute-start | bytes 1966088 | tf_op jit(solution)/shard_map/ppermute | solution.py:442
  48.8 4.8 %collective-permute-done.11.refs_2_ = bf16[256,1024]{1,0:T(8,128)(2,1)S(1)} collective-permute-done((bf16[256,1024]{1,0:T(8,128)(2,1)S(1)}, bf16[256,1024]{1,0:T(8,128)(2,1)S(1)}, u32[]{:S(2)}, u32[]{:S(2)}) %collective-permute-start.11) | collective-permute-done | bytes 524320 | tf_op jit(solution)/shard_map/ppermute | solution.py:436
  54.1 1.5 %collective-permute-done.22.refs_4_.refs_9_ = bf16[128,1024]{1,0:T(8,128)(2,1)S(1)} collective-permute-done((bf16[128,1024]{1,0:T(8,128)(2,1)S(1)}, bf16[128,1024]{1,0:T(8,128)(2,1)S(1)}, u32[]{:S(2)}, u32[]{:S(2)}) %collective-permute-start.22) | collective-permute-done | bytes 262176 | tf_op jit(solution)/shard_map/ppermute | solution.py:433
  55.7 1.5 %collective-permute-start.23 = (bf16[128,512]{1,0:T(8,128)(2,1)S(1)}, bf16[128,512]{1,0:T(8,128)(2,1)S(1)}, u32[]{:S(2)}, u32[]{:S(2)}) collective-permute-start(bf16[128,512]{1,0:T(8,128)(2,1)S(1)} %chip_total_kernel.3), channel_id=1, source_target_pairs={{16,0},{24,8},{17,1},{25,9},{18,2},{26,10},{19,3},{27,11},{20,4},{... | collective-permute-start | bytes 393224 | tf_op jit(solution)/shard_map/ppermute | solution.py:559
  57.2 1.9 %local_grads_kernel.1 = (f32[256,1024]{1,0:T(8,128)S(1)}, f32[256,256]{1,0:T(8,128)S(1)}, f32[256,128]{1,0:T(8,128)S(1)}) custom-call(f32[8,1024]{1,0:T(8,128)S(1)} %get-tuple-element.47.refs_1_.refs_0_, bf16[256,1024]{1,0:T(8,128)(2,1)S(1)} %bitcast.13, bf16[256,1024]{1,0:T(8,128)(2,1)S(1)} %get-tuple-element.71.refs_2_, bf16[256,128]{1,0:T(8,128)(2,1)S(1)} %bitcast.21, ...), custom_call_target="tpu_custom_call" | custom-call | tf_op jit(solution)/shard_map/local_grads_kernel/pallas_call | solution.py:46
  59.1 0.9 %group_sums_kernel.1 = (f32[256,128]{1,0:T(8,128)S(1)}, f32[256,128]{1,0:T(8,128)}) custom-call(bf16[256,128]{1,0:T(8,128)(2,1)S(1)} %bitcast.22, bf16[256,128]{1,0:T(8,128)(2,1)S(1)} %bitcast.18, f32[256,256]{1,0:T(8,128)S(1)} %get-tuple-element.75.refs_2_, f32[256,128]{1,0:T(8,128)S(1)} %get-tuple-element.76.refs_3_), custom_call_target="tpu_custom_call" | custom-call | tf_op jit(solution)/shard_map/group_sums_kernel/pallas_call | solution.py:46
  60.0 3.1 %collective-permute-done.23.refs_7_ = bf16[128,512]{1,0:T(8,128)(2,1)S(1)} collective-permute-done((bf16[128,512]{1,0:T(8,128)(2,1)S(1)}, bf16[128,512]{1,0:T(8,128)(2,1)S(1)}, u32[]{:S(2)}, u32[]{:S(2)}) %collective-permute-start.23) | collective-permute-done | bytes 131104 | tf_op jit(solution)/shard_map/ppermute | solution.py:559
  63.2 1.3 %collective-permute-done.24.refs_8_ = bf16[128,512]{1,0:T(8,128)(2,1)S(1)} collective-permute-done((bf16[128,512]{1,0:T(8,128)(2,1)S(1)}, bf16[128,512]{1,0:T(8,128)(2,1)S(1)}, u32[]{:S(2)}, u32[]{:S(2)}) %collective-permute-start.24) | collective-permute-done | bytes 131104 | tf_op jit(solution)/shard_map/ppermute | solution.py:433
  64.5 1.3 %final_kernel.1 = (bf16[256,1024]{1,0:T(8,128)(2,1)}, f32[256,128]{1,0:T(8,128)}, f32[8,128]{1,0:T(8,128)S(1)}) custom-call(f32[8,1024]{1,0:T(8,128)S(1)} %get-tuple-element.47.refs_1_.refs_0_, bf16[256,128]{1,0:T(8,128)(2,1)S(1)} %bitcast.23, f32[256,1024]{1,0:T(8,128)S(1)} %get-tuple-element.48.refs_2_, f32[256,128]{1,0:T(8,128)S(1)} %get-tuple-element.77.refs_3_, ...), custom_call_target="tpu_custom_call" | custom-call | tf_op jit(solution)/shard_map/final_kernel/pallas_call | solution.py:46
  65.8 1.7 %add_kernel.1 = f32[512,1024]{1,0:T(8,128)} custom-call(f32[512,384]{1,0:T(8,128)S(1)} %get-tuple-element.87.refs_0_, f32[512,640]{1,0:T(8,128)S(1)} %get-tuple-element.88.refs_1_, bf16[512,384]{1,0:T(8,128)(2,1)S(1)} %collective-permute-done.17.refs_5_.refs_2_, bf16[512,640]{1,0:T(8,128)(2,1)S(1)} %collective-permute-done.25.refs_3_, ...), custom_call_target="tpu_custom_call" | custom-call | tf_op jit(solution)/shard_map/add_kernel/pallas_call | solution.py:46
  (58 shorter events, 5.8 us)
Async XLA Ops:
  0.6 7.1 %copy-start.7 = (f32[1,16,256]{2,1,0:T(8,128)S(1)}, f32[1,16,256]{2,1,0:T(8,128)}, u32[]{:S(2)}) copy-start(f32[1,16,256]{2,1,0:T(8,128)} %param.12) | copy-start | bytes 49156
  0.6 7.1 %copy-start.8 = (f32[16]{0:T(128)S(1)}, f32[16]{0:T(128)}, u32[]{:S(2)}) copy-start(f32[16]{0:T(128)} %refs_1_.1) | copy-start | bytes 196
  0.7 7.1 %copy-start.9 = (f32[16]{0:T(128)S(1)}, f32[16]{0:T(128)}, u32[]{:S(2)}) copy-start(f32[16]{0:T(128)} %refs_3_.1) | copy-start | bytes 196
  0.7 7.0 %collective-permute-start = (bf16[512,1024]{1,0:T(8,128)(2,1)}, bf16[512,1024]{1,0:T(8,128)(2,1)S(1)}, u32[]{:S(2)}, u32[]{:S(2)}) collective-permute-start(bf16[512,1024]{1,0:T(8,128)(2,1)} %refs_6_.1), channel_id=1, source_target_pairs={{0,8},{8,0},{16,24},{24,16},{1,9},{9,1},{17,25},{25,17},{2,10},{10... | collective-permute-start | bytes 3145736 | tf_op jit(solution)/shard_map/ppermute | solution.py:433
  1.2 26.6 %collective-permute-start.8 = (bf16[512,1024]{1,0:T(8,128)(2,1)}, bf16[512,1024]{1,0:T(8,128)(2,1)S(1)}, u32[]{:S(2)}, u32[]{:S(2)}) collective-permute-start(bf16[512,1024]{1,0:T(8,128)(2,1)} %refs_6_.1), channel_id=1, source_target_pairs={{0,1},{1,0},{2,3},{3,2},{4,5},{5,4},{6,7},{7,6},{8,9},{9,8},{10,11... | collective-permute-start | bytes 3145736 | tf_op jit(solution)/shard_map/ppermute | solution.py:442
  5.4 5.5 %copy-start.1 = (bf16[1,256,4096]{2,1,0:T(8,128)(2,1)S(1)}, bf16[1,256,4096]{2,1,0:T(8,128)(2,1)}, u32[]{:S(2)}) copy-start(bf16[1,256,4096]{2,1,0:T(8,128)(2,1)} %param.16) | copy-start | bytes 6291460
  5.5 14.1 %collective-permute-start.1 = (bf16[256,1024]{1,0:T(8,128)(2,1)S(1)}, bf16[256,1024]{1,0:T(8,128)(2,1)S(1)}, u32[]{:S(2)}, u32[]{:S(2)}) collective-permute-start(bf16[256,1024]{1,0:T(8,128)(2,1)S(1)} %send_kernel.1.refs_8_), channel_id=1, source_target_pairs={{0,16},{8,24},{16,0},{24,8},{1,17},{9,25},{17,1},{25,9},{2,18},{10... | collective-permute-start | bytes 1572872 | tf_op jit(solution)/shard_map/ppermute | solution.py:436
  11.0 13.2 %collective-permute-start.7 = (bf16[256,1024]{1,0:T(8,128)(2,1)S(1)}, bf16[256,1024]{1,0:T(8,128)(2,1)S(1)}, u32[]{:S(2)}, u32[]{:S(2)}) collective-permute-start(bf16[256,1024]{1,0:T(8,128)(2,1)S(1)} %get-tuple-element.50.refs_1_), channel_id=1, source_target_pairs={{0,8},{8,0},{16,24},{24,16},{1,9},{9,1},{17,25},{25,17},{2,10},{10... | collective-permute-start | bytes 1572872 | tf_op jit(solution)/shard_map/ppermute | solution.py:433
  11.1 1.9 %collective-permute-start.3 = (f32[8,1024]{1,0:T(8,128)S(1)}, f32[8,1024]{1,0:T(8,128)S(1)}, u32[]{:S(2)}, u32[]{:S(2)}) collective-permute-start(f32[8,1024]{1,0:T(8,128)S(1)} %get-tuple-element.47.refs_1_.refs_0_), channel_id=1, source_target_pairs={{0,8},{8,0},{16,24},{24,16},{1,9},{9,1},{17,25},{25,17},{2,10},{10... | collective-permute-start | bytes 98312 | tf_op jit(solution)/shard_map/ppermute | solution.py:433
  11.6 2.7 %collective-permute-start.4 = (bf16[128,512]{1,0:T(8,128)(2,1)S(1)}, bf16[128,512]{1,0:T(8,128)(2,1)S(1)}, u32[]{:S(2)}, u32[]{:S(2)}) collective-permute-start(bf16[128,512]{1,0:T(8,128)(2,1)S(1)} %get-tuple-element.56), channel_id=1, source_target_pairs={{0,8},{8,0},{16,24},{24,16},{1,9},{9,1},{17,25},{25,17},{2,10},{10... | collective-permute-start | bytes 393224 | tf_op jit(solution)/shard_map/ppermute | solution.py:433
  13.0 1.3 %collective-permute-start.5 = (bf16[128,512]{1,0:T(8,128)(2,1)S(1)}, bf16[128,512]{1,0:T(8,128)(2,1)S(1)}, u32[]{:S(2)}, u32[]{:S(2)}) collective-permute-start(bf16[128,512]{1,0:T(8,128)(2,1)S(1)} %get-tuple-element.57), channel_id=1, source_target_pairs={{0,8},{8,0},{16,24},{24,16},{1,9},{9,1},{17,25},{25,17},{2,10},{10... | collective-permute-start | bytes 393224 | tf_op jit(solution)/shard_map/ppermute | solution.py:433
  14.5 9.7 %collective-permute-start.6 = (bf16[128,1024]{1,0:T(8,128)(2,1)S(1)}, bf16[128,1024]{1,0:T(8,128)(2,1)S(1)}, u32[]{:S(2)}, u32[]{:S(2)}) collective-permute-start(bf16[128,1024]{1,0:T(8,128)(2,1)S(1)} %chip_total_kernel.2), channel_id=1, source_target_pairs={{0,16},{8,24},{1,17},{9,25},{2,18},{10,26},{3,19},{11,27},{4,20},{... | collective-permute-start | bytes 786440 | tf_op jit(solution)/shard_map/ppermute | solution.py:492
  19.5 13.2 %collective-permute-start.2 = (bf16[256,1024]{1,0:T(8,128)(2,1)S(1)}, bf16[256,1024]{1,0:T(8,128)(2,1)S(1)}, u32[]{:S(2)}, u32[]{:S(2)}) collective-permute-start(bf16[256,1024]{1,0:T(8,128)(2,1)S(1)} %collective-permute-done.1.refs_1_), channel_id=1, source_target_pairs={{0,2},{2,0},{4,6},{6,4},{1,3},{3,1},{5,7},{7,5},{8,10},{10,8},{12,... | collective-permute-start | bytes 1572872 | tf_op jit(solution)/shard_map/ppermute | solution.py:439
  24.5 8.9 %copy-start.6 = (bf16[512,1024]{1,0:T(8,128)(2,1)S(1)}, bf16[512,1024]{1,0:T(8,128)(2,1)}, u32[]{:S(2)}) copy-start(bf16[512,1024]{1,0:T(8,128)(2,1)} %refs_6_.1) | copy-start | bytes 3145732
  27.8 5.1 %collective-permute-start.10 = (bf16[256,1024]{1,0:T(8,128)(2,1)S(1)}, bf16[256,1024]{1,0:T(8,128)(2,1)S(1)}, u32[]{:S(2)}, u32[]{:S(2)}) collective-permute-start(bf16[256,1024]{1,0:T(8,128)(2,1)S(1)} %get-tuple-element.90), channel_id=1, source_target_pairs={{0,8},{8,0},{16,24},{24,16},{1,9},{9,1},{17,25},{25,17},{2,10},{10... | collective-permute-start | bytes 1572872 | tf_op jit(solution)/shard_map/ppermute | solution.py:433
  27.9 5.5 %collective-permute-start.9 = (bf16[256,1024]{1,0:T(8,128)(2,1)S(1)}, bf16[256,1024]{1,0:T(8,128)(2,1)S(1)}, u32[]{:S(2)}, u32[]{:S(2)}) collective-permute-start(bf16[256,1024]{1,0:T(8,128)(2,1)S(1)} %get-tuple-element.91), channel_id=1, source_target_pairs={{0,8},{8,0},{16,24},{24,16},{1,9},{9,1},{17,25},{25,17},{2,10},{10... | collective-permute-start | bytes 1572872 | tf_op jit(solution)/shard_map/ppermute | solution.py:433
  28.4 7.8 %collective-permute-start.14 = (bf16[256,384]{1,0:T(8,128)(2,1)S(1)}, bf16[256,384]{1,0:T(8,128)(2,1)S(1)}, u32[]{:S(2)}, u32[]{:S(2)}) collective-permute-start(bf16[256,384]{1,0:T(8,128)(2,1)S(1)} %get-tuple-element.66.refs_6_), channel_id=1, source_target_pairs={{0,16},{8,24},{16,0},{24,8},{1,17},{9,25},{17,1},{25,9},{2,18},{10... | collective-permute-start | bytes 589832 | tf_op jit(solution)/shard_map/ppermute | solution.py:436
  30.1 13.1 %collective-permute-start.18 = (bf16[256,640]{1,0:T(8,128)(2,1)S(1)}, bf16[256,640]{1,0:T(8,128)(2,1)S(1)}, u32[]{:S(2)}, u32[]{:S(2)}) collective-permute-start(bf16[256,640]{1,0:T(8,128)(2,1)S(1)} %get-tuple-element.58.refs_3_.refs_6_), channel_id=1, source_target_pairs={{0,16},{8,24},{16,0},{24,8},{1,17},{9,25},{17,1},{25,9},{2,18},{10... | collective-permute-start | bytes 983048 | tf_op jit(solution)/shard_map/ppermute | solution.py:436
  32.8 3.9 %collective-permute-start.12 = (bf16[256,512]{1,0:T(8,128)(2,1)S(1)}, bf16[256,512]{1,0:T(8,128)(2,1)S(1)}, u32[]{:S(2)}, u32[]{:S(2)}) collective-permute-start(bf16[256,512]{1,0:T(8,128)(2,1)S(1)} %get-tuple-element.61.refs_4_), channel_id=1, source_target_pairs={{0,8},{8,0},{16,24},{24,16},{1,9},{9,1},{17,25},{25,17},{2,10},{10... | collective-permute-start | bytes 786440 | tf_op jit(solution)/shard_map/ppermute | solution.py:433
  32.9 5.5 %collective-permute-start.13 = (bf16[256,512]{1,0:T(8,128)(2,1)S(1)}, bf16[256,512]{1,0:T(8,128)(2,1)S(1)}, u32[]{:S(2)}, u32[]{:S(2)}) collective-permute-start(bf16[256,512]{1,0:T(8,128)(2,1)S(1)} %get-tuple-element.62.refs_5_), channel_id=1, source_target_pairs={{0,8},{8,0},{16,24},{24,16},{1,9},{9,1},{17,25},{25,17},{2,10},{10... | collective-permute-start | bytes 786440 | tf_op jit(solution)/shard_map/ppermute | solution.py:433
  33.4 2.9 %collective-permute-start.15 = (bf16[256,384]{1,0:T(8,128)(2,1)S(1)}, bf16[256,384]{1,0:T(8,128)(2,1)S(1)}, u32[]{:S(2)}, u32[]{:S(2)}) collective-permute-start(bf16[256,384]{1,0:T(8,128)(2,1)S(1)} %get-tuple-element.66.refs_6_), channel_id=1, source_target_pairs={{0,8},{8,0},{16,24},{24,16},{1,9},{9,1},{17,25},{25,17},{2,10},{10... | collective-permute-start | bytes 589832 | tf_op jit(solution)/shard_map/ppermute | solution.py:433
  36.1 2.3 %collective-permute-start.16 = (bf16[256,384]{1,0:T(8,128)(2,1)S(1)}, bf16[256,384]{1,0:T(8,128)(2,1)S(1)}, u32[]{:S(2)}, u32[]{:S(2)}) collective-permute-start(bf16[256,384]{1,0:T(8,128)(2,1)S(1)} %collective-permute-done.14.refs_7_), channel_id=1, source_target_pairs={{0,8},{8,0},{16,24},{24,16},{1,9},{9,1},{17,25},{25,17},{2,10},{10... | collective-permute-start | bytes 589832 | tf_op jit(solution)/shard_map/ppermute | solution.py:433
  36.3 7.6 %collective-permute-start.19 = (bf16[256,640]{1,0:T(8,128)(2,1)S(1)}, bf16[256,640]{1,0:T(8,128)(2,1)S(1)}, u32[]{:S(2)}, u32[]{:S(2)}) collective-permute-start(bf16[256,640]{1,0:T(8,128)(2,1)S(1)} %get-tuple-element.58.refs_3_.refs_6_), channel_id=1, source_target_pairs={{0,8},{8,0},{16,24},{24,16},{1,9},{9,1},{17,25},{25,17},{2,10},{10... | collective-permute-start | bytes 983048 | tf_op jit(solution)/shard_map/ppermute | solution.py:433
  36.7 16.9 %collective-permute-start.11 = (bf16[256,1024]{1,0:T(8,128)(2,1)S(1)}, bf16[256,1024]{1,0:T(8,128)(2,1)S(1)}, u32[]{:S(2)}, u32[]{:S(2)}) collective-permute-start(bf16[256,1024]{1,0:T(8,128)(2,1)S(1)} %get-tuple-element.65), channel_id=1, source_target_pairs={{0,16},{8,24},{16,0},{24,8},{1,17},{9,25},{17,1},{25,9},{2,18},{10... | collective-permute-start | bytes 1572872 | tf_op jit(solution)/shard_map/ppermute | solution.py:436
  39.7 13.9 %collective-permute-start.17 = (bf16[512,384]{1,0:T(8,128)(2,1)S(1)}, bf16[512,384]{1,0:T(8,128)(2,1)S(1)}, u32[]{:S(2)}, u32[]{:S(2)}) collective-permute-start(bf16[512,384]{1,0:T(8,128)(2,1)S(1)} %get-tuple-element.68.refs_12_.refs_6_), channel_id=1, source_target_pairs={{0,1},{1,0},{2,3},{3,2},{4,5},{5,4},{6,7},{7,6},{8,9},{9,8},{10,11... | collective-permute-start | bytes 1179656 | tf_op jit(solution)/shard_map/ppermute | solution.py:442
  43.3 1.5 %collective-permute-start.20 = (bf16[256,320]{1,0:T(8,128)(2,1)S(1)}, bf16[256,320]{1,0:T(8,128)(2,1)S(1)}, u32[]{:S(2)}, u32[]{:S(2)}) collective-permute-start(bf16[256,320]{1,0:T(8,128)(2,1)S(1)} %get-tuple-element.93), channel_id=1, source_target_pairs={{0,8},{8,0},{16,24},{24,16},{1,9},{9,1},{17,25},{25,17},{2,10},{10... | collective-permute-start | bytes 491528 | tf_op jit(solution)/shard_map/ppermute | solution.py:433
  43.4 1.7 %collective-permute-start.21 = (bf16[256,320]{1,0:T(8,128)(2,1)S(1)}, bf16[256,320]{1,0:T(8,128)(2,1)S(1)}, u32[]{:S(2)}, u32[]{:S(2)}) collective-permute-start(bf16[256,320]{1,0:T(8,128)(2,1)S(1)} %get-tuple-element.92), channel_id=1, source_target_pairs={{0,8},{8,0},{16,24},{24,16},{1,9},{9,1},{17,25},{25,17},{2,10},{10... | collective-permute-start | bytes 491528 | tf_op jit(solution)/shard_map/ppermute | solution.py:433
  46.9 10.3 %copy-start.5 = (bf16[1,256,128]{2,1,0:T(8,128)(2,1)S(1)}, bf16[1,256,128]{2,1,0:T(8,128)(2,1)}, u32[]{:S(2)}) copy-start(bf16[1,256,128]{2,1,0:T(8,128)(2,1)} %param.10) | copy-start | bytes 196612
  46.9 18.9 %collective-permute-start.25 = (bf16[512,640]{1,0:T(8,128)(2,1)S(1)}, bf16[512,640]{1,0:T(8,128)(2,1)S(1)}, u32[]{:S(2)}, u32[]{:S(2)}) collective-permute-start(bf16[512,640]{1,0:T(8,128)(2,1)S(1)} %get-tuple-element.70.refs_7_), channel_id=1, source_target_pairs={{0,1},{1,0},{2,3},{3,2},{4,5},{5,4},{6,7},{7,6},{8,9},{9,8},{10,11... | collective-permute-start | bytes 1966088 | tf_op jit(solution)/shard_map/ppermute | solution.py:442
  54.0 1.6 %collective-permute-start.22 = (bf16[128,1024]{1,0:T(8,128)(2,1)S(1)}, bf16[128,1024]{1,0:T(8,128)(2,1)S(1)}, u32[]{:S(2)}, u32[]{:S(2)}) collective-permute-start(bf16[128,1024]{1,0:T(8,128)(2,1)S(1)} %get-tuple-element.82), channel_id=1, source_target_pairs={{0,8},{8,0},{16,24},{24,16},{1,9},{9,1},{17,25},{25,17},{2,10},{10... | collective-permute-start | bytes 786440 | tf_op jit(solution)/shard_map/ppermute | solution.py:433
  55.7 7.4 %collective-permute-start.23 = (bf16[128,512]{1,0:T(8,128)(2,1)S(1)}, bf16[128,512]{1,0:T(8,128)(2,1)S(1)}, u32[]{:S(2)}, u32[]{:S(2)}) collective-permute-start(bf16[128,512]{1,0:T(8,128)(2,1)S(1)} %chip_total_kernel.3), channel_id=1, source_target_pairs={{16,0},{24,8},{17,1},{25,9},{18,2},{26,10},{19,3},{27,11},{20,4},{... | collective-permute-start | bytes 393224 | tf_op jit(solution)/shard_map/ppermute | solution.py:559
  63.2 1.3 %collective-permute-start.24 = (bf16[128,512]{1,0:T(8,128)(2,1)S(1)}, bf16[128,512]{1,0:T(8,128)(2,1)S(1)}, u32[]{:S(2)}, u32[]{:S(2)}) collective-permute-start(bf16[128,512]{1,0:T(8,128)(2,1)S(1)} %collective-permute-done.23.refs_7_), channel_id=1, source_target_pairs={{0,8},{8,0},{16,24},{24,16},{1,9},{9,1},{17,25},{25,17},{2,10},{10... | collective-permute-start | bytes 393224 | tf_op jit(solution)/shard_map/ppermute | solution.py:433
  (4 other events, 9.4 us)

commit v7 on v6

--- a/solution.py
+++ b/solution.py
@@ -570,13 +570,17 @@
         + (*entering, core_swap(later(entering[0], grad_c)), adjoint_partner),
         [((Q, wide), BF), ((Q, N), F32), ((8, 128), F32)],
     )
-    grad_weight, = call(
-        functools.partial(add_kernel, len(widths)),
-        (),
-        (*kept, *sums),
-        [((depth, wide), F32)],
-        after=[token],
-    )
+    step = depth // 2
+    grad_weight = pl.pallas_call(
+        lambda *refs: add_kernel(len(widths), *refs[:-2], refs[-1]),
+        grid=(depth // step,),
+        out_shape=jax.ShapeDtypeStruct((depth, wide), F32),
+        in_specs=[pl.BlockSpec((step, item.shape[1]), lambda i: (i, 0)) for item in (*kept, *sums)] + [ANY],
+        out_specs=pl.BlockSpec((step, wide), lambda i: (i, 0)),
+        cost_estimate=FREE,
+        compiler_params=LIMIT,
+        name="add_kernel",
+    )(*kept, *sums, token)
     return grad_in[None], grad_b[None], grad_c[None], grad_weight
 
 

time: 67.8 us -> 67.5 us (level)
    pallas_call x14 -> x13, Pallas kernels: 15.7 us -> 14 us  [call(): pl.pallas_call(run, grid=(1,), out_shape=[jax.ShapeDtypeStruct(shape, kin...]
    pallas_call x0 -> x1, Pallas kernels: none -> 1.47 us  [body(): pl.pallas_call(lambda *refs: add_kernel(len(widths), *refs[:-2], refs[-1]...]
where the time goes in v7:
time: 67.5 us; the launch traced here: 67.3 us
  waiting for transfers between devices  26.8 us (40%)
  starting transfers between devices  20.6 us (31%)
  Pallas kernels  15.7 us (23%)
  local copies, waits for them, and re-layouts  2.65 us (4%)
  between operations  1.56 us (2%)
    pallas_call x13, Pallas kernels, call(): pl.pallas_call(run, grid=(1,), out_shape=[jax.ShapeDtypeStruct(shape, kin...  14 us
    ppermute x4, waiting for transfers between devices, chip_shift(): lax.ppermute(value, 'seq', [(i, (i + 2 * by) % seq) for i in range(seq)])  9.55 us
    ppermute x3, starting transfers between devices, dialogue_swap(): return lax.ppermute(value, 'dp', [(0, 1), (1, 0)])  6 us
    ppermute x16, waiting for transfers between devices, core_swap(): return lax.ppermute(value, 'seq', across)  5.53 us
    ppermute x4, starting transfers between devices, chip_shift(): lax.ppermute(value, 'seq', [(i, (i + 2 * by) % seq) for i in range(seq)])  5.31 us
    ppermute x16, starting transfers between devices, core_swap(): return lax.ppermute(value, 'seq', across)  3.67 us
    ppermute x3, waiting for transfers between devices, dialogue_swap(): return lax.ppermute(value, 'dp', [(0, 1), (1, 0)])  3.2 us
    ppermute x1, waiting for transfers between devices, body(): entering = [lax.ppermute(total, 'seq', [(i, i - 2) for i in range(2, seq)])]  3.14 us
  transfers between devices with their start and end apart: 26, of which 14 were waited for; matrix products, arithmetic and copies ran while one was open for 0% of the time, Pallas kernels for 21%

profile of v7, /device:TPU:0, one launch (start us, length us, event | category | flops | bytes accessed | tf_op | source)
XLA Modules:
  0.0 67.3 jit_solution(15102456588079867189)
XLA Ops:
  0.7 0.5 collective-permute-start
  1.2 2.6 %collective-permute-start.8 = (bf16[512,1024]{1,0:T(8,128)(2,1)}, bf16[512,1024]{1,0:T(8,128)(2,1)S(1)}, u32[]{:S(2)}, u32[]{:S(2)}) collective-permute-start(bf16[512,1024]{1,0:T(8,128)(2,1)} %refs_6_.1), channel_id=1, source_target_pairs={{0,1},{1,0},{2,3},{3,2},{4,5},{5,4},{6,7},{7,6},{8,9},{9,8},{10,11... | collective-permute-start | bytes 3145736 | tf_op jit(solution)/shard_map/ppermute | solution.py:442
  3.8 1.6 %copy-done = bf16[1,256,4096]{2,1,0:T(8,128)(2,1)S(1)} copy-done((bf16[1,256,4096]{2,1,0:T(8,128)(2,1)S(1)}, bf16[1,256,4096]{2,1,0:T(8,128)(2,1)}, u32[]{:S(2)}) %copy-start) | copy-done | bytes 2097176
  5.5 1.6 %collective-permute-start.1 = (bf16[256,1024]{1,0:T(8,128)(2,1)S(1)}, bf16[256,1024]{1,0:T(8,128)(2,1)S(1)}, u32[]{:S(2)}, u32[]{:S(2)}) collective-permute-start(bf16[256,1024]{1,0:T(8,128)(2,1)S(1)} %send_kernel.1.refs_8_), channel_id=1, source_target_pairs={{0,16},{8,24},{16,0},{24,8},{1,17},{9,25},{17,1},{25,9},{2,18},{10... | collective-permute-start | bytes 1572872 | tf_op jit(solution)/shard_map/ppermute | solution.py:436
  7.8 0.8 %copy-done.4 = bf16[1,256,128]{2,1,0:T(8,128)(2,1)S(1)} copy-done((bf16[1,256,128]{2,1,0:T(8,128)(2,1)S(1)}, bf16[1,256,128]{2,1,0:T(8,128)(2,1)}, u32[]{:S(2)}) %copy-start.4) | copy-done | bytes 65560
  8.6 2.2 %tables_kernel.1 = (f32[128,512]{1,0:T(8,128)S(1)}, f32[128,512]{1,0:T(8,128)S(1)}, bf16[128,512]{1,0:T(8,128)(2,1)S(1)}, bf16[128,512]{1,0:T(8,128)(2,1)S(1)}, ...) custom-call(s32[1]{0:T(128)} %bitcast.ids_ref.refs_0_, ...), custom_call_target="tpu_custom_call" | custom-call | tf_op jit(solution)/shard_map/tables_kernel/pallas_call | solution.py:46
  11.7 1.4 %collective-permute-done.3.refs_1_.refs_4_.refs_5_ = f32[8,1024]{1,0:T(8,128)S(1)} collective-permute-done((f32[8,1024]{1,0:T(8,128)S(1)}, f32[8,1024]{1,0:T(8,128)S(1)}, u32[]{:S(2)}, u32[]{:S(2)}) %collective-permute-start.3) | collective-permute-done | bytes 32800 | tf_op jit(solution)/shard_map/ppermute | solution.py:433
  13.2 1.1 %local_output_kernel.1.refs_6_.refs_1_ = f32[256,1024]{1,0:T(8,128)S(1)} custom-call(f32[8,1024]{1,0:T(8,128)S(1)} %get-tuple-element.47.refs_1_.refs_0_, bf16[256,1024]{1,0:T(8,128)(2,1)S(1)} %bitcast.12, bf16[256,128]{1,0:T(8,128)(2,1)S(1)} %bitcast.20, bf16[256,128]{1,0:T(8,128)(2,1)S(1)} %bitcast.14, f32[16,256]{1,0:T(8,128)S(1)} %get-tuple-element.51.refs_4_.refs_5_, ...), custom_call_target="tpu_custom_call" | custom-call | tf_op jit(solution)/shard_map/local_output_kernel/pallas_call | solution.py:46
  14.5 2.5 %collective-permute-start.6 = (bf16[128,1024]{1,0:T(8,128)(2,1)S(1)}, bf16[128,1024]{1,0:T(8,128)(2,1)S(1)}, u32[]{:S(2)}, u32[]{:S(2)}) collective-permute-start(bf16[128,1024]{1,0:T(8,128)(2,1)S(1)} %chip_total_kernel.2), channel_id=1, source_target_pairs={{0,16},{8,24},{1,17},{9,25},{2,18},{10,26},{3,19},{11,27},{4,20},{... | collective-permute-start | bytes 786440 | tf_op jit(solution)/shard_map/ppermute | solution.py:492
  17.0 2.5 %collective-permute-done.1.refs_1_ = bf16[256,1024]{1,0:T(8,128)(2,1)S(1)} collective-permute-done((bf16[256,1024]{1,0:T(8,128)(2,1)S(1)}, bf16[256,1024]{1,0:T(8,128)(2,1)S(1)}, u32[]{:S(2)}, u32[]{:S(2)}) %collective-permute-start.1) | collective-permute-done | bytes 524320 | tf_op jit(solution)/shard_map/ppermute | solution.py:436
  19.5 1.6 %collective-permute-start.2 = (bf16[256,1024]{1,0:T(8,128)(2,1)S(1)}, bf16[256,1024]{1,0:T(8,128)(2,1)S(1)}, u32[]{:S(2)}, u32[]{:S(2)}) collective-permute-start(bf16[256,1024]{1,0:T(8,128)(2,1)S(1)} %collective-permute-done.1.refs_1_), channel_id=1, source_target_pairs={{0,2},{2,0},{4,6},{6,4},{1,3},{3,1},{5,7},{7,5},{8,10},{10,8},{12,... | collective-permute-start | bytes 1572872 | tf_op jit(solution)/shard_map/ppermute | solution.py:439
  21.1 3.1 %collective-permute-done.6.refs_5_ = bf16[128,1024]{1,0:T(8,128)(2,1)S(1)} collective-permute-done((bf16[128,1024]{1,0:T(8,128)(2,1)S(1)}, bf16[128,1024]{1,0:T(8,128)(2,1)S(1)}, u32[]{:S(2)}, u32[]{:S(2)}) %collective-permute-start.6) | collective-permute-done | bytes 262176 | tf_op jit(solution)/shard_map/ppermute | solution.py:492
  24.5 3.2 %collective-permute-done.8.refs_7_ = bf16[512,1024]{1,0:T(8,128)(2,1)S(1)} collective-permute-done((bf16[512,1024]{1,0:T(8,128)(2,1)}, bf16[512,1024]{1,0:T(8,128)(2,1)S(1)}, u32[]{:S(2)}, u32[]{:S(2)}) %collective-permute-start.8) | collective-permute-done | bytes 1048608 | tf_op jit(solution)/shard_map/ppermute | solution.py:442
  28.4 1.7 %collective-permute-start.14 = (bf16[256,384]{1,0:T(8,128)(2,1)S(1)}, bf16[256,384]{1,0:T(8,128)(2,1)S(1)}, u32[]{:S(2)}, u32[]{:S(2)}) collective-permute-start(bf16[256,384]{1,0:T(8,128)(2,1)S(1)} %get-tuple-element.66.refs_6_), channel_id=1, source_target_pairs={{0,16},{8,24},{16,0},{24,8},{1,17},{9,25},{17,1},{25,9},{2,18},{10... | collective-permute-start | bytes 589832 | tf_op jit(solution)/shard_map/ppermute | solution.py:436
  30.4 2.3 %collective-permute-done.2.refs_2_ = bf16[256,1024]{1,0:T(8,128)(2,1)S(1)} collective-permute-done((bf16[256,1024]{1,0:T(8,128)(2,1)S(1)}, bf16[256,1024]{1,0:T(8,128)(2,1)S(1)}, u32[]{:S(2)}, u32[]{:S(2)}) %collective-permute-start.2) | collective-permute-done | bytes 524320 | tf_op jit(solution)/shard_map/ppermute | solution.py:439
  33.5 2.3 %head_partial_kernel.1 = (f32[256,1024]{1,0:T(8,128)S(1)}, bf16[256,1024]{1,0:T(8,128)(2,1)S(1)}) custom-call(bf16[256,1024]{1,0:T(8,128)(2,1)S(1)} %get-tuple-element.49.refs_0_, bf16[256,1024]{1,0:T(8,128)(2,1)S(1)} %get-tuple-element.50.refs_1_, bf16[256,512]{1,0:T(8,128)(2,1)S(1)} %get-tuple-element.59.refs_2_, ...), custom_call_target="tpu_custom_call" | custom-call | tf_op jit(solution)/shard_map/head_partial_kernel/pallas_call | solution.py:46
  36.7 1.7 %collective-permute-start.11 = (bf16[256,1024]{1,0:T(8,128)(2,1)S(1)}, bf16[256,1024]{1,0:T(8,128)(2,1)S(1)}, u32[]{:S(2)}, u32[]{:S(2)}) collective-permute-start(bf16[256,1024]{1,0:T(8,128)(2,1)S(1)} %get-tuple-element.65), channel_id=1, source_target_pairs={{0,16},{8,24},{16,0},{24,8},{1,17},{9,25},{17,1},{25,9},{2,18},{10... | collective-permute-start | bytes 1572872 | tf_op jit(solution)/shard_map/ppermute | solution.py:436
  38.4 1.3 %weight_partial_kernel.2 = (f32[512,384]{1,0:T(8,128)S(1)}, bf16[512,384]{1,0:T(8,128)(2,1)S(1)}) custom-call(bf16[256,1024]{1,0:T(8,128)(2,1)S(1)} %get-tuple-element.49.refs_0_, bf16[256,1024]{1,0:T(8,128)(2,1)S(1)} %collective-permute-done.7.refs_8_.refs_1_, bf16[256,512]{1,0:T(8,128)(2,1)S(1)} %get-tuple-element.59.refs_2_, ...), custom_call_target="tpu_custom_call" | custom-call | tf_op jit(solution)/shard_map/weight_partial_kernel/pallas_call | solution.py:46
  39.7 1.6 %collective-permute-start.17 = (bf16[512,384]{1,0:T(8,128)(2,1)S(1)}, bf16[512,384]{1,0:T(8,128)(2,1)S(1)}, u32[]{:S(2)}, u32[]{:S(2)}) collective-permute-start(bf16[512,384]{1,0:T(8,128)(2,1)S(1)} %get-tuple-element.68.refs_12_.refs_6_), channel_id=1, source_target_pairs={{0,1},{1,0},{2,3},{3,2},{4,5},{5,4},{6,7},{7,6},{8,9},{9,8},{10,11... | collective-permute-start | bytes 1179656 | tf_op jit(solution)/shard_map/ppermute | solution.py:442
  41.3 1.9 %collective-permute-done.18.refs_7_ = bf16[256,640]{1,0:T(8,128)(2,1)S(1)} collective-permute-done((bf16[256,640]{1,0:T(8,128)(2,1)S(1)}, bf16[256,640]{1,0:T(8,128)(2,1)S(1)}, u32[]{:S(2)}, u32[]{:S(2)}) %collective-permute-start.18) | collective-permute-done | bytes 327712 | tf_op jit(solution)/shard_map/ppermute | solution.py:436
  43.9 0.9 %collective-permute-done.20.refs_9_ = bf16[256,320]{1,0:T(8,128)(2,1)S(1)} collective-permute-done((bf16[256,320]{1,0:T(8,128)(2,1)S(1)}, bf16[256,320]{1,0:T(8,128)(2,1)S(1)}, u32[]{:S(2)}, u32[]{:S(2)}) %collective-permute-start.20) | collective-permute-done | bytes 163872 | tf_op jit(solution)/shard_map/ppermute | solution.py:433
  45.1 1.8 %weight_partial_kernel.3 = (f32[512,640]{1,0:T(8,128)S(1)}, bf16[512,640]{1,0:T(8,128)(2,1)S(1)}) custom-call(bf16[256,1024]{1,0:T(8,128)(2,1)S(1)} %get-tuple-element.49.refs_0_, bf16[256,1024]{1,0:T(8,128)(2,1)S(1)} %collective-permute-done.7.refs_8_.refs_1_, bf16[256,512]{1,0:T(8,128)(2,1)S(1)} %get-tuple-element.59.refs_2_, ...), custom_call_target="tpu_custom_call" | custom-call | tf_op jit(solution)/shard_map/weight_partial_kernel/pallas_call | solution.py:46
  46.9 1.8 %collective-permute-start.25 = (bf16[512,640]{1,0:T(8,128)(2,1)S(1)}, bf16[512,640]{1,0:T(8,128)(2,1)S(1)}, u32[]{:S(2)}, u32[]{:S(2)}) collective-permute-start(bf16[512,640]{1,0:T(8,128)(2,1)S(1)} %get-tuple-element.70.refs_7_), channel_id=1, source_target_pairs={{0,1},{1,0},{2,3},{3,2},{4,5},{5,4},{6,7},{7,6},{8,9},{9,8},{10,11... | collective-permute-start | bytes 1966088 | tf_op jit(solution)/shard_map/ppermute | solution.py:442
  48.8 4.8 %collective-permute-done.11.refs_2_ = bf16[256,1024]{1,0:T(8,128)(2,1)S(1)} collective-permute-done((bf16[256,1024]{1,0:T(8,128)(2,1)S(1)}, bf16[256,1024]{1,0:T(8,128)(2,1)S(1)}, u32[]{:S(2)}, u32[]{:S(2)}) %collective-permute-start.11) | collective-permute-done | bytes 524320 | tf_op jit(solution)/shard_map/ppermute | solution.py:436
  54.1 1.5 %collective-permute-done.22.refs_4_.refs_9_ = bf16[128,1024]{1,0:T(8,128)(2,1)S(1)} collective-permute-done((bf16[128,1024]{1,0:T(8,128)(2,1)S(1)}, bf16[128,1024]{1,0:T(8,128)(2,1)S(1)}, u32[]{:S(2)}, u32[]{:S(2)}) %collective-permute-start.22) | collective-permute-done | bytes 262176 | tf_op jit(solution)/shard_map/ppermute | solution.py:433
  55.7 1.5 %collective-permute-start.23 = (bf16[128,512]{1,0:T(8,128)(2,1)S(1)}, bf16[128,512]{1,0:T(8,128)(2,1)S(1)}, u32[]{:S(2)}, u32[]{:S(2)}) collective-permute-start(bf16[128,512]{1,0:T(8,128)(2,1)S(1)} %chip_total_kernel.3), channel_id=1, source_target_pairs={{16,0},{24,8},{17,1},{25,9},{18,2},{26,10},{19,3},{27,11},{20,4},{... | collective-permute-start | bytes 393224 | tf_op jit(solution)/shard_map/ppermute | solution.py:559
  57.2 1.9 %local_grads_kernel.1 = (f32[256,1024]{1,0:T(8,128)S(1)}, f32[256,256]{1,0:T(8,128)S(1)}, f32[256,128]{1,0:T(8,128)S(1)}) custom-call(f32[8,1024]{1,0:T(8,128)S(1)} %get-tuple-element.47.refs_1_.refs_0_, bf16[256,1024]{1,0:T(8,128)(2,1)S(1)} %bitcast.13, bf16[256,1024]{1,0:T(8,128)(2,1)S(1)} %get-tuple-element.71.refs_2_, bf16[256,128]{1,0:T(8,128)(2,1)S(1)} %bitcast.21, ...), custom_call_target="tpu_custom_call" | custom-call | tf_op jit(solution)/shard_map/local_grads_kernel/pallas_call | solution.py:46
  59.1 0.9 %group_sums_kernel.1 = (f32[256,128]{1,0:T(8,128)S(1)}, f32[256,128]{1,0:T(8,128)}) custom-call(bf16[256,128]{1,0:T(8,128)(2,1)S(1)} %bitcast.22, bf16[256,128]{1,0:T(8,128)(2,1)S(1)} %bitcast.18, f32[256,256]{1,0:T(8,128)S(1)} %get-tuple-element.75.refs_2_, f32[256,128]{1,0:T(8,128)S(1)} %get-tuple-element.76.refs_3_), custom_call_target="tpu_custom_call" | custom-call | tf_op jit(solution)/shard_map/group_sums_kernel/pallas_call | solution.py:46
  60.0 3.1 %collective-permute-done.23.refs_7_ = bf16[128,512]{1,0:T(8,128)(2,1)S(1)} collective-permute-done((bf16[128,512]{1,0:T(8,128)(2,1)S(1)}, bf16[128,512]{1,0:T(8,128)(2,1)S(1)}, u32[]{:S(2)}, u32[]{:S(2)}) %collective-permute-start.23) | collective-permute-done | bytes 131104 | tf_op jit(solution)/shard_map/ppermute | solution.py:559
  63.2 1.3 %collective-permute-done.24.refs_8_ = bf16[128,512]{1,0:T(8,128)(2,1)S(1)} collective-permute-done((bf16[128,512]{1,0:T(8,128)(2,1)S(1)}, bf16[128,512]{1,0:T(8,128)(2,1)S(1)}, u32[]{:S(2)}, u32[]{:S(2)}) %collective-permute-start.24) | collective-permute-done | bytes 131104 | tf_op jit(solution)/shard_map/ppermute | solution.py:433
  64.5 1.3 %final_kernel.1 = (bf16[256,1024]{1,0:T(8,128)(2,1)}, f32[256,128]{1,0:T(8,128)}, f32[8,128]{1,0:T(8,128)S(1)}) custom-call(f32[8,1024]{1,0:T(8,128)S(1)} %get-tuple-element.47.refs_1_.refs_0_, bf16[256,128]{1,0:T(8,128)(2,1)S(1)} %bitcast.23, f32[256,1024]{1,0:T(8,128)S(1)} %get-tuple-element.48.refs_2_, f32[256,128]{1,0:T(8,128)S(1)} %get-tuple-element.77.refs_3_, ...), custom_call_target="tpu_custom_call" | custom-call | tf_op jit(solution)/shard_map/final_kernel/pallas_call | solution.py:46
  65.8 1.5 %add_kernel.1 = f32[512,1024]{1,0:T(8,128)} custom-call(f32[512,384]{1,0:T(8,128)S(1)} %get-tuple-element.87.refs_0_, f32[512,640]{1,0:T(8,128)S(1)} %get-tuple-element.88.refs_1_, bf16[512,384]{1,0:T(8,128)(2,1)S(1)} %collective-permute-done.17.refs_5_.refs_2_, bf16[512,640]{1,0:T(8,128)(2,1)S(1)} %collective-permute-done.25.refs_3_, ...), custom_call_target="tpu_custom_call" | custom-call | tf_op jit(solution)/shard_map/add_kernel/pallas_call | solution.py:574
  (58 shorter events, 5.8 us)
Async XLA Ops:
  0.6 7.1 %copy-start.7 = (f32[1,16,256]{2,1,0:T(8,128)S(1)}, f32[1,16,256]{2,1,0:T(8,128)}, u32[]{:S(2)}) copy-start(f32[1,16,256]{2,1,0:T(8,128)} %param.12) | copy-start | bytes 49156
  0.6 7.1 %copy-start.8 = (f32[16]{0:T(128)S(1)}, f32[16]{0:T(128)}, u32[]{:S(2)}) copy-start(f32[16]{0:T(128)} %refs_1_.1) | copy-start | bytes 196
  0.7 7.1 %copy-start.9 = (f32[16]{0:T(128)S(1)}, f32[16]{0:T(128)}, u32[]{:S(2)}) copy-start(f32[16]{0:T(128)} %refs_3_.1) | copy-start | bytes 196
  0.7 7.0 %collective-permute-start = (bf16[512,1024]{1,0:T(8,128)(2,1)}, bf16[512,1024]{1,0:T(8,128)(2,1)S(1)}, u32[]{:S(2)}, u32[]{:S(2)}) collective-permute-start(bf16[512,1024]{1,0:T(8,128)(2,1)} %refs_6_.1), channel_id=1, source_target_pairs={{0,8},{8,0},{16,24},{24,16},{1,9},{9,1},{17,25},{25,17},{2,10},{10... | collective-permute-start | bytes 3145736 | tf_op jit(solution)/shard_map/ppermute | solution.py:433
  1.2 26.6 %collective-permute-start.8 = (bf16[512,1024]{1,0:T(8,128)(2,1)}, bf16[512,1024]{1,0:T(8,128)(2,1)S(1)}, u32[]{:S(2)}, u32[]{:S(2)}) collective-permute-start(bf16[512,1024]{1,0:T(8,128)(2,1)} %refs_6_.1), channel_id=1, source_target_pairs={{0,1},{1,0},{2,3},{3,2},{4,5},{5,4},{6,7},{7,6},{8,9},{9,8},{10,11... | collective-permute-start | bytes 3145736 | tf_op jit(solution)/shard_map/ppermute | solution.py:442
  5.4 5.5 %copy-start.1 = (bf16[1,256,4096]{2,1,0:T(8,128)(2,1)S(1)}, bf16[1,256,4096]{2,1,0:T(8,128)(2,1)}, u32[]{:S(2)}) copy-start(bf16[1,256,4096]{2,1,0:T(8,128)(2,1)} %param.16) | copy-start | bytes 6291460
  5.5 14.1 %collective-permute-start.1 = (bf16[256,1024]{1,0:T(8,128)(2,1)S(1)}, bf16[256,1024]{1,0:T(8,128)(2,1)S(1)}, u32[]{:S(2)}, u32[]{:S(2)}) collective-permute-start(bf16[256,1024]{1,0:T(8,128)(2,1)S(1)} %send_kernel.1.refs_8_), channel_id=1, source_target_pairs={{0,16},{8,24},{16,0},{24,8},{1,17},{9,25},{17,1},{25,9},{2,18},{10... | collective-permute-start | bytes 1572872 | tf_op jit(solution)/shard_map/ppermute | solution.py:436
  11.0 13.2 %collective-permute-start.7 = (bf16[256,1024]{1,0:T(8,128)(2,1)S(1)}, bf16[256,1024]{1,0:T(8,128)(2,1)S(1)}, u32[]{:S(2)}, u32[]{:S(2)}) collective-permute-start(bf16[256,1024]{1,0:T(8,128)(2,1)S(1)} %get-tuple-element.50.refs_1_), channel_id=1, source_target_pairs={{0,8},{8,0},{16,24},{24,16},{1,9},{9,1},{17,25},{25,17},{2,10},{10... | collective-permute-start | bytes 1572872 | tf_op jit(solution)/shard_map/ppermute | solution.py:433
  11.1 1.9 %collective-permute-start.3 = (f32[8,1024]{1,0:T(8,128)S(1)}, f32[8,1024]{1,0:T(8,128)S(1)}, u32[]{:S(2)}, u32[]{:S(2)}) collective-permute-start(f32[8,1024]{1,0:T(8,128)S(1)} %get-tuple-element.47.refs_1_.refs_0_), channel_id=1, source_target_pairs={{0,8},{8,0},{16,24},{24,16},{1,9},{9,1},{17,25},{25,17},{2,10},{10... | collective-permute-start | bytes 98312 | tf_op jit(solution)/shard_map/ppermute | solution.py:433
  11.6 2.7 %collective-permute-start.4 = (bf16[128,512]{1,0:T(8,128)(2,1)S(1)}, bf16[128,512]{1,0:T(8,128)(2,1)S(1)}, u32[]{:S(2)}, u32[]{:S(2)}) collective-permute-start(bf16[128,512]{1,0:T(8,128)(2,1)S(1)} %get-tuple-element.56), channel_id=1, source_target_pairs={{0,8},{8,0},{16,24},{24,16},{1,9},{9,1},{17,25},{25,17},{2,10},{10... | collective-permute-start | bytes 393224 | tf_op jit(solution)/shard_map/ppermute | solution.py:433
  13.0 1.3 %collective-permute-start.5 = (bf16[128,512]{1,0:T(8,128)(2,1)S(1)}, bf16[128,512]{1,0:T(8,128)(2,1)S(1)}, u32[]{:S(2)}, u32[]{:S(2)}) collective-permute-start(bf16[128,512]{1,0:T(8,128)(2,1)S(1)} %get-tuple-element.57), channel_id=1, source_target_pairs={{0,8},{8,0},{16,24},{24,16},{1,9},{9,1},{17,25},{25,17},{2,10},{10... | collective-permute-start | bytes 393224 | tf_op jit(solution)/shard_map/ppermute | solution.py:433
  14.5 9.7 %collective-permute-start.6 = (bf16[128,1024]{1,0:T(8,128)(2,1)S(1)}, bf16[128,1024]{1,0:T(8,128)(2,1)S(1)}, u32[]{:S(2)}, u32[]{:S(2)}) collective-permute-start(bf16[128,1024]{1,0:T(8,128)(2,1)S(1)} %chip_total_kernel.2), channel_id=1, source_target_pairs={{0,16},{8,24},{1,17},{9,25},{2,18},{10,26},{3,19},{11,27},{4,20},{... | collective-permute-start | bytes 786440 | tf_op jit(solution)/shard_map/ppermute | solution.py:492
  19.5 13.2 %collective-permute-start.2 = (bf16[256,1024]{1,0:T(8,128)(2,1)S(1)}, bf16[256,1024]{1,0:T(8,128)(2,1)S(1)}, u32[]{:S(2)}, u32[]{:S(2)}) collective-permute-start(bf16[256,1024]{1,0:T(8,128)(2,1)S(1)} %collective-permute-done.1.refs_1_), channel_id=1, source_target_pairs={{0,2},{2,0},{4,6},{6,4},{1,3},{3,1},{5,7},{7,5},{8,10},{10,8},{12,... | collective-permute-start | bytes 1572872 | tf_op jit(solution)/shard_map/ppermute | solution.py:439
  24.5 8.9 %copy-start.6 = (bf16[512,1024]{1,0:T(8,128)(2,1)S(1)}, bf16[512,1024]{1,0:T(8,128)(2,1)}, u32[]{:S(2)}) copy-start(bf16[512,1024]{1,0:T(8,128)(2,1)} %refs_6_.1) | copy-start | bytes 3145732
  27.8 5.1 %collective-permute-start.10 = (bf16[256,1024]{1,0:T(8,128)(2,1)S(1)}, bf16[256,1024]{1,0:T(8,128)(2,1)S(1)}, u32[]{:S(2)}, u32[]{:S(2)}) collective-permute-start(bf16[256,1024]{1,0:T(8,128)(2,1)S(1)} %get-tuple-element.90), channel_id=1, source_target_pairs={{0,8},{8,0},{16,24},{24,16},{1,9},{9,1},{17,25},{25,17},{2,10},{10... | collective-permute-start | bytes 1572872 | tf_op jit(solution)/shard_map/ppermute | solution.py:433
  27.9 5.5 %collective-permute-start.9 = (bf16[256,1024]{1,0:T(8,128)(2,1)S(1)}, bf16[256,1024]{1,0:T(8,128)(2,1)S(1)}, u32[]{:S(2)}, u32[]{:S(2)}) collective-permute-start(bf16[256,1024]{1,0:T(8,128)(2,1)S(1)} %get-tuple-element.91), channel_id=1, source_target_pairs={{0,8},{8,0},{16,24},{24,16},{1,9},{9,1},{17,25},{25,17},{2,10},{10... | collective-permute-start | bytes 1572872 | tf_op jit(solution)/shard_map/ppermute | solution.py:433
  28.4 7.8 %collective-permute-start.14 = (bf16[256,384]{1,0:T(8,128)(2,1)S(1)}, bf16[256,384]{1,0:T(8,128)(2,1)S(1)}, u32[]{:S(2)}, u32[]{:S(2)}) collective-permute-start(bf16[256,384]{1,0:T(8,128)(2,1)S(1)} %get-tuple-element.66.refs_6_), channel_id=1, source_target_pairs={{0,16},{8,24},{16,0},{24,8},{1,17},{9,25},{17,1},{25,9},{2,18},{10... | collective-permute-start | bytes 589832 | tf_op jit(solution)/shard_map/ppermute | solution.py:436
  30.1 13.1 %collective-permute-start.18 = (bf16[256,640]{1,0:T(8,128)(2,1)S(1)}, bf16[256,640]{1,0:T(8,128)(2,1)S(1)}, u32[]{:S(2)}, u32[]{:S(2)}) collective-permute-start(bf16[256,640]{1,0:T(8,128)(2,1)S(1)} %get-tuple-element.58.refs_3_.refs_6_), channel_id=1, source_target_pairs={{0,16},{8,24},{16,0},{24,8},{1,17},{9,25},{17,1},{25,9},{2,18},{10... | collective-permute-start | bytes 983048 | tf_op jit(solution)/shard_map/ppermute | solution.py:436
  32.8 3.9 %collective-permute-start.12 = (bf16[256,512]{1,0:T(8,128)(2,1)S(1)}, bf16[256,512]{1,0:T(8,128)(2,1)S(1)}, u32[]{:S(2)}, u32[]{:S(2)}) collective-permute-start(bf16[256,512]{1,0:T(8,128)(2,1)S(1)} %get-tuple-element.61.refs_4_), channel_id=1, source_target_pairs={{0,8},{8,0},{16,24},{24,16},{1,9},{9,1},{17,25},{25,17},{2,10},{10... | collective-permute-start | bytes 786440 | tf_op jit(solution)/shard_map/ppermute | solution.py:433
  32.9 5.5 %collective-permute-start.13 = (bf16[256,512]{1,0:T(8,128)(2,1)S(1)}, bf16[256,512]{1,0:T(8,128)(2,1)S(1)}, u32[]{:S(2)}, u32[]{:S(2)}) collective-permute-start(bf16[256,512]{1,0:T(8,128)(2,1)S(1)} %get-tuple-element.62.refs_5_), channel_id=1, source_target_pairs={{0,8},{8,0},{16,24},{24,16},{1,9},{9,1},{17,25},{25,17},{2,10},{10... | collective-permute-start | bytes 786440 | tf_op jit(solution)/shard_map/ppermute | solution.py:433
  33.4 2.9 %collective-permute-start.15 = (bf16[256,384]{1,0:T(8,128)(2,1)S(1)}, bf16[256,384]{1,0:T(8,128)(2,1)S(1)}, u32[]{:S(2)}, u32[]{:S(2)}) collective-permute-start(bf16[256,384]{1,0:T(8,128)(2,1)S(1)} %get-tuple-element.66.refs_6_), channel_id=1, source_target_pairs={{0,8},{8,0},{16,24},{24,16},{1,9},{9,1},{17,25},{25,17},{2,10},{10... | collective-permute-start | bytes 589832 | tf_op jit(solution)/shard_map/ppermute | solution.py:433
  36.1 2.3 %collective-permute-start.16 = (bf16[256,384]{1,0:T(8,128)(2,1)S(1)}, bf16[256,384]{1,0:T(8,128)(2,1)S(1)}, u32[]{:S(2)}, u32[]{:S(2)}) collective-permute-start(bf16[256,384]{1,0:T(8,128)(2,1)S(1)} %collective-permute-done.14.refs_7_), channel_id=1, source_target_pairs={{0,8},{8,0},{16,24},{24,16},{1,9},{9,1},{17,25},{25,17},{2,10},{10... | collective-permute-start | bytes 589832 | tf_op jit(solution)/shard_map/ppermute | solution.py:433
  36.3 7.6 %collective-permute-start.19 = (bf16[256,640]{1,0:T(8,128)(2,1)S(1)}, bf16[256,640]{1,0:T(8,128)(2,1)S(1)}, u32[]{:S(2)}, u32[]{:S(2)}) collective-permute-start(bf16[256,640]{1,0:T(8,128)(2,1)S(1)} %get-tuple-element.58.refs_3_.refs_6_), channel_id=1, source_target_pairs={{0,8},{8,0},{16,24},{24,16},{1,9},{9,1},{17,25},{25,17},{2,10},{10... | collective-permute-start | bytes 983048 | tf_op jit(solution)/shard_map/ppermute | solution.py:433
  36.7 16.9 %collective-permute-start.11 = (bf16[256,1024]{1,0:T(8,128)(2,1)S(1)}, bf16[256,1024]{1,0:T(8,128)(2,1)S(1)}, u32[]{:S(2)}, u32[]{:S(2)}) collective-permute-start(bf16[256,1024]{1,0:T(8,128)(2,1)S(1)} %get-tuple-element.65), channel_id=1, source_target_pairs={{0,16},{8,24},{16,0},{24,8},{1,17},{9,25},{17,1},{25,9},{2,18},{10... | collective-permute-start | bytes 1572872 | tf_op jit(solution)/shard_map/ppermute | solution.py:436
  39.7 13.9 %collective-permute-start.17 = (bf16[512,384]{1,0:T(8,128)(2,1)S(1)}, bf16[512,384]{1,0:T(8,128)(2,1)S(1)}, u32[]{:S(2)}, u32[]{:S(2)}) collective-permute-start(bf16[512,384]{1,0:T(8,128)(2,1)S(1)} %get-tuple-element.68.refs_12_.refs_6_), channel_id=1, source_target_pairs={{0,1},{1,0},{2,3},{3,2},{4,5},{5,4},{6,7},{7,6},{8,9},{9,8},{10,11... | collective-permute-start | bytes 1179656 | tf_op jit(solution)/shard_map/ppermute | solution.py:442
  43.3 1.5 %collective-permute-start.20 = (bf16[256,320]{1,0:T(8,128)(2,1)S(1)}, bf16[256,320]{1,0:T(8,128)(2,1)S(1)}, u32[]{:S(2)}, u32[]{:S(2)}) collective-permute-start(bf16[256,320]{1,0:T(8,128)(2,1)S(1)} %get-tuple-element.93), channel_id=1, source_target_pairs={{0,8},{8,0},{16,24},{24,16},{1,9},{9,1},{17,25},{25,17},{2,10},{10... | collective-permute-start | bytes 491528 | tf_op jit(solution)/shard_map/ppermute | solution.py:433
  43.4 1.7 %collective-permute-start.21 = (bf16[256,320]{1,0:T(8,128)(2,1)S(1)}, bf16[256,320]{1,0:T(8,128)(2,1)S(1)}, u32[]{:S(2)}, u32[]{:S(2)}) collective-permute-start(bf16[256,320]{1,0:T(8,128)(2,1)S(1)} %get-tuple-element.92), channel_id=1, source_target_pairs={{0,8},{8,0},{16,24},{24,16},{1,9},{9,1},{17,25},{25,17},{2,10},{10... | collective-permute-start | bytes 491528 | tf_op jit(solution)/shard_map/ppermute | solution.py:433
  46.9 10.3 %copy-start.5 = (bf16[1,256,128]{2,1,0:T(8,128)(2,1)S(1)}, bf16[1,256,128]{2,1,0:T(8,128)(2,1)}, u32[]{:S(2)}) copy-start(bf16[1,256,128]{2,1,0:T(8,128)(2,1)} %param.10) | copy-start | bytes 196612
  46.9 18.9 %collective-permute-start.25 = (bf16[512,640]{1,0:T(8,128)(2,1)S(1)}, bf16[512,640]{1,0:T(8,128)(2,1)S(1)}, u32[]{:S(2)}, u32[]{:S(2)}) collective-permute-start(bf16[512,640]{1,0:T(8,128)(2,1)S(1)} %get-tuple-element.70.refs_7_), channel_id=1, source_target_pairs={{0,1},{1,0},{2,3},{3,2},{4,5},{5,4},{6,7},{7,6},{8,9},{9,8},{10,11... | collective-permute-start | bytes 1966088 | tf_op jit(solution)/shard_map/ppermute | solution.py:442
  54.0 1.6 %collective-permute-start.22 = (bf16[128,1024]{1,0:T(8,128)(2,1)S(1)}, bf16[128,1024]{1,0:T(8,128)(2,1)S(1)}, u32[]{:S(2)}, u32[]{:S(2)}) collective-permute-start(bf16[128,1024]{1,0:T(8,128)(2,1)S(1)} %get-tuple-element.82), channel_id=1, source_target_pairs={{0,8},{8,0},{16,24},{24,16},{1,9},{9,1},{17,25},{25,17},{2,10},{10... | collective-permute-start | bytes 786440 | tf_op jit(solution)/shard_map/ppermute | solution.py:433
  55.7 7.4 %collective-permute-start.23 = (bf16[128,512]{1,0:T(8,128)(2,1)S(1)}, bf16[128,512]{1,0:T(8,128)(2,1)S(1)}, u32[]{:S(2)}, u32[]{:S(2)}) collective-permute-start(bf16[128,512]{1,0:T(8,128)(2,1)S(1)} %chip_total_kernel.3), channel_id=1, source_target_pairs={{16,0},{24,8},{17,1},{25,9},{18,2},{26,10},{19,3},{27,11},{20,4},{... | collective-permute-start | bytes 393224 | tf_op jit(solution)/shard_map/ppermute | solution.py:559
  63.2 1.3 %collective-permute-start.24 = (bf16[128,512]{1,0:T(8,128)(2,1)S(1)}, bf16[128,512]{1,0:T(8,128)(2,1)S(1)}, u32[]{:S(2)}, u32[]{:S(2)}) collective-permute-start(bf16[128,512]{1,0:T(8,128)(2,1)S(1)} %collective-permute-done.23.refs_7_), channel_id=1, source_target_pairs={{0,8},{8,0},{16,24},{24,16},{1,9},{9,1},{17,25},{25,17},{2,10},{10... | collective-permute-start | bytes 393224 | tf_op jit(solution)/shard_map/ppermute | solution.py:433
  (4 other events, 9.4 us)

commit v8 on v6

--- a/solution.py
+++ b/solution.py
@@ -355,8 +355,7 @@
 
 
 def final_kernel(table_ref, b_ref, end_ref, sums_ref, weighted_ref, through_ref, local_ref, *refs):
-    entered, partner_ref, (in_ref, grad_b_ref, token_ref) = refs[:2], refs[2], refs[3:]
-    token_ref[...] = jnp.zeros_like(token_ref)
+    entered, partner_ref, (in_ref, grad_b_ref) = refs[:2], refs[2], refs[3:]
     grad_b = sums_ref[...]
     width = partner_ref.shape[1] // 2
     for half in range(2):
@@ -382,6 +381,11 @@
             at = slice(start, start + ref.shape[1])
             out_ref[:, at] = out_ref[:, at] + ref[...].astype(F32) if change else ref[...]
             start += ref.shape[1]
+
+
+def last_kernel(parts, *refs):
+    add_kernel(parts, *refs[-3 - 2 * parts : -3], refs[-1])
+    final_kernel(*refs[: -3 - 2 * parts], *refs[-3:-1])
 
 
 def weight_partial_kernel(chips, pieces, *refs):
@@ -563,19 +567,13 @@
         (b_rows, c_rows, paired, c_part),
         [((Q, N), F32), ((Q, N), F32)],
     )
-    grad_in, grad_b, token = call(
-        final_kernel,
+    grad_in, grad_b, grad_weight = call(
+        functools.partial(last_kernel, len(widths)),
         (),
         (through, b_rows, to_end, grad_b, weighted_in, through_partner, local_in)
-        + (*entering, core_swap(later(entering[0], grad_c)), adjoint_partner),
-        [((Q, wide), BF), ((Q, N), F32), ((8, 128), F32)],
-    )
-    grad_weight, = call(
-        functools.partial(add_kernel, len(widths)),
-        (),
-        (*kept, *sums),
-        [((depth, wide), F32)],
-        after=[token],
+        + (*entering, core_swap(later(entering[0], grad_c)), adjoint_partner)
+        + (*kept, *sums),
+        [((Q, wide), BF), ((Q, N), F32), ((depth, wide), F32)],
     )
     return grad_in[None], grad_b[None], grad_c[None], grad_weight
 

time: 67.8 us -> 67 us (0.988)
  Pallas kernels: 16 us -> 15.1 us
    ppermute x3, waiting for transfers between devices: 3.2 us -> 4.63 us  [dialogue_swap(): return lax.ppermute(value, 'dp', [(0, 1), (1, 0)])]
    ppermute x16, waiting for transfers between devices: 5.53 us -> 4.19 us  [core_swap(): return lax.ppermute(value, 'seq', across)]
    pallas_call x14 -> x13, Pallas kernels: 15.7 us -> 14.8 us  [call(): pl.pallas_call(run, grid=(1,), out_shape=[jax.ShapeDtypeStruct(shape, kin...]
  transfers between devices with their start and end apart: 26 -> 26, of which waited for: 14 -> 14; matrix products, arithmetic and copies ran while one was open for 0% -> 0% of each run, Pallas kernels for 21% -> 19%
where the time goes in v8:
time: 67 us; the launch traced here: 66.7 us
  waiting for transfers between devices  26.9 us (40%)
  starting transfers between devices  20.6 us (31%)
  Pallas kernels  15.1 us (23%)
  local copies, waits for them, and re-layouts  2.65 us (4%)
  between operations  1.56 us (2%)
    pallas_call x13, Pallas kernels, call(): pl.pallas_call(run, grid=(1,), out_shape=[jax.ShapeDtypeStruct(shape, kin...  14.8 us
    ppermute x4, waiting for transfers between devices, chip_shift(): lax.ppermute(value, 'seq', [(i, (i + 2 * by) % seq) for i in range(seq)])  9.55 us
    ppermute x3, starting transfers between devices, dialogue_swap(): return lax.ppermute(value, 'dp', [(0, 1), (1, 0)])  6 us
    ppermute x4, starting transfers between devices, chip_shift(): lax.ppermute(value, 'seq', [(i, (i + 2 * by) % seq) for i in range(seq)])  5.31 us
    ppermute x3, waiting for transfers between devices, dialogue_swap(): return lax.ppermute(value, 'dp', [(0, 1), (1, 0)])  4.63 us
    ppermute x16, waiting for transfers between devices, core_swap(): return lax.ppermute(value, 'seq', across)  4.19 us
    ppermute x16, starting transfers between devices, core_swap(): return lax.ppermute(value, 'seq', across)  3.67 us
    ppermute x1, waiting for transfers between devices, body(): entering = [lax.ppermute(total, 'seq', [(i, i - 2) for i in range(2, seq)])]  3.14 us
  transfers between devices with their start and end apart: 26, of which 14 were waited for; matrix products, arithmetic and copies ran while one was open for 0% of the time, Pallas kernels for 19%

profile of v8, /device:TPU:0, one launch (start us, length us, event | category | flops | bytes accessed | tf_op | source)
XLA Modules:
  0.0 66.7 jit_solution(16751980443166766053)
XLA Ops:
  0.7 0.5 collective-permute-start
  1.2 2.6 %collective-permute-start.8 = (bf16[512,1024]{1,0:T(8,128)(2,1)}, bf16[512,1024]{1,0:T(8,128)(2,1)S(1)}, u32[]{:S(2)}, u32[]{:S(2)}) collective-permute-start(bf16[512,1024]{1,0:T(8,128)(2,1)} %refs_6_.1), channel_id=1, source_target_pairs={{0,1},{1,0},{2,3},{3,2},{4,5},{5,4},{6,7},{7,6},{8,9},{9,8},{10,11... | collective-permute-start | bytes 3145736 | tf_op jit(solution)/shard_map/ppermute | solution.py:446
  3.8 1.6 %copy-done = bf16[1,256,4096]{2,1,0:T(8,128)(2,1)S(1)} copy-done((bf16[1,256,4096]{2,1,0:T(8,128)(2,1)S(1)}, bf16[1,256,4096]{2,1,0:T(8,128)(2,1)}, u32[]{:S(2)}) %copy-start) | copy-done | bytes 2097176
  5.5 1.6 %collective-permute-start.1 = (bf16[256,1024]{1,0:T(8,128)(2,1)S(1)}, bf16[256,1024]{1,0:T(8,128)(2,1)S(1)}, u32[]{:S(2)}, u32[]{:S(2)}) collective-permute-start(bf16[256,1024]{1,0:T(8,128)(2,1)S(1)} %send_kernel.1.refs_8_), channel_id=1, source_target_pairs={{0,16},{8,24},{16,0},{24,8},{1,17},{9,25},{17,1},{25,9},{2,18},{10... | collective-permute-start | bytes 1572872 | tf_op jit(solution)/shard_map/ppermute | solution.py:440
  7.8 0.8 %copy-done.4 = bf16[1,256,128]{2,1,0:T(8,128)(2,1)S(1)} copy-done((bf16[1,256,128]{2,1,0:T(8,128)(2,1)S(1)}, bf16[1,256,128]{2,1,0:T(8,128)(2,1)}, u32[]{:S(2)}) %copy-start.4) | copy-done | bytes 65560
  8.6 2.2 %tables_kernel.1 = (f32[128,512]{1,0:T(8,128)S(1)}, f32[128,512]{1,0:T(8,128)S(1)}, bf16[128,512]{1,0:T(8,128)(2,1)S(1)}, bf16[128,512]{1,0:T(8,128)(2,1)S(1)}, ...) custom-call(s32[1]{0:T(128)} %bitcast.ids_ref.refs_0_, ...), custom_call_target="tpu_custom_call" | custom-call | tf_op jit(solution)/shard_map/tables_kernel/pallas_call | solution.py:46
  11.7 1.4 %collective-permute-done.3.refs_1_.refs_4_.refs_5_ = f32[8,1024]{1,0:T(8,128)S(1)} collective-permute-done((f32[8,1024]{1,0:T(8,128)S(1)}, f32[8,1024]{1,0:T(8,128)S(1)}, u32[]{:S(2)}, u32[]{:S(2)}) %collective-permute-start.3) | collective-permute-done | bytes 32800 | tf_op jit(solution)/shard_map/ppermute | solution.py:437
  13.2 1.1 %local_output_kernel.1.refs_6_.refs_1_ = f32[256,1024]{1,0:T(8,128)S(1)} custom-call(f32[8,1024]{1,0:T(8,128)S(1)} %get-tuple-element.47.refs_1_.refs_0_, bf16[256,1024]{1,0:T(8,128)(2,1)S(1)} %bitcast.12, bf16[256,128]{1,0:T(8,128)(2,1)S(1)} %bitcast.20, bf16[256,128]{1,0:T(8,128)(2,1)S(1)} %bitcast.14, f32[16,256]{1,0:T(8,128)S(1)} %get-tuple-element.51.refs_4_.refs_5_, ...), custom_call_target="tpu_custom_call" | custom-call | tf_op jit(solution)/shard_map/local_output_kernel/pallas_call | solution.py:46
  14.5 2.5 %collective-permute-start.6 = (bf16[128,1024]{1,0:T(8,128)(2,1)S(1)}, bf16[128,1024]{1,0:T(8,128)(2,1)S(1)}, u32[]{:S(2)}, u32[]{:S(2)}) collective-permute-start(bf16[128,1024]{1,0:T(8,128)(2,1)S(1)} %chip_total_kernel.2), channel_id=1, source_target_pairs={{0,16},{8,24},{1,17},{9,25},{2,18},{10,26},{3,19},{11,27},{4,20},{... | collective-permute-start | bytes 786440 | tf_op jit(solution)/shard_map/ppermute | solution.py:496
  17.0 2.5 %collective-permute-done.1.refs_1_ = bf16[256,1024]{1,0:T(8,128)(2,1)S(1)} collective-permute-done((bf16[256,1024]{1,0:T(8,128)(2,1)S(1)}, bf16[256,1024]{1,0:T(8,128)(2,1)S(1)}, u32[]{:S(2)}, u32[]{:S(2)}) %collective-permute-start.1) | collective-permute-done | bytes 524320 | tf_op jit(solution)/shard_map/ppermute | solution.py:440
  19.5 1.6 %collective-permute-start.2 = (bf16[256,1024]{1,0:T(8,128)(2,1)S(1)}, bf16[256,1024]{1,0:T(8,128)(2,1)S(1)}, u32[]{:S(2)}, u32[]{:S(2)}) collective-permute-start(bf16[256,1024]{1,0:T(8,128)(2,1)S(1)} %collective-permute-done.1.refs_1_), channel_id=1, source_target_pairs={{0,2},{2,0},{4,6},{6,4},{1,3},{3,1},{5,7},{7,5},{8,10},{10,8},{12,... | collective-permute-start | bytes 1572872 | tf_op jit(solution)/shard_map/ppermute | solution.py:443
  21.1 3.1 %collective-permute-done.6.refs_5_ = bf16[128,1024]{1,0:T(8,128)(2,1)S(1)} collective-permute-done((bf16[128,1024]{1,0:T(8,128)(2,1)S(1)}, bf16[128,1024]{1,0:T(8,128)(2,1)S(1)}, u32[]{:S(2)}, u32[]{:S(2)}) %collective-permute-start.6) | collective-permute-done | bytes 262176 | tf_op jit(solution)/shard_map/ppermute | solution.py:496
  24.5 3.2 %collective-permute-done.8.refs_7_ = bf16[512,1024]{1,0:T(8,128)(2,1)S(1)} collective-permute-done((bf16[512,1024]{1,0:T(8,128)(2,1)}, bf16[512,1024]{1,0:T(8,128)(2,1)S(1)}, u32[]{:S(2)}, u32[]{:S(2)}) %collective-permute-start.8) | collective-permute-done | bytes 1048608 | tf_op jit(solution)/shard_map/ppermute | solution.py:446
  28.4 1.7 %collective-permute-start.14 = (bf16[256,384]{1,0:T(8,128)(2,1)S(1)}, bf16[256,384]{1,0:T(8,128)(2,1)S(1)}, u32[]{:S(2)}, u32[]{:S(2)}) collective-permute-start(bf16[256,384]{1,0:T(8,128)(2,1)S(1)} %get-tuple-element.66.refs_6_), channel_id=1, source_target_pairs={{0,16},{8,24},{16,0},{24,8},{1,17},{9,25},{17,1},{25,9},{2,18},{10... | collective-permute-start | bytes 589832 | tf_op jit(solution)/shard_map/ppermute | solution.py:440
  30.4 2.3 %collective-permute-done.2.refs_2_ = bf16[256,1024]{1,0:T(8,128)(2,1)S(1)} collective-permute-done((bf16[256,1024]{1,0:T(8,128)(2,1)S(1)}, bf16[256,1024]{1,0:T(8,128)(2,1)S(1)}, u32[]{:S(2)}, u32[]{:S(2)}) %collective-permute-start.2) | collective-permute-done | bytes 524320 | tf_op jit(solution)/shard_map/ppermute | solution.py:443
  33.5 2.3 %head_partial_kernel.1 = (f32[256,1024]{1,0:T(8,128)S(1)}, bf16[256,1024]{1,0:T(8,128)(2,1)S(1)}) custom-call(bf16[256,1024]{1,0:T(8,128)(2,1)S(1)} %get-tuple-element.49.refs_0_, bf16[256,1024]{1,0:T(8,128)(2,1)S(1)} %get-tuple-element.50.refs_1_, bf16[256,512]{1,0:T(8,128)(2,1)S(1)} %get-tuple-element.59.refs_2_, ...), custom_call_target="tpu_custom_call" | custom-call | tf_op jit(solution)/shard_map/head_partial_kernel/pallas_call | solution.py:46
  36.7 1.7 %collective-permute-start.11 = (bf16[256,1024]{1,0:T(8,128)(2,1)S(1)}, bf16[256,1024]{1,0:T(8,128)(2,1)S(1)}, u32[]{:S(2)}, u32[]{:S(2)}) collective-permute-start(bf16[256,1024]{1,0:T(8,128)(2,1)S(1)} %get-tuple-element.65), channel_id=1, source_target_pairs={{0,16},{8,24},{16,0},{24,8},{1,17},{9,25},{17,1},{25,9},{2,18},{10... | collective-permute-start | bytes 1572872 | tf_op jit(solution)/shard_map/ppermute | solution.py:440
  38.4 1.3 %weight_partial_kernel.2 = (f32[512,384]{1,0:T(8,128)S(1)}, bf16[512,384]{1,0:T(8,128)(2,1)S(1)}) custom-call(bf16[256,1024]{1,0:T(8,128)(2,1)S(1)} %get-tuple-element.49.refs_0_, bf16[256,1024]{1,0:T(8,128)(2,1)S(1)} %collective-permute-done.7.refs_8_.refs_1_, bf16[256,512]{1,0:T(8,128)(2,1)S(1)} %get-tuple-element.59.refs_2_, ...), custom_call_target="tpu_custom_call" | custom-call | tf_op jit(solution)/shard_map/weight_partial_kernel/pallas_call | solution.py:46
  39.7 1.6 %collective-permute-start.17 = (bf16[512,384]{1,0:T(8,128)(2,1)S(1)}, bf16[512,384]{1,0:T(8,128)(2,1)S(1)}, u32[]{:S(2)}, u32[]{:S(2)}) collective-permute-start(bf16[512,384]{1,0:T(8,128)(2,1)S(1)} %get-tuple-element.68.refs_12_.refs_6_), channel_id=1, source_target_pairs={{0,1},{1,0},{2,3},{3,2},{4,5},{5,4},{6,7},{7,6},{8,9},{9,8},{10,11... | collective-permute-start | bytes 1179656 | tf_op jit(solution)/shard_map/ppermute | solution.py:446
  41.3 1.9 %collective-permute-done.18.refs_7_ = bf16[256,640]{1,0:T(8,128)(2,1)S(1)} collective-permute-done((bf16[256,640]{1,0:T(8,128)(2,1)S(1)}, bf16[256,640]{1,0:T(8,128)(2,1)S(1)}, u32[]{:S(2)}, u32[]{:S(2)}) %collective-permute-start.18) | collective-permute-done | bytes 327712 | tf_op jit(solution)/shard_map/ppermute | solution.py:440
  43.4 0.5 collective-permute-start.21
  43.9 0.9 %collective-permute-done.20.refs_9_ = bf16[256,320]{1,0:T(8,128)(2,1)S(1)} collective-permute-done((bf16[256,320]{1,0:T(8,128)(2,1)S(1)}, bf16[256,320]{1,0:T(8,128)(2,1)S(1)}, u32[]{:S(2)}, u32[]{:S(2)}) %collective-permute-start.20) | collective-permute-done | bytes 163872 | tf_op jit(solution)/shard_map/ppermute | solution.py:437
  45.1 1.8 %weight_partial_kernel.3 = (f32[512,640]{1,0:T(8,128)S(1)}, bf16[512,640]{1,0:T(8,128)(2,1)S(1)}) custom-call(bf16[256,1024]{1,0:T(8,128)(2,1)S(1)} %get-tuple-element.49.refs_0_, bf16[256,1024]{1,0:T(8,128)(2,1)S(1)} %collective-permute-done.7.refs_8_.refs_1_, bf16[256,512]{1,0:T(8,128)(2,1)S(1)} %get-tuple-element.59.refs_2_, ...), custom_call_target="tpu_custom_call" | custom-call | tf_op jit(solution)/shard_map/weight_partial_kernel/pallas_call | solution.py:46
  46.9 1.8 %collective-permute-start.25 = (bf16[512,640]{1,0:T(8,128)(2,1)S(1)}, bf16[512,640]{1,0:T(8,128)(2,1)S(1)}, u32[]{:S(2)}, u32[]{:S(2)}) collective-permute-start(bf16[512,640]{1,0:T(8,128)(2,1)S(1)} %get-tuple-element.70.refs_7_), channel_id=1, source_target_pairs={{0,1},{1,0},{2,3},{3,2},{4,5},{5,4},{6,7},{7,6},{8,9},{9,8},{10,11... | collective-permute-start | bytes 1966088 | tf_op jit(solution)/shard_map/ppermute | solution.py:446
  48.8 4.8 %collective-permute-done.11.refs_2_ = bf16[256,1024]{1,0:T(8,128)(2,1)S(1)} collective-permute-done((bf16[256,1024]{1,0:T(8,128)(2,1)S(1)}, bf16[256,1024]{1,0:T(8,128)(2,1)S(1)}, u32[]{:S(2)}, u32[]{:S(2)}) %collective-permute-start.11) | collective-permute-done | bytes 524320 | tf_op jit(solution)/shard_map/ppermute | solution.py:440
  54.1 1.5 %collective-permute-done.22.refs_4_.refs_9_ = bf16[128,1024]{1,0:T(8,128)(2,1)S(1)} collective-permute-done((bf16[128,1024]{1,0:T(8,128)(2,1)S(1)}, bf16[128,1024]{1,0:T(8,128)(2,1)S(1)}, u32[]{:S(2)}, u32[]{:S(2)}) %collective-permute-start.22) | collective-permute-done | bytes 262176 | tf_op jit(solution)/shard_map/ppermute | solution.py:437
  55.7 1.5 %collective-permute-start.23 = (bf16[128,512]{1,0:T(8,128)(2,1)S(1)}, bf16[128,512]{1,0:T(8,128)(2,1)S(1)}, u32[]{:S(2)}, u32[]{:S(2)}) collective-permute-start(bf16[128,512]{1,0:T(8,128)(2,1)S(1)} %chip_total_kernel.3), channel_id=1, source_target_pairs={{16,0},{24,8},{17,1},{25,9},{18,2},{26,10},{19,3},{27,11},{20,4},{... | collective-permute-start | bytes 393224 | tf_op jit(solution)/shard_map/ppermute | solution.py:563
  57.2 1.9 %local_grads_kernel.1 = (f32[256,1024]{1,0:T(8,128)S(1)}, f32[256,256]{1,0:T(8,128)S(1)}, f32[256,128]{1,0:T(8,128)S(1)}) custom-call(f32[8,1024]{1,0:T(8,128)S(1)} %get-tuple-element.47.refs_1_.refs_0_, bf16[256,1024]{1,0:T(8,128)(2,1)S(1)} %bitcast.13, bf16[256,1024]{1,0:T(8,128)(2,1)S(1)} %get-tuple-element.71.refs_2_, bf16[256,128]{1,0:T(8,128)(2,1)S(1)} %bitcast.21, ...), custom_call_target="tpu_custom_call" | custom-call | tf_op jit(solution)/shard_map/local_grads_kernel/pallas_call | solution.py:46
  59.1 0.9 %group_sums_kernel.1 = (f32[256,128]{1,0:T(8,128)S(1)}, f32[256,128]{1,0:T(8,128)}) custom-call(bf16[256,128]{1,0:T(8,128)(2,1)S(1)} %bitcast.22, bf16[256,128]{1,0:T(8,128)(2,1)S(1)} %bitcast.18, f32[256,256]{1,0:T(8,128)S(1)} %get-tuple-element.75.refs_2_, f32[256,128]{1,0:T(8,128)S(1)} %get-tuple-element.76.refs_3_), custom_call_target="tpu_custom_call" | custom-call | tf_op jit(solution)/shard_map/group_sums_kernel/pallas_call | solution.py:46
  60.0 3.1 %collective-permute-done.23.refs_7_ = bf16[128,512]{1,0:T(8,128)(2,1)S(1)} collective-permute-done((bf16[128,512]{1,0:T(8,128)(2,1)S(1)}, bf16[128,512]{1,0:T(8,128)(2,1)S(1)}, u32[]{:S(2)}, u32[]{:S(2)}) %collective-permute-start.23) | collective-permute-done | bytes 131104 | tf_op jit(solution)/shard_map/ppermute | solution.py:563
  63.2 1.4 %collective-permute-done.25.refs_13_ = bf16[512,640]{1,0:T(8,128)(2,1)S(1)} collective-permute-done((bf16[512,640]{1,0:T(8,128)(2,1)S(1)}, bf16[512,640]{1,0:T(8,128)(2,1)S(1)}, u32[]{:S(2)}, u32[]{:S(2)}) %collective-permute-start.25) | collective-permute-done | bytes 655392 | tf_op jit(solution)/shard_map/ppermute | solution.py:446
  64.6 2.1 %last_kernel.1 = (bf16[256,1024]{1,0:T(8,128)(2,1)}, f32[256,128]{1,0:T(8,128)}, f32[512,1024]{1,0:T(8,128)}) custom-call(f32[8,1024]{1,0:T(8,128)S(1)} %get-tuple-element.47.refs_1_.refs_0_, bf16[256,128]{1,0:T(8,128)(2,1)S(1)} %bitcast.23, f32[256,1024]{1,0:T(8,128)S(1)} %get-tuple-element.48.refs_2_, f32[256,128]{1,0:T(8,128)S(1)} %get-tuple-element.77.refs_3_, ...), custom_call_target="tpu_custom_call" | custom-call | tf_op jit(solution)/shard_map/last_kernel/pallas_call | solution.py:46
  (57 shorter events, 5.3 us)
Async XLA Ops:
  0.6 7.1 %copy-start.7 = (f32[1,16,256]{2,1,0:T(8,128)S(1)}, f32[1,16,256]{2,1,0:T(8,128)}, u32[]{:S(2)}) copy-start(f32[1,16,256]{2,1,0:T(8,128)} %param.12) | copy-start | bytes 49156
  0.6 7.1 %copy-start.8 = (f32[16]{0:T(128)S(1)}, f32[16]{0:T(128)}, u32[]{:S(2)}) copy-start(f32[16]{0:T(128)} %refs_1_.1) | copy-start | bytes 196
  0.7 7.1 %copy-start.9 = (f32[16]{0:T(128)S(1)}, f32[16]{0:T(128)}, u32[]{:S(2)}) copy-start(f32[16]{0:T(128)} %refs_3_.1) | copy-start | bytes 196
  0.7 7.0 %collective-permute-start = (bf16[512,1024]{1,0:T(8,128)(2,1)}, bf16[512,1024]{1,0:T(8,128)(2,1)S(1)}, u32[]{:S(2)}, u32[]{:S(2)}) collective-permute-start(bf16[512,1024]{1,0:T(8,128)(2,1)} %refs_6_.1), channel_id=1, source_target_pairs={{0,8},{8,0},{16,24},{24,16},{1,9},{9,1},{17,25},{25,17},{2,10},{10... | collective-permute-start | bytes 3145736 | tf_op jit(solution)/shard_map/ppermute | solution.py:437
  1.2 26.6 %collective-permute-start.8 = (bf16[512,1024]{1,0:T(8,128)(2,1)}, bf16[512,1024]{1,0:T(8,128)(2,1)S(1)}, u32[]{:S(2)}, u32[]{:S(2)}) collective-permute-start(bf16[512,1024]{1,0:T(8,128)(2,1)} %refs_6_.1), channel_id=1, source_target_pairs={{0,1},{1,0},{2,3},{3,2},{4,5},{5,4},{6,7},{7,6},{8,9},{9,8},{10,11... | collective-permute-start | bytes 3145736 | tf_op jit(solution)/shard_map/ppermute | solution.py:446
  5.4 5.5 %copy-start.1 = (bf16[1,256,4096]{2,1,0:T(8,128)(2,1)S(1)}, bf16[1,256,4096]{2,1,0:T(8,128)(2,1)}, u32[]{:S(2)}) copy-start(bf16[1,256,4096]{2,1,0:T(8,128)(2,1)} %param.16) | copy-start | bytes 6291460
  5.5 14.1 %collective-permute-start.1 = (bf16[256,1024]{1,0:T(8,128)(2,1)S(1)}, bf16[256,1024]{1,0:T(8,128)(2,1)S(1)}, u32[]{:S(2)}, u32[]{:S(2)}) collective-permute-start(bf16[256,1024]{1,0:T(8,128)(2,1)S(1)} %send_kernel.1.refs_8_), channel_id=1, source_target_pairs={{0,16},{8,24},{16,0},{24,8},{1,17},{9,25},{17,1},{25,9},{2,18},{10... | collective-permute-start | bytes 1572872 | tf_op jit(solution)/shard_map/ppermute | solution.py:440
  11.0 13.2 %collective-permute-start.7 = (bf16[256,1024]{1,0:T(8,128)(2,1)S(1)}, bf16[256,1024]{1,0:T(8,128)(2,1)S(1)}, u32[]{:S(2)}, u32[]{:S(2)}) collective-permute-start(bf16[256,1024]{1,0:T(8,128)(2,1)S(1)} %get-tuple-element.50.refs_1_), channel_id=1, source_target_pairs={{0,8},{8,0},{16,24},{24,16},{1,9},{9,1},{17,25},{25,17},{2,10},{10... | collective-permute-start | bytes 1572872 | tf_op jit(solution)/shard_map/ppermute | solution.py:437
  11.1 1.9 %collective-permute-start.3 = (f32[8,1024]{1,0:T(8,128)S(1)}, f32[8,1024]{1,0:T(8,128)S(1)}, u32[]{:S(2)}, u32[]{:S(2)}) collective-permute-start(f32[8,1024]{1,0:T(8,128)S(1)} %get-tuple-element.47.refs_1_.refs_0_), channel_id=1, source_target_pairs={{0,8},{8,0},{16,24},{24,16},{1,9},{9,1},{17,25},{25,17},{2,10},{10... | collective-permute-start | bytes 98312 | tf_op jit(solution)/shard_map/ppermute | solution.py:437
  11.6 2.7 %collective-permute-start.4 = (bf16[128,512]{1,0:T(8,128)(2,1)S(1)}, bf16[128,512]{1,0:T(8,128)(2,1)S(1)}, u32[]{:S(2)}, u32[]{:S(2)}) collective-permute-start(bf16[128,512]{1,0:T(8,128)(2,1)S(1)} %get-tuple-element.56), channel_id=1, source_target_pairs={{0,8},{8,0},{16,24},{24,16},{1,9},{9,1},{17,25},{25,17},{2,10},{10... | collective-permute-start | bytes 393224 | tf_op jit(solution)/shard_map/ppermute | solution.py:437
  13.0 1.3 %collective-permute-start.5 = (bf16[128,512]{1,0:T(8,128)(2,1)S(1)}, bf16[128,512]{1,0:T(8,128)(2,1)S(1)}, u32[]{:S(2)}, u32[]{:S(2)}) collective-permute-start(bf16[128,512]{1,0:T(8,128)(2,1)S(1)} %get-tuple-element.57), channel_id=1, source_target_pairs={{0,8},{8,0},{16,24},{24,16},{1,9},{9,1},{17,25},{25,17},{2,10},{10... | collective-permute-start | bytes 393224 | tf_op jit(solution)/shard_map/ppermute | solution.py:437
  14.5 9.7 %collective-permute-start.6 = (bf16[128,1024]{1,0:T(8,128)(2,1)S(1)}, bf16[128,1024]{1,0:T(8,128)(2,1)S(1)}, u32[]{:S(2)}, u32[]{:S(2)}) collective-permute-start(bf16[128,1024]{1,0:T(8,128)(2,1)S(1)} %chip_total_kernel.2), channel_id=1, source_target_pairs={{0,16},{8,24},{1,17},{9,25},{2,18},{10,26},{3,19},{11,27},{4,20},{... | collective-permute-start | bytes 786440 | tf_op jit(solution)/shard_map/ppermute | solution.py:496
  19.5 13.2 %collective-permute-start.2 = (bf16[256,1024]{1,0:T(8,128)(2,1)S(1)}, bf16[256,1024]{1,0:T(8,128)(2,1)S(1)}, u32[]{:S(2)}, u32[]{:S(2)}) collective-permute-start(bf16[256,1024]{1,0:T(8,128)(2,1)S(1)} %collective-permute-done.1.refs_1_), channel_id=1, source_target_pairs={{0,2},{2,0},{4,6},{6,4},{1,3},{3,1},{5,7},{7,5},{8,10},{10,8},{12,... | collective-permute-start | bytes 1572872 | tf_op jit(solution)/shard_map/ppermute | solution.py:443
  24.5 8.9 %copy-start.6 = (bf16[512,1024]{1,0:T(8,128)(2,1)S(1)}, bf16[512,1024]{1,0:T(8,128)(2,1)}, u32[]{:S(2)}) copy-start(bf16[512,1024]{1,0:T(8,128)(2,1)} %refs_6_.1) | copy-start | bytes 3145732
  27.8 5.1 %collective-permute-start.10 = (bf16[256,1024]{1,0:T(8,128)(2,1)S(1)}, bf16[256,1024]{1,0:T(8,128)(2,1)S(1)}, u32[]{:S(2)}, u32[]{:S(2)}) collective-permute-start(bf16[256,1024]{1,0:T(8,128)(2,1)S(1)} %get-tuple-element.90), channel_id=1, source_target_pairs={{0,8},{8,0},{16,24},{24,16},{1,9},{9,1},{17,25},{25,17},{2,10},{10... | collective-permute-start | bytes 1572872 | tf_op jit(solution)/shard_map/ppermute | solution.py:437
  27.9 5.5 %collective-permute-start.9 = (bf16[256,1024]{1,0:T(8,128)(2,1)S(1)}, bf16[256,1024]{1,0:T(8,128)(2,1)S(1)}, u32[]{:S(2)}, u32[]{:S(2)}) collective-permute-start(bf16[256,1024]{1,0:T(8,128)(2,1)S(1)} %get-tuple-element.91), channel_id=1, source_target_pairs={{0,8},{8,0},{16,24},{24,16},{1,9},{9,1},{17,25},{25,17},{2,10},{10... | collective-permute-start | bytes 1572872 | tf_op jit(solution)/shard_map/ppermute | solution.py:437
  28.4 7.8 %collective-permute-start.14 = (bf16[256,384]{1,0:T(8,128)(2,1)S(1)}, bf16[256,384]{1,0:T(8,128)(2,1)S(1)}, u32[]{:S(2)}, u32[]{:S(2)}) collective-permute-start(bf16[256,384]{1,0:T(8,128)(2,1)S(1)} %get-tuple-element.66.refs_6_), channel_id=1, source_target_pairs={{0,16},{8,24},{16,0},{24,8},{1,17},{9,25},{17,1},{25,9},{2,18},{10... | collective-permute-start | bytes 589832 | tf_op jit(solution)/shard_map/ppermute | solution.py:440
  30.1 13.1 %collective-permute-start.18 = (bf16[256,640]{1,0:T(8,128)(2,1)S(1)}, bf16[256,640]{1,0:T(8,128)(2,1)S(1)}, u32[]{:S(2)}, u32[]{:S(2)}) collective-permute-start(bf16[256,640]{1,0:T(8,128)(2,1)S(1)} %get-tuple-element.58.refs_3_.refs_6_), channel_id=1, source_target_pairs={{0,16},{8,24},{16,0},{24,8},{1,17},{9,25},{17,1},{25,9},{2,18},{10... | collective-permute-start | bytes 983048 | tf_op jit(solution)/shard_map/ppermute | solution.py:440
  32.8 3.9 %collective-permute-start.12 = (bf16[256,512]{1,0:T(8,128)(2,1)S(1)}, bf16[256,512]{1,0:T(8,128)(2,1)S(1)}, u32[]{:S(2)}, u32[]{:S(2)}) collective-permute-start(bf16[256,512]{1,0:T(8,128)(2,1)S(1)} %get-tuple-element.61.refs_4_), channel_id=1, source_target_pairs={{0,8},{8,0},{16,24},{24,16},{1,9},{9,1},{17,25},{25,17},{2,10},{10... | collective-permute-start | bytes 786440 | tf_op jit(solution)/shard_map/ppermute | solution.py:437
  32.9 5.5 %collective-permute-start.13 = (bf16[256,512]{1,0:T(8,128)(2,1)S(1)}, bf16[256,512]{1,0:T(8,128)(2,1)S(1)}, u32[]{:S(2)}, u32[]{:S(2)}) collective-permute-start(bf16[256,512]{1,0:T(8,128)(2,1)S(1)} %get-tuple-element.62.refs_5_), channel_id=1, source_target_pairs={{0,8},{8,0},{16,24},{24,16},{1,9},{9,1},{17,25},{25,17},{2,10},{10... | collective-permute-start | bytes 786440 | tf_op jit(solution)/shard_map/ppermute | solution.py:437
  33.4 2.9 %collective-permute-start.15 = (bf16[256,384]{1,0:T(8,128)(2,1)S(1)}, bf16[256,384]{1,0:T(8,128)(2,1)S(1)}, u32[]{:S(2)}, u32[]{:S(2)}) collective-permute-start(bf16[256,384]{1,0:T(8,128)(2,1)S(1)} %get-tuple-element.66.refs_6_), channel_id=1, source_target_pairs={{0,8},{8,0},{16,24},{24,16},{1,9},{9,1},{17,25},{25,17},{2,10},{10... | collective-permute-start | bytes 589832 | tf_op jit(solution)/shard_map/ppermute | solution.py:437
  36.1 2.3 %collective-permute-start.16 = (bf16[256,384]{1,0:T(8,128)(2,1)S(1)}, bf16[256,384]{1,0:T(8,128)(2,1)S(1)}, u32[]{:S(2)}, u32[]{:S(2)}) collective-permute-start(bf16[256,384]{1,0:T(8,128)(2,1)S(1)} %collective-permute-done.14.refs_7_), channel_id=1, source_target_pairs={{0,8},{8,0},{16,24},{24,16},{1,9},{9,1},{17,25},{25,17},{2,10},{10... | collective-permute-start | bytes 589832 | tf_op jit(solution)/shard_map/ppermute | solution.py:437
  36.3 7.6 %collective-permute-start.19 = (bf16[256,640]{1,0:T(8,128)(2,1)S(1)}, bf16[256,640]{1,0:T(8,128)(2,1)S(1)}, u32[]{:S(2)}, u32[]{:S(2)}) collective-permute-start(bf16[256,640]{1,0:T(8,128)(2,1)S(1)} %get-tuple-element.58.refs_3_.refs_6_), channel_id=1, source_target_pairs={{0,8},{8,0},{16,24},{24,16},{1,9},{9,1},{17,25},{25,17},{2,10},{10... | collective-permute-start | bytes 983048 | tf_op jit(solution)/shard_map/ppermute | solution.py:437
  36.7 16.9 %collective-permute-start.11 = (bf16[256,1024]{1,0:T(8,128)(2,1)S(1)}, bf16[256,1024]{1,0:T(8,128)(2,1)S(1)}, u32[]{:S(2)}, u32[]{:S(2)}) collective-permute-start(bf16[256,1024]{1,0:T(8,128)(2,1)S(1)} %get-tuple-element.65), channel_id=1, source_target_pairs={{0,16},{8,24},{16,0},{24,8},{1,17},{9,25},{17,1},{25,9},{2,18},{10... | collective-permute-start | bytes 1572872 | tf_op jit(solution)/shard_map/ppermute | solution.py:440
  39.7 13.9 %collective-permute-start.17 = (bf16[512,384]{1,0:T(8,128)(2,1)S(1)}, bf16[512,384]{1,0:T(8,128)(2,1)S(1)}, u32[]{:S(2)}, u32[]{:S(2)}) collective-permute-start(bf16[512,384]{1,0:T(8,128)(2,1)S(1)} %get-tuple-element.68.refs_12_.refs_6_), channel_id=1, source_target_pairs={{0,1},{1,0},{2,3},{3,2},{4,5},{5,4},{6,7},{7,6},{8,9},{9,8},{10,11... | collective-permute-start | bytes 1179656 | tf_op jit(solution)/shard_map/ppermute | solution.py:446
  43.3 1.5 %collective-permute-start.20 = (bf16[256,320]{1,0:T(8,128)(2,1)S(1)}, bf16[256,320]{1,0:T(8,128)(2,1)S(1)}, u32[]{:S(2)}, u32[]{:S(2)}) collective-permute-start(bf16[256,320]{1,0:T(8,128)(2,1)S(1)} %get-tuple-element.93), channel_id=1, source_target_pairs={{0,8},{8,0},{16,24},{24,16},{1,9},{9,1},{17,25},{25,17},{2,10},{10... | collective-permute-start | bytes 491528 | tf_op jit(solution)/shard_map/ppermute | solution.py:437
  43.4 1.7 %collective-permute-start.21 = (bf16[256,320]{1,0:T(8,128)(2,1)S(1)}, bf16[256,320]{1,0:T(8,128)(2,1)S(1)}, u32[]{:S(2)}, u32[]{:S(2)}) collective-permute-start(bf16[256,320]{1,0:T(8,128)(2,1)S(1)} %get-tuple-element.92), channel_id=1, source_target_pairs={{0,8},{8,0},{16,24},{24,16},{1,9},{9,1},{17,25},{25,17},{2,10},{10... | collective-permute-start | bytes 491528 | tf_op jit(solution)/shard_map/ppermute | solution.py:437
  46.9 10.3 %copy-start.5 = (bf16[1,256,128]{2,1,0:T(8,128)(2,1)S(1)}, bf16[1,256,128]{2,1,0:T(8,128)(2,1)}, u32[]{:S(2)}) copy-start(bf16[1,256,128]{2,1,0:T(8,128)(2,1)} %param.10) | copy-start | bytes 196612
  46.9 17.7 %collective-permute-start.25 = (bf16[512,640]{1,0:T(8,128)(2,1)S(1)}, bf16[512,640]{1,0:T(8,128)(2,1)S(1)}, u32[]{:S(2)}, u32[]{:S(2)}) collective-permute-start(bf16[512,640]{1,0:T(8,128)(2,1)S(1)} %get-tuple-element.70.refs_7_), channel_id=1, source_target_pairs={{0,1},{1,0},{2,3},{3,2},{4,5},{5,4},{6,7},{7,6},{8,9},{9,8},{10,11... | collective-permute-start | bytes 1966088 | tf_op jit(solution)/shard_map/ppermute | solution.py:446
  54.0 1.6 %collective-permute-start.22 = (bf16[128,1024]{1,0:T(8,128)(2,1)S(1)}, bf16[128,1024]{1,0:T(8,128)(2,1)S(1)}, u32[]{:S(2)}, u32[]{:S(2)}) collective-permute-start(bf16[128,1024]{1,0:T(8,128)(2,1)S(1)} %get-tuple-element.82), channel_id=1, source_target_pairs={{0,8},{8,0},{16,24},{24,16},{1,9},{9,1},{17,25},{25,17},{2,10},{10... | collective-permute-start | bytes 786440 | tf_op jit(solution)/shard_map/ppermute | solution.py:437
  55.7 7.4 %collective-permute-start.23 = (bf16[128,512]{1,0:T(8,128)(2,1)S(1)}, bf16[128,512]{1,0:T(8,128)(2,1)S(1)}, u32[]{:S(2)}, u32[]{:S(2)}) collective-permute-start(bf16[128,512]{1,0:T(8,128)(2,1)S(1)} %chip_total_kernel.3), channel_id=1, source_target_pairs={{16,0},{24,8},{17,1},{25,9},{18,2},{26,10},{19,3},{27,11},{20,4},{... | collective-permute-start | bytes 393224 | tf_op jit(solution)/shard_map/ppermute | solution.py:563
  63.2 1.4 %collective-permute-start.24 = (bf16[128,512]{1,0:T(8,128)(2,1)S(1)}, bf16[128,512]{1,0:T(8,128)(2,1)S(1)}, u32[]{:S(2)}, u32[]{:S(2)}) collective-permute-start(bf16[128,512]{1,0:T(8,128)(2,1)S(1)} %collective-permute-done.23.refs_7_), channel_id=1, source_target_pairs={{0,8},{8,0},{16,24},{24,16},{1,9},{9,1},{17,25},{25,17},{2,10},{10... | collective-permute-start | bytes 393224 | tf_op jit(solution)/shard_map/ppermute | solution.py:437
  (4 other events, 9.4 us)
